TPU v7x, 128 devices: a whole 4x4x4 slice. The times are simulated.
128 devices in a mesh: samp: 8 (over x_hi, z), cent: 16 (over x_lo, y, core).
Axes of the slice: x: 4 (x_hi: 2, x_lo: 2; x = x_hi * 2 + x_lo), y: 4, z: 4, core: 2. Of those that a mesh axis runs over, the one named last changes fastest.
Arguments:
- embeddings: bfloat16 [8192, 1024], P(('samp', 'cent'))
- destination: int32 [8192], P(('samp', 'cent')), may hold values from 0 to 8191, as said below
- centroids: bfloat16 [65536, 1024], P('cent')
Outputs:
- new_centroids: float32 [65536, 1024], P(('cent', 'samp'))
- row_lse: float32 [8192], P(('samp', 'cent'))
Inputs may be any that keep to these rules, and one draw needn't show every extreme that they name: destination is a permutation of the 8192 rows; of the 64 rows that each device holds in file order, exactly 8 fall in each aligned block of 1024 logical rows.
All inputs are finite; a program needn't handle non-finite values.
Results may differ from a plain program's by a relative error of at most 0.00125.
Values may be sent and summed in bfloat16 or wider, within the bound.
No kernel may reach another device: no remote copies, remote signals or barrier semaphores. Data moves between devices by JAX's collectives and lax.ppermute only.
A program may use at most 128 MiB of HBM per device.

v0:
```python
import math

import jax
import jax.numpy as jnp
from jax import lax
from jax.sharding import PartitionSpec as P

inv_temp = 2.5
prior_mass = 0.25


def shards(embeddings, destination, centroids):
    rows_local = embeddings.shape[0]
    width = embeddings.shape[1]
    samp_count = lax.axis_size("samp")
    group_size = rows_local * lax.axis_size("cent")
    ordering = jnp.argsort(destination // group_size, stable=True)
    sent_rows = embeddings[ordering]
    sent_ids = destination[ordering]
    recv_rows, recv_ids = (
        lax.all_to_all(sent_rows, "samp", split_axis=0, concat_axis=0, tiled=True),
        lax.all_to_all(sent_ids, "samp", split_axis=0, concat_axis=0, tiled=True),
    )
    member_rows, row_ids = (
        lax.all_gather(recv_rows, "cent", axis=0, tiled=True),
        lax.all_gather(recv_ids, "cent", axis=0, tiled=True),
    )
    scale = inv_temp / math.sqrt(width)
    scores = (
        lax.dot_general(
            member_rows, centroids, (((1,), (1,)), ((), ())), preferred_element_type=jnp.float32
        )
        * scale
    )
    local_max = jnp.max(scores, axis=1)
    row_top = lax.pmax(local_max, "cent")
    row_total = lax.psum(jnp.sum(jnp.exp(scores - row_top[:, None]), axis=1), "cent")
    group_lse = row_top + jnp.log(row_total)
    weights = jnp.exp(scores - group_lse[:, None]).astype(jnp.bfloat16)
    positions = row_ids - lax.axis_index("samp") * group_size
    arranged = jnp.zeros((group_size,), jnp.float32).at[positions].set(group_lse)
    own_lse = lax.dynamic_slice_in_dim(arranged, lax.axis_index("cent") * rows_local, rows_local, 0)
    share = centroids.shape[0] // samp_count
    own_centers = lax.dynamic_slice_in_dim(centroids, lax.axis_index("samp") * share, share, 0)
    partial_sums = lax.dot_general(
        weights, member_rows, (((0,), (0,)), ((), ())), preferred_element_type=jnp.float32
    )
    partial_mass = jnp.sum(weights.astype(jnp.float32), axis=0)
    center_sums, soft_mass = (
        lax.psum_scatter(partial_sums, "samp", scatter_dimension=0, tiled=True),
        lax.psum_scatter(partial_mass, "samp", scatter_dimension=0, tiled=True),
    )
    new_centers = (center_sums + prior_mass * own_centers.astype(jnp.float32)) / (
        soft_mass + prior_mass
    )[:, None]
    return (new_centers, own_lse)


def solution(mesh):
    in_specs = (P(("samp", "cent"), None), P(("samp", "cent")), P("cent", None))
    out_specs = (P(("cent", "samp"), None), P(("samp", "cent")))
    return jax.shard_map(shards, mesh=mesh, in_specs=in_specs, out_specs=out_specs, check_vma=False)
```

profile of v0, /device:TPU:1, one launch (start us, length us, event | category | flops | bytes accessed | tf_op | source)
XLA Modules:
  0.0 356.0 jit_solution(17566504679550288717)
XLA Ops:
  7.2 0.0 all-gather.2.cloned.1.call-start
  7.2 0.7 and_select_fusion
  7.9 2.0 sort.17
  10.0 0.7 gather_fusion
  10.7 15.2 %all_to_all.24 = bf16[8,8,1024]{2,1,0:T(8,128)(2,1)} all-to-all(bf16[8,8,1024]{2,1,0:T(8,128)(2,1)S(1)} %bitcast.9), channel_id=1, replica_groups=mesh['samp'=8,'cent'=16] {'samp'}, dimensions={0} | all-to-all | bytes 262144 | tf_op jit(solution)/shard_map/all_to_all | solution.py:21
  25.9 0.0 all-gather.2.cloned.1.call-update
  25.9 0.0 reduce-scatter.2.cloned.1.call-start
  25.9 33.3 %all-gather.2.cloned.1.call-done = bf16[1024,1024]{1,0:T(8,128)(2,1)} async-done(((bf16[64,1024]{1,0:T(8,128)(2,1)}), bf16[1024,1024]{1,0:T(8,128)(2,1)}) %all-gather.2.cloned.1.call-update) | async-done | bytes 2097168 | tf_op jit(solution)/shard_map/all_gather | solution.py:25
  59.2 16.1 %multiply_reduce_fusion = (f32[1024]{0:T(1024)S(1)}, f32[1024,4096]{1,0:T(8,128)}) fusion(bf16[1024,1024]{1,0:T(8,128)(2,1)} %all-gather.2.cloned.1.call-done, bf16[4096,1024]{1,0:T(8,128)(2,1)} %param.5), kind=kOutput, calls=%fused_computation.6 | convolution fusion | flops 8598322176 | bytes 27267072 | tf_op jit(solution)/shard_map/dot_general | solution.py:30
  75.4 26.9 %pmax.7 = f32[1024]{0:T(1024)S(1)} all-reduce(f32[1024]{0:T(1024)S(1)} %get-tuple-element.4), channel_id=1, replica_groups=mesh['samp'=8,'cent'=16] {'cent'}, use_global_device_ids=true, to_apply=%region_2.3 | all-reduce | flops 1024 | bytes 8192 | tf_op jit(solution)/shard_map/pmax | solution.py:36
  102.2 8.6 %exponential_reduce_fusion = f32[1024]{0:T(1024)S(1)} fusion(f32[1024,4096]{1,0:T(8,128)} %get-tuple-element.5, f32[1024]{0:T(1024)S(1)} %pmax.7), kind=kLoop, calls=%fused_computation.5 | loop fusion | flops 12581888 | bytes 16785408 | tf_op jit(solution)/shard_map/reduce_sum | solution.py:37
  110.9 29.0 %psum.7 = f32[1024]{0:T(1024)S(1)} all-reduce(f32[1024]{0:T(1024)S(1)} %exponential_reduce_fusion), channel_id=1, replica_groups=mesh['samp'=8,'cent'=16] {'cent'}, use_global_device_ids=true, to_apply=%region_4.5 | all-reduce | flops 1024 | bytes 8192 | tf_op jit(solution)/shard_map/psum | solution.py:37
  139.9 16.2 %fusion.2 = f32[4096,1024]{1,0:T(8,128)} fusion(bf16[1024,1024]{1,0:T(8,128)(2,1)S(1)} %copy-done.2, f32[1024,4096]{1,0:T(8,128)} %get-tuple-element.5, f32[1024]{0:T(1024)S(1)} %log_add_fusion), kind=kOutput, calls=%fused_computation.19 | convolution fusion | flops 8602517504 | bytes 35655680 | tf_op jit(solution)/shard_map/dot_general | solution.py:45
  156.1 0.6 copy-done.1
  156.7 0.8 gather_fusion.1
  157.5 0.7 all_to_all.19
  158.2 6.3 %all-to-all-start.1 = ((s32[8,8,1]{1,2,0:T(1,128)}), s32[8,8,1]{1,2,0:T(1,128)S(1)}, u32[]{:S(2)}, u32[]{:S(2)}) async-start(s32[8,8,1]{1,2,0:T(1,128)} %bitcast.2), calls=%async_computation.2 | async-start | bytes 8192 | tf_op jit(solution)/shard_map/all_to_all | solution.py:22
  164.5 0.6 dynamic-slice.1
  165.7 0.6 dynamic-slice
  167.0 4.0 %all-to-all-done.1 = s32[8,8,1]{1,2,0:T(1,128)S(1)} async-done(((s32[8,8,1]{1,2,0:T(1,128)}), s32[8,8,1]{1,2,0:T(1,128)S(1)}, u32[]{:S(2)}, u32[]{:S(2)}) %all-to-all-start.1) | async-done | bytes 288 | tf_op jit(solution)/shard_map/all_to_all | solution.py:22
  170.9 0.5 broadcast.30
  171.4 0.7 reduce.3
  172.1 0.1 reshape.38
  172.2 0.2 dynamic-update-slice
  172.4 7.1 %all-reduce = s32[1024]{0:T(1024)S(1)} all-reduce(s32[1024]{0:T(1024)S(1)} %dynamic-update-slice), channel_id=1, replica_groups=mesh['samp'=8,'cent'=16] {'cent'}, use_global_device_ids=true, to_apply=%add | all-reduce | flops 1024 | bytes 8192
  179.5 4.3 %scatter_custom_fusion = f32[1024]{0:T(1024)S(1)} fusion(s32[1024]{0:T(1024)S(1)} %compare_select_fusion, f32[1024]{0:T(1024)S(1)} %log_add_fusion, f32[]{:T(128)} %constant.15.clone.1), kind=kCustom, calls=%fused_computation.13 | custom fusion | bytes 4100 | tf_op jit(solution)/shard_map/scatter | solution.py:41
  183.8 0.6 dynamic_slice.7
  184.4 10.0 %convert_reduce_fusion = f32[4096]{0:T(1024)S(1)} fusion(f32[1024]{0:T(1024)S(1)} %log_add_fusion, f32[1024,4096]{1,0:T(8,128)} %get-tuple-element.5), kind=kLoop, calls=%fused_computation.3 | loop fusion | flops 20967424 | bytes 16797696 | tf_op jit(solution)/shard_map/reduce_sum | solution.py:48
  194.4 32.7 %all-reduce.1 = f32[4096]{0:T(1024)S(1)} all-reduce(f32[4096]{0:T(1024)S(1)} %convert_reduce_fusion), channel_id=3, replica_groups=mesh['samp'=8,'cent'=16] {'samp'}, use_global_device_ids=true, to_apply=%region_7.8.clone | all-reduce | flops 4096 | bytes 32768
  227.1 0.1 dynamic-slice_add_fusion
  227.1 118.4 %reduce-scatter.2.cloned.1.call-done = f32[512,1024]{1,0:T(8,128)} async-done(((f32[4096,1024]{1,0:T(8,128)}), f32[512,1024]{1,0:T(8,128)}) %reduce-scatter.2.cloned.1.call-update) | async-done | bytes 2097168 | tf_op jit(solution)/shard_map/reduce_scatter | solution.py:50
  345.5 3.6 %add_divide_fusion = f32[512,1024]{1,0:T(8,128)} fusion(f32[512,1024]{1,0:T(8,128)} %reduce-scatter.2.cloned.1.call-done, f32[512]{0:T(512)S(1)} %dynamic-slice_add_fusion, bf16[4096,1024]{1,0:T(8,128)(2,1)} %param.5, s32[]{:T(128)S(6)} %select_n.20), kind=kLoop, calls=%fused_computation.7 | loop fusion | flops 2097152 | bytes 5244932 | tf_op jit(solution)/shard_map/div | solution.py:53
  (16 shorter events, 0.1 us)
Async XLA Ops:
  7.2 2.8 copy-start
  7.2 52.1 %all-gather.2.cloned.1.call-start = ((), (), s32[]{:S(2)}) async-start(), calls=%async_computation.3 | async-start | bytes 2228224 | tf_op jit(solution)/shard_map/all_gather | solution.py:25
  25.9 319.7 %reduce-scatter.2.cloned.1.call-start = ((), (), s32[]{:S(2)}) async-start(), calls=%async_computation.4 | async-start | bytes 18874368 | tf_op jit(solution)/shard_map/reduce_scatter | solution.py:50
  75.4 64.6 %copy-start.2 = (bf16[1024,1024]{1,0:T(8,128)(2,1)S(1)}, bf16[1024,1024]{1,0:T(8,128)(2,1)}, u32[]{:S(2)}) copy-start(bf16[1024,1024]{1,0:T(8,128)(2,1)} %all-gather.2.cloned.1.call-done) | copy-start | bytes 6291460
  156.1 0.7 copy-start.1
  156.1 8.4 %copy-start.4 = (u32[128]{0:T(128)S(1)}, u32[128]{0:T(128)}, u32[]{:S(2)}) copy-start(u32[128]{0:T(128)} %constant.57) | copy-start | bytes 1540
  156.1 9.7 %copy-start.3 = (u32[128]{0:T(128)S(1)}, u32[128]{0:T(128)}, u32[]{:S(2)}) copy-start(u32[128]{0:T(128)} %constant.51) | copy-start | bytes 1540
  158.2 12.7 %all-to-all-start.1 = ((s32[8,8,1]{1,2,0:T(1,128)}), s32[8,8,1]{1,2,0:T(1,128)S(1)}, u32[]{:S(2)}, u32[]{:S(2)}) async-start(s32[8,8,1]{1,2,0:T(1,128)} %bitcast.2), calls=%async_computation.2 | async-start | bytes 8192 | tf_op jit(solution)/shard_map/all_to_all | solution.py:22
Sparse Core Ops, SparseCore 0:
  26.0 33.2 all-gather.1
  156.2 189.2 reduce-scatter.1
where the time goes:
time: 358 us; the launch traced here: 356 us
  waiting for transfers between devices  156 us (44%)
  blocking collectives  111 us (31%)
  matrix products  32.3 us (9%)
  other arithmetic  25.7 us (7%)
  between operations  15.4 us (4%)
  local copies, waits for them, and re-layouts  9.7 us (3%)
  starting transfers between devices  6.38 us (2%)
    reduce_scatter x1, waiting for transfers between devices, shards(): lax.psum_scatter(partial_sums, 'samp', scatter_dimension=0, tiled=True)  118 us
    unnamed x2, blocking collectives  39.8 us
    all_gather x1, waiting for transfers between devices, shards(): lax.all_gather(recv_rows, 'cent', axis=0, tiled=True)  33.3 us
    psum x1, blocking collectives, shards(): lax.psum(jnp.sum(jnp.exp(scores - row_top[:, None]), axis=1), 'cent')  29 us
    pmax x1, blocking collectives, shards(): row_top = lax.pmax(local_max, 'cent')  26.9 us
    dot_general x1, matrix products, shards(): lax.dot_general(weights, member_rows, (((0,), (0,)), ((), ())), preferred...  16.2 us
    dot_general x1, matrix products, shards(): lax.dot_general(member_rows, centroids, (((1,), (1,)), ((), ())), preferr...  16.1 us
    all_to_all x1, blocking collectives, shards(): lax.all_to_all(sent_rows, 'samp', split_axis=0, concat_axis=0, tiled=True)  15.2 us
  transfers between devices with their start and end apart: 3, of which 3 were waited for; matrix products, arithmetic and copies ran while one was open for 5% of the time, Pallas kernels for 0%

commit v1 on v0

v1 whole, which is shorter than its diff:
```python
import functools
import math

import jax
import jax.numpy as jnp
from jax import lax
from jax.experimental import pallas as pl
from jax.experimental.pallas import tpu as pltpu
from jax.sharding import PartitionSpec as P

inv_temp = 2.5
prior_mass = 0.25
BOTH = ("samp", "cent")
BIG, SMALL = 40, 24
TILE = 256
X, Y, Z = 0, 1, 2
ORDER_0 = (X, Y, Z)
ORDER_1 = (Z, X, Y)
ORDER_S = (Y, Z, X)


def place(x, y, z, core):
    return ((x // 2) * 4 + z) * 16 + (x % 2) * 8 + y * 2 + core


def fetch(value, axes, offset):
    pairs = []
    for x in range(4):
        for y in range(4):
            for z in range(4):
                for core in range(2):
                    at = [x, y, z]
                    at[axes[core]] = (at[axes[core]] + offset) % 4
                    pairs.append((place(*at, core), place(x, y, z, core)))
    return lax.ppermute(value, BOTH, pairs)


def swap_cores(value):
    pairs = [(i, i ^ 1) for i in range(128)]
    return lax.ppermute(value, BOTH, pairs)


def scores_kernel(factor, mine_ref, other_ref, rows_ref, p_ref, stat_ref):
    rows = rows_ref[...]
    tops, sums = [], []
    for half, cents in enumerate((mine_ref, other_ref)):
        for part in range(512 // TILE):
            s = lax.dot_general(
                cents[part * TILE : (part + 1) * TILE, :],
                rows,
                (((1,), (1,)), ((), ())),
                preferred_element_type=jnp.float32,
            )
            s = s * factor
            top = jnp.max(s, axis=0, keepdims=True)
            e = jnp.exp2(s - top)
            first = half * 512 + part * TILE
            p_ref[first : first + TILE, :] = e
            tops.append(top)
            sums.append(jnp.sum(e, axis=0, keepdims=True))
    stat_ref[...] = jnp.concatenate(tops + sums, axis=0)


def scores_call(mine, other, rows):
    n, width = rows.shape
    factor = inv_temp / math.sqrt(width) * math.log2(math.e)
    return pl.pallas_call(
        functools.partial(scores_kernel, factor),
        out_shape=(
            jax.ShapeDtypeStruct((1024, n), jnp.float32),
            jax.ShapeDtypeStruct((8, n), jnp.float32),
        ),
        compiler_params=pltpu.CompilerParams(vmem_limit_bytes=24 << 20),
        cost_estimate=pl.CostEstimate(
            flops=2 * 1024 * n * width, bytes_accessed=n * 6144 + (2 << 20), transcendentals=1024 * n
        ),
        name="scores",
    )(mine, other, rows)


def first_kernel(*refs):
    out_ref = refs[-1]
    at = 0
    for ref in refs[:-1]:
        n = ref.shape[1]
        top = jnp.max(ref[0:4, :], axis=0, keepdims=True)
        total = jnp.sum(ref[4:8, :] * jnp.exp2(ref[0:4, :] - top), axis=0, keepdims=True)
        out_ref[0:1, at : at + n] = top
        out_ref[1:2, at : at + n] = total
        at += n


def roll_within(value, dim, step, unit):
    inner = unit * 4**dim
    group = inner * 4
    size = value.shape[1]
    lane = lax.broadcasted_iota(jnp.int32, value.shape, 1) % group
    ahead = pltpu.roll(value, step * inner, 1)
    back = pltpu.roll(value, size - (group - step * inner), 1)
    return jnp.where(lane >= step * inner, ahead, back)


def merge_kernel(stage, core_ref, own_ref, one_ref, two_ref, three_ref, out_ref):
    first_core = core_ref[0] == 0
    cut = 64 * BIG
    small_0 = ORDER_S.index(ORDER_0[stage])
    small_1 = ORDER_S.index(ORDER_1[stage])
    big = [(own_ref[0:1, :cut], own_ref[1:2, :cut])]
    small = [(own_ref[0:1, cut:], own_ref[1:2, cut:])]
    for step, ref in ((1, one_ref), (2, two_ref), (3, three_ref)):
        big.append(tuple(roll_within(ref[k : k + 1, :cut], stage, step, BIG) for k in range(2)))
        pair = []
        for k in range(2):
            v = ref[k : k + 1, cut:]
            pair.append(
                jnp.where(first_core, roll_within(v, small_0, step, SMALL), roll_within(v, small_1, step, SMALL))
            )
        small.append(tuple(pair))
    for group, lanes in ((big, slice(0, cut)), (small, slice(cut, 4096))):
        top = functools.reduce(jnp.maximum, [t for t, _ in group])
        total = sum(l * jnp.exp2(t - top) for t, l in group)
        out_ref[0:1, lanes] = top
        out_ref[1:2, lanes] = total


def merge(stage, core, own):
    axes = (ORDER_0[stage], ORDER_1[stage])
    others = [fetch(own, axes, step) for step in (1, 2, 3)]
    vmem = pl.BlockSpec(memory_space=pltpu.VMEM)
    return pl.pallas_call(
        functools.partial(merge_kernel, stage),
        out_shape=jax.ShapeDtypeStruct(own.shape, own.dtype),
        in_specs=[pl.BlockSpec(memory_space=pltpu.SMEM), vmem, vmem, vmem, vmem],
        name="merge",
    )(core, own, *others)


def sums_kernel(half, count, pairs_ref, *refs):
    stats = refs[:count]
    ps = refs[count : 2 * count]
    rows = refs[2 * count : 3 * count]
    out_ref = refs[3 * count]
    p_bufs = refs[3 * count + 1 : 4 * count + 1]
    row_bufs = refs[4 * count + 1 : 5 * count + 1]
    sems = refs[5 * count + 1]
    copies = []
    for k in range(count):
        pair = (
            pltpu.make_async_copy(ps[k].at[pl.ds(half * 512, 512)], p_bufs[k], sems.at[0, k]),
            pltpu.make_async_copy(rows[k], row_bufs[k], sems.at[1, k]),
        )
        for copy in pair:
            copy.start()
        copies.append(pair)
    width = rows[0].shape[1]
    lse = pairs_ref[0:1, :] + jnp.log2(pairs_ref[1:2, :])
    at = 0
    for k in range(count):
        n = rows[k].shape[0]
        for copy in copies[k]:
            copy.wait()
        for part in range(512 // TILE):
            tile = half * (512 // TILE) + part
            lines = slice(part * TILE, (part + 1) * TILE)
            f = jnp.exp2(stats[k][tile : tile + 1, :] - lse[:, at : at + n])
            w = (p_bufs[k][lines, :] * f).astype(jnp.bfloat16)
            add = jnp.dot(w, row_bufs[k][...], preferred_element_type=jnp.float32)
            wide = w.astype(jnp.float32)
            mass = sum(wide[:, c : c + 128] for c in range(0, n, 128))
            if k == 0:
                out_ref[lines, :width] = add
                out_ref[lines, width:] = mass
            else:
                out_ref[lines, :width] += add
                out_ref[lines, width:] += mass
        at += n


def sums_call(half, pairs, stats, ps, rows):
    count = len(rows)
    width = rows[0].shape[1]
    vmem = pl.BlockSpec(memory_space=pltpu.VMEM)
    hbm = pl.BlockSpec(memory_space=pl.ANY)
    return pl.pallas_call(
        functools.partial(sums_kernel, half, count),
        out_shape=jax.ShapeDtypeStruct((512, width + 128), jnp.float32),
        in_specs=[vmem] * (1 + count) + [hbm] * (2 * count),
        scratch_shapes=[pltpu.VMEM((512, r.shape[0]), jnp.float32) for r in rows]
        + [pltpu.VMEM(r.shape, r.dtype) for r in rows]
        + [pltpu.SemaphoreType.DMA((2, count))],
        compiler_params=pltpu.CompilerParams(vmem_limit_bytes=40 << 20),
        cost_estimate=pl.CostEstimate(
            flops=2 * 512 * 4096 * width, bytes_accessed=18 << 20, transcendentals=8192
        ),
        name="sums",
    )(pairs, *stats, *ps, *rows)


def shards(embeddings, destination, centroids):
    core = lax.rem(lax.axis_index("cent"), 2)
    share = centroids.shape[0] // 8
    mine = lax.dynamic_slice_in_dim(centroids, lax.axis_index("samp") * share, share, 0)
    other = swap_cores(mine)
    big, small = embeddings[:BIG], embeddings[BIG:]
    for stage in range(3):
        big_axes = (ORDER_0[stage], ORDER_1[stage])
        small_axes = (ORDER_S[stage], ORDER_S[stage])
        bigs = [big] + [fetch(big, big_axes, step) for step in (1, 2, 3)]
        smalls = [small] + [fetch(small, small_axes, step) for step in (1, 2, 3)]
        if stage < 2:
            big, small = jnp.concatenate(bigs), jnp.concatenate(smalls)
    chunks = bigs + smalls
    ps, stats = zip(*[scores_call(mine, other, rows) for rows in chunks])
    pairs = pl.pallas_call(
        first_kernel, out_shape=jax.ShapeDtypeStruct((2, 4096), jnp.float32), name="first"
    )(*stats)
    core_word = core.astype(jnp.int32).reshape(1)
    for stage in range(3):
        pairs = merge(stage, core_word, pairs)
    theirs = sums_call(1, pairs, stats, ps, chunks)
    received = swap_cores(theirs)
    ours = sums_call(0, pairs, stats, ps, chunks)
    lse = (pairs[0] + jnp.log2(pairs[1])) * math.log(2.0)
    own = jnp.concatenate([lse[:BIG], lse[64 * BIG : 64 * BIG + SMALL]])
    spots = lax.broadcasted_iota(jnp.int32, (64, 8192), 1)
    spread = jnp.sum(jnp.where(spots == destination[:, None], own[:, None], 0.0), axis=0)
    arrived = lax.all_to_all(spread.reshape(128, 64), BOTH, split_axis=0, concat_axis=0, tiled=True)
    row_lse = jnp.sum(arrived, axis=0)
    width = embeddings.shape[1]
    both = ours + received
    mass = jnp.sum(both[:, width:], axis=1)
    new_centers = (both[:, :width] + prior_mass * mine.astype(jnp.float32)) / (mass + prior_mass)[:, None]
    return new_centers, row_lse


def solution(mesh):
    in_specs = (P(BOTH, None), P(BOTH), P("cent", None))
    out_specs = (P(("cent", "samp"), None), P(BOTH))
    return jax.shard_map(shards, mesh=mesh, in_specs=in_specs, out_specs=out_specs, check_vma=False)
```

time: 358 us -> 202 us (0.56)
  waiting for transfers between devices: 156 us -> 37.9 us
  blocking collectives: 111 us -> 0 us
  starting transfers between devices: 6.38 us -> 64.6 us
  Pallas kernels: 0 us -> 42.1 us
  local copies, waits for them, and re-layouts: 9.7 us -> 48.1 us
  matrix products: 32.3 us -> 0 us
  other arithmetic: 25.7 us -> 6.87 us
  between operations: 15.4 us -> 1.05 us
    reduce_scatter x1 -> x0, waiting for transfers between devices: 118 us -> none  [shards(): lax.psum_scatter(partial_sums, 'samp', scatter_dimension=0, tiled=True)]
    ppermute x0 -> x29, starting transfers between devices: none -> 60.1 us  [the longest x27 53.3 us: fetch(): return lax.ppermute(value, BOTH, pairs)]
    pallas_call x0 -> x14, Pallas kernels: none -> 42.1 us  [the longest x2 18.6 us: sums_call(): pl.pallas_call(functools.partial(sums_kernel, half, count), out_shape=jax...]
    unnamed x2 -> x0, blocking collectives: 39.8 us -> none
    unnamed x14 -> x122, local copies, waits for them, and re-layouts: 2.05 us -> 41.7 us
    ppermute x0 -> x29, waiting for transfers between devices: none -> 37.9 us  [the longest x27 37.9 us: fetch(): return lax.ppermute(value, BOTH, pairs)]
    all_gather x1 -> x0, waiting for transfers between devices: 33.3 us -> none  [shards(): lax.all_gather(recv_rows, 'cent', axis=0, tiled=True)]
    dot_general x2 -> x0, matrix products: 32.3 us -> none  [the longest x1 16.2 us: shards(): lax.dot_general(weights, member_rows, (((0,), (0,)), ((), ())), preferred...]
  transfers between devices with their start and end apart: 3 -> 30, of which waited for: 3 -> 12; matrix products, arithmetic and copies ran while one was open for 5% -> 6% of each run, Pallas kernels for 0% -> 12%
where the time goes in v1:
time: 202 us; the launch traced here: 201 us
  starting transfers between devices  64.6 us (32%)
  local copies, waits for them, and re-layouts  48.1 us (24%)
  Pallas kernels  42.1 us (21%)
  waiting for transfers between devices  37.9 us (19%)
  other arithmetic  6.87 us (3%)
    ppermute x27, starting transfers between devices, fetch(): return lax.ppermute(value, BOTH, pairs)  53.3 us
    unnamed x122, local copies, waits for them, and re-layouts  41.7 us
    ppermute x27, waiting for transfers between devices, fetch(): return lax.ppermute(value, BOTH, pairs)  37.9 us
    pallas_call x2, Pallas kernels, sums_call(): pl.pallas_call(functools.partial(sums_kernel, half, count), out_shape=jax...  18.6 us
    pallas_call x8, Pallas kernels, scores_call(): pl.pallas_call(functools.partial(scores_kernel, factor), out_shape=(jax.S...  16.5 us
    ppermute x2, starting transfers between devices, swap_cores(): return lax.ppermute(value, BOTH, pairs)  6.8 us
    pallas_call x3, Pallas kernels, merge(): pl.pallas_call(functools.partial(merge_kernel, stage), out_shape=jax.Shap...  5.49 us
    all_to_all x1, starting transfers between devices, shards(): lax.all_to_all(spread.reshape(128, 64), BOTH, split_axis=0, concat_axis=0...  4.52 us
  transfers between devices with their start and end apart: 30, of which 12 were waited for; matrix products, arithmetic and copies ran while one was open for 6% of the time, Pallas kernels for 12%

profile of v1, /device:TPU:1, one launch (start us, length us, event | category | flops | bytes accessed | tf_op | source)
XLA Modules:
  0.0 200.6 jit_solution(4402207284787877028)
XLA Ops:
  0.6 1.5 fusion.5
  2.2 4.6 %collective-permute-start.1 = (bf16[40,1024]{1,0:T(8,128)(2,1)S(1)}, bf16[40,1024]{1,0:T(8,128)(2,1)S(1)}, u32[]{:S(2)}, u32[]{:S(2)}) collective-permute-start(bf16[40,1024]{1,0:T(8,128)(2,1)S(1)} %get-tuple-element.36), channel_id=1, source_target_pairs={{8,0},{17,1},{24,16},{33,17},{40,32},{49,33},{56,48},{1,49},{10,2}... | collective-permute-start | bytes 245768 | tf_op jit(solution)/shard_map/ppermute | solution.py:35
  8.2 2.7 %collective-permute-start.10 = (bf16[24,1024]{1,0:T(8,128)(2,1)S(1)}, bf16[24,1024]{1,0:T(8,128)(2,1)S(1)}, u32[]{:S(2)}, u32[]{:S(2)}) collective-permute-start(bf16[24,1024]{1,0:T(8,128)(2,1)S(1)} %get-tuple-element.34), channel_id=1, source_target_pairs={{2,0},{3,1},{18,16},{19,17},{34,32},{35,33},{50,48},{51,49},{4,2},... | collective-permute-start | bytes 147464 | tf_op jit(solution)/shard_map/ppermute | solution.py:35
  15.4 1.9 collective-permute-start
  17.3 3.8 %collective-permute-start.13 = (bf16[96,1024]{1,0:T(8,128)(2,1)S(1)}, bf16[96,1024]{1,0:T(8,128)(2,1)S(1)}, u32[]{:S(2)}, u32[]{:S(2)}) collective-permute-start(bf16[96,1024]{1,0:T(8,128)(2,1)S(1)} %pad_maximum_fusion.1), channel_id=1, source_target_pairs={{16,0},{17,1},{32,16},{33,17},{48,32},{49,33},{0,48},{1,49},{18,2}... | collective-permute-start | bytes 589832 | tf_op jit(solution)/shard_map/ppermute | solution.py:35
  23.7 1.8 collective-permute-start.4
  26.2 2.8 %collective-permute-done.13 = bf16[96,1024]{1,0:T(8,128)(2,1)S(1)} collective-permute-done((bf16[96,1024]{1,0:T(8,128)(2,1)S(1)}, bf16[96,1024]{1,0:T(8,128)(2,1)S(1)}, u32[]{:S(2)}, u32[]{:S(2)}) %collective-permute-start.13) | collective-permute-done | bytes 196640 | tf_op jit(solution)/shard_map/ppermute | solution.py:35
  28.9 2.5 %collective-permute-start.5 = (bf16[160,1024]{1,0:T(8,128)(2,1)S(1)}, bf16[160,1024]{1,0:T(8,128)(2,1)S(1)}, u32[]{:S(2)}, u32[]{:S(2)}) collective-permute-start(bf16[160,1024]{1,0:T(8,128)(2,1)S(1)} %pad_maximum_fusion), channel_id=1, source_target_pairs={{4,0},{65,1},{20,16},{81,17},{36,32},{97,33},{52,48},{113,49},{6,2... | collective-permute-start | bytes 983048 | tf_op jit(solution)/shard_map/ppermute | solution.py:35
  32.8 2.3 %collective-permute-done.15 = bf16[96,1024]{1,0:T(8,128)(2,1)S(1)} collective-permute-done((bf16[96,1024]{1,0:T(8,128)(2,1)S(1)}, bf16[96,1024]{1,0:T(8,128)(2,1)S(1)}, u32[]{:S(2)}, u32[]{:S(2)}) %collective-permute-start.15) | collective-permute-done | bytes 196640 | tf_op jit(solution)/shard_map/ppermute | solution.py:35
  44.3 10.1 %collective-permute-done.16.rows_ref.refs_21_ = bf16[384,1024]{1,0:T(8,128)(2,1)S(1)} collective-permute-done((bf16[384,1024]{1,0:T(8,128)(2,1)}, bf16[384,1024]{1,0:T(8,128)(2,1)S(1)}, u32[]{:S(2)}, u32[]{:S(2)}) %collective-permute-start.16) | collective-permute-done | bytes 786464 | tf_op jit(solution)/shard_map/ppermute | solution.py:35
  54.5 1.7 collective-permute-start.18
  56.2 2.6 %scores.12 = (f32[1024,384]{1,0:T(8,128)S(1)}, f32[8,384]{1,0:T(8,128)S(1)}) custom-call(bf16[512,1024]{1,0:T(8,128)(2,1)S(1)} %constant_dynamic-slice_fusion.mine_ref, bf16[512,1024]{1,0:T(8,128)(2,1)S(1)} %collective-permute-done.other_ref, bf16[384,1024]{1,0:T(8,128)(2,1)} %constant_dynamic-update-slice_fusion.7.rows_ref.refs_20_), custom_call_target="tpu_custom_call" | custom-call | flops 805306368 | bytes 4456448 | tf_op jit(solution)/shard_map/scores/pallas_call | solution.py:67
  63.3 9.2 %collective-permute-done.18.rows_ref.refs_23_ = bf16[384,1024]{1,0:T(8,128)(2,1)S(1)} collective-permute-done((bf16[384,1024]{1,0:T(8,128)(2,1)}, bf16[384,1024]{1,0:T(8,128)(2,1)S(1)}, u32[]{:S(2)}, u32[]{:S(2)}) %collective-permute-start.18) | collective-permute-done | bytes 786464 | tf_op jit(solution)/shard_map/ppermute | solution.py:35
  76.5 3.4 %scores.8 = (f32[1024,640]{1,0:T(8,128)S(1)}, f32[8,640]{1,0:T(8,128)S(1)}) custom-call(bf16[512,1024]{1,0:T(8,128)(2,1)S(1)} %constant_dynamic-slice_fusion.mine_ref, bf16[512,1024]{1,0:T(8,128)(2,1)S(1)} %collective-permute-done.other_ref, bf16[640,1024]{1,0:T(8,128)(2,1)} %constant_dynamic-update-slice_fusion.rows_ref.refs_16_), custom_call_target="tpu_custom_call" | custom-call | flops 1342177280 | bytes 6029312 | tf_op jit(solution)/shard_map/scores/pallas_call | solution.py:67
  82.0 2.1 %scores.9 = (f32[1024,640]{1,0:T(8,128)S(1)}, f32[8,640]{1,0:T(8,128)S(1)}) custom-call(bf16[512,1024]{1,0:T(8,128)(2,1)S(1)} %constant_dynamic-slice_fusion.mine_ref, bf16[512,1024]{1,0:T(8,128)(2,1)S(1)} %collective-permute-done.other_ref, bf16[640,1024]{1,0:T(8,128)(2,1)S(1)} %collective-permute-done.7.rows_ref.refs_17_), custom_call_target="tpu_custom_call" | custom-call | flops 1342177280 | bytes 6029312 | tf_op jit(solution)/shard_map/scores/pallas_call | solution.py:67
  86.2 2.1 %scores.10 = (f32[1024,640]{1,0:T(8,128)S(1)}, f32[8,640]{1,0:T(8,128)S(1)}) custom-call(bf16[512,1024]{1,0:T(8,128)(2,1)S(1)} %constant_dynamic-slice_fusion.mine_ref, bf16[512,1024]{1,0:T(8,128)(2,1)S(1)} %collective-permute-done.other_ref, bf16[640,1024]{1,0:T(8,128)(2,1)S(1)} %collective-permute-done.8.rows_ref.refs_18_), custom_call_target="tpu_custom_call" | custom-call | flops 1342177280 | bytes 6029312 | tf_op jit(solution)/shard_map/scores/pallas_call | solution.py:67
  89.8 2.3 %scores.11 = (f32[1024,640]{1,0:T(8,128)S(1)}, f32[8,640]{1,0:T(8,128)S(1)}) custom-call(bf16[512,1024]{1,0:T(8,128)(2,1)S(1)} %constant_dynamic-slice_fusion.mine_ref, bf16[512,1024]{1,0:T(8,128)(2,1)S(1)} %collective-permute-done.other_ref, bf16[640,1024]{1,0:T(8,128)(2,1)S(1)} %collective-permute-done.9.rows_ref.refs_19_), custom_call_target="tpu_custom_call" | custom-call | flops 1342177280 | bytes 6029312 | tf_op jit(solution)/shard_map/scores/pallas_call | solution.py:67
  94.2 1.6 first.1.own_ref
  95.7 22.7 %collective-permute-start.19 = (f32[2,4096]{1,0:T(2,128)}, f32[2,4096]{1,0:T(2,128)S(1)}, u32[]{:S(2)}, u32[]{:S(2)}) collective-permute-start(f32[2,4096]{1,0:T(2,128)} %first.1.own_ref), channel_id=1, source_target_pairs={{8,0},{17,1},{24,16},{33,17},{40,32},{49,33},{56,48},{1,49},{10,2}... | collective-permute-start | bytes 98312 | tf_op jit(solution)/shard_map/ppermute | solution.py:35
  119.7 3.2 %collective-permute-done.20.two_ref = f32[2,4096]{1,0:T(2,128)S(1)} collective-permute-done((f32[2,4096]{1,0:T(2,128)}, f32[2,4096]{1,0:T(2,128)S(1)}, u32[]{:S(2)}, u32[]{:S(2)}) %collective-permute-start.20) | collective-permute-done | bytes 32800 | tf_op jit(solution)/shard_map/ppermute | solution.py:35
  123.6 1.9 merge.3.own_ref
  128.4 2.8 %collective-permute-done.23.two_ref = f32[2,4096]{1,0:T(2,128)S(1)} collective-permute-done((f32[2,4096]{1,0:T(2,128)}, f32[2,4096]{1,0:T(2,128)S(1)}, u32[]{:S(2)}, u32[]{:S(2)}) %collective-permute-start.23) | collective-permute-done | bytes 32800 | tf_op jit(solution)/shard_map/ppermute | solution.py:35
  132.4 1.8 merge.4.own_ref
  134.2 3.3 %collective-permute-start.25 = (f32[2,4096]{1,0:T(2,128)}, f32[2,4096]{1,0:T(2,128)S(1)}, u32[]{:S(2)}, u32[]{:S(2)}) collective-permute-start(f32[2,4096]{1,0:T(2,128)} %merge.4.own_ref), channel_id=1, source_target_pairs={{16,0},{3,1},{32,16},{19,17},{48,32},{35,33},{0,48},{51,49},{18,2}... | collective-permute-start | bytes 98312 | tf_op jit(solution)/shard_map/ppermute | solution.py:35
  138.9 3.2 %collective-permute-done.26.two_ref = f32[2,4096]{1,0:T(2,128)S(1)} collective-permute-done((f32[2,4096]{1,0:T(2,128)}, f32[2,4096]{1,0:T(2,128)S(1)}, u32[]{:S(2)}, u32[]{:S(2)}) %collective-permute-start.26) | collective-permute-done | bytes 32800 | tf_op jit(solution)/shard_map/ppermute | solution.py:35
  143.3 1.8 merge.5.pairs_ref
  156.1 9.4 %sums.3 = f32[512,1152]{1,0:T(8,128)} custom-call(f32[2,4096]{1,0:T(2,128)S(1)} %copy-done.26, f32[8,640]{1,0:T(8,128)S(1)} %copy-done.29, f32[8,640]{1,0:T(8,128)S(1)} %copy-done.31, f32[8,640]{1,0:T(8,128)S(1)} %copy-done.33, f32[8,640]{1,0:T(8,128)S(1)} %copy-done.36, f32[8,384]{1,0:T(8,128)S(1)} %copy-done.39, f32[8,384]{1,0:T(8,128)S(1)} %copy-done.41, ...), custom_call_target="tpu_custom_call" | custom-call | flops 4294967296 | bytes 18874368 | tf_op jit(solution)/shard_map/sums/pallas_call | solution.py:184
  165.5 4.9 %collective-permute-start.28 = (f32[512,1152]{1,0:T(8,128)}, f32[512,1152]{1,0:T(8,128)}, u32[]{:S(2)}, u32[]{:S(2)}) collective-permute-start(f32[512,1152]{1,0:T(8,128)} %sums.3), channel_id=1, source_target_pairs={{0,1},{1,0},{2,3},{3,2},{4,5},{5,4},{6,7},{7,6},{8,9},{9,8},{10,11... | collective-permute-start | bytes 7077896 | tf_op jit(solution)/shard_map/ppermute | solution.py:40
  171.6 4.5 %all-to-all-start = ((f32[128,1,64]{2,1,0:T(1,128)}), f32[128,1,64]{2,1,0:T(1,128)S(1)}, u32[]{:S(2)}, u32[]{:S(2)}) async-start(f32[128,1,64]{2,1,0:T(1,128)} %bitcast.3), calls=%async_computation | async-start | bytes 131072 | tf_op jit(solution)/shard_map/all_to_all | solution.py:227
  184.9 9.2 %sums.2 = f32[512,1152]{1,0:T(8,128)} custom-call(f32[2,4096]{1,0:T(2,128)S(1)} %copy-done.27, f32[8,640]{1,0:T(8,128)S(1)} %copy-done.29, f32[8,640]{1,0:T(8,128)S(1)} %copy-done.31, f32[8,640]{1,0:T(8,128)S(1)} %copy-done.34, f32[8,640]{1,0:T(8,128)S(1)} %copy-done.37, f32[8,384]{1,0:T(8,128)S(1)} %copy-done.39, f32[8,384]{1,0:T(8,128)S(1)} %copy-done.41, ...), custom_call_target="tpu_custom_call" | custom-call | flops 4294967296 | bytes 18874368 | tf_op jit(solution)/shard_map/sums/pallas_call | solution.py:184
  194.9 2.6 %add.24 = f32[512,1152]{1,0:T(8,128)S(1)} add(f32[512,1152]{1,0:T(8,128)} %sums.2, f32[512,1152]{1,0:T(8,128)} %collective-permute-done.28) | non-fusion elementwise | flops 589824 | bytes 7077888 | tf_op jit(solution)/shard_map/add | solution.py:230
  197.6 3.0 %fusion = f32[512,1024]{1,0:T(8,128)} fusion(f32[512,1152]{1,0:T(8,128)S(1)} %add.24, f32[512]{0:T(512)S(1)} %broadcast_add_fusion, bf16[4096,1024]{1,0:T(8,128)(2,1)} %param.5, s32[]{:T(128)S(6)} %select_n.7), kind=kLoop, calls=%fused_computation.1 | loop fusion | flops 2097152 | bytes 5244932 | tf_op jit(solution)/shard_map/div | solution.py:232
  (182 shorter events, 66.7 us)
Async XLA Ops:
  2.2 20.8 %collective-permute-start.1 = (bf16[40,1024]{1,0:T(8,128)(2,1)S(1)}, bf16[40,1024]{1,0:T(8,128)(2,1)S(1)}, u32[]{:S(2)}, u32[]{:S(2)}) collective-permute-start(bf16[40,1024]{1,0:T(8,128)(2,1)S(1)} %get-tuple-element.36), channel_id=1, source_target_pairs={{8,0},{17,1},{24,16},{33,17},{40,32},{49,33},{56,48},{1,49},{10,2}... | collective-permute-start | bytes 245768 | tf_op jit(solution)/shard_map/ppermute | solution.py:35
  6.7 16.2 %collective-permute-start.2 = (bf16[40,1024]{1,0:T(8,128)(2,1)S(1)}, bf16[40,1024]{1,0:T(8,128)(2,1)S(1)}, u32[]{:S(2)}, u32[]{:S(2)}) collective-permute-start(bf16[40,1024]{1,0:T(8,128)(2,1)S(1)} %get-tuple-element.36), channel_id=1, source_target_pairs={{64,0},{33,1},{80,16},{49,17},{96,32},{1,33},{112,48},{17,49},{66,... | collective-permute-start | bytes 245768 | tf_op jit(solution)/shard_map/ppermute | solution.py:35
  8.2 5.1 %collective-permute-start.10 = (bf16[24,1024]{1,0:T(8,128)(2,1)S(1)}, bf16[24,1024]{1,0:T(8,128)(2,1)S(1)}, u32[]{:S(2)}, u32[]{:S(2)}) collective-permute-start(bf16[24,1024]{1,0:T(8,128)(2,1)S(1)} %get-tuple-element.34), channel_id=1, source_target_pairs={{2,0},{3,1},{18,16},{19,17},{34,32},{35,33},{50,48},{51,49},{4,2},... | collective-permute-start | bytes 147464 | tf_op jit(solution)/shard_map/ppermute | solution.py:35
  10.9 4.5 %collective-permute-start.11 = (bf16[24,1024]{1,0:T(8,128)(2,1)S(1)}, bf16[24,1024]{1,0:T(8,128)(2,1)S(1)}, u32[]{:S(2)}, u32[]{:S(2)}) collective-permute-start(bf16[24,1024]{1,0:T(8,128)(2,1)S(1)} %get-tuple-element.34), channel_id=1, source_target_pairs={{4,0},{5,1},{20,16},{21,17},{36,32},{37,33},{52,48},{53,49},{6,2},... | collective-permute-start | bytes 147464 | tf_op jit(solution)/shard_map/ppermute | solution.py:35
  11.3 6.0 %collective-permute-start.12 = (bf16[24,1024]{1,0:T(8,128)(2,1)S(1)}, bf16[24,1024]{1,0:T(8,128)(2,1)S(1)}, u32[]{:S(2)}, u32[]{:S(2)}) collective-permute-start(bf16[24,1024]{1,0:T(8,128)(2,1)S(1)} %get-tuple-element.34), channel_id=1, source_target_pairs={{6,0},{7,1},{22,16},{23,17},{38,32},{39,33},{54,48},{55,49},{0,2},... | collective-permute-start | bytes 147464 | tf_op jit(solution)/shard_map/ppermute | solution.py:35
  13.2 10.4 %collective-permute-start.3 = (bf16[40,1024]{1,0:T(8,128)(2,1)S(1)}, bf16[40,1024]{1,0:T(8,128)(2,1)S(1)}, u32[]{:S(2)}, u32[]{:S(2)}) collective-permute-start(bf16[40,1024]{1,0:T(8,128)(2,1)S(1)} %get-tuple-element.36), channel_id=1, source_target_pairs={{72,0},{49,1},{88,16},{1,17},{104,32},{17,33},{120,48},{33,49},{74... | collective-permute-start | bytes 245768 | tf_op jit(solution)/shard_map/ppermute | solution.py:35
  15.4 39.1 %collective-permute-start = (bf16[512,1024]{1,0:T(8,128)(2,1)S(1)}, bf16[512,1024]{1,0:T(8,128)(2,1)S(1)}, u32[]{:S(2)}, u32[]{:S(2)}) collective-permute-start(bf16[512,1024]{1,0:T(8,128)(2,1)S(1)} %constant_dynamic-slice_fusion.mine_ref), channel_id=1, source_target_pairs={{0,1},{1,0},{2,3},{3,2},{4,5},{5,4},{6,7},{7,6},{8,9},{9,8},{10,11... | collective-permute-start | bytes 3145736 | tf_op jit(solution)/shard_map/ppermute | solution.py:40
  17.3 11.7 %collective-permute-start.13 = (bf16[96,1024]{1,0:T(8,128)(2,1)S(1)}, bf16[96,1024]{1,0:T(8,128)(2,1)S(1)}, u32[]{:S(2)}, u32[]{:S(2)}) collective-permute-start(bf16[96,1024]{1,0:T(8,128)(2,1)S(1)} %pad_maximum_fusion.1), channel_id=1, source_target_pairs={{16,0},{17,1},{32,16},{33,17},{48,32},{49,33},{0,48},{1,49},{18,2}... | collective-permute-start | bytes 589832 | tf_op jit(solution)/shard_map/ppermute | solution.py:35
  23.0 9.1 %collective-permute-start.14 = (bf16[96,1024]{1,0:T(8,128)(2,1)S(1)}, bf16[96,1024]{1,0:T(8,128)(2,1)S(1)}, u32[]{:S(2)}, u32[]{:S(2)}) collective-permute-start(bf16[96,1024]{1,0:T(8,128)(2,1)S(1)} %pad_maximum_fusion.1), channel_id=1, source_target_pairs={{32,0},{33,1},{48,16},{49,17},{0,32},{1,33},{16,48},{17,49},{34,2}... | collective-permute-start | bytes 589832 | tf_op jit(solution)/shard_map/ppermute | solution.py:35
  23.0 12.1 %collective-permute-start.15 = (bf16[96,1024]{1,0:T(8,128)(2,1)S(1)}, bf16[96,1024]{1,0:T(8,128)(2,1)S(1)}, u32[]{:S(2)}, u32[]{:S(2)}) collective-permute-start(bf16[96,1024]{1,0:T(8,128)(2,1)S(1)} %pad_maximum_fusion.1), channel_id=1, source_target_pairs={{48,0},{49,1},{0,16},{1,17},{16,32},{17,33},{32,48},{33,49},{50,2}... | collective-permute-start | bytes 589832 | tf_op jit(solution)/shard_map/ppermute | solution.py:35
  23.7 14.6 %collective-permute-start.4 = (bf16[160,1024]{1,0:T(8,128)(2,1)S(1)}, bf16[160,1024]{1,0:T(8,128)(2,1)S(1)}, u32[]{:S(2)}, u32[]{:S(2)}) collective-permute-start(bf16[160,1024]{1,0:T(8,128)(2,1)S(1)} %pad_maximum_fusion), channel_id=1, source_target_pairs={{2,0},{9,1},{18,16},{25,17},{34,32},{41,33},{50,48},{57,49},{4,2},... | collective-permute-start | bytes 983048 | tf_op jit(solution)/shard_map/ppermute | solution.py:35
  28.9 10.2 %collective-permute-start.5 = (bf16[160,1024]{1,0:T(8,128)(2,1)S(1)}, bf16[160,1024]{1,0:T(8,128)(2,1)S(1)}, u32[]{:S(2)}, u32[]{:S(2)}) collective-permute-start(bf16[160,1024]{1,0:T(8,128)(2,1)S(1)} %pad_maximum_fusion), channel_id=1, source_target_pairs={{4,0},{65,1},{20,16},{81,17},{36,32},{97,33},{52,48},{113,49},{6,2... | collective-permute-start | bytes 983048 | tf_op jit(solution)/shard_map/ppermute | solution.py:35
  32.1 8.1 %collective-permute-start.6 = (bf16[160,1024]{1,0:T(8,128)(2,1)S(1)}, bf16[160,1024]{1,0:T(8,128)(2,1)S(1)}, u32[]{:S(2)}, u32[]{:S(2)}) collective-permute-start(bf16[160,1024]{1,0:T(8,128)(2,1)S(1)} %pad_maximum_fusion), channel_id=1, source_target_pairs={{6,0},{73,1},{22,16},{89,17},{38,32},{105,33},{54,48},{121,49},{0,... | collective-permute-start | bytes 983048 | tf_op jit(solution)/shard_map/ppermute | solution.py:35
  35.8 18.6 %collective-permute-start.16 = (bf16[384,1024]{1,0:T(8,128)(2,1)}, bf16[384,1024]{1,0:T(8,128)(2,1)S(1)}, u32[]{:S(2)}, u32[]{:S(2)}) collective-permute-start(bf16[384,1024]{1,0:T(8,128)(2,1)} %constant_dynamic-update-slice_fusion.7.rows_ref.refs_20_), channel_id=1, source_target_pairs={{8,0},{9,1},{24,16},{25,17},{40,32},{41,33},{56,48},{57,49},{10,2}... | collective-permute-start | bytes 2359304 | tf_op jit(solution)/shard_map/ppermute | solution.py:35
  40.9 41.1 %collective-permute-start.7 = (bf16[640,1024]{1,0:T(8,128)(2,1)}, bf16[640,1024]{1,0:T(8,128)(2,1)S(1)}, u32[]{:S(2)}, u32[]{:S(2)}) collective-permute-start(bf16[640,1024]{1,0:T(8,128)(2,1)} %constant_dynamic-update-slice_fusion.rows_ref.refs_16_), channel_id=1, source_target_pairs={{16,0},{3,1},{32,16},{19,17},{48,32},{35,33},{0,48},{51,49},{18,2}... | collective-permute-start | bytes 3932168 | tf_op jit(solution)/shard_map/ppermute | solution.py:35
  42.2 44.0 %collective-permute-start.8 = (bf16[640,1024]{1,0:T(8,128)(2,1)}, bf16[640,1024]{1,0:T(8,128)(2,1)S(1)}, u32[]{:S(2)}, u32[]{:S(2)}) collective-permute-start(bf16[640,1024]{1,0:T(8,128)(2,1)} %constant_dynamic-update-slice_fusion.rows_ref.refs_16_), channel_id=1, source_target_pairs={{32,0},{5,1},{48,16},{21,17},{0,32},{37,33},{16,48},{53,49},{34,2}... | collective-permute-start | bytes 3932168 | tf_op jit(solution)/shard_map/ppermute | solution.py:35
  43.1 17.1 %collective-permute-start.17 = (bf16[384,1024]{1,0:T(8,128)(2,1)}, bf16[384,1024]{1,0:T(8,128)(2,1)S(1)}, u32[]{:S(2)}, u32[]{:S(2)}) collective-permute-start(bf16[384,1024]{1,0:T(8,128)(2,1)} %constant_dynamic-update-slice_fusion.7.rows_ref.refs_20_), channel_id=1, source_target_pairs={{64,0},{65,1},{80,16},{81,17},{96,32},{97,33},{112,48},{113,49},{6... | collective-permute-start | bytes 2359304 | tf_op jit(solution)/shard_map/ppermute | solution.py:35
  54.4 35.4 %collective-permute-start.9 = (bf16[640,1024]{1,0:T(8,128)(2,1)}, bf16[640,1024]{1,0:T(8,128)(2,1)S(1)}, u32[]{:S(2)}, u32[]{:S(2)}) collective-permute-start(bf16[640,1024]{1,0:T(8,128)(2,1)} %constant_dynamic-update-slice_fusion.rows_ref.refs_16_), channel_id=1, source_target_pairs={{48,0},{7,1},{0,16},{23,17},{16,32},{39,33},{32,48},{55,49},{50,2}... | collective-permute-start | bytes 3932168 | tf_op jit(solution)/shard_map/ppermute | solution.py:35
  54.5 18.0 %collective-permute-start.18 = (bf16[384,1024]{1,0:T(8,128)(2,1)}, bf16[384,1024]{1,0:T(8,128)(2,1)S(1)}, u32[]{:S(2)}, u32[]{:S(2)}) collective-permute-start(bf16[384,1024]{1,0:T(8,128)(2,1)} %constant_dynamic-update-slice_fusion.7.rows_ref.refs_20_), channel_id=1, source_target_pairs={{72,0},{73,1},{88,16},{89,17},{104,32},{105,33},{120,48},{121,49},... | collective-permute-start | bytes 2359304 | tf_op jit(solution)/shard_map/ppermute | solution.py:35
  89.8 55.3 %copy-start.41 = (f32[8,384]{1,0:T(8,128)S(1)}, f32[8,384]{1,0:T(8,128)}, u32[]{:S(2)}) copy-start(f32[8,384]{1,0:T(8,128)} %copy-done.40) | copy-start | bytes 36868
  89.8 55.3 %copy-start.43 = (f32[8,384]{1,0:T(8,128)S(1)}, f32[8,384]{1,0:T(8,128)}, u32[]{:S(2)}) copy-start(f32[8,384]{1,0:T(8,128)} %copy-done.42) | copy-start | bytes 36868
  95.7 24.0 %collective-permute-start.19 = (f32[2,4096]{1,0:T(2,128)}, f32[2,4096]{1,0:T(2,128)S(1)}, u32[]{:S(2)}, u32[]{:S(2)}) collective-permute-start(f32[2,4096]{1,0:T(2,128)} %first.1.own_ref), channel_id=1, source_target_pairs={{8,0},{17,1},{24,16},{33,17},{40,32},{49,33},{56,48},{1,49},{10,2}... | collective-permute-start | bytes 98312 | tf_op jit(solution)/shard_map/ppermute | solution.py:35
  118.4 4.5 %collective-permute-start.20 = (f32[2,4096]{1,0:T(2,128)}, f32[2,4096]{1,0:T(2,128)S(1)}, u32[]{:S(2)}, u32[]{:S(2)}) collective-permute-start(f32[2,4096]{1,0:T(2,128)} %first.1.own_ref), channel_id=1, source_target_pairs={{64,0},{33,1},{80,16},{49,17},{96,32},{1,33},{112,48},{17,49},{66,... | collective-permute-start | bytes 98312 | tf_op jit(solution)/shard_map/ppermute | solution.py:35
  118.4 4.5 %collective-permute-start.21 = (f32[2,4096]{1,0:T(2,128)}, f32[2,4096]{1,0:T(2,128)S(1)}, u32[]{:S(2)}, u32[]{:S(2)}) collective-permute-start(f32[2,4096]{1,0:T(2,128)} %first.1.own_ref), channel_id=1, source_target_pairs={{72,0},{49,1},{88,16},{1,17},{104,32},{17,33},{120,48},{33,49},{74... | collective-permute-start | bytes 98312 | tf_op jit(solution)/shard_map/ppermute | solution.py:35
  125.4 3.0 %collective-permute-start.22 = (f32[2,4096]{1,0:T(2,128)}, f32[2,4096]{1,0:T(2,128)S(1)}, u32[]{:S(2)}, u32[]{:S(2)}) collective-permute-start(f32[2,4096]{1,0:T(2,128)} %merge.3.own_ref), channel_id=1, source_target_pairs={{2,0},{9,1},{18,16},{25,17},{34,32},{41,33},{50,48},{57,49},{4,2},... | collective-permute-start | bytes 98312 | tf_op jit(solution)/shard_map/ppermute | solution.py:35
  126.6 4.6 %collective-permute-start.23 = (f32[2,4096]{1,0:T(2,128)}, f32[2,4096]{1,0:T(2,128)S(1)}, u32[]{:S(2)}, u32[]{:S(2)}) collective-permute-start(f32[2,4096]{1,0:T(2,128)} %merge.3.own_ref), channel_id=1, source_target_pairs={{4,0},{65,1},{20,16},{81,17},{36,32},{97,33},{52,48},{113,49},{6,2... | collective-permute-start | bytes 98312 | tf_op jit(solution)/shard_map/ppermute | solution.py:35
  126.6 4.6 %collective-permute-start.24 = (f32[2,4096]{1,0:T(2,128)}, f32[2,4096]{1,0:T(2,128)S(1)}, u32[]{:S(2)}, u32[]{:S(2)}) collective-permute-start(f32[2,4096]{1,0:T(2,128)} %merge.3.own_ref), channel_id=1, source_target_pairs={{6,0},{73,1},{22,16},{89,17},{38,32},{105,33},{54,48},{121,49},{0,... | collective-permute-start | bytes 98312 | tf_op jit(solution)/shard_map/ppermute | solution.py:35
  134.2 4.6 %collective-permute-start.25 = (f32[2,4096]{1,0:T(2,128)}, f32[2,4096]{1,0:T(2,128)S(1)}, u32[]{:S(2)}, u32[]{:S(2)}) collective-permute-start(f32[2,4096]{1,0:T(2,128)} %merge.4.own_ref), channel_id=1, source_target_pairs={{16,0},{3,1},{32,16},{19,17},{48,32},{35,33},{0,48},{51,49},{18,2}... | collective-permute-start | bytes 98312 | tf_op jit(solution)/shard_map/ppermute | solution.py:35
  137.5 4.5 %collective-permute-start.26 = (f32[2,4096]{1,0:T(2,128)}, f32[2,4096]{1,0:T(2,128)S(1)}, u32[]{:S(2)}, u32[]{:S(2)}) collective-permute-start(f32[2,4096]{1,0:T(2,128)} %merge.4.own_ref), channel_id=1, source_target_pairs={{32,0},{5,1},{48,16},{21,17},{0,32},{37,33},{16,48},{53,49},{34,2}... | collective-permute-start | bytes 98312 | tf_op jit(solution)/shard_map/ppermute | solution.py:35
  137.5 4.5 %collective-permute-start.27 = (f32[2,4096]{1,0:T(2,128)}, f32[2,4096]{1,0:T(2,128)S(1)}, u32[]{:S(2)}, u32[]{:S(2)}) collective-permute-start(f32[2,4096]{1,0:T(2,128)} %merge.4.own_ref), channel_id=1, source_target_pairs={{48,0},{7,1},{0,16},{23,17},{16,32},{39,33},{32,48},{55,49},{50,2}... | collective-permute-start | bytes 98312 | tf_op jit(solution)/shard_map/ppermute | solution.py:35
  165.5 29.4 %collective-permute-start.28 = (f32[512,1152]{1,0:T(8,128)}, f32[512,1152]{1,0:T(8,128)}, u32[]{:S(2)}, u32[]{:S(2)}) collective-permute-start(f32[512,1152]{1,0:T(8,128)} %sums.3), channel_id=1, source_target_pairs={{0,1},{1,0},{2,3},{3,2},{4,5},{5,4},{6,7},{7,6},{8,9},{9,8},{10,11... | collective-permute-start | bytes 7077896 | tf_op jit(solution)/shard_map/ppermute | solution.py:40
  171.6 22.6 %all-to-all-start = ((f32[128,1,64]{2,1,0:T(1,128)}), f32[128,1,64]{2,1,0:T(1,128)S(1)}, u32[]{:S(2)}, u32[]{:S(2)}) async-start(f32[128,1,64]{2,1,0:T(1,128)} %bitcast.3), calls=%async_computation | async-start | bytes 131072 | tf_op jit(solution)/shard_map/all_to_all | solution.py:227
  (54 other events, 381.2 us)

commit v2 on v1

v2 whole, which is shorter than its diff:
```python
import functools
import math

import jax
import jax.numpy as jnp
from jax import lax
from jax.experimental import pallas as pl
from jax.experimental.pallas import tpu as pltpu
from jax.sharding import PartitionSpec as P

inv_temp = 2.5
prior_mass = 0.25
BOTH = ("samp", "cent")
UNIT = 64
TILE = 512
X, Y, Z = 0, 1, 2
ORDERS = ((X, Y, Z), (Z, X, Y))


def place(x, y, z, core):
    return ((x // 2) * 4 + z) * 16 + (x % 2) * 8 + y * 2 + core


def fetch(value, stage, offset):
    pairs = []
    for x in range(4):
        for y in range(4):
            for z in range(4):
                for core in range(2):
                    at = [x, y, z]
                    axis = ORDERS[core][stage]
                    at[axis] = (at[axis] + offset) % 4
                    pairs.append((place(*at, core), place(x, y, z, core)))
    return lax.ppermute(value, BOTH, pairs)


def swap_cores(value):
    pairs = [(i, i ^ 1) for i in range(128)]
    return lax.ppermute(value, BOTH, pairs)


def scores_kernel(factor, mine_ref, other_ref, rows_ref, p_ref, stat_ref, buf, sems):
    rows = rows_ref[...]
    tops, sums, copies = [], [], []
    for half, cents in enumerate((mine_ref, other_ref)):
        s = lax.dot_general(
            cents[...], rows, (((1,), (1,)), ((), ())), preferred_element_type=jnp.float32
        )
        s = s * factor
        top = jnp.max(s, axis=0, keepdims=True)
        e = jnp.exp2(s - top)
        buf[half] = e
        copy = pltpu.make_async_copy(buf.at[half], p_ref.at[half], sems.at[half])
        copy.start()
        copies.append(copy)
        tops.append(top)
        sums.append(jnp.sum(e, axis=0, keepdims=True))
    stat_ref[...] = jnp.concatenate(tops + sums, axis=0)
    for copy in copies:
        copy.wait()


def scores_call(mine, other, rows):
    n, width = rows.shape
    factor = inv_temp / math.sqrt(width) * math.log2(math.e)
    vmem = pl.BlockSpec(memory_space=pltpu.VMEM)
    return pl.pallas_call(
        functools.partial(scores_kernel, factor),
        out_shape=(
            jax.ShapeDtypeStruct((2, 512, n), jnp.float32),
            jax.ShapeDtypeStruct((4, n), jnp.float32),
        ),
        in_specs=[vmem] * 3,
        out_specs=(pl.BlockSpec(memory_space=pl.ANY), vmem),
        scratch_shapes=[pltpu.VMEM((2, 512, n), jnp.float32), pltpu.SemaphoreType.DMA((2,))],
        compiler_params=pltpu.CompilerParams(vmem_limit_bytes=32 << 20),
        cost_estimate=pl.CostEstimate(
            flops=2 * 1024 * n * width, bytes_accessed=n * 6144 + (2 << 20), transcendentals=1024 * n
        ),
        name="scores",
    )(mine, other, rows)


def roll_within(value, dim, step):
    inner = UNIT * 4**dim
    group = inner * 4
    size = value.shape[1]
    lane = lax.broadcasted_iota(jnp.int32, value.shape, 1) % group
    ahead = pltpu.roll(value, step * inner, 1)
    back = pltpu.roll(value, size - group + step * inner, 1)
    return jnp.where(lane >= step * inner, ahead, back)


def first_kernel(spot_ref, *refs):
    out_ref = refs[-1]
    parts = []
    for ref in refs[:-1]:
        top = jnp.max(ref[0:2, :], axis=0, keepdims=True)
        total = jnp.sum(ref[2:4, :] * jnp.exp2(ref[0:2, :] - top), axis=0, keepdims=True)
        parts.append(top + jnp.log2(total))
    value = jnp.concatenate(parts, axis=1)
    for dim in range(3):
        value = roll_within(value, dim, spot_ref[dim])
    for line in range(8):
        piece = value[:, line * 512 : (line + 1) * 512]
        out_ref[:, line, :] = jnp.broadcast_to(piece, (64, 512))


def merge_kernel(spot_ref, all_ref, whole_ref, own_ref):
    top = jnp.max(all_ref[...], axis=0)
    total = jnp.sum(jnp.exp2(all_ref[...] - top[None]), axis=0)
    lse = top + jnp.log2(total)
    whole_ref[...] = lse
    value = jnp.concatenate([lse[line : line + 1, :] for line in range(8)], axis=1)
    for dim in range(3):
        value = roll_within(value, dim, (4 - spot_ref[dim]) % 4)
    own_ref[...] = value


def sums_kernel(half, count, lse_ref, *refs):
    stats = refs[:count]
    ps = refs[count : 2 * count]
    rows = refs[2 * count : 3 * count]
    out_ref = refs[3 * count]
    p_bufs = refs[3 * count + 1 : 4 * count + 1]
    row_bufs = refs[4 * count + 1 : 5 * count + 1]
    sems = refs[5 * count + 1]
    copies = []
    for k in range(count):
        pair = (
            pltpu.make_async_copy(ps[k].at[half], p_bufs[k], sems.at[0, k]),
            pltpu.make_async_copy(rows[k], row_bufs[k], sems.at[1, k]),
        )
        for copy in pair:
            copy.start()
        copies.append(pair)
    width = rows[0].shape[1]
    at = 0
    for k in range(count):
        n = rows[k].shape[0]
        for copy in copies[k]:
            copy.wait()
        f = jnp.exp2(stats[k][half : half + 1, :] - lse_ref[:, at : at + n])
        w = (p_bufs[k][...] * f).astype(jnp.bfloat16)
        add = jnp.dot(w, row_bufs[k][...], preferred_element_type=jnp.float32)
        wide = w.astype(jnp.float32)
        mass = sum(wide[:, c : c + 128] for c in range(0, n, 128))
        if k == 0:
            out_ref[:, :width] = add
            out_ref[:, width:] = mass
        else:
            out_ref[:, :width] += add
            out_ref[:, width:] += mass
        at += n


def sums_call(half, lse, stats, ps, rows):
    count = len(rows)
    width = rows[0].shape[1]
    vmem = pl.BlockSpec(memory_space=pltpu.VMEM)
    hbm = pl.BlockSpec(memory_space=pl.ANY)
    return pl.pallas_call(
        functools.partial(sums_kernel, half, count),
        out_shape=jax.ShapeDtypeStruct((512, width + 128), jnp.float32),
        in_specs=[vmem] * (1 + count) + [hbm] * (2 * count),
        scratch_shapes=[pltpu.VMEM((512, r.shape[0]), jnp.float32) for r in rows]
        + [pltpu.VMEM(r.shape, r.dtype) for r in rows]
        + [pltpu.SemaphoreType.DMA((2, count))],
        compiler_params=pltpu.CompilerParams(vmem_limit_bytes=58 << 20),
        cost_estimate=pl.CostEstimate(
            flops=2 * 512 * 4096 * width, bytes_accessed=18 << 20, transcendentals=8192
        ),
        name="sums",
    )(lse, *stats, *ps, *rows)


def shards(embeddings, destination, centroids):
    samp, cent = lax.axis_index("samp"), lax.axis_index("cent")
    core = cent % 2
    x, y, z = (samp // 4) * 2 + cent // 8, (cent // 2) % 4, samp % 4
    spot = jnp.where(core == 0, jnp.stack([x, y, z]), jnp.stack([z, x, y])).astype(jnp.int32)
    share = centroids.shape[0] // 8
    width = embeddings.shape[1]
    mine = lax.dynamic_slice_in_dim(centroids, samp * share, share, 0)
    other = swap_cores(mine)
    line = jnp.concatenate([embeddings] + [fetch(embeddings, 0, step) for step in (1, 2, 3)])
    plane = jnp.concatenate([line] + [fetch(line, 1, step) for step in (1, 2, 3)])
    after, before = fetch(plane, 2, 1), fetch(plane, 2, 3)
    far = [fetch(after[:512], 2, 1), fetch(before[512:], 2, 3)]
    chunks = [plane, after] + far + [before]

    late, _ = lax.optimization_barrier((destination, plane))
    start = core * 4096 + ((spot[2] * 4 + spot[1]) * 4 + spot[0]) * UNIT
    spots = lax.broadcasted_iota(jnp.int32, (UNIT, 8192), 1)
    keys = (start + jnp.arange(UNIT, dtype=jnp.int32))[:, None]
    spread = jnp.sum(jnp.where(spots == late[:, None], keys, 0), axis=0)
    arrived = lax.all_to_all(spread.reshape(128, UNIT), BOTH, split_axis=0, concat_axis=0, tiled=True)
    keys = jnp.sum(arrived, axis=0)

    results = {k: scores_call(mine, other, chunks[k]) for k in (0, 1, 4, 2, 3)}
    ps = [results[k][0] for k in range(5)]
    stats = [results[k][1] for k in range(5)]
    smem = pl.BlockSpec(memory_space=pltpu.SMEM)
    vmem = pl.BlockSpec(memory_space=pltpu.VMEM)
    local = pl.pallas_call(
        first_kernel,
        out_shape=jax.ShapeDtypeStruct((64, 8, 512), jnp.float32),
        in_specs=[smem] + [vmem] * 5,
        name="first",
    )(spot, *stats)
    chips = [
        [place(i // 16, i // 4 % 4, i % 4, side) for i in range(64)] for side in range(2)
    ]
    shared = lax.all_to_all(local, BOTH, split_axis=0, concat_axis=0, tiled=True, axis_index_groups=chips)
    whole, lse = pl.pallas_call(
        merge_kernel,
        out_shape=(
            jax.ShapeDtypeStruct((8, 512), jnp.float32),
            jax.ShapeDtypeStruct((1, 4096), jnp.float32),
        ),
        in_specs=[smem, vmem],
        name="merge",
    )(spot, shared)
    theirs = sums_call(1, lse, stats, ps, chunks)
    received = swap_cores(theirs)
    ours = sums_call(0, lse, stats, ps, chunks)
    whole = whole.reshape(4096)
    partner = swap_cores(whole)
    every = jnp.where(core == 0, jnp.concatenate([whole, partner]), jnp.concatenate([partner, whole]))
    row_lse = jnp.sum(jnp.where(spots == keys[:, None], every[None, :], 0.0), axis=1) * math.log(2.0)
    both = ours + received
    mass = jnp.sum(both[:, width:], axis=1)
    new_centers = (both[:, :width] + prior_mass * mine.astype(jnp.float32)) / (mass + prior_mass)[:, None]
    return new_centers, row_lse


def solution(mesh):
    in_specs = (P(BOTH, None), P(BOTH), P("cent", None))
    out_specs = (P(("cent", "samp"), None), P(BOTH))
    return jax.shard_map(shards, mesh=mesh, in_specs=in_specs, out_specs=out_specs, check_vma=False)
```

time: 202 us -> 174 us (0.86)
  starting transfers between devices: 64.6 us -> 24.1 us
  blocking collectives: 0 us -> 32.8 us
  local copies, waits for them, and re-layouts: 48.1 us -> 23.6 us
  Pallas kernels: 42.1 us -> 49.1 us
  waiting for transfers between devices: 37.9 us -> 33.7 us
    ppermute x27 -> x10, starting transfers between devices: 53.3 us -> 14 us  [fetch(): return lax.ppermute(value, BOTH, pairs)]
    all_to_all x0 -> x2, blocking collectives: none -> 32.8 us  [the longest x1 19.7 us: shards(): lax.all_to_all(local, BOTH, split_axis=0, concat_axis=0, tiled=True, axis...]
    unnamed x122 -> x36, local copies, waits for them, and re-layouts: 41.7 us -> 15.6 us
    pallas_call x8 -> x5, Pallas kernels: 16.5 us -> 25.3 us  [scores_call(): pl.pallas_call(functools.partial(scores_kernel, factor), out_shape=(jax.S...]
    all_to_all x1 -> x0, starting transfers between devices: 4.52 us -> none  [shards(): lax.all_to_all(spread.reshape(128, 64), BOTH, split_axis=0, concat_axis=0...]
    ppermute x27 -> x10, waiting for transfers between devices: 37.9 us -> 33.7 us  [fetch(): return lax.ppermute(value, BOTH, pairs)]
    ppermute x2 -> x3, starting transfers between devices: 6.8 us -> 10.1 us  [swap_cores(): return lax.ppermute(value, BOTH, pairs)]
    pallas_call x4 -> x2, Pallas kernels: 7.04 us -> 4.96 us  [the longest x1 2.5 us: shards(): pl.pallas_call(first_kernel, out_shape=jax.ShapeDtypeStruct((64, 8, 512),...]
  transfers between devices with their start and end apart: 30 -> 13, of which waited for: 12 -> 6; matrix products, arithmetic and copies ran while one was open for 6% -> 8% of each run, Pallas kernels for 12% -> 18%
where the time goes in v2:
time: 174 us; the launch traced here: 173 us
  Pallas kernels  49.1 us (28%)
  waiting for transfers between devices  33.7 us (19%)
  blocking collectives  32.8 us (19%)
  starting transfers between devices  24.1 us (14%)
  local copies, waits for them, and re-layouts  23.6 us (14%)
  other arithmetic  7.14 us (4%)
  between operations  2.73 us (2%)
    ppermute x10, waiting for transfers between devices, fetch(): return lax.ppermute(value, BOTH, pairs)  33.7 us
    pallas_call x5, Pallas kernels, scores_call(): pl.pallas_call(functools.partial(scores_kernel, factor), out_shape=(jax.S...  25.3 us
    all_to_all x1, blocking collectives, shards(): lax.all_to_all(local, BOTH, split_axis=0, concat_axis=0, tiled=True, axis...  19.7 us
    pallas_call x2, Pallas kernels, sums_call(): pl.pallas_call(functools.partial(sums_kernel, half, count), out_shape=jax...  18.9 us
    unnamed x36, local copies, waits for them, and re-layouts  15.6 us
    ppermute x10, starting transfers between devices, fetch(): return lax.ppermute(value, BOTH, pairs)  14 us
    all_to_all x1, blocking collectives, shards(): lax.all_to_all(spread.reshape(128, UNIT), BOTH, split_axis=0, concat_axis...  13.1 us
    ppermute x3, starting transfers between devices, swap_cores(): return lax.ppermute(value, BOTH, pairs)  10.1 us
  transfers between devices with their start and end apart: 13, of which 6 were waited for; matrix products, arithmetic and copies ran while one was open for 8% of the time, Pallas kernels for 18%

profile of v2, /device:TPU:1, one launch (start us, length us, event | category | flops | bytes accessed | tf_op | source)
XLA Modules:
  0.0 173.1 jit_solution(9624675481313756094)
XLA Ops:
  0.6 4.7 %collective-permute-start.1 = (bf16[64,1024]{1,0:T(8,128)(2,1)}, bf16[64,1024]{1,0:T(8,128)(2,1)S(1)}, u32[]{:S(2)}, u32[]{:S(2)}) collective-permute-start(bf16[64,1024]{1,0:T(8,128)(2,1)} %param.3), channel_id=1, source_target_pairs={{8,0},{17,1},{24,16},{33,17},{40,32},{49,33},{56,48},{1,49},{10,2}... | collective-permute-start | bytes 393224 | tf_op jit(solution)/shard_map/ppermute | solution.py:34
  6.0 1.6 constant_dynamic-update-slice_fusion.3
  7.6 1.4 collective-permute-done.1
  9.6 1.5 collective-permute-done.2
  12.9 2.2 %collective-permute-start.4 = (bf16[256,1024]{1,0:T(8,128)(2,1)S(1)}, bf16[256,1024]{1,0:T(8,128)(2,1)S(1)}, u32[]{:S(2)}, u32[]{:S(2)}) collective-permute-start(bf16[256,1024]{1,0:T(8,128)(2,1)S(1)} %get-tuple-element.28), channel_id=1, source_target_pairs={{2,0},{9,1},{18,16},{25,17},{34,32},{41,33},{50,48},{57,49},{4,2},... | collective-permute-start | bytes 1572872 | tf_op jit(solution)/shard_map/ppermute | solution.py:34
  16.2 10.6 %collective-permute-done.4 = bf16[256,1024]{1,0:T(8,128)(2,1)S(1)} collective-permute-done((bf16[256,1024]{1,0:T(8,128)(2,1)S(1)}, bf16[256,1024]{1,0:T(8,128)(2,1)S(1)}, u32[]{:S(2)}, u32[]{:S(2)}) %collective-permute-start.4) | collective-permute-done | bytes 524320 | tf_op jit(solution)/shard_map/ppermute | solution.py:34
  28.5 2.0 %collective-permute-done.6 = bf16[256,1024]{1,0:T(8,128)(2,1)S(1)} collective-permute-done((bf16[256,1024]{1,0:T(8,128)(2,1)S(1)}, bf16[256,1024]{1,0:T(8,128)(2,1)S(1)}, u32[]{:S(2)}, u32[]{:S(2)}) %collective-permute-start.6) | collective-permute-done | bytes 524320 | tf_op jit(solution)/shard_map/ppermute | solution.py:34
  32.4 1.7 collective-permute-start.7
  34.0 2.3 %constant_dynamic-slice_fusion.mine_ref = bf16[512,1024]{1,0:T(8,128)(2,1)} fusion(bf16[4096,1024]{1,0:T(8,128)(2,1)} %param.5, s32[]{:T(128)S(6)} %select_n.64), kind=kLoop, calls=%fused_computation.23 | loop fusion | bytes 2097156 | tf_op jit(solution)/shard_map/dynamic_slice | solution.py:184
  36.3 3.9 %collective-permute-start = (bf16[512,1024]{1,0:T(8,128)(2,1)}, bf16[512,1024]{1,0:T(8,128)(2,1)}, u32[]{:S(2)}, u32[]{:S(2)}) collective-permute-start(bf16[512,1024]{1,0:T(8,128)(2,1)} %constant_dynamic-slice_fusion.mine_ref), channel_id=1, source_target_pairs={{0,1},{1,0},{2,3},{3,2},{4,5},{5,4},{6,7},{7,6},{8,9},{9,8},{10,11... | collective-permute-start | bytes 3145736 | tf_op jit(solution)/shard_map/ppermute | solution.py:39
  40.2 17.8 %collective-permute-done.9.rows_ref.refs_14_ = bf16[1024,1024]{1,0:T(8,128)(2,1)S(1)} collective-permute-done((bf16[1024,1024]{1,0:T(8,128)(2,1)}, bf16[1024,1024]{1,0:T(8,128)(2,1)S(1)}, u32[]{:S(2)}, u32[]{:S(2)}) %collective-permute-start.9) | collective-permute-done | bytes 2097184 | tf_op jit(solution)/shard_map/ppermute | solution.py:34
  59.1 2.3 %slice.28 = bf16[512,1024]{1,0:T(8,128)(2,1)} slice(bf16[1024,1024]{1,0:T(8,128)(2,1)} %collective-permute-done.7.rows_ref.refs_11_), slice={[0:512], [0:1024]} | slice | bytes 2097152 | tf_op jit(solution)/shard_map/slice | solution.py:189
  61.4 2.7 %collective-permute-start.8 = (bf16[512,1024]{1,0:T(8,128)(2,1)}, bf16[512,1024]{1,0:T(8,128)(2,1)}, u32[]{:S(2)}, u32[]{:S(2)}) collective-permute-start(bf16[512,1024]{1,0:T(8,128)(2,1)} %slice.28), channel_id=1, source_target_pairs={{16,0},{3,1},{32,16},{19,17},{48,32},{35,33},{0,48},{51,49},{18,2}... | collective-permute-start | bytes 3145736 | tf_op jit(solution)/shard_map/ppermute | solution.py:34
  64.8 5.9 %scores.5 = (f32[2,512,1024]{2,1,0:T(8,128)S(1)}, f32[4,1024]{1,0:T(4,128)S(1)}) custom-call(bf16[512,1024]{1,0:T(8,128)(2,1)} %constant_dynamic-slice_fusion.mine_ref, bf16[512,1024]{1,0:T(8,128)(2,1)} %collective-permute-done.other_ref, bf16[1024,1024]{1,0:T(8,128)(2,1)} %constant_dynamic-update-slice_fusion.4.rows_ref.refs_10_), custom_call_target="tpu_custom_call" | custom-call | flops 2147483648 | bytes 8388608 | tf_op jit(solution)/shard_map/scores/pallas_call | solution.py:67
  70.7 1.9 %copy-done = f32[2,512,1024]{2,1,0:T(8,128)} copy-done((f32[2,512,1024]{2,1,0:T(8,128)}, f32[2,512,1024]{2,1,0:T(8,128)S(1)}, u32[]{:S(2)}) %copy-start) | copy-done | bytes 4194328
  73.2 5.9 %scores.6 = (f32[2,512,1024]{2,1,0:T(8,128)S(1)}, f32[4,1024]{1,0:T(4,128)S(1)}) custom-call(bf16[512,1024]{1,0:T(8,128)(2,1)} %constant_dynamic-slice_fusion.mine_ref, bf16[512,1024]{1,0:T(8,128)(2,1)} %collective-permute-done.other_ref, bf16[1024,1024]{1,0:T(8,128)(2,1)} %collective-permute-done.7.rows_ref.refs_11_), custom_call_target="tpu_custom_call" | custom-call | flops 2147483648 | bytes 8388608 | tf_op jit(solution)/shard_map/scores/pallas_call | solution.py:67
  79.2 2.0 %copy-done.1 = f32[2,512,1024]{2,1,0:T(8,128)} copy-done((f32[2,512,1024]{2,1,0:T(8,128)}, f32[2,512,1024]{2,1,0:T(8,128)S(1)}, u32[]{:S(2)}) %copy-start.1) | copy-done | bytes 4194328
  81.8 5.2 %scores.9 = (f32[2,512,1024]{2,1,0:T(8,128)S(1)}, f32[4,1024]{1,0:T(4,128)S(1)}) custom-call(bf16[512,1024]{1,0:T(8,128)(2,1)} %constant_dynamic-slice_fusion.mine_ref, bf16[512,1024]{1,0:T(8,128)(2,1)} %collective-permute-done.other_ref, bf16[1024,1024]{1,0:T(8,128)(2,1)S(1)} %collective-permute-done.9.rows_ref.refs_14_), custom_call_target="tpu_custom_call" | custom-call | flops 2147483648 | bytes 8388608 | tf_op jit(solution)/shard_map/scores/pallas_call | solution.py:67
  87.1 2.0 %copy-done.2 = f32[2,512,1024]{2,1,0:T(8,128)} copy-done((f32[2,512,1024]{2,1,0:T(8,128)}, f32[2,512,1024]{2,1,0:T(8,128)S(1)}, u32[]{:S(2)}) %copy-start.2) | copy-done | bytes 4194328
  89.1 4.1 %scores.8 = (f32[2,512,512]{2,1,0:T(8,128)S(1)}, f32[4,512]{1,0:T(4,128)S(1)}) custom-call(bf16[512,1024]{1,0:T(8,128)(2,1)} %constant_dynamic-slice_fusion.mine_ref, bf16[512,1024]{1,0:T(8,128)(2,1)} %collective-permute-done.other_ref, bf16[512,1024]{1,0:T(8,128)(2,1)S(1)} %collective-permute-done.10.rows_ref.refs_13_), custom_call_target="tpu_custom_call" | custom-call | flops 1073741824 | bytes 5242880 | tf_op jit(solution)/shard_map/scores/pallas_call | solution.py:67
  93.2 1.3 copy-done.4
  95.1 4.0 %scores.7 = (f32[2,512,512]{2,1,0:T(8,128)S(1)}, f32[4,512]{1,0:T(4,128)S(1)}) custom-call(bf16[512,1024]{1,0:T(8,128)(2,1)} %constant_dynamic-slice_fusion.mine_ref, bf16[512,1024]{1,0:T(8,128)(2,1)} %collective-permute-done.other_ref, bf16[512,1024]{1,0:T(8,128)(2,1)} %collective-permute-done.8.rows_ref.refs_12_), custom_call_target="tpu_custom_call" | custom-call | flops 1073741824 | bytes 5242880 | tf_op jit(solution)/shard_map/scores/pallas_call | solution.py:67
  99.2 1.4 copy-done.5
  101.1 2.5 %first.1 = f32[64,8,512]{2,1,0:T(8,128)} custom-call(s32[3]{0:T(128)} %broadcast_select_fusion.spot_ref, f32[4,1024]{1,0:T(4,128)} %copy-done.7, f32[4,1024]{1,0:T(4,128)} %copy-done.8, f32[4,512]{1,0:T(4,128)} %copy-done.11, f32[4,512]{1,0:T(4,128)} %copy-done.10, f32[4,1024]{1,0:T(4,128)} %copy-done.9), custom_call_target="tpu_custom_call" | custom-call | tf_op jit(solution)/shard_map/first/pallas_call | solution.py:205
  103.6 19.7 %all_to_all.14.all_ref = f32[64,8,512]{2,1,0:T(8,128)} all-to-all(f32[64,8,512]{2,1,0:T(8,128)} %first.1), channel_id=1, replica_groups={{0,16,32,48,2,18,34,50,4,20,36,52,6,22,38,54,8,24,40,56,10,26,42,58,12,..., dimensions={0} | all-to-all | bytes 2097152 | tf_op jit(solution)/shard_map/all_to_all | solution.py:214
  123.3 2.5 %merge.1 = (f32[8,512]{1,0:T(8,128)}, f32[1,4096]{1,0:T(1,128)}) custom-call(s32[3]{0:T(128)} %broadcast_select_fusion.spot_ref, f32[64,8,512]{2,1,0:T(8,128)} %all_to_all.14.all_ref), custom_call_target="tpu_custom_call" | custom-call | tf_op jit(solution)/shard_map/merge/pallas_call | solution.py:215
  125.8 9.4 %sums.3 = f32[512,1152]{1,0:T(8,128)} custom-call(f32[1,4096]{1,0:T(1,128)} %get-tuple-element.20.lse_ref, f32[4,1024]{1,0:T(4,128)} %copy-done.7, f32[4,1024]{1,0:T(4,128)} %copy-done.8, f32[4,512]{1,0:T(4,128)} %copy-done.11, f32[4,512]{1,0:T(4,128)} %copy-done.10, f32[4,1024]{1,0:T(4,128)} %copy-done.9, f32[2,512,1024]{2,1,0:T(8,128)} %copy-done, ...), custom_call_target="tpu_custom_call" | custom-call | flops 4294967296 | bytes 18874368 | tf_op jit(solution)/shard_map/sums/pallas_call | solution.py:162
  135.2 5.5 %collective-permute-start.11 = (f32[512,1152]{1,0:T(8,128)}, f32[512,1152]{1,0:T(8,128)S(1)}, u32[]{:S(2)}, u32[]{:S(2)}) collective-permute-start(f32[512,1152]{1,0:T(8,128)} %sums.3), channel_id=1, source_target_pairs={{0,1},{1,0},{2,3},{3,2},{4,5},{5,4},{6,7},{7,6},{8,9},{9,8},{10,11... | collective-permute-start | bytes 7077896 | tf_op jit(solution)/shard_map/ppermute | solution.py:39
  143.7 13.1 %all_to_all.15 = s32[128,1,64]{2,1,0:T(1,128)S(1)} all-to-all(s32[128,1,64]{2,1,0:T(1,128)S(1)} %bitcast.7), channel_id=1, replica_groups=mesh['samp'=8,'cent'=16] {'samp','cent'}, dimensions={0} | all-to-all | bytes 65536 | tf_op jit(solution)/shard_map/all_to_all | solution.py:197
  157.7 9.4 %sums.2 = f32[512,1152]{1,0:T(8,128)} custom-call(f32[1,4096]{1,0:T(1,128)} %get-tuple-element.20.lse_ref, f32[4,1024]{1,0:T(4,128)} %copy-done.7, f32[4,1024]{1,0:T(4,128)} %copy-done.8, f32[4,512]{1,0:T(4,128)} %copy-done.11, f32[4,512]{1,0:T(4,128)} %copy-done.10, f32[4,1024]{1,0:T(4,128)} %copy-done.9, f32[2,512,1024]{2,1,0:T(8,128)} %copy-done, ...), custom_call_target="tpu_custom_call" | custom-call | flops 4294967296 | bytes 18874368 | tf_op jit(solution)/shard_map/sums/pallas_call | solution.py:162
  168.1 1.9 %add.63 = f32[512,1152]{1,0:T(8,128)S(1)} add(f32[512,1152]{1,0:T(8,128)} %sums.2, f32[512,1152]{1,0:T(8,128)S(1)} %collective-permute-done.11) | non-fusion elementwise | flops 589824 | bytes 7077888 | tf_op jit(solution)/shard_map/add | solution.py:231
  170.2 3.0 %fusion = f32[512,1024]{1,0:T(8,128)} fusion(f32[512,1152]{1,0:T(8,128)S(1)} %add.63, f32[512]{0:T(512)S(1)} %broadcast_add_fusion, bf16[4096,1024]{1,0:T(8,128)(2,1)} %param.5, s32[]{:T(128)S(6)} %select_n.64), kind=kLoop, calls=%fused_computation.1 | loop fusion | flops 2097152 | bytes 5244932 | tf_op jit(solution)/shard_map/div | solution.py:233
  (59 shorter events, 15.0 us)
Async XLA Ops:
  0.6 8.3 %collective-permute-start.1 = (bf16[64,1024]{1,0:T(8,128)(2,1)}, bf16[64,1024]{1,0:T(8,128)(2,1)S(1)}, u32[]{:S(2)}, u32[]{:S(2)}) collective-permute-start(bf16[64,1024]{1,0:T(8,128)(2,1)} %param.3), channel_id=1, source_target_pairs={{8,0},{17,1},{24,16},{33,17},{40,32},{49,33},{56,48},{1,49},{10,2}... | collective-permute-start | bytes 393224 | tf_op jit(solution)/shard_map/ppermute | solution.py:34
  5.3 5.9 %collective-permute-start.2 = (bf16[64,1024]{1,0:T(8,128)(2,1)}, bf16[64,1024]{1,0:T(8,128)(2,1)S(1)}, u32[]{:S(2)}, u32[]{:S(2)}) collective-permute-start(bf16[64,1024]{1,0:T(8,128)(2,1)} %param.3), channel_id=1, source_target_pairs={{64,0},{33,1},{80,16},{49,17},{96,32},{1,33},{112,48},{17,49},{66,... | collective-permute-start | bytes 393224 | tf_op jit(solution)/shard_map/ppermute | solution.py:34
  5.3 6.9 %collective-permute-start.3 = (bf16[64,1024]{1,0:T(8,128)(2,1)}, bf16[64,1024]{1,0:T(8,128)(2,1)S(1)}, u32[]{:S(2)}, u32[]{:S(2)}) collective-permute-start(bf16[64,1024]{1,0:T(8,128)(2,1)} %param.3), channel_id=1, source_target_pairs={{72,0},{49,1},{88,16},{1,17},{104,32},{17,33},{120,48},{33,49},{74... | collective-permute-start | bytes 393224 | tf_op jit(solution)/shard_map/ppermute | solution.py:34
  12.9 13.9 %collective-permute-start.4 = (bf16[256,1024]{1,0:T(8,128)(2,1)S(1)}, bf16[256,1024]{1,0:T(8,128)(2,1)S(1)}, u32[]{:S(2)}, u32[]{:S(2)}) collective-permute-start(bf16[256,1024]{1,0:T(8,128)(2,1)S(1)} %get-tuple-element.28), channel_id=1, source_target_pairs={{2,0},{9,1},{18,16},{25,17},{34,32},{41,33},{50,48},{57,49},{4,2},... | collective-permute-start | bytes 1572872 | tf_op jit(solution)/shard_map/ppermute | solution.py:34
  15.1 12.6 %collective-permute-start.5 = (bf16[256,1024]{1,0:T(8,128)(2,1)S(1)}, bf16[256,1024]{1,0:T(8,128)(2,1)S(1)}, u32[]{:S(2)}, u32[]{:S(2)}) collective-permute-start(bf16[256,1024]{1,0:T(8,128)(2,1)S(1)} %get-tuple-element.28), channel_id=1, source_target_pairs={{4,0},{65,1},{20,16},{81,17},{36,32},{97,33},{52,48},{113,49},{6,2... | collective-permute-start | bytes 1572872 | tf_op jit(solution)/shard_map/ppermute | solution.py:34
  15.6 14.9 %collective-permute-start.6 = (bf16[256,1024]{1,0:T(8,128)(2,1)S(1)}, bf16[256,1024]{1,0:T(8,128)(2,1)S(1)}, u32[]{:S(2)}, u32[]{:S(2)}) collective-permute-start(bf16[256,1024]{1,0:T(8,128)(2,1)S(1)} %get-tuple-element.28), channel_id=1, source_target_pairs={{6,0},{73,1},{22,16},{89,17},{38,32},{105,33},{54,48},{121,49},{0,... | collective-permute-start | bytes 1572872 | tf_op jit(solution)/shard_map/ppermute | solution.py:34
  31.4 26.6 %collective-permute-start.9 = (bf16[1024,1024]{1,0:T(8,128)(2,1)}, bf16[1024,1024]{1,0:T(8,128)(2,1)S(1)}, u32[]{:S(2)}, u32[]{:S(2)}) collective-permute-start(bf16[1024,1024]{1,0:T(8,128)(2,1)} %constant_dynamic-update-slice_fusion.4.rows_ref.refs_10_), channel_id=1, source_target_pairs={{48,0},{7,1},{0,16},{23,17},{16,32},{39,33},{32,48},{55,49},{50,2}... | collective-permute-start | bytes 6291464 | tf_op jit(solution)/shard_map/ppermute | solution.py:34
  32.4 26.7 %collective-permute-start.7 = (bf16[1024,1024]{1,0:T(8,128)(2,1)}, bf16[1024,1024]{1,0:T(8,128)(2,1)}, u32[]{:S(2)}, u32[]{:S(2)}) collective-permute-start(bf16[1024,1024]{1,0:T(8,128)(2,1)} %constant_dynamic-update-slice_fusion.4.rows_ref.refs_10_), channel_id=1, source_target_pairs={{16,0},{3,1},{32,16},{19,17},{48,32},{35,33},{0,48},{51,49},{18,2}... | collective-permute-start | bytes 6291464 | tf_op jit(solution)/shard_map/ppermute | solution.py:34
  36.3 28.4 %collective-permute-start = (bf16[512,1024]{1,0:T(8,128)(2,1)}, bf16[512,1024]{1,0:T(8,128)(2,1)}, u32[]{:S(2)}, u32[]{:S(2)}) collective-permute-start(bf16[512,1024]{1,0:T(8,128)(2,1)} %constant_dynamic-slice_fusion.mine_ref), channel_id=1, source_target_pairs={{0,1},{1,0},{2,3},{3,2},{4,5},{5,4},{6,7},{7,6},{8,9},{9,8},{10,11... | collective-permute-start | bytes 3145736 | tf_op jit(solution)/shard_map/ppermute | solution.py:39
  58.0 21.2 %copy-start.3 = (bf16[1024,1024]{1,0:T(8,128)(2,1)}, bf16[1024,1024]{1,0:T(8,128)(2,1)S(1)}, u32[]{:S(2)}) copy-start(bf16[1024,1024]{1,0:T(8,128)(2,1)S(1)} %collective-permute-done.9.rows_ref.refs_14_) | copy-start | bytes 6291460
  59.1 30.0 %collective-permute-start.10 = (bf16[512,1024]{1,0:T(8,128)(2,1)}, bf16[512,1024]{1,0:T(8,128)(2,1)S(1)}, u32[]{:S(2)}, u32[]{:S(2)}) collective-permute-start(bf16[512,1024]{1,0:T(8,128)(2,1)} %slice.29), channel_id=1, source_target_pairs={{48,0},{7,1},{0,16},{23,17},{16,32},{39,33},{32,48},{55,49},{50,2}... | collective-permute-start | bytes 3145736 | tf_op jit(solution)/shard_map/ppermute | solution.py:34
  61.4 33.7 %collective-permute-start.8 = (bf16[512,1024]{1,0:T(8,128)(2,1)}, bf16[512,1024]{1,0:T(8,128)(2,1)}, u32[]{:S(2)}, u32[]{:S(2)}) collective-permute-start(bf16[512,1024]{1,0:T(8,128)(2,1)} %slice.28), channel_id=1, source_target_pairs={{16,0},{3,1},{32,16},{19,17},{48,32},{35,33},{0,48},{51,49},{18,2}... | collective-permute-start | bytes 3145736 | tf_op jit(solution)/shard_map/ppermute | solution.py:34
  70.7 2.0 %copy-start = (f32[2,512,1024]{2,1,0:T(8,128)}, f32[2,512,1024]{2,1,0:T(8,128)S(1)}, u32[]{:S(2)}) copy-start(f32[2,512,1024]{2,1,0:T(8,128)S(1)} %get-tuple-element.21.refs_5_) | copy-start | bytes 12582916
  72.7 0.6 copy-start.7
  79.2 2.0 %copy-start.1 = (f32[2,512,1024]{2,1,0:T(8,128)}, f32[2,512,1024]{2,1,0:T(8,128)S(1)}, u32[]{:S(2)}) copy-start(f32[2,512,1024]{2,1,0:T(8,128)S(1)} %get-tuple-element.22.refs_6_) | copy-start | bytes 12582916
  81.2 0.6 copy-start.8
  87.1 2.0 %copy-start.2 = (f32[2,512,1024]{2,1,0:T(8,128)}, f32[2,512,1024]{2,1,0:T(8,128)S(1)}, u32[]{:S(2)}) copy-start(f32[2,512,1024]{2,1,0:T(8,128)S(1)} %get-tuple-element.25.refs_9_) | copy-start | bytes 12582916
  89.1 4.1 %copy-start.9 = (f32[4,1024]{1,0:T(4,128)}, f32[4,1024]{1,0:T(4,128)S(1)}, u32[]{:S(2)}) copy-start(f32[4,1024]{1,0:T(4,128)S(1)} %get-tuple-element.19.refs_4_) | copy-start | bytes 49156
  89.1 10.1 %copy-start.6 = (bf16[512,1024]{1,0:T(8,128)(2,1)}, bf16[512,1024]{1,0:T(8,128)(2,1)S(1)}, u32[]{:S(2)}) copy-start(bf16[512,1024]{1,0:T(8,128)(2,1)S(1)} %collective-permute-done.10.rows_ref.refs_13_) | copy-start | bytes 3145732
  93.2 1.3 copy-start.4
  94.5 0.6 copy-start.10
  99.2 1.4 copy-start.5
  100.5 0.6 copy-start.11
  125.8 14.9 %copy-start.12 = (s32[3]{0:T(128)S(1)}, s32[3]{0:T(128)}, u32[]{:S(2)}) copy-start(s32[3]{0:T(128)} %broadcast_select_fusion.spot_ref) | copy-start | bytes 40
  125.8 17.5 %copy-start.14 = (s32[64]{0:T(128)S(1)}, s32[64]{0:T(128)}, u32[]{:S(2)}) copy-start(s32[64]{0:T(128)} %param.4) | copy-start | bytes 772
  125.8 31.2 %copy-start.13 = (f32[8,512]{1,0:T(8,128)S(1)}, f32[8,512]{1,0:T(8,128)}, u32[]{:S(2)}) copy-start(f32[8,512]{1,0:T(8,128)} %get-tuple-element.27) | copy-start | bytes 49156
  135.2 32.9 %collective-permute-start.11 = (f32[512,1152]{1,0:T(8,128)}, f32[512,1152]{1,0:T(8,128)S(1)}, u32[]{:S(2)}, u32[]{:S(2)}) collective-permute-start(f32[512,1152]{1,0:T(8,128)} %sums.3), channel_id=1, source_target_pairs={{0,1},{1,0},{2,3},{3,2},{4,5},{5,4},{6,7},{7,6},{8,9},{9,8},{10,11... | collective-permute-start | bytes 7077896 | tf_op jit(solution)/shard_map/ppermute | solution.py:39
  157.0 10.1 %collective-permute-start.12 = (f32[4096]{0:T(1024)S(1)}, f32[4096]{0:T(1024)S(1)}, u32[]{:S(2)}, u32[]{:S(2)}) collective-permute-start(f32[4096]{0:T(1024)S(1)} %bitcast.8), channel_id=1, source_target_pairs={{0,1},{1,0},{2,3},{3,2},{4,5},{5,4},{6,7},{7,6},{8,9},{9,8},{10,11... | collective-permute-start | bytes 49160 | tf_op jit(solution)/shard_map/ppermute | solution.py:39

commit v3 on v2

v3 whole, which is shorter than its diff:
```python
import functools
import math

import jax
import jax.numpy as jnp
from jax import lax
from jax.experimental import pallas as pl
from jax.experimental.pallas import tpu as pltpu
from jax.sharding import PartitionSpec as P

inv_temp = 2.5
prior_mass = 0.25
BOTH = ("samp", "cent")
UNIT = 64
X, Y, Z = 0, 1, 2
ORDERS = ((X, Y, Z), (Z, X, Y))


def place(x, y, z, core):
    return ((x // 2) * 4 + z) * 16 + (x % 2) * 8 + y * 2 + core


def fetch(value, stage, offset):
    pairs = []
    for x in range(4):
        for y in range(4):
            for z in range(4):
                for core in range(2):
                    at = [x, y, z]
                    axis = ORDERS[core][stage]
                    at[axis] = (at[axis] + offset) % 4
                    pairs.append((place(*at, core), place(x, y, z, core)))
    return lax.ppermute(value, BOTH, pairs)


def swap_cores(value):
    pairs = [(i, i ^ 1) for i in range(128)]
    return lax.ppermute(value, BOTH, pairs)


def scores_kernel(factor, count, mine_ref, other_ref, *refs):
    rows = refs[:count]
    ps = refs[count : 2 * count]
    stat_ref = refs[2 * count]
    tiles = [(k, part, half) for k in range(count) for part in range(2) for half in range(2)]

    def product(tile):
        k, part, half = tile
        return lax.dot_general(
            (mine_ref, other_ref)[half][...],
            rows[k][part * 256 : (part + 1) * 256, :],
            (((1,), (1,)), ((), ())),
            preferred_element_type=jnp.float32,
        )

    following = product(tiles[0])
    for i, (k, part, half) in enumerate(tiles):
        s = following * factor
        if i + 1 < len(tiles):
            following = product(tiles[i + 1])
        top = jnp.max(s, axis=0, keepdims=True)
        e = jnp.exp2(s - top)
        ps[k][half, :, part * 256 : (part + 1) * 256] = e
        lanes = slice(k * 512 + part * 256, k * 512 + (part + 1) * 256)
        stat_ref[half : half + 1, lanes] = top
        stat_ref[2 + half : 3 + half, lanes] = jnp.sum(e, axis=0, keepdims=True)


def scores_call(mine, other, rows):
    count = len(rows)
    n, width = rows[0].shape
    factor = inv_temp / math.sqrt(width) * math.log2(math.e)
    vmem = pl.BlockSpec(memory_space=pltpu.VMEM)
    *ps, stat = pl.pallas_call(
        functools.partial(scores_kernel, factor, count),
        out_shape=tuple([jax.ShapeDtypeStruct((2, 512, n), jnp.float32)] * count)
        + (jax.ShapeDtypeStruct((4, count * n), jnp.float32),),
        in_specs=[vmem] * (2 + count),
        out_specs=tuple([vmem] * (count + 1)),
        compiler_params=pltpu.CompilerParams(vmem_limit_bytes=16 << 20),
        cost_estimate=pl.CostEstimate(
            flops=4 * 1024 * n * width * count,
            bytes_accessed=count * n * 6144 + (2 << 20),
            transcendentals=1024 * n * count,
        ),
        name="scores",
    )(mine, other, *rows)
    return ps, stat


def roll_within(value, dim, step):
    inner = UNIT * 4**dim
    group = inner * 4
    size = value.shape[1]
    lane = lax.broadcasted_iota(jnp.int32, value.shape, 1) % group
    ahead = pltpu.roll(value, step * inner, 1)
    back = pltpu.roll(value, size - group + step * inner, 1)
    return jnp.where(lane >= step * inner, ahead, back)


def first_kernel(order, spot_ref, *refs):
    *stats, out_ref, top_ref = refs
    parts = []
    for k, (ref, piece) in enumerate(order):
        lanes = slice(piece * 512, (piece + 1) * 512)
        tops = stats[ref][0:2, lanes]
        top = jnp.max(tops, axis=0, keepdims=True)
        total = jnp.sum(stats[ref][2:4, lanes] * jnp.exp2(tops - top), axis=0, keepdims=True)
        parts.append(top + jnp.log2(total))
        top_ref[:, k * 512 : (k + 1) * 512] = tops
    value = jnp.concatenate(parts, axis=1)
    for dim in range(3):
        value = roll_within(value, dim, spot_ref[dim])
    for line in range(8):
        piece = value[:, line * 512 : (line + 1) * 512]
        out_ref[:, line, :] = jnp.broadcast_to(piece, (64, 512))


def merge_kernel(spot_ref, all_ref, whole_ref, own_ref):
    top = jnp.max(all_ref[...], axis=0)
    total = jnp.sum(jnp.exp2(all_ref[...] - top[None]), axis=0)
    lse = top + jnp.log2(total)
    whole_ref[...] = lse
    value = jnp.concatenate([lse[line : line + 1, :] for line in range(8)], axis=1)
    for dim in range(3):
        value = roll_within(value, dim, (4 - spot_ref[dim]) % 4)
    own_ref[...] = value


def sums_kernel(half, count, lse_ref, top_ref, *refs):
    ps = refs[:count]
    rows = refs[count : 2 * count]
    out_ref, row_buf, sems = refs[2 * count :]
    n, width = rows[0].shape
    loads = [pltpu.make_async_copy(rows[k], row_buf.at[k], sems.at[k]) for k in range(count)]
    for load in loads:
        load.start()

    def weights(k):
        lanes = slice(k * n, (k + 1) * n)
        f = jnp.exp2(top_ref[half : half + 1, lanes] - lse_ref[:, lanes])
        w = (ps[k][half] * f).astype(jnp.bfloat16)
        wide = w.astype(jnp.float32)
        return w, sum(wide[:, c : c + 128] for c in range(0, n, 128))

    w, mass = weights(0)
    for k in range(count):
        now = w
        if k + 1 < count:
            w, more = weights(k + 1)
            mass = mass + more
        loads[k].wait()
        add = jnp.dot(now, row_buf[k], preferred_element_type=jnp.float32)
        if k == 0:
            out_ref[:, :width] = add
        else:
            out_ref[:, :width] += add
    out_ref[:, width:] = mass


def sums_call(half, lse, tops, ps, rows):
    count = len(rows)
    n, width = rows[0].shape
    vmem = pl.BlockSpec(memory_space=pltpu.VMEM)
    hbm = pl.BlockSpec(memory_space=pltpu.HBM)
    return pl.pallas_call(
        functools.partial(sums_kernel, half, count),
        out_shape=jax.ShapeDtypeStruct((512, width + 128), jnp.float32),
        in_specs=[vmem] * (2 + count) + [hbm] * count,
        scratch_shapes=[pltpu.VMEM((count, n, width), jnp.bfloat16), pltpu.SemaphoreType.DMA((count,))],
        compiler_params=pltpu.CompilerParams(vmem_limit_bytes=20 << 20),
        cost_estimate=pl.CostEstimate(
            flops=2 * 512 * 4096 * width, bytes_accessed=18 << 20, transcendentals=8192
        ),
        name="sums",
    )(lse, tops, *ps, *rows)


def final_kernel(ours_ref, theirs_ref, mine_ref, out_ref):
    width = out_ref.shape[1]
    mass = jnp.sum(ours_ref[:, width:] + theirs_ref[:, width:], axis=1, keepdims=True) + prior_mass
    total = ours_ref[:, :width] + theirs_ref[:, :width] + prior_mass * mine_ref[...].astype(jnp.float32)
    out_ref[...] = total * (1.0 / mass)


def share_kernel(at_ref, cents_ref, out_ref, sem):
    size = out_ref.shape[0]
    first = pl.multiple_of(at_ref[0] * size, size)
    copy = pltpu.make_async_copy(cents_ref.at[pl.ds(first, size)], out_ref, sem)
    copy.start()
    copy.wait()


def shards(embeddings, destination, centroids):
    samp, cent = lax.axis_index("samp"), lax.axis_index("cent")
    core = cent % 2
    x, y, z = (samp // 4) * 2 + cent // 8, (cent // 2) % 4, samp % 4
    spot = jnp.where(core == 0, jnp.stack([x, y, z]), jnp.stack([z, x, y])).astype(jnp.int32)
    share = centroids.shape[0] // 8
    width = embeddings.shape[1]
    smem = pl.BlockSpec(memory_space=pltpu.SMEM)
    vmem = pl.BlockSpec(memory_space=pltpu.VMEM)
    mine = pl.pallas_call(
        share_kernel,
        out_shape=jax.ShapeDtypeStruct((share, width), centroids.dtype),
        in_specs=[smem, pl.BlockSpec(memory_space=pltpu.HBM)],
        out_specs=vmem,
        scratch_shapes=[pltpu.SemaphoreType.DMA(())],
        name="share",
    )(samp.astype(jnp.int32).reshape(1), centroids)
    other = swap_cores(mine)
    line = jnp.concatenate([embeddings] + [fetch(embeddings, 0, step) for step in (1, 2, 3)])
    near, across, back = [fetch(line, 1, step) for step in (1, 2, 3)]
    upper, lower = jnp.concatenate([line, near]), jnp.concatenate([across, back])
    upper, lower, other = lax.optimization_barrier((upper, lower, other))
    after_upper, before_lower = fetch(upper, 2, 1), fetch(lower, 2, 3)

    late, _, _ = lax.optimization_barrier((destination, upper, lower))
    start = core * 4096 + ((spot[2] * 4 + spot[1]) * 4 + spot[0]) * UNIT
    spots = lax.broadcasted_iota(jnp.int32, (UNIT, 8192), 1)
    keys = (start + jnp.arange(UNIT, dtype=jnp.int32))[:, None]
    spread = jnp.sum(jnp.where(spots == late[:, None], keys, 0), axis=0)
    arrived = lax.all_to_all(spread.reshape(128, UNIT), BOTH, split_axis=0, concat_axis=0, tiled=True)
    keys = jnp.sum(arrived, axis=0)

    p_upper, stat_upper = scores_call(mine, other, [upper])
    upper_again, lower_again, _ = lax.optimization_barrier((upper, lower, stat_upper))
    after_lower, before_upper = fetch(lower_again, 2, 1), fetch(upper_again, 2, 3)
    p_lower, stat_lower = scores_call(mine, other, [lower])
    passed_up, passed_down, keys, _ = lax.optimization_barrier((after_upper, before_lower, keys, stat_lower))
    far_upper, far_lower = fetch(passed_up, 2, 1), fetch(passed_down, 2, 3)
    p_first, stat_first = scores_call(mine, other, [after_upper, before_lower])
    p_second, stat_second = scores_call(mine, other, [after_lower, before_upper])
    p_far, stat_far = scores_call(mine, other, [far_upper, far_lower])
    chunks = [upper, lower, after_upper, after_lower, far_upper, far_lower, before_upper, before_lower]
    ps = p_upper + p_lower + [p_first[0], p_second[0]] + p_far + [p_second[1], p_first[1]]
    order = ((0, 0), (1, 0), (2, 0), (3, 0), (4, 0), (4, 1), (3, 1), (2, 1))

    local, tops = pl.pallas_call(
        functools.partial(first_kernel, order),
        out_shape=(
            jax.ShapeDtypeStruct((64, 8, 512), jnp.float32),
            jax.ShapeDtypeStruct((2, 4096), jnp.float32),
        ),
        in_specs=[smem] + [vmem] * 5,
        name="first",
    )(spot, stat_upper, stat_lower, stat_first, stat_second, stat_far)
    chips = [
        [place(i // 16, i // 4 % 4, i % 4, side) for i in range(64)] for side in range(2)
    ]
    shared = lax.all_to_all(local, BOTH, split_axis=0, concat_axis=0, tiled=True, axis_index_groups=chips)
    whole, lse = pl.pallas_call(
        merge_kernel,
        out_shape=(
            jax.ShapeDtypeStruct((8, 512), jnp.float32),
            jax.ShapeDtypeStruct((1, 4096), jnp.float32),
        ),
        in_specs=[smem, vmem],
        name="merge",
    )(spot, shared)
    theirs = sums_call(1, lse, tops, ps, chunks)
    received = swap_cores(theirs)
    ours = sums_call(0, lse, tops, ps, chunks)
    whole = whole.reshape(4096)
    partner = swap_cores(whole)
    every = jnp.where(core == 0, jnp.concatenate([whole, partner]), jnp.concatenate([partner, whole]))
    row_lse = jnp.sum(jnp.where(spots == keys[:, None], every[None, :], 0.0), axis=1) * math.log(2.0)
    new_centers = pl.pallas_call(
        final_kernel, out_shape=jax.ShapeDtypeStruct((share, width), jnp.float32), name="final",
        compiler_params=pltpu.CompilerParams(vmem_limit_bytes=16 << 20),
    )(ours, received, mine)
    return new_centers, row_lse


def solution(mesh):
    in_specs = (P(BOTH, None), P(BOTH), P("cent", None))
    out_specs = (P(("cent", "samp"), None), P(BOTH))
    return jax.shard_map(shards, mesh=mesh, in_specs=in_specs, out_specs=out_specs, check_vma=False)
```

time: 174 us -> 157 us (0.902)
  local copies, waits for them, and re-layouts: 23.6 us -> 40 us
  waiting for transfers between devices: 33.7 us -> 18.5 us
  blocking collectives: 32.8 us -> 23.5 us
  Pallas kernels: 49.1 us -> 40.3 us
  other arithmetic: 7.14 us -> 1.63 us
  starting transfers between devices: 24.1 us -> 29.5 us
    unnamed x36 -> x78, local copies, waits for them, and re-layouts: 15.6 us -> 37.2 us
    ppermute x10 -> x12, waiting for transfers between devices: 33.7 us -> 13.8 us  [fetch(): return lax.ppermute(value, BOTH, pairs)]
    all_to_all x1 -> x0, blocking collectives: 13.1 us -> none  [shards(): lax.all_to_all(spread.reshape(128, UNIT), BOTH, split_axis=0, concat_axis...]
    all_to_all x0 -> x1, starting transfers between devices: none -> 9.55 us  [shards(): lax.all_to_all(spread.reshape(128, UNIT), BOTH, split_axis=0, concat_axis...]
    ppermute x3, starting transfers between devices: 10.1 us -> 3.99 us  [swap_cores(): return lax.ppermute(value, BOTH, pairs)]
    pallas_call x6 -> x8, Pallas kernels: 27.8 us -> 22.9 us  [the longest x5 16.5 us: scores_call(): pl.pallas_call(functools.partial(scores_kernel, factor, count), out_shape...]
    all_to_all x0 -> x1, waiting for transfers between devices: none -> 4.67 us  [shards(): lax.all_to_all(spread.reshape(128, UNIT), BOTH, split_axis=0, concat_axis...]
    pallas_call x2, Pallas kernels: 18.9 us -> 14.9 us  [sums_call(): pl.pallas_call(functools.partial(sums_kernel, half, count), out_shape=jax...]
  transfers between devices with their start and end apart: 13 -> 16, of which waited for: 6 -> 5; matrix products, arithmetic and copies ran while one was open for 8% -> 4% of each run, Pallas kernels for 18% -> 15%
where the time goes in v3:
time: 157 us; the launch traced here: 156 us
  Pallas kernels  40.3 us (26%)
  local copies, waits for them, and re-layouts  40 us (25%)
  starting transfers between devices  29.5 us (19%)
  blocking collectives  23.5 us (15%)
  waiting for transfers between devices  18.5 us (12%)
  between operations  2.82 us (2%)
  other arithmetic  1.63 us (1%)
    unnamed x78, local copies, waits for them, and re-layouts  37.2 us
    all_to_all x1, blocking collectives, shards(): lax.all_to_all(local, BOTH, split_axis=0, concat_axis=0, tiled=True, axis...  23.5 us
    pallas_call x5, Pallas kernels, scores_call(): pl.pallas_call(functools.partial(scores_kernel, factor, count), out_shape...  16.5 us
    ppermute x12, starting transfers between devices, fetch(): return lax.ppermute(value, BOTH, pairs)  15.9 us
    pallas_call x2, Pallas kernels, sums_call(): pl.pallas_call(functools.partial(sums_kernel, half, count), out_shape=jax...  14.9 us
    ppermute x12, waiting for transfers between devices, fetch(): return lax.ppermute(value, BOTH, pairs)  13.8 us
    all_to_all x1, starting transfers between devices, shards(): lax.all_to_all(spread.reshape(128, UNIT), BOTH, split_axis=0, concat_axis...  9.55 us
    all_to_all x1, waiting for transfers between devices, shards(): lax.all_to_all(spread.reshape(128, UNIT), BOTH, split_axis=0, concat_axis...  4.67 us
  transfers between devices with their start and end apart: 16, of which 5 were waited for; matrix products, arithmetic and copies ran while one was open for 4% of the time, Pallas kernels for 15%

profile of v3, /device:TPU:1, one launch (start us, length us, event | category | flops | bytes accessed | tf_op | source)
XLA Modules:
  0.0 156.3 jit_solution(4075927939433434062)
XLA Ops:
  0.6 4.7 %collective-permute-start = (bf16[64,1024]{1,0:T(8,128)(2,1)}, bf16[64,1024]{1,0:T(8,128)(2,1)S(1)}, u32[]{:S(2)}, u32[]{:S(2)}) collective-permute-start(bf16[64,1024]{1,0:T(8,128)(2,1)} %param.3), channel_id=1, source_target_pairs={{8,0},{17,1},{24,16},{33,17},{40,32},{49,33},{56,48},{1,49},{10,2}... | collective-permute-start | bytes 393224 | tf_op jit(solution)/shard_map/ppermute | solution.py:33
  6.0 2.2 %share.1.mine_ref = bf16[512,1024]{1,0:T(8,128)(2,1)} custom-call(s32[1]{0:T(128)} %bitcast.3.at_ref, bf16[4096,1024]{1,0:T(8,128)(2,1)} %cents_ref.1), custom_call_target="tpu_custom_call" | custom-call | tf_op jit(solution)/shard_map/share/pallas_call | solution.py:203
  12.9 2.2 %collective-permute-start.3 = (bf16[256,1024]{1,0:T(8,128)(2,1)S(1)}, bf16[256,1024]{1,0:T(8,128)(2,1)S(1)}, u32[]{:S(2)}, u32[]{:S(2)}) collective-permute-start(bf16[256,1024]{1,0:T(8,128)(2,1)S(1)} %get-tuple-element.54), channel_id=1, source_target_pairs={{2,0},{9,1},{18,16},{25,17},{34,32},{41,33},{50,48},{57,49},{4,2},... | collective-permute-start | bytes 1572872 | tf_op jit(solution)/shard_map/ppermute | solution.py:33
  15.1 1.7 %collective-permute-start.4 = (bf16[256,1024]{1,0:T(8,128)(2,1)S(1)}, bf16[256,1024]{1,0:T(8,128)(2,1)S(1)}, u32[]{:S(2)}, u32[]{:S(2)}) collective-permute-start(bf16[256,1024]{1,0:T(8,128)(2,1)S(1)} %get-tuple-element.54), channel_id=1, source_target_pairs={{4,0},{65,1},{20,16},{81,17},{36,32},{97,33},{52,48},{113,49},{6,2... | collective-permute-start | bytes 1572872 | tf_op jit(solution)/shard_map/ppermute | solution.py:33
  16.8 10.0 %collective-permute-done.3 = bf16[256,1024]{1,0:T(8,128)(2,1)S(1)} collective-permute-done((bf16[256,1024]{1,0:T(8,128)(2,1)S(1)}, bf16[256,1024]{1,0:T(8,128)(2,1)S(1)}, u32[]{:S(2)}, u32[]{:S(2)}) %collective-permute-start.3) | collective-permute-done | bytes 524320 | tf_op jit(solution)/shard_map/ppermute | solution.py:33
  27.7 2.6 %collective-permute-done.5 = bf16[256,1024]{1,0:T(8,128)(2,1)S(1)} collective-permute-done((bf16[256,1024]{1,0:T(8,128)(2,1)S(1)}, bf16[256,1024]{1,0:T(8,128)(2,1)S(1)}, u32[]{:S(2)}, u32[]{:S(2)}) %collective-permute-start.5) | collective-permute-done | bytes 524320 | tf_op jit(solution)/shard_map/ppermute | solution.py:33
  31.3 2.4 %collective-permute-start.7 = (bf16[512,1024]{1,0:T(8,128)(2,1)}, bf16[512,1024]{1,0:T(8,128)(2,1)}, u32[]{:S(2)}, u32[]{:S(2)}) collective-permute-start(bf16[512,1024]{1,0:T(8,128)(2,1)} %constant_dynamic-update-slice_fusion.4.refs_0_.refs_8_), channel_id=1, source_target_pairs={{16,0},{3,1},{32,16},{19,17},{48,32},{35,33},{0,48},{51,49},{18,2}... | collective-permute-start | bytes 3145736 | tf_op jit(solution)/shard_map/ppermute | solution.py:33
  39.0 2.9 %scores.5 = (f32[2,512,512]{2,1,0:T(8,128)S(1)}, f32[4,512]{1,0:T(4,128)S(1)}) custom-call(bf16[512,1024]{1,0:T(8,128)(2,1)S(1)} %copy-done.14, bf16[512,1024]{1,0:T(8,128)(2,1)S(1)} %copy-done.30, bf16[512,1024]{1,0:T(8,128)(2,1)} %constant_dynamic-update-slice_fusion.4.refs_0_.refs_8_), custom_call_target="tpu_custom_call" | custom-call | flops 2147483648 | bytes 5242880 | tf_op jit(solution)/shard_map/scores/pallas_call | solution.py:74
  42.4 2.7 %collective-permute-start.9 = (bf16[512,1024]{1,0:T(8,128)(2,1)S(1)}, bf16[512,1024]{1,0:T(8,128)(2,1)}, u32[]{:S(2)}, u32[]{:S(2)}) collective-permute-start(bf16[512,1024]{1,0:T(8,128)(2,1)S(1)} %pad_maximum_fusion.refs_0_.refs_9_), channel_id=1, source_target_pairs={{16,0},{3,1},{32,16},{19,17},{48,32},{35,33},{0,48},{51,49},{18,2}... | collective-permute-start | bytes 3145736 | tf_op jit(solution)/shard_map/ppermute | solution.py:33
  46.1 9.6 %all-to-all-start = ((s32[128,1,64]{2,1,0:T(1,128)}), s32[128,1,64]{2,1,0:T(1,128)S(1)}, u32[]{:S(2)}, u32[]{:S(2)}) async-start(s32[128,1,64]{2,1,0:T(1,128)} %bitcast.5), calls=%async_computation | async-start | bytes 131072 | tf_op jit(solution)/shard_map/all_to_all | solution.py:223
  58.2 1.6 %scores.6 = (f32[2,512,512]{2,1,0:T(8,128)S(1)}, f32[4,512]{1,0:T(4,128)S(1)}) custom-call(bf16[512,1024]{1,0:T(8,128)(2,1)S(1)} %copy-done.15, bf16[512,1024]{1,0:T(8,128)(2,1)S(1)} %copy-done.31, bf16[512,1024]{1,0:T(8,128)(2,1)S(1)} %pad_maximum_fusion.refs_0_.refs_9_), custom_call_target="tpu_custom_call" | custom-call | flops 2147483648 | bytes 5242880 | tf_op jit(solution)/shard_map/scores/pallas_call | solution.py:74
  61.7 4.7 %all-to-all-done = s32[128,1,64]{2,1,0:T(1,128)S(1)} async-done(((s32[128,1,64]{2,1,0:T(1,128)}), s32[128,1,64]{2,1,0:T(1,128)S(1)}, u32[]{:S(2)}, u32[]{:S(2)}) %all-to-all-start) | async-done | bytes 32800 | tf_op jit(solution)/shard_map/all_to_all | solution.py:223
  70.5 4.5 %scores.7 = (f32[2,512,512]{2,1,0:T(8,128)S(1)}, f32[2,512,512]{2,1,0:T(8,128)S(1)}, f32[4,1024]{1,0:T(4,128)S(1)}) custom-call(bf16[512,1024]{1,0:T(8,128)(2,1)S(1)} %copy-done.16, bf16[512,1024]{1,0:T(8,128)(2,1)S(1)} %copy-done.32, bf16[512,1024]{1,0:T(8,128)(2,1)} %collective-permute-done.7.refs_0_.refs_10_, ...), custom_call_target="tpu_custom_call" | custom-call | flops 4294967296 | bytes 8388608 | tf_op jit(solution)/shard_map/scores/pallas_call | solution.py:74
  76.4 1.4 copy-done.4
  78.4 4.5 %scores.8 = (f32[2,512,512]{2,1,0:T(8,128)S(1)}, f32[2,512,512]{2,1,0:T(8,128)S(1)}, f32[4,1024]{1,0:T(4,128)S(1)}) custom-call(bf16[512,1024]{1,0:T(8,128)(2,1)S(1)} %copy-done.16, bf16[512,1024]{1,0:T(8,128)(2,1)S(1)} %copy-done.32, bf16[512,1024]{1,0:T(8,128)(2,1)} %collective-permute-done.9.refs_0_.refs_11_, ...), custom_call_target="tpu_custom_call" | custom-call | flops 4294967296 | bytes 8388608 | tf_op jit(solution)/shard_map/scores/pallas_call | solution.py:74
  84.2 1.4 copy-done.8
  86.2 3.0 %scores.9 = (f32[2,512,512]{2,1,0:T(8,128)S(1)}, f32[2,512,512]{2,1,0:T(8,128)S(1)}, f32[4,1024]{1,0:T(4,128)S(1)}) custom-call(bf16[512,1024]{1,0:T(8,128)(2,1)S(1)} %copy-done.16, bf16[512,1024]{1,0:T(8,128)(2,1)S(1)} %copy-done.32, bf16[512,1024]{1,0:T(8,128)(2,1)S(1)} %collective-permute-done.11.refs_0_.refs_12_, ...), custom_call_target="tpu_custom_call" | custom-call | flops 4294967296 | bytes 8388608 | tf_op jit(solution)/shard_map/scores/pallas_call | solution.py:74
  90.5 1.4 copy-done.12
  92.5 2.5 %first.1 = (f32[64,8,512]{2,1,0:T(8,128)}, f32[2,4096]{1,0:T(2,128)}) custom-call(s32[3]{0:T(128)} %copy-done.34, f32[4,512]{1,0:T(4,128)} %copy-done.27, f32[4,512]{1,0:T(4,128)} %copy-done.28, f32[4,1024]{1,0:T(4,128)} %copy-done.24, f32[4,1024]{1,0:T(4,128)} %copy-done.25, f32[4,1024]{1,0:T(4,128)} %copy-done.26), custom_call_target="tpu_custom_call" | custom-call | tf_op jit(solution)/shard_map/first/pallas_call | solution.py:239
  95.1 23.5 %all_to_all.14.all_ref = f32[64,8,512]{2,1,0:T(8,128)} all-to-all(f32[64,8,512]{2,1,0:T(8,128)} %get-tuple-element.41), channel_id=1, replica_groups={{0,16,32,48,2,18,34,50,4,20,36,52,6,22,38,54,8,24,40,56,10,26,42,58,12,..., dimensions={0} | all-to-all | bytes 2097152 | tf_op jit(solution)/shard_map/all_to_all | solution.py:251
  118.6 2.5 %merge.1 = (f32[8,512]{1,0:T(8,128)}, f32[1,4096]{1,0:T(1,128)}) custom-call(s32[3]{0:T(128)} %copy-done.34, f32[64,8,512]{2,1,0:T(8,128)} %all_to_all.14.all_ref), custom_call_target="tpu_custom_call" | custom-call | tf_op jit(solution)/shard_map/merge/pallas_call | solution.py:252
  121.1 1.6 %copy-done.1 = f32[2,512,512]{2,1,0:T(8,128)S(1)} copy-done((f32[2,512,512]{2,1,0:T(8,128)S(1)}, f32[2,512,512]{2,1,0:T(8,128)}, u32[]{:S(2)}) %copy-start.1) | copy-done | bytes 2097176
  122.7 1.6 %copy-done.3 = f32[2,512,512]{2,1,0:T(8,128)S(1)} copy-done((f32[2,512,512]{2,1,0:T(8,128)S(1)}, f32[2,512,512]{2,1,0:T(8,128)}, u32[]{:S(2)}) %copy-start.3) | copy-done | bytes 2097176
  124.2 1.6 %copy-done.5 = f32[2,512,512]{2,1,0:T(8,128)S(1)} copy-done((f32[2,512,512]{2,1,0:T(8,128)S(1)}, f32[2,512,512]{2,1,0:T(8,128)}, u32[]{:S(2)}) %copy-start.5) | copy-done | bytes 2097176
  125.8 1.6 %copy-done.7 = f32[2,512,512]{2,1,0:T(8,128)S(1)} copy-done((f32[2,512,512]{2,1,0:T(8,128)S(1)}, f32[2,512,512]{2,1,0:T(8,128)}, u32[]{:S(2)}) %copy-start.7) | copy-done | bytes 2097176
  127.4 1.6 %copy-done.9 = f32[2,512,512]{2,1,0:T(8,128)S(1)} copy-done((f32[2,512,512]{2,1,0:T(8,128)S(1)}, f32[2,512,512]{2,1,0:T(8,128)}, u32[]{:S(2)}) %copy-start.9) | copy-done | bytes 2097176
  129.0 1.6 %copy-done.11 = f32[2,512,512]{2,1,0:T(8,128)S(1)} copy-done((f32[2,512,512]{2,1,0:T(8,128)S(1)}, f32[2,512,512]{2,1,0:T(8,128)}, u32[]{:S(2)}) %copy-start.11) | copy-done | bytes 2097176
  130.6 1.6 %copy-done.13 = f32[2,512,512]{2,1,0:T(8,128)S(1)} copy-done((f32[2,512,512]{2,1,0:T(8,128)S(1)}, f32[2,512,512]{2,1,0:T(8,128)}, u32[]{:S(2)}) %copy-start.13) | copy-done | bytes 2097176
  135.4 7.4 %sums.3 = f32[512,1152]{1,0:T(8,128)S(1)} custom-call(f32[1,4096]{1,0:T(1,128)S(1)} %copy-done.23, f32[2,4096]{1,0:T(2,128)S(1)} %copy-done.22, f32[2,512,512]{2,1,0:T(8,128)S(1)} %get-tuple-element.44.refs_0_, f32[2,512,512]{2,1,0:T(8,128)S(1)} %copy-done.1, f32[2,512,512]{2,1,0:T(8,128)S(1)} %copy-done.3, f32[2,512,512]{2,1,0:T(8,128)S(1)} %copy-done.7, ...), custom_call_target="tpu_custom_call" | custom-call | flops 4294967296 | bytes 18874368 | tf_op jit(solution)/shard_map/sums/pallas_call | solution.py:166
  142.8 3.1 %collective-permute-start.13 = (f32[512,1152]{1,0:T(8,128)S(1)}, f32[512,1152]{1,0:T(8,128)S(1)}, u32[]{:S(2)}, u32[]{:S(2)}) collective-permute-start(f32[512,1152]{1,0:T(8,128)S(1)} %sums.3), channel_id=1, source_target_pairs={{0,1},{1,0},{2,3},{3,2},{4,5},{5,4},{6,7},{7,6},{8,9},{9,8},{10,11... | collective-permute-start | bytes 7077896 | tf_op jit(solution)/shard_map/ppermute | solution.py:38
  146.1 7.5 %sums.2.ours_ref = f32[512,1152]{1,0:T(8,128)S(1)} custom-call(f32[1,4096]{1,0:T(1,128)S(1)} %copy-done.23, f32[2,4096]{1,0:T(2,128)S(1)} %copy-done.22, f32[2,512,512]{2,1,0:T(8,128)S(1)} %get-tuple-element.44.refs_0_, f32[2,512,512]{2,1,0:T(8,128)S(1)} %copy-done.1, f32[2,512,512]{2,1,0:T(8,128)S(1)} %copy-done.3, f32[2,512,512]{2,1,0:T(8,128)S(1)} %copy-done.7, ...), custom_call_target="tpu_custom_call" | custom-call | flops 4294967296 | bytes 18874368 | tf_op jit(solution)/shard_map/sums/pallas_call | solution.py:166
  154.5 1.7 %final.1 = f32[512,1024]{1,0:T(8,128)} custom-call(f32[512,1152]{1,0:T(8,128)S(1)} %sums.2.ours_ref, f32[512,1152]{1,0:T(8,128)S(1)} %collective-permute-done.13.theirs_ref, bf16[512,1024]{1,0:T(8,128)(2,1)S(1)} %copy-done.17), custom_call_target="tpu_custom_call" | custom-call | tf_op jit(solution)/shard_map/final/pallas_call | solution.py:268
  (102 shorter events, 30.7 us)
Async XLA Ops:
  0.6 9.0 %collective-permute-start = (bf16[64,1024]{1,0:T(8,128)(2,1)}, bf16[64,1024]{1,0:T(8,128)(2,1)S(1)}, u32[]{:S(2)}, u32[]{:S(2)}) collective-permute-start(bf16[64,1024]{1,0:T(8,128)(2,1)} %param.3), channel_id=1, source_target_pairs={{8,0},{17,1},{24,16},{33,17},{40,32},{49,33},{56,48},{1,49},{10,2}... | collective-permute-start | bytes 393224 | tf_op jit(solution)/shard_map/ppermute | solution.py:33
  5.3 5.9 %collective-permute-start.1 = (bf16[64,1024]{1,0:T(8,128)(2,1)}, bf16[64,1024]{1,0:T(8,128)(2,1)S(1)}, u32[]{:S(2)}, u32[]{:S(2)}) collective-permute-start(bf16[64,1024]{1,0:T(8,128)(2,1)} %param.3), channel_id=1, source_target_pairs={{64,0},{33,1},{80,16},{49,17},{96,32},{1,33},{112,48},{17,49},{66,... | collective-permute-start | bytes 393224 | tf_op jit(solution)/shard_map/ppermute | solution.py:33
  5.3 6.9 %collective-permute-start.2 = (bf16[64,1024]{1,0:T(8,128)(2,1)}, bf16[64,1024]{1,0:T(8,128)(2,1)S(1)}, u32[]{:S(2)}, u32[]{:S(2)}) collective-permute-start(bf16[64,1024]{1,0:T(8,128)(2,1)} %param.3), channel_id=1, source_target_pairs={{72,0},{49,1},{88,16},{1,17},{104,32},{17,33},{120,48},{33,49},{74... | collective-permute-start | bytes 393224 | tf_op jit(solution)/shard_map/ppermute | solution.py:33
  6.0 3.0 %copy-start.33 = (bf16[64,1024]{1,0:T(8,128)(2,1)S(1)}, bf16[64,1024]{1,0:T(8,128)(2,1)}, u32[]{:S(2)}) copy-start(bf16[64,1024]{1,0:T(8,128)(2,1)} %param.3) | copy-start | bytes 393220
  8.2 22.1 %collective-permute-start.6 = (bf16[512,1024]{1,0:T(8,128)(2,1)}, bf16[512,1024]{1,0:T(8,128)(2,1)S(1)}, u32[]{:S(2)}, u32[]{:S(2)}) collective-permute-start(bf16[512,1024]{1,0:T(8,128)(2,1)} %share.1.mine_ref), channel_id=1, source_target_pairs={{0,1},{1,0},{2,3},{3,2},{4,5},{5,4},{6,7},{7,6},{8,9},{9,8},{10,11... | collective-permute-start | bytes 3145736 | tf_op jit(solution)/shard_map/ppermute | solution.py:38
  12.9 13.9 %collective-permute-start.3 = (bf16[256,1024]{1,0:T(8,128)(2,1)S(1)}, bf16[256,1024]{1,0:T(8,128)(2,1)S(1)}, u32[]{:S(2)}, u32[]{:S(2)}) collective-permute-start(bf16[256,1024]{1,0:T(8,128)(2,1)S(1)} %get-tuple-element.54), channel_id=1, source_target_pairs={{2,0},{9,1},{18,16},{25,17},{34,32},{41,33},{50,48},{57,49},{4,2},... | collective-permute-start | bytes 1572872 | tf_op jit(solution)/shard_map/ppermute | solution.py:33
  15.1 15.2 %collective-permute-start.5 = (bf16[256,1024]{1,0:T(8,128)(2,1)S(1)}, bf16[256,1024]{1,0:T(8,128)(2,1)S(1)}, u32[]{:S(2)}, u32[]{:S(2)}) collective-permute-start(bf16[256,1024]{1,0:T(8,128)(2,1)S(1)} %get-tuple-element.54), channel_id=1, source_target_pairs={{6,0},{73,1},{22,16},{89,17},{38,32},{105,33},{54,48},{121,49},{0,... | collective-permute-start | bytes 1572872 | tf_op jit(solution)/shard_map/ppermute | solution.py:33
  15.1 15.2 %collective-permute-start.4 = (bf16[256,1024]{1,0:T(8,128)(2,1)S(1)}, bf16[256,1024]{1,0:T(8,128)(2,1)S(1)}, u32[]{:S(2)}, u32[]{:S(2)}) collective-permute-start(bf16[256,1024]{1,0:T(8,128)(2,1)S(1)} %get-tuple-element.54), channel_id=1, source_target_pairs={{4,0},{65,1},{20,16},{81,17},{36,32},{97,33},{52,48},{113,49},{6,2... | collective-permute-start | bytes 1572872 | tf_op jit(solution)/shard_map/ppermute | solution.py:33
  31.3 35.2 %collective-permute-start.7 = (bf16[512,1024]{1,0:T(8,128)(2,1)}, bf16[512,1024]{1,0:T(8,128)(2,1)}, u32[]{:S(2)}, u32[]{:S(2)}) collective-permute-start(bf16[512,1024]{1,0:T(8,128)(2,1)} %constant_dynamic-update-slice_fusion.4.refs_0_.refs_8_), channel_id=1, source_target_pairs={{16,0},{3,1},{32,16},{19,17},{48,32},{35,33},{0,48},{51,49},{18,2}... | collective-permute-start | bytes 3145736 | tf_op jit(solution)/shard_map/ppermute | solution.py:33
  33.8 32.7 %collective-permute-start.8 = (bf16[512,1024]{1,0:T(8,128)(2,1)S(1)}, bf16[512,1024]{1,0:T(8,128)(2,1)}, u32[]{:S(2)}, u32[]{:S(2)}) collective-permute-start(bf16[512,1024]{1,0:T(8,128)(2,1)S(1)} %pad_maximum_fusion.refs_0_.refs_9_), channel_id=1, source_target_pairs={{48,0},{7,1},{0,16},{23,17},{16,32},{39,33},{32,48},{55,49},{50,2}... | collective-permute-start | bytes 3145736 | tf_op jit(solution)/shard_map/ppermute | solution.py:33
  33.9 7.9 %copy-start.34 = (s32[3]{0:T(128)}, s32[3]{0:T(128)S(1)}, u32[]{:S(2)}) copy-start(s32[3]{0:T(128)S(1)} %broadcast_select_fusion.spot_ref) | copy-start | bytes 40
  38.9 6.1 %copy-start.36 = (s32[64]{0:T(128)S(1)}, s32[64]{0:T(128)}, u32[]{:S(2)}) copy-start(s32[64]{0:T(128)} %param.4) | copy-start | bytes 772
  42.4 35.9 %collective-permute-start.9 = (bf16[512,1024]{1,0:T(8,128)(2,1)S(1)}, bf16[512,1024]{1,0:T(8,128)(2,1)}, u32[]{:S(2)}, u32[]{:S(2)}) collective-permute-start(bf16[512,1024]{1,0:T(8,128)(2,1)S(1)} %pad_maximum_fusion.refs_0_.refs_9_), channel_id=1, source_target_pairs={{16,0},{3,1},{32,16},{19,17},{48,32},{35,33},{0,48},{51,49},{18,2}... | collective-permute-start | bytes 3145736 | tf_op jit(solution)/shard_map/ppermute | solution.py:33
  45.1 33.3 %collective-permute-start.10 = (bf16[512,1024]{1,0:T(8,128)(2,1)}, bf16[512,1024]{1,0:T(8,128)(2,1)}, u32[]{:S(2)}, u32[]{:S(2)}) collective-permute-start(bf16[512,1024]{1,0:T(8,128)(2,1)} %constant_dynamic-update-slice_fusion.4.refs_0_.refs_8_), channel_id=1, source_target_pairs={{48,0},{7,1},{0,16},{23,17},{16,32},{39,33},{32,48},{55,49},{50,2}... | collective-permute-start | bytes 3145736 | tf_op jit(solution)/shard_map/ppermute | solution.py:33
  46.1 20.2 %all-to-all-start = ((s32[128,1,64]{2,1,0:T(1,128)}), s32[128,1,64]{2,1,0:T(1,128)S(1)}, u32[]{:S(2)}, u32[]{:S(2)}) async-start(s32[128,1,64]{2,1,0:T(1,128)} %bitcast.5), calls=%async_computation | async-start | bytes 131072 | tf_op jit(solution)/shard_map/all_to_all | solution.py:223
  66.5 19.7 %collective-permute-start.11 = (bf16[512,1024]{1,0:T(8,128)(2,1)}, bf16[512,1024]{1,0:T(8,128)(2,1)S(1)}, u32[]{:S(2)}, u32[]{:S(2)}) collective-permute-start(bf16[512,1024]{1,0:T(8,128)(2,1)} %collective-permute-done.7.refs_0_.refs_10_), channel_id=1, source_target_pairs={{16,0},{3,1},{32,16},{19,17},{48,32},{35,33},{0,48},{51,49},{18,2}... | collective-permute-start | bytes 3145736 | tf_op jit(solution)/shard_map/ppermute | solution.py:33
  67.1 19.1 %collective-permute-start.12 = (bf16[512,1024]{1,0:T(8,128)(2,1)}, bf16[512,1024]{1,0:T(8,128)(2,1)S(1)}, u32[]{:S(2)}, u32[]{:S(2)}) collective-permute-start(bf16[512,1024]{1,0:T(8,128)(2,1)} %collective-permute-done.8.refs_1_.refs_15_), channel_id=1, source_target_pairs={{48,0},{7,1},{0,16},{23,17},{16,32},{39,33},{32,48},{55,49},{50,2}... | collective-permute-start | bytes 3145736 | tf_op jit(solution)/shard_map/ppermute | solution.py:33
  86.2 3.0 %copy-start.18 = (bf16[512,1024]{1,0:T(8,128)(2,1)}, bf16[512,1024]{1,0:T(8,128)(2,1)S(1)}, u32[]{:S(2)}) copy-start(bf16[512,1024]{1,0:T(8,128)(2,1)S(1)} %collective-permute-done.11.refs_0_.refs_12_) | copy-start | bytes 3145732
  86.2 3.0 %copy-start.20 = (bf16[512,1024]{1,0:T(8,128)(2,1)}, bf16[512,1024]{1,0:T(8,128)(2,1)S(1)}, u32[]{:S(2)}) copy-start(bf16[512,1024]{1,0:T(8,128)(2,1)S(1)} %collective-permute-done.12.refs_1_.refs_13_) | copy-start | bytes 3145732
  90.5 1.4 copy-start.12
  95.0 26.0 %copy-start.22 = (f32[2,4096]{1,0:T(2,128)S(1)}, f32[2,4096]{1,0:T(2,128)}, u32[]{:S(2)}) copy-start(f32[2,4096]{1,0:T(2,128)} %get-tuple-element.43.top_ref) | copy-start | bytes 98308
  121.1 1.6 %copy-start.1 = (f32[2,512,512]{2,1,0:T(8,128)S(1)}, f32[2,512,512]{2,1,0:T(8,128)}, u32[]{:S(2)}) copy-start(f32[2,512,512]{2,1,0:T(8,128)} %copy-done) | copy-start | bytes 6291460
  122.7 1.6 %copy-start.3 = (f32[2,512,512]{2,1,0:T(8,128)S(1)}, f32[2,512,512]{2,1,0:T(8,128)}, u32[]{:S(2)}) copy-start(f32[2,512,512]{2,1,0:T(8,128)} %copy-done.2) | copy-start | bytes 6291460
  124.2 1.6 %copy-start.5 = (f32[2,512,512]{2,1,0:T(8,128)S(1)}, f32[2,512,512]{2,1,0:T(8,128)}, u32[]{:S(2)}) copy-start(f32[2,512,512]{2,1,0:T(8,128)} %copy-done.4) | copy-start | bytes 6291460
  125.8 1.6 %copy-start.7 = (f32[2,512,512]{2,1,0:T(8,128)S(1)}, f32[2,512,512]{2,1,0:T(8,128)}, u32[]{:S(2)}) copy-start(f32[2,512,512]{2,1,0:T(8,128)} %copy-done.6) | copy-start | bytes 6291460
  127.4 1.6 %copy-start.9 = (f32[2,512,512]{2,1,0:T(8,128)S(1)}, f32[2,512,512]{2,1,0:T(8,128)}, u32[]{:S(2)}) copy-start(f32[2,512,512]{2,1,0:T(8,128)} %copy-done.8) | copy-start | bytes 6291460
  129.0 1.6 %copy-start.11 = (f32[2,512,512]{2,1,0:T(8,128)S(1)}, f32[2,512,512]{2,1,0:T(8,128)}, u32[]{:S(2)}) copy-start(f32[2,512,512]{2,1,0:T(8,128)} %copy-done.10) | copy-start | bytes 6291460
  130.6 1.6 %copy-start.13 = (f32[2,512,512]{2,1,0:T(8,128)S(1)}, f32[2,512,512]{2,1,0:T(8,128)}, u32[]{:S(2)}) copy-start(f32[2,512,512]{2,1,0:T(8,128)} %copy-done.12) | copy-start | bytes 6291460
  135.4 10.6 %copy-start.35 = (f32[8,512]{1,0:T(8,128)S(1)}, f32[8,512]{1,0:T(8,128)}, u32[]{:S(2)}) copy-start(f32[8,512]{1,0:T(8,128)} %get-tuple-element.53) | copy-start | bytes 49156
  142.8 11.7 %collective-permute-start.13 = (f32[512,1152]{1,0:T(8,128)S(1)}, f32[512,1152]{1,0:T(8,128)S(1)}, u32[]{:S(2)}, u32[]{:S(2)}) collective-permute-start(f32[512,1152]{1,0:T(8,128)S(1)} %sums.3), channel_id=1, source_target_pairs={{0,1},{1,0},{2,3},{3,2},{4,5},{5,4},{6,7},{7,6},{8,9},{9,8},{10,11... | collective-permute-start | bytes 7077896 | tf_op jit(solution)/shard_map/ppermute | solution.py:38
  145.9 8.6 %copy-start.17 = (bf16[512,1024]{1,0:T(8,128)(2,1)S(1)}, bf16[512,1024]{1,0:T(8,128)(2,1)}, u32[]{:S(2)}) copy-start(bf16[512,1024]{1,0:T(8,128)(2,1)} %share.1.mine_ref) | copy-start | bytes 3145732
  145.9 7.6 %collective-permute-start.14 = (f32[4096]{0:T(1024)S(1)}, f32[4096]{0:T(1024)S(1)}, u32[]{:S(2)}, u32[]{:S(2)}) collective-permute-start(f32[4096]{0:T(1024)S(1)} %bitcast.8), channel_id=1, source_target_pairs={{0,1},{1,0},{2,3},{3,2},{4,5},{5,4},{6,7},{7,6},{8,9},{9,8},{10,11... | collective-permute-start | bytes 49160 | tf_op jit(solution)/shard_map/ppermute | solution.py:38
  (21 other events, 22.6 us)

commit v4 on v3

--- a/solution.py
+++ b/solution.py
@@ -77,7 +77,7 @@
         + (jax.ShapeDtypeStruct((4, count * n), jnp.float32),),
         in_specs=[vmem] * (2 + count),
         out_specs=tuple([vmem] * (count + 1)),
-        compiler_params=pltpu.CompilerParams(vmem_limit_bytes=16 << 20),
+        compiler_params=pltpu.CompilerParams(vmem_limit_bytes=12 << 20),
         cost_estimate=pl.CostEstimate(
             flops=4 * 1024 * n * width * count,
             bytes_accessed=count * n * 6144 + (2 << 20),
@@ -130,11 +130,8 @@
 def sums_kernel(half, count, lse_ref, top_ref, *refs):
     ps = refs[:count]
     rows = refs[count : 2 * count]
-    out_ref, row_buf, sems = refs[2 * count :]
+    out_ref = refs[2 * count]
     n, width = rows[0].shape
-    loads = [pltpu.make_async_copy(rows[k], row_buf.at[k], sems.at[k]) for k in range(count)]
-    for load in loads:
-        load.start()
 
     def weights(k):
         lanes = slice(k * n, (k + 1) * n)
@@ -149,8 +146,7 @@
         if k + 1 < count:
             w, more = weights(k + 1)
             mass = mass + more
-        loads[k].wait()
-        add = jnp.dot(now, row_buf[k], preferred_element_type=jnp.float32)
+        add = jnp.dot(now, rows[k][...], preferred_element_type=jnp.float32)
         if k == 0:
             out_ref[:, :width] = add
         else:
@@ -160,15 +156,13 @@
 
 def sums_call(half, lse, tops, ps, rows):
     count = len(rows)
-    n, width = rows[0].shape
+    width = rows[0].shape[1]
     vmem = pl.BlockSpec(memory_space=pltpu.VMEM)
-    hbm = pl.BlockSpec(memory_space=pltpu.HBM)
     return pl.pallas_call(
         functools.partial(sums_kernel, half, count),
         out_shape=jax.ShapeDtypeStruct((512, width + 128), jnp.float32),
-        in_specs=[vmem] * (2 + count) + [hbm] * count,
-        scratch_shapes=[pltpu.VMEM((count, n, width), jnp.bfloat16), pltpu.SemaphoreType.DMA((count,))],
-        compiler_params=pltpu.CompilerParams(vmem_limit_bytes=20 << 20),
+        in_specs=[vmem] * (2 + 2 * count),
+        compiler_params=pltpu.CompilerParams(vmem_limit_bytes=10 << 20),
         cost_estimate=pl.CostEstimate(
             flops=2 * 512 * 4096 * width, bytes_accessed=18 << 20, transcendentals=8192
         ),
@@ -193,8 +187,9 @@
 
 def shards(embeddings, destination, centroids):
     samp, cent = lax.axis_index("samp"), lax.axis_index("cent")
-    core = cent % 2
-    x, y, z = (samp // 4) * 2 + cent // 8, (cent // 2) % 4, samp % 4
+    core = lax.bitwise_and(cent, 1)
+    x = lax.shift_right_logical(samp, 2) * 2 + lax.shift_right_logical(cent, 3)
+    y, z = lax.bitwise_and(lax.shift_right_logical(cent, 1), 3), lax.bitwise_and(samp, 3)
     spot = jnp.where(core == 0, jnp.stack([x, y, z]), jnp.stack([z, x, y])).astype(jnp.int32)
     share = centroids.shape[0] // 8
     width = embeddings.shape[1]
@@ -206,16 +201,12 @@
         in_specs=[smem, pl.BlockSpec(memory_space=pltpu.HBM)],
         out_specs=vmem,
         scratch_shapes=[pltpu.SemaphoreType.DMA(())],
+        compiler_params=pltpu.CompilerParams(vmem_limit_bytes=8 << 20),
         name="share",
     )(samp.astype(jnp.int32).reshape(1), centroids)
     other = swap_cores(mine)
     line = jnp.concatenate([embeddings] + [fetch(embeddings, 0, step) for step in (1, 2, 3)])
-    near, across, back = [fetch(line, 1, step) for step in (1, 2, 3)]
-    upper, lower = jnp.concatenate([line, near]), jnp.concatenate([across, back])
-    upper, lower, other = lax.optimization_barrier((upper, lower, other))
-    after_upper, before_lower = fetch(upper, 2, 1), fetch(lower, 2, 3)
-
-    late, _, _ = lax.optimization_barrier((destination, upper, lower))
+    late, spot, _ = lax.optimization_barrier((destination, spot, line))
     start = core * 4096 + ((spot[2] * 4 + spot[1]) * 4 + spot[0]) * UNIT
     spots = lax.broadcasted_iota(jnp.int32, (UNIT, 8192), 1)
     keys = (start + jnp.arange(UNIT, dtype=jnp.int32))[:, None]
@@ -223,11 +214,16 @@
     arrived = lax.all_to_all(spread.reshape(128, UNIT), BOTH, split_axis=0, concat_axis=0, tiled=True)
     keys = jnp.sum(arrived, axis=0)
 
+    near, across, back = [fetch(line, 1, step) for step in (1, 2, 3)]
+    upper, lower = jnp.concatenate([line, near]), jnp.concatenate([across, back])
+    upper, lower, other, keys = lax.optimization_barrier((upper, lower, other, keys))
+    after_upper, before_lower = fetch(upper, 2, 1), fetch(lower, 2, 3)
+
     p_upper, stat_upper = scores_call(mine, other, [upper])
     upper_again, lower_again, _ = lax.optimization_barrier((upper, lower, stat_upper))
     after_lower, before_upper = fetch(lower_again, 2, 1), fetch(upper_again, 2, 3)
     p_lower, stat_lower = scores_call(mine, other, [lower])
-    passed_up, passed_down, keys, _ = lax.optimization_barrier((after_upper, before_lower, keys, stat_lower))
+    passed_up, passed_down, _ = lax.optimization_barrier((after_upper, before_lower, stat_lower))
     far_upper, far_lower = fetch(passed_up, 2, 1), fetch(passed_down, 2, 3)
     p_first, stat_first = scores_call(mine, other, [after_upper, before_lower])
     p_second, stat_second = scores_call(mine, other, [after_lower, before_upper])
@@ -243,6 +239,7 @@
             jax.ShapeDtypeStruct((2, 4096), jnp.float32),
         ),
         in_specs=[smem] + [vmem] * 5,
+        compiler_params=pltpu.CompilerParams(vmem_limit_bytes=8 << 20),
         name="first",
     )(spot, stat_upper, stat_lower, stat_first, stat_second, stat_far)
     chips = [
@@ -256,6 +253,7 @@
             jax.ShapeDtypeStruct((1, 4096), jnp.float32),
         ),
         in_specs=[smem, vmem],
+        compiler_params=pltpu.CompilerParams(vmem_limit_bytes=8 << 20),
         name="merge",
     )(spot, shared)
     theirs = sums_call(1, lse, tops, ps, chunks)
@@ -267,7 +265,7 @@
     row_lse = jnp.sum(jnp.where(spots == keys[:, None], every[None, :], 0.0), axis=1) * math.log(2.0)
     new_centers = pl.pallas_call(
         final_kernel, out_shape=jax.ShapeDtypeStruct((share, width), jnp.float32), name="final",
-        compiler_params=pltpu.CompilerParams(vmem_limit_bytes=16 << 20),
+        compiler_params=pltpu.CompilerParams(vmem_limit_bytes=8 << 20),
     )(ours, received, mine)
     return new_centers, row_lse
 

time: 157 us -> 123 us (0.78)
  local copies, waits for them, and re-layouts: 40 us -> 8.9 us
  blocking collectives: 23.5 us -> 39.2 us
  Pallas kernels: 40.3 us -> 25.7 us
  starting transfers between devices: 29.5 us -> 18.8 us
  waiting for transfers between devices: 18.5 us -> 24.2 us
    unnamed x78 -> x11, local copies, waits for them, and re-layouts: 37.2 us -> 7.09 us
    all_to_all x0 -> x1, blocking collectives: none -> 19.4 us  [shards(): lax.all_to_all(spread.reshape(128, UNIT), BOTH, split_axis=0, concat_axis...]
    ppermute x12, waiting for transfers between devices: 13.8 us -> 24.2 us  [fetch(): return lax.ppermute(value, BOTH, pairs)]
    all_to_all x1 -> x0, starting transfers between devices: 9.55 us -> none  [shards(): lax.all_to_all(spread.reshape(128, UNIT), BOTH, split_axis=0, concat_axis...]
    pallas_call x2, Pallas kernels: 14.9 us -> 9.17 us  [sums_call(): pl.pallas_call(functools.partial(sums_kernel, half, count), out_shape=jax...]
    all_to_all x1 -> x0, waiting for transfers between devices: 4.67 us -> none  [shards(): lax.all_to_all(spread.reshape(128, UNIT), BOTH, split_axis=0, concat_axis...]
    pallas_call x5, Pallas kernels: 16.5 us -> 12.3 us  [scores_call(): pl.pallas_call(functools.partial(scores_kernel, factor, count), out_shape...]
    all_to_all x1, blocking collectives: 23.5 us -> 19.9 us  [shards(): lax.all_to_all(local, BOTH, split_axis=0, concat_axis=0, tiled=True, axis...]
  transfers between devices with their start and end apart: 16 -> 15, of which waited for: 5 -> 6; matrix products, arithmetic and copies ran while one was open for 4% -> 7% of each run, Pallas kernels for 15% -> 11%
where the time goes in v4:
time: 123 us; the launch traced here: 122 us
  blocking collectives  39.2 us (32%)
  Pallas kernels  25.7 us (21%)
  waiting for transfers between devices  24.2 us (20%)
  starting transfers between devices  18.8 us (15%)
  local copies, waits for them, and re-layouts  8.9 us (7%)
  other arithmetic  2.83 us (2%)
  between operations  2.67 us (2%)
    ppermute x12, waiting for transfers between devices, fetch(): return lax.ppermute(value, BOTH, pairs)  24.2 us
    all_to_all x1, blocking collectives, shards(): lax.all_to_all(local, BOTH, split_axis=0, concat_axis=0, tiled=True, axis...  19.9 us
    all_to_all x1, blocking collectives, shards(): lax.all_to_all(spread.reshape(128, UNIT), BOTH, split_axis=0, concat_axis...  19.4 us
    ppermute x12, starting transfers between devices, fetch(): return lax.ppermute(value, BOTH, pairs)  14.4 us
    pallas_call x5, Pallas kernels, scores_call(): pl.pallas_call(functools.partial(scores_kernel, factor, count), out_shape...  12.3 us
    pallas_call x2, Pallas kernels, sums_call(): pl.pallas_call(functools.partial(sums_kernel, half, count), out_shape=jax...  9.17 us
    unnamed x11, local copies, waits for them, and re-layouts  7.09 us
    ppermute x3, starting transfers between devices, swap_cores(): return lax.ppermute(value, BOTH, pairs)  4.38 us
  transfers between devices with their start and end apart: 15, of which 6 were waited for; matrix products, arithmetic and copies ran while one was open for 7% of the time, Pallas kernels for 11%

profile of v4, /device:TPU:1, one launch (start us, length us, event | category | flops | bytes accessed | tf_op | source)
XLA Modules:
  0.0 122.3 jit_solution(9683827579865791784)
XLA Ops:
  0.6 4.7 %collective-permute-start = (bf16[64,1024]{1,0:T(8,128)(2,1)}, bf16[64,1024]{1,0:T(8,128)(2,1)}, u32[]{:S(2)}, u32[]{:S(2)}) collective-permute-start(bf16[64,1024]{1,0:T(8,128)(2,1)} %param.3), channel_id=1, source_target_pairs={{8,0},{17,1},{24,16},{33,17},{40,32},{49,33},{56,48},{1,49},{10,2}... | collective-permute-start | bytes 393224 | tf_op jit(solution)/shard_map/ppermute | solution.py:33
  5.3 0.7 collective-permute-start.2
  6.0 3.4 %copy-done = bf16[4096,1024]{1,0:T(8,128)(2,1)S(1)} copy-done((bf16[4096,1024]{1,0:T(8,128)(2,1)S(1)}, bf16[4096,1024]{1,0:T(8,128)(2,1)}, u32[]{:S(2)}) %copy-start) | copy-done | bytes 8388632
  9.5 0.7 collective-permute-start.6
  11.0 1.6 %constant_dynamic-update-slice_fusion.7 = (bf16[512,1024]{1,0:T(8,128)(2,1)S(1)}, bf16[256,1024]{1,0:T(8,128)(2,1)}) fusion(bf16[512,1024]{1,0:T(8,128)(2,1)S(1)} %get-tuple-element.62, bf16[64,1024]{1,0:T(8,128)(2,1)} %collective-permute-done, bf16[256,1024]{1,0:T(8,128)(2,1)} %get-tuple-element.63), kind=kLoop, calls=%fused_computation.13 | loop fusion | bytes 393216
  12.5 0.7 constant_dynamic-update-slice_fusion.6
  13.9 2.5 %collective-permute-start.3 = (bf16[256,1024]{1,0:T(8,128)(2,1)}, bf16[256,1024]{1,0:T(8,128)(2,1)}, u32[]{:S(2)}, u32[]{:S(2)}) collective-permute-start(bf16[256,1024]{1,0:T(8,128)(2,1)} %get-tuple-element.57), channel_id=1, source_target_pairs={{2,0},{9,1},{18,16},{25,17},{34,32},{41,33},{50,48},{57,49},{4,2},... | collective-permute-start | bytes 1572872 | tf_op jit(solution)/shard_map/ppermute | solution.py:33
  16.5 1.7 %collective-permute-start.4 = (bf16[256,1024]{1,0:T(8,128)(2,1)}, bf16[256,1024]{1,0:T(8,128)(2,1)}, u32[]{:S(2)}, u32[]{:S(2)}) collective-permute-start(bf16[256,1024]{1,0:T(8,128)(2,1)} %get-tuple-element.57), channel_id=1, source_target_pairs={{4,0},{65,1},{20,16},{81,17},{36,32},{97,33},{52,48},{113,49},{6,2... | collective-permute-start | bytes 1572872 | tf_op jit(solution)/shard_map/ppermute | solution.py:33
  21.2 19.4 %all_to_all.14 = s32[128,1,64]{2,1,0:T(1,128)S(1)} all-to-all(s32[128,1,64]{2,1,0:T(1,128)S(1)} %bitcast.9), channel_id=1, replica_groups=mesh['samp'=8,'cent'=16] {'samp','cent'}, dimensions={0} | all-to-all | bytes 65536 | tf_op jit(solution)/shard_map/all_to_all | solution.py:214
  40.7 1.1 constant_dynamic-update-slice_fusion.4.refs_0_.refs_8_
  41.8 1.3 %pad_maximum_fusion.refs_0_.refs_9_ = bf16[512,1024]{1,0:T(8,128)(2,1)S(1)} fusion(bf16[256,1024]{1,0:T(8,128)(2,1)} %collective-permute-done.5, bf16[256,1024]{1,0:T(8,128)(2,1)} %collective-permute-done.4), kind=kLoop, calls=%fused_computation.4 | loop fusion | flops 2097152 | bytes 2097152 | tf_op jit(solution)/shard_map/concatenate | solution.py:218
  43.7 0.9 collective-permute-start.8
  44.7 1.6 %scores.5 = (f32[2,512,512]{2,1,0:T(8,128)S(1)}, f32[4,512]{1,0:T(4,128)S(1)}) custom-call(bf16[512,1024]{1,0:T(8,128)(2,1)S(1)} %share.1.mine_ref, bf16[512,1024]{1,0:T(8,128)(2,1)S(1)} %collective-permute-done.6.other_ref, bf16[512,1024]{1,0:T(8,128)(2,1)S(1)} %constant_dynamic-update-slice_fusion.4.refs_0_.refs_8_), custom_call_target="tpu_custom_call" | custom-call | flops 2147483648 | bytes 5242880 | tf_op jit(solution)/shard_map/scores/pallas_call | solution.py:74
  46.3 1.8 %collective-permute-start.9 = (bf16[512,1024]{1,0:T(8,128)(2,1)S(1)}, bf16[512,1024]{1,0:T(8,128)(2,1)S(1)}, u32[]{:S(2)}, u32[]{:S(2)}) collective-permute-start(bf16[512,1024]{1,0:T(8,128)(2,1)S(1)} %pad_maximum_fusion.refs_0_.refs_9_), channel_id=1, source_target_pairs={{16,0},{3,1},{32,16},{19,17},{48,32},{35,33},{0,48},{51,49},{18,2}... | collective-permute-start | bytes 3145736 | tf_op jit(solution)/shard_map/ppermute | solution.py:33
  48.1 1.7 %scores.6 = (f32[2,512,512]{2,1,0:T(8,128)S(1)}, f32[4,512]{1,0:T(4,128)S(1)}) custom-call(bf16[512,1024]{1,0:T(8,128)(2,1)S(1)} %share.1.mine_ref, bf16[512,1024]{1,0:T(8,128)(2,1)S(1)} %collective-permute-done.6.other_ref, bf16[512,1024]{1,0:T(8,128)(2,1)S(1)} %pad_maximum_fusion.refs_0_.refs_9_), custom_call_target="tpu_custom_call" | custom-call | flops 2147483648 | bytes 5242880 | tf_op jit(solution)/shard_map/scores/pallas_call | solution.py:74
  49.8 7.4 %collective-permute-done.7.refs_0_.refs_10_ = bf16[512,1024]{1,0:T(8,128)(2,1)S(1)} collective-permute-done((bf16[512,1024]{1,0:T(8,128)(2,1)S(1)}, bf16[512,1024]{1,0:T(8,128)(2,1)S(1)}, u32[]{:S(2)}, u32[]{:S(2)}) %collective-permute-start.7) | collective-permute-done | bytes 1048608 | tf_op jit(solution)/shard_map/ppermute | solution.py:33
  57.1 1.8 %collective-permute-done.8.refs_1_.refs_15_ = bf16[512,1024]{1,0:T(8,128)(2,1)S(1)} collective-permute-done((bf16[512,1024]{1,0:T(8,128)(2,1)S(1)}, bf16[512,1024]{1,0:T(8,128)(2,1)S(1)}, u32[]{:S(2)}, u32[]{:S(2)}) %collective-permute-start.8) | collective-permute-done | bytes 1048608 | tf_op jit(solution)/shard_map/ppermute | solution.py:33
  58.9 1.5 %collective-permute-start.12 = (bf16[512,1024]{1,0:T(8,128)(2,1)S(1)}, bf16[512,1024]{1,0:T(8,128)(2,1)S(1)}, u32[]{:S(2)}, u32[]{:S(2)}) collective-permute-start(bf16[512,1024]{1,0:T(8,128)(2,1)S(1)} %collective-permute-done.8.refs_1_.refs_15_), channel_id=1, source_target_pairs={{48,0},{7,1},{0,16},{23,17},{16,32},{39,33},{32,48},{55,49},{50,2}... | collective-permute-start | bytes 3145736 | tf_op jit(solution)/shard_map/ppermute | solution.py:33
  60.4 3.0 %scores.7 = (f32[2,512,512]{2,1,0:T(8,128)S(1)}, f32[2,512,512]{2,1,0:T(8,128)S(1)}, f32[4,1024]{1,0:T(4,128)S(1)}) custom-call(bf16[512,1024]{1,0:T(8,128)(2,1)S(1)} %share.1.mine_ref, bf16[512,1024]{1,0:T(8,128)(2,1)S(1)} %collective-permute-done.6.other_ref, bf16[512,1024]{1,0:T(8,128)(2,1)S(1)} %collective-permute-done.7.refs_0_.refs_10_, ...), custom_call_target="tpu_custom_call" | custom-call | flops 4294967296 | bytes 8388608 | tf_op jit(solution)/shard_map/scores/pallas_call | solution.py:74
  63.3 5.1 %collective-permute-done.9.refs_0_.refs_11_ = bf16[512,1024]{1,0:T(8,128)(2,1)S(1)} collective-permute-done((bf16[512,1024]{1,0:T(8,128)(2,1)S(1)}, bf16[512,1024]{1,0:T(8,128)(2,1)S(1)}, u32[]{:S(2)}, u32[]{:S(2)}) %collective-permute-start.9) | collective-permute-done | bytes 1048608 | tf_op jit(solution)/shard_map/ppermute | solution.py:33
  68.4 1.8 %collective-permute-done.10.refs_1_.refs_14_ = bf16[512,1024]{1,0:T(8,128)(2,1)S(1)} collective-permute-done((bf16[512,1024]{1,0:T(8,128)(2,1)S(1)}, bf16[512,1024]{1,0:T(8,128)(2,1)S(1)}, u32[]{:S(2)}, u32[]{:S(2)}) %collective-permute-start.10) | collective-permute-done | bytes 1048608 | tf_op jit(solution)/shard_map/ppermute | solution.py:33
  70.1 3.0 %scores.8 = (f32[2,512,512]{2,1,0:T(8,128)S(1)}, f32[2,512,512]{2,1,0:T(8,128)S(1)}, f32[4,1024]{1,0:T(4,128)S(1)}) custom-call(bf16[512,1024]{1,0:T(8,128)(2,1)S(1)} %share.1.mine_ref, bf16[512,1024]{1,0:T(8,128)(2,1)S(1)} %collective-permute-done.6.other_ref, bf16[512,1024]{1,0:T(8,128)(2,1)S(1)} %collective-permute-done.9.refs_0_.refs_11_, ...), custom_call_target="tpu_custom_call" | custom-call | flops 4294967296 | bytes 8388608 | tf_op jit(solution)/shard_map/scores/pallas_call | solution.py:74
  73.2 6.5 %collective-permute-done.11.refs_0_.refs_12_ = bf16[512,1024]{1,0:T(8,128)(2,1)S(1)} collective-permute-done((bf16[512,1024]{1,0:T(8,128)(2,1)S(1)}, bf16[512,1024]{1,0:T(8,128)(2,1)S(1)}, u32[]{:S(2)}, u32[]{:S(2)}) %collective-permute-start.11) | collective-permute-done | bytes 1048608 | tf_op jit(solution)/shard_map/ppermute | solution.py:33
  79.6 1.8 %collective-permute-done.12.refs_1_.refs_13_ = bf16[512,1024]{1,0:T(8,128)(2,1)S(1)} collective-permute-done((bf16[512,1024]{1,0:T(8,128)(2,1)S(1)}, bf16[512,1024]{1,0:T(8,128)(2,1)S(1)}, u32[]{:S(2)}, u32[]{:S(2)}) %collective-permute-start.12) | collective-permute-done | bytes 1048608 | tf_op jit(solution)/shard_map/ppermute | solution.py:33
  81.4 3.0 %scores.9 = (f32[2,512,512]{2,1,0:T(8,128)S(1)}, f32[2,512,512]{2,1,0:T(8,128)S(1)}, f32[4,1024]{1,0:T(4,128)S(1)}) custom-call(bf16[512,1024]{1,0:T(8,128)(2,1)S(1)} %share.1.mine_ref, bf16[512,1024]{1,0:T(8,128)(2,1)S(1)} %collective-permute-done.6.other_ref, bf16[512,1024]{1,0:T(8,128)(2,1)S(1)} %collective-permute-done.11.refs_0_.refs_12_, ...), custom_call_target="tpu_custom_call" | custom-call | flops 4294967296 | bytes 8388608 | tf_op jit(solution)/shard_map/scores/pallas_call | solution.py:74
  84.4 1.3 %first.1 = (f32[64,8,512]{2,1,0:T(8,128)S(1)}, f32[2,4096]{1,0:T(2,128)S(1)}) custom-call(s32[3]{0:T(128)S(1)} %broadcast_select_fusion.spot_ref, f32[4,512]{1,0:T(4,128)S(1)} %get-tuple-element.33.refs_0_, f32[4,512]{1,0:T(4,128)S(1)} %get-tuple-element.35.refs_1_, f32[4,1024]{1,0:T(4,128)S(1)} %get-tuple-element.36.refs_2_, ...), custom_call_target="tpu_custom_call" | custom-call | tf_op jit(solution)/shard_map/first/pallas_call | solution.py:235
  85.7 19.9 %all_to_all.15.all_ref = f32[64,8,512]{2,1,0:T(8,128)S(1)} all-to-all(f32[64,8,512]{2,1,0:T(8,128)S(1)} %get-tuple-element.43), channel_id=1, replica_groups={{0,16,32,48,2,18,34,50,4,20,36,52,6,22,38,54,8,24,40,56,10,26,42,58,12,..., dimensions={0} | all-to-all | bytes 2097152 | tf_op jit(solution)/shard_map/all_to_all | solution.py:248
  105.5 1.2 merge.1
  106.7 4.6 %sums.3 = f32[512,1152]{1,0:T(8,128)S(1)} custom-call(f32[1,4096]{1,0:T(1,128)S(1)} %get-tuple-element.44.lse_ref, f32[2,4096]{1,0:T(2,128)S(1)} %get-tuple-element.45.top_ref, f32[2,512,512]{2,1,0:T(8,128)S(1)} %get-tuple-element.46.refs_0_, f32[2,512,512]{2,1,0:T(8,128)S(1)} %get-tuple-element.47.refs_1_, f32[2,512,512]{2,1,0:T(8,128)S(1)} %get-tuple-element.48.refs_2_, ...), custom_call_target="tpu_custom_call" | custom-call | flops 4294967296 | bytes 18874368 | tf_op jit(solution)/shard_map/sums/pallas_call | solution.py:161
  111.3 3.5 %collective-permute-start.13 = (f32[512,1152]{1,0:T(8,128)S(1)}, f32[512,1152]{1,0:T(8,128)S(1)}, u32[]{:S(2)}, u32[]{:S(2)}) collective-permute-start(f32[512,1152]{1,0:T(8,128)S(1)} %sums.3), channel_id=1, source_target_pairs={{0,1},{1,0},{2,3},{3,2},{4,5},{5,4},{6,7},{7,6},{8,9},{9,8},{10,11... | collective-permute-start | bytes 7077896 | tf_op jit(solution)/shard_map/ppermute | solution.py:38
  114.9 4.6 %sums.2.ours_ref = f32[512,1152]{1,0:T(8,128)S(1)} custom-call(f32[1,4096]{1,0:T(1,128)S(1)} %get-tuple-element.44.lse_ref, f32[2,4096]{1,0:T(2,128)S(1)} %get-tuple-element.45.top_ref, f32[2,512,512]{2,1,0:T(8,128)S(1)} %get-tuple-element.46.refs_0_, f32[2,512,512]{2,1,0:T(8,128)S(1)} %get-tuple-element.47.refs_1_, ...), custom_call_target="tpu_custom_call" | custom-call | flops 4294967296 | bytes 18874368 | tf_op jit(solution)/shard_map/sums/pallas_call | solution.py:161
  120.5 1.8 %final.1 = f32[512,1024]{1,0:T(8,128)} custom-call(f32[512,1152]{1,0:T(8,128)S(1)} %sums.2.ours_ref, f32[512,1152]{1,0:T(8,128)S(1)} %collective-permute-done.13.theirs_ref, bf16[512,1024]{1,0:T(8,128)(2,1)S(1)} %share.1.mine_ref), custom_call_target="tpu_custom_call" | custom-call | tf_op jit(solution)/shard_map/final/pallas_call | solution.py:266
  (33 shorter events, 4.6 us)
Async XLA Ops:
  0.6 10.3 %collective-permute-start = (bf16[64,1024]{1,0:T(8,128)(2,1)}, bf16[64,1024]{1,0:T(8,128)(2,1)}, u32[]{:S(2)}, u32[]{:S(2)}) collective-permute-start(bf16[64,1024]{1,0:T(8,128)(2,1)} %param.3), channel_id=1, source_target_pairs={{8,0},{17,1},{24,16},{33,17},{40,32},{49,33},{56,48},{1,49},{10,2}... | collective-permute-start | bytes 393224 | tf_op jit(solution)/shard_map/ppermute | solution.py:33
  5.3 7.3 %collective-permute-start.1 = (bf16[64,1024]{1,0:T(8,128)(2,1)}, bf16[64,1024]{1,0:T(8,128)(2,1)S(1)}, u32[]{:S(2)}, u32[]{:S(2)}) collective-permute-start(bf16[64,1024]{1,0:T(8,128)(2,1)} %param.3), channel_id=1, source_target_pairs={{64,0},{33,1},{80,16},{49,17},{96,32},{1,33},{112,48},{17,49},{66,... | collective-permute-start | bytes 393224 | tf_op jit(solution)/shard_map/ppermute | solution.py:33
  5.3 7.9 %collective-permute-start.2 = (bf16[64,1024]{1,0:T(8,128)(2,1)}, bf16[64,1024]{1,0:T(8,128)(2,1)S(1)}, u32[]{:S(2)}, u32[]{:S(2)}) collective-permute-start(bf16[64,1024]{1,0:T(8,128)(2,1)} %param.3), channel_id=1, source_target_pairs={{72,0},{49,1},{88,16},{1,17},{104,32},{17,33},{120,48},{33,49},{74... | collective-permute-start | bytes 393224 | tf_op jit(solution)/shard_map/ppermute | solution.py:33
  6.0 3.4 %copy-start = (bf16[4096,1024]{1,0:T(8,128)(2,1)S(1)}, bf16[4096,1024]{1,0:T(8,128)(2,1)}, u32[]{:S(2)}) copy-start(bf16[4096,1024]{1,0:T(8,128)(2,1)} %cents_ref.1) | copy-start | bytes 25165828
  9.4 0.9 copy-start.1
  9.4 11.4 %copy-start.2 = (s32[64]{0:T(128)S(1)}, s32[64]{0:T(128)}, u32[]{:S(2)}) copy-start(s32[64]{0:T(128)} %param.4) | copy-start | bytes 772
  9.5 33.7 %collective-permute-start.6 = (bf16[512,1024]{1,0:T(8,128)(2,1)S(1)}, bf16[512,1024]{1,0:T(8,128)(2,1)S(1)}, u32[]{:S(2)}, u32[]{:S(2)}) collective-permute-start(bf16[512,1024]{1,0:T(8,128)(2,1)S(1)} %share.1.mine_ref), channel_id=1, source_target_pairs={{0,1},{1,0},{2,3},{3,2},{4,5},{5,4},{6,7},{7,6},{8,9},{9,8},{10,11... | collective-permute-start | bytes 3145736 | tf_op jit(solution)/shard_map/ppermute | solution.py:38
  13.9 26.8 %collective-permute-start.3 = (bf16[256,1024]{1,0:T(8,128)(2,1)}, bf16[256,1024]{1,0:T(8,128)(2,1)}, u32[]{:S(2)}, u32[]{:S(2)}) collective-permute-start(bf16[256,1024]{1,0:T(8,128)(2,1)} %get-tuple-element.57), channel_id=1, source_target_pairs={{2,0},{9,1},{18,16},{25,17},{34,32},{41,33},{50,48},{57,49},{4,2},... | collective-permute-start | bytes 1572872 | tf_op jit(solution)/shard_map/ppermute | solution.py:33
  16.5 25.4 %collective-permute-start.5 = (bf16[256,1024]{1,0:T(8,128)(2,1)}, bf16[256,1024]{1,0:T(8,128)(2,1)}, u32[]{:S(2)}, u32[]{:S(2)}) collective-permute-start(bf16[256,1024]{1,0:T(8,128)(2,1)} %get-tuple-element.57), channel_id=1, source_target_pairs={{6,0},{73,1},{22,16},{89,17},{38,32},{105,33},{54,48},{121,49},{0,... | collective-permute-start | bytes 1572872 | tf_op jit(solution)/shard_map/ppermute | solution.py:33
  16.5 25.3 %collective-permute-start.4 = (bf16[256,1024]{1,0:T(8,128)(2,1)}, bf16[256,1024]{1,0:T(8,128)(2,1)}, u32[]{:S(2)}, u32[]{:S(2)}) collective-permute-start(bf16[256,1024]{1,0:T(8,128)(2,1)} %get-tuple-element.57), channel_id=1, source_target_pairs={{4,0},{65,1},{20,16},{81,17},{36,32},{97,33},{52,48},{113,49},{6,2... | collective-permute-start | bytes 1572872 | tf_op jit(solution)/shard_map/ppermute | solution.py:33
  43.1 14.0 %collective-permute-start.7 = (bf16[512,1024]{1,0:T(8,128)(2,1)S(1)}, bf16[512,1024]{1,0:T(8,128)(2,1)S(1)}, u32[]{:S(2)}, u32[]{:S(2)}) collective-permute-start(bf16[512,1024]{1,0:T(8,128)(2,1)S(1)} %constant_dynamic-update-slice_fusion.4.refs_0_.refs_8_), channel_id=1, source_target_pairs={{16,0},{3,1},{32,16},{19,17},{48,32},{35,33},{0,48},{51,49},{18,2}... | collective-permute-start | bytes 3145736 | tf_op jit(solution)/shard_map/ppermute | solution.py:33
  43.7 15.2 %collective-permute-start.8 = (bf16[512,1024]{1,0:T(8,128)(2,1)S(1)}, bf16[512,1024]{1,0:T(8,128)(2,1)S(1)}, u32[]{:S(2)}, u32[]{:S(2)}) collective-permute-start(bf16[512,1024]{1,0:T(8,128)(2,1)S(1)} %pad_maximum_fusion.refs_0_.refs_9_), channel_id=1, source_target_pairs={{48,0},{7,1},{0,16},{23,17},{16,32},{39,33},{32,48},{55,49},{50,2}... | collective-permute-start | bytes 3145736 | tf_op jit(solution)/shard_map/ppermute | solution.py:33
  46.3 22.1 %collective-permute-start.9 = (bf16[512,1024]{1,0:T(8,128)(2,1)S(1)}, bf16[512,1024]{1,0:T(8,128)(2,1)S(1)}, u32[]{:S(2)}, u32[]{:S(2)}) collective-permute-start(bf16[512,1024]{1,0:T(8,128)(2,1)S(1)} %pad_maximum_fusion.refs_0_.refs_9_), channel_id=1, source_target_pairs={{16,0},{3,1},{32,16},{19,17},{48,32},{35,33},{0,48},{51,49},{18,2}... | collective-permute-start | bytes 3145736 | tf_op jit(solution)/shard_map/ppermute | solution.py:33
  48.1 22.0 %collective-permute-start.10 = (bf16[512,1024]{1,0:T(8,128)(2,1)S(1)}, bf16[512,1024]{1,0:T(8,128)(2,1)S(1)}, u32[]{:S(2)}, u32[]{:S(2)}) collective-permute-start(bf16[512,1024]{1,0:T(8,128)(2,1)S(1)} %constant_dynamic-update-slice_fusion.4.refs_0_.refs_8_), channel_id=1, source_target_pairs={{48,0},{7,1},{0,16},{23,17},{16,32},{39,33},{32,48},{55,49},{50,2}... | collective-permute-start | bytes 3145736 | tf_op jit(solution)/shard_map/ppermute | solution.py:33
  58.9 20.7 %collective-permute-start.11 = (bf16[512,1024]{1,0:T(8,128)(2,1)S(1)}, bf16[512,1024]{1,0:T(8,128)(2,1)S(1)}, u32[]{:S(2)}, u32[]{:S(2)}) collective-permute-start(bf16[512,1024]{1,0:T(8,128)(2,1)S(1)} %collective-permute-done.7.refs_0_.refs_10_), channel_id=1, source_target_pairs={{16,0},{3,1},{32,16},{19,17},{48,32},{35,33},{0,48},{51,49},{18,2}... | collective-permute-start | bytes 3145736 | tf_op jit(solution)/shard_map/ppermute | solution.py:33
  58.9 22.5 %collective-permute-start.12 = (bf16[512,1024]{1,0:T(8,128)(2,1)S(1)}, bf16[512,1024]{1,0:T(8,128)(2,1)S(1)}, u32[]{:S(2)}, u32[]{:S(2)}) collective-permute-start(bf16[512,1024]{1,0:T(8,128)(2,1)S(1)} %collective-permute-done.8.refs_1_.refs_15_), channel_id=1, source_target_pairs={{48,0},{7,1},{0,16},{23,17},{16,32},{39,33},{32,48},{55,49},{50,2}... | collective-permute-start | bytes 3145736 | tf_op jit(solution)/shard_map/ppermute | solution.py:33
  111.3 9.2 %collective-permute-start.13 = (f32[512,1152]{1,0:T(8,128)S(1)}, f32[512,1152]{1,0:T(8,128)S(1)}, u32[]{:S(2)}, u32[]{:S(2)}) collective-permute-start(f32[512,1152]{1,0:T(8,128)S(1)} %sums.3), channel_id=1, source_target_pairs={{0,1},{1,0},{2,3},{3,2},{4,5},{5,4},{6,7},{7,6},{8,9},{9,8},{10,11... | collective-permute-start | bytes 7077896 | tf_op jit(solution)/shard_map/ppermute | solution.py:38
  114.8 4.7 %collective-permute-start.14 = (f32[4096]{0:T(1024)S(1)}, f32[4096]{0:T(1024)S(1)}, u32[]{:S(2)}, u32[]{:S(2)}) collective-permute-start(f32[4096]{0:T(1024)S(1)} %bitcast.10), channel_id=1, source_target_pairs={{0,1},{1,0},{2,3},{3,2},{4,5},{5,4},{6,7},{7,6},{8,9},{9,8},{10,11... | collective-permute-start | bytes 49160 | tf_op jit(solution)/shard_map/ppermute | solution.py:38

commit v5 on v4

--- a/solution.py
+++ b/solution.py
@@ -98,7 +98,7 @@
     return jnp.where(lane >= step * inner, ahead, back)
 
 
-def first_kernel(order, spot_ref, *refs):
+def first_kernel(order, spot_ref, ids_ref, *refs):
     *stats, out_ref, top_ref = refs
     parts = []
     for k, (ref, piece) in enumerate(order):
@@ -113,18 +113,62 @@
         value = roll_within(value, dim, spot_ref[dim])
     for line in range(8):
         piece = value[:, line * 512 : (line + 1) * 512]
-        out_ref[:, line, :] = jnp.broadcast_to(piece, (64, 512))
+        out_ref[:, line, 0:512] = jnp.broadcast_to(piece, (64, 512))
+    lane = lax.broadcasted_iota(jnp.int32, (1, 128), 1)
+    ids = jnp.where(lane // UNIT == spot_ref[0] % 2, ids_ref[...], -1.0)
+    out_ref[:, :, 512:640] = jnp.broadcast_to(ids.reshape(1, 1, 128), (64, 8, 128))
 
 
 def merge_kernel(spot_ref, all_ref, whole_ref, own_ref):
-    top = jnp.max(all_ref[...], axis=0)
-    total = jnp.sum(jnp.exp2(all_ref[...] - top[None]), axis=0)
+    values = all_ref[:, :, 0:512]
+    top = jnp.max(values, axis=0)
+    total = jnp.sum(jnp.exp2(values - top[None]), axis=0)
     lse = top + jnp.log2(total)
     whole_ref[...] = lse
     value = jnp.concatenate([lse[line : line + 1, :] for line in range(8)], axis=1)
     for dim in range(3):
         value = roll_within(value, dim, (4 - spot_ref[dim]) % 4)
     own_ref[...] = value
+
+
+def pack_kernel(whole_ref, all_ref, out_ref):
+    for line in range(32):
+        tile = line % 4
+        out_ref[line : line + 1, :] = whole_ref[line // 4 : line // 4 + 1, tile * 128 : (tile + 1) * 128]
+        pair = jnp.maximum(all_ref[2 * line, 0:1, 512:640], all_ref[2 * line + 1, 0:1, 512:640])
+        out_ref[32 + line : 33 + line, :] = pair
+
+
+def route_kernel(at_ref, mine_ref, other_ref, out_ref):
+    first = (at_ref[0] * 16 + at_ref[1]) * UNIT
+    rows = (lax.broadcasted_iota(jnp.int32, (UNIT, 128), 0) + first).astype(jnp.float32)
+    total = jnp.zeros((UNIT, 128), jnp.float32)
+    for ref in (mine_ref, other_ref):
+        for line in range(32):
+            hit = ref[32 + line : 33 + line, :] == rows
+            total = total + jnp.where(hit, ref[line : line + 1, :], 0.0)
+    out_ref[...] = total
+
+
+def join_kernel(*refs):
+    *parts, out_ref = refs
+    at = 0
+    for part in parts:
+        out_ref[at : at + part.shape[0], :] = part[...]
+        at += part.shape[0]
+
+
+def join(*parts):
+    vmem = pl.BlockSpec(memory_space=pltpu.VMEM)
+    shape = (sum(part.shape[0] for part in parts), parts[0].shape[1])
+    return pl.pallas_call(
+        join_kernel,
+        out_shape=jax.ShapeDtypeStruct(shape, parts[0].dtype),
+        in_specs=[vmem] * len(parts),
+        out_specs=vmem,
+        compiler_params=pltpu.CompilerParams(vmem_limit_bytes=8 << 20),
+        name="join",
+    )(*parts)
 
 
 def sums_kernel(half, count, lse_ref, top_ref, *refs):
@@ -195,28 +239,23 @@
     width = embeddings.shape[1]
     smem = pl.BlockSpec(memory_space=pltpu.SMEM)
     vmem = pl.BlockSpec(memory_space=pltpu.VMEM)
+    small = pltpu.CompilerParams(vmem_limit_bytes=8 << 20)
+    line = join(embeddings, *[fetch(embeddings, 0, step) for step in (1, 2, 3)])
+    spot, destination, _ = lax.optimization_barrier((spot, destination, line))
     mine = pl.pallas_call(
         share_kernel,
         out_shape=jax.ShapeDtypeStruct((share, width), centroids.dtype),
         in_specs=[smem, pl.BlockSpec(memory_space=pltpu.HBM)],
         out_specs=vmem,
         scratch_shapes=[pltpu.SemaphoreType.DMA(())],
-        compiler_params=pltpu.CompilerParams(vmem_limit_bytes=8 << 20),
+        compiler_params=pltpu.CompilerParams(vmem_limit_bytes=56 << 20),
         name="share",
     )(samp.astype(jnp.int32).reshape(1), centroids)
     other = swap_cores(mine)
-    line = jnp.concatenate([embeddings] + [fetch(embeddings, 0, step) for step in (1, 2, 3)])
-    late, spot, _ = lax.optimization_barrier((destination, spot, line))
-    start = core * 4096 + ((spot[2] * 4 + spot[1]) * 4 + spot[0]) * UNIT
-    spots = lax.broadcasted_iota(jnp.int32, (UNIT, 8192), 1)
-    keys = (start + jnp.arange(UNIT, dtype=jnp.int32))[:, None]
-    spread = jnp.sum(jnp.where(spots == late[:, None], keys, 0), axis=0)
-    arrived = lax.all_to_all(spread.reshape(128, UNIT), BOTH, split_axis=0, concat_axis=0, tiled=True)
-    keys = jnp.sum(arrived, axis=0)
-
+    ids = jnp.tile(destination.astype(jnp.float32), 2).reshape(1, 128)
     near, across, back = [fetch(line, 1, step) for step in (1, 2, 3)]
-    upper, lower = jnp.concatenate([line, near]), jnp.concatenate([across, back])
-    upper, lower, other, keys = lax.optimization_barrier((upper, lower, other, keys))
+    upper, lower = join(line, near), join(across, back)
+    upper, lower, other, ids = lax.optimization_barrier((upper, lower, other, ids))
     after_upper, before_lower = fetch(upper, 2, 1), fetch(lower, 2, 3)
 
     p_upper, stat_upper = scores_call(mine, other, [upper])
@@ -227,24 +266,31 @@
     far_upper, far_lower = fetch(passed_up, 2, 1), fetch(passed_down, 2, 3)
     p_first, stat_first = scores_call(mine, other, [after_upper, before_lower])
     p_second, stat_second = scores_call(mine, other, [after_lower, before_upper])
-    p_far, stat_far = scores_call(mine, other, [far_upper, far_lower])
+    p_third, stat_third = scores_call(mine, other, [far_upper])
+    p_fourth, stat_fourth = scores_call(mine, other, [far_lower])
     chunks = [upper, lower, after_upper, after_lower, far_upper, far_lower, before_upper, before_lower]
-    ps = p_upper + p_lower + [p_first[0], p_second[0]] + p_far + [p_second[1], p_first[1]]
-    order = ((0, 0), (1, 0), (2, 0), (3, 0), (4, 0), (4, 1), (3, 1), (2, 1))
+    ps = p_upper + p_lower + [p_first[0], p_second[0]] + p_third + p_fourth + [p_second[1], p_first[1]]
+    order = ((0, 0), (1, 0), (2, 0), (3, 0), (4, 0), (5, 0), (3, 1), (2, 1))
 
     local, tops = pl.pallas_call(
         functools.partial(first_kernel, order),
         out_shape=(
-            jax.ShapeDtypeStruct((64, 8, 512), jnp.float32),
+            jax.ShapeDtypeStruct((64, 8, 640), jnp.float32),
             jax.ShapeDtypeStruct((2, 4096), jnp.float32),
         ),
-        in_specs=[smem] + [vmem] * 5,
-        compiler_params=pltpu.CompilerParams(vmem_limit_bytes=8 << 20),
+        in_specs=[smem] + [vmem] * 7,
+        compiler_params=small,
         name="first",
-    )(spot, stat_upper, stat_lower, stat_first, stat_second, stat_far)
-    chips = [
-        [place(i // 16, i // 4 % 4, i % 4, side) for i in range(64)] for side in range(2)
-    ]
+    )(spot, ids, stat_upper, stat_lower, stat_first, stat_second, stat_third, stat_fourth)
+    chips = []
+    for side in range(2):
+        group = []
+        for i in range(64):
+            at = [0, 0, 0]
+            for dim in range(3):
+                at[ORDERS[side][dim]] = i // 4**dim % 4
+            group.append(place(*at, side))
+        chips.append(group)
     shared = lax.all_to_all(local, BOTH, split_axis=0, concat_axis=0, tiled=True, axis_index_groups=chips)
     whole, lse = pl.pallas_call(
         merge_kernel,
@@ -253,16 +299,29 @@
             jax.ShapeDtypeStruct((1, 4096), jnp.float32),
         ),
         in_specs=[smem, vmem],
-        compiler_params=pltpu.CompilerParams(vmem_limit_bytes=8 << 20),
+        compiler_params=small,
         name="merge",
     )(spot, shared)
     theirs = sums_call(1, lse, tops, ps, chunks)
     received = swap_cores(theirs)
+    whole, shared, _ = lax.optimization_barrier((whole, shared, theirs))
+    pack = pl.pallas_call(
+        pack_kernel,
+        out_shape=jax.ShapeDtypeStruct((64, 128), jnp.float32),
+        in_specs=[vmem] * 2,
+        compiler_params=small,
+        name="pack",
+    )(whole, shared)
+    partner = swap_cores(pack)
     ours = sums_call(0, lse, tops, ps, chunks)
-    whole = whole.reshape(4096)
-    partner = swap_cores(whole)
-    every = jnp.where(core == 0, jnp.concatenate([whole, partner]), jnp.concatenate([partner, whole]))
-    row_lse = jnp.sum(jnp.where(spots == keys[:, None], every[None, :], 0.0), axis=1) * math.log(2.0)
+    spread = pl.pallas_call(
+        route_kernel,
+        out_shape=jax.ShapeDtypeStruct((UNIT, 128), jnp.float32),
+        in_specs=[smem, vmem, vmem],
+        compiler_params=small,
+        name="route",
+    )(jnp.stack([samp, cent]).astype(jnp.int32), pack, partner)
+    row_lse = jnp.sum(spread, axis=1) * math.log(2.0)
     new_centers = pl.pallas_call(
         final_kernel, out_shape=jax.ShapeDtypeStruct((share, width), jnp.float32), name="final",
         compiler_params=pltpu.CompilerParams(vmem_limit_bytes=8 << 20),

time: 123 us -> 123 us (level)
  blocking collectives: 39.2 us -> 21.2 us
  waiting for transfers between devices: 24.2 us -> 38 us
  Pallas kernels: 25.7 us -> 39.3 us
  local copies, waits for them, and re-layouts: 8.9 us -> 0.1 us
  starting transfers between devices: 18.8 us -> 22.9 us
  other arithmetic: 2.83 us -> 0.79 us
  between operations: 2.67 us -> 0.76 us
    all_to_all x1 -> x0, blocking collectives: 19.4 us -> none  [shards(): lax.all_to_all(spread.reshape(128, UNIT), BOTH, split_axis=0, concat_axis...]
    ppermute x12, waiting for transfers between devices: 24.2 us -> 38 us  [fetch(): return lax.ppermute(value, BOTH, pairs)]
    pallas_call x5 -> x6, Pallas kernels: 12.3 us -> 19.8 us  [scores_call(): pl.pallas_call(functools.partial(scores_kernel, factor, count), out_shape...]
    unnamed x11 -> x6, local copies, waits for them, and re-layouts: 7.09 us -> 0.01 us
    ppermute x3, starting transfers between devices: 4.38 us -> 6.79 us  [swap_cores(): return lax.ppermute(value, BOTH, pairs)]
    pallas_call x1, Pallas kernels: 0.08 us -> 2.24 us  [shards(): pl.pallas_call(share_kernel, out_shape=jax.ShapeDtypeStruct((share, width...]
    ppermute x12, starting transfers between devices: 14.4 us -> 16.1 us  [fetch(): return lax.ppermute(value, BOTH, pairs)]
    pallas_call x1, Pallas kernels: 1.76 us -> 3.37 us  [shards(): pl.pallas_call(final_kernel, out_shape=jax.ShapeDtypeStruct((share, width...]
  transfers between devices with their start and end apart: 15 -> 15, of which waited for: 6 -> 9; matrix products, arithmetic and copies ran while one was open for 7% -> 1% of each run, Pallas kernels for 11% -> 18%
where the time goes in v5:
time: 123 us
  Pallas kernels  39.3 us (32%)
  waiting for transfers between devices  38 us (31%)
  starting transfers between devices  22.9 us (19%)
  blocking collectives  21.2 us (17%)
    ppermute x12, waiting for transfers between devices, fetch(): return lax.ppermute(value, BOTH, pairs)  38 us
    all_to_all x1, blocking collectives, shards(): lax.all_to_all(local, BOTH, split_axis=0, concat_axis=0, tiled=True, axis...  21.2 us
    pallas_call x6, Pallas kernels, scores_call(): pl.pallas_call(functools.partial(scores_kernel, factor, count), out_shape...  19.8 us
    ppermute x12, starting transfers between devices, fetch(): return lax.ppermute(value, BOTH, pairs)  16.1 us
    pallas_call x2, Pallas kernels, sums_call(): pl.pallas_call(functools.partial(sums_kernel, half, count), out_shape=jax...  10.4 us
    ppermute x3, starting transfers between devices, swap_cores(): return lax.ppermute(value, BOTH, pairs)  6.79 us
    pallas_call x1, Pallas kernels, shards(): pl.pallas_call(final_kernel, out_shape=jax.ShapeDtypeStruct((share, width...  3.37 us
  transfers between devices with their start and end apart: 15, of which 9 were waited for; matrix products, arithmetic and copies ran while one was open for 1% of the time, Pallas kernels for 18%

profile of v5, /device:TPU:1, one launch (start us, length us, event | category | flops | bytes accessed | tf_op | source)
XLA Modules:
  0.0 123.0 jit_solution(9519192028115818173)
XLA Ops:
  0.7 2.2 %share.1.mine_ref = bf16[512,1024]{1,0:T(8,128)(2,1)} custom-call(s32[1]{0:T(128)} %bitcast.3.at_ref, bf16[4096,1024]{1,0:T(8,128)(2,1)} %cents_ref.1), custom_call_target="tpu_custom_call" | custom-call | tf_op jit(solution)/shard_map/share/pallas_call | solution.py:245
  2.9 1.5 %collective-permute-start.6 = (bf16[512,1024]{1,0:T(8,128)(2,1)}, bf16[512,1024]{1,0:T(8,128)(2,1)}, u32[]{:S(2)}, u32[]{:S(2)}) collective-permute-start(bf16[512,1024]{1,0:T(8,128)(2,1)} %share.1.mine_ref), channel_id=1, source_target_pairs={{0,1},{1,0},{2,3},{3,2},{4,5},{5,4},{6,7},{7,6},{8,9},{9,8},{10,11... | collective-permute-start | bytes 3145736 | tf_op jit(solution)/shard_map/ppermute | solution.py:38
  4.4 3.8 %collective-permute-start = (bf16[64,1024]{1,0:T(8,128)(2,1)S(1)}, bf16[64,1024]{1,0:T(8,128)(2,1)S(1)}, u32[]{:S(2)}, u32[]{:S(2)}) collective-permute-start(bf16[64,1024]{1,0:T(8,128)(2,1)S(1)} %copy-done.1), channel_id=1, source_target_pairs={{8,0},{17,1},{24,16},{33,17},{40,32},{49,33},{56,48},{1,49},{10,2}... | collective-permute-start | bytes 393224 | tf_op jit(solution)/shard_map/ppermute | solution.py:33
  8.3 0.7 collective-permute-start.2
  8.9 2.6 %collective-permute-done.refs_1_ = bf16[64,1024]{1,0:T(8,128)(2,1)S(1)} collective-permute-done((bf16[64,1024]{1,0:T(8,128)(2,1)S(1)}, bf16[64,1024]{1,0:T(8,128)(2,1)S(1)}, u32[]{:S(2)}, u32[]{:S(2)}) %collective-permute-start) | collective-permute-done | bytes 131104 | tf_op jit(solution)/shard_map/ppermute | solution.py:33
  11.6 2.1 %collective-permute-done.1.refs_2_ = bf16[64,1024]{1,0:T(8,128)(2,1)S(1)} collective-permute-done((bf16[64,1024]{1,0:T(8,128)(2,1)S(1)}, bf16[64,1024]{1,0:T(8,128)(2,1)S(1)}, u32[]{:S(2)}, u32[]{:S(2)}) %collective-permute-start.1) | collective-permute-done | bytes 131104 | tf_op jit(solution)/shard_map/ppermute | solution.py:33
  13.7 1.1 collective-permute-done.2.refs_3_
  14.9 2.4 %collective-permute-start.3 = (bf16[256,1024]{1,0:T(8,128)(2,1)S(1)}, bf16[256,1024]{1,0:T(8,128)(2,1)S(1)}, u32[]{:S(2)}, u32[]{:S(2)}) collective-permute-start(bf16[256,1024]{1,0:T(8,128)(2,1)S(1)} %join.3.refs_0_), channel_id=1, source_target_pairs={{2,0},{9,1},{18,16},{25,17},{34,32},{41,33},{50,48},{57,49},{4,2},... | collective-permute-start | bytes 1572872 | tf_op jit(solution)/shard_map/ppermute | solution.py:33
  17.8 0.6 collective-permute-start.5
  18.6 10.4 %collective-permute-done.3.refs_1_ = bf16[256,1024]{1,0:T(8,128)(2,1)S(1)} collective-permute-done((bf16[256,1024]{1,0:T(8,128)(2,1)S(1)}, bf16[256,1024]{1,0:T(8,128)(2,1)S(1)}, u32[]{:S(2)}, u32[]{:S(2)}) %collective-permute-start.3) | collective-permute-done | bytes 524320 | tf_op jit(solution)/shard_map/ppermute | solution.py:33
  29.1 3.6 %collective-permute-done.5.refs_1_ = bf16[256,1024]{1,0:T(8,128)(2,1)S(1)} collective-permute-done((bf16[256,1024]{1,0:T(8,128)(2,1)S(1)}, bf16[256,1024]{1,0:T(8,128)(2,1)S(1)}, u32[]{:S(2)}, u32[]{:S(2)}) %collective-permute-start.5) | collective-permute-done | bytes 524320 | tf_op jit(solution)/shard_map/ppermute | solution.py:33
  32.8 2.5 %collective-permute-start.7 = (bf16[512,1024]{1,0:T(8,128)(2,1)S(1)}, bf16[512,1024]{1,0:T(8,128)(2,1)S(1)}, u32[]{:S(2)}, u32[]{:S(2)}) collective-permute-start(bf16[512,1024]{1,0:T(8,128)(2,1)S(1)} %join.4.refs_0_.refs_8_), channel_id=1, source_target_pairs={{16,0},{3,1},{32,16},{19,17},{48,32},{35,33},{0,48},{51,49},{18,2}... | collective-permute-start | bytes 3145736 | tf_op jit(solution)/shard_map/ppermute | solution.py:33
  35.3 2.9 %scores.6 = (f32[2,512,512]{2,1,0:T(8,128)S(1)}, f32[4,512]{1,0:T(4,128)S(1)}) custom-call(bf16[512,1024]{1,0:T(8,128)(2,1)S(1)} %copy-done, bf16[512,1024]{1,0:T(8,128)(2,1)} %collective-permute-done.6.other_ref, bf16[512,1024]{1,0:T(8,128)(2,1)S(1)} %join.4.refs_0_.refs_8_), custom_call_target="tpu_custom_call" | custom-call | flops 2147483648 | bytes 5242880 | tf_op jit(solution)/shard_map/scores/pallas_call | solution.py:74
  38.3 2.7 %collective-permute-start.9 = (bf16[512,1024]{1,0:T(8,128)(2,1)S(1)}, bf16[512,1024]{1,0:T(8,128)(2,1)S(1)}, u32[]{:S(2)}, u32[]{:S(2)}) collective-permute-start(bf16[512,1024]{1,0:T(8,128)(2,1)S(1)} %join.5.refs_0_.refs_9_), channel_id=1, source_target_pairs={{16,0},{3,1},{32,16},{19,17},{48,32},{35,33},{0,48},{51,49},{18,2}... | collective-permute-start | bytes 3145736 | tf_op jit(solution)/shard_map/ppermute | solution.py:33
  41.0 2.8 %scores.7 = (f32[2,512,512]{2,1,0:T(8,128)S(1)}, f32[4,512]{1,0:T(4,128)S(1)}) custom-call(bf16[512,1024]{1,0:T(8,128)(2,1)S(1)} %copy-done, bf16[512,1024]{1,0:T(8,128)(2,1)} %collective-permute-done.6.other_ref, bf16[512,1024]{1,0:T(8,128)(2,1)S(1)} %join.5.refs_0_.refs_9_), custom_call_target="tpu_custom_call" | custom-call | flops 2147483648 | bytes 5242880 | tf_op jit(solution)/shard_map/scores/pallas_call | solution.py:74
  43.8 3.2 %collective-permute-done.7.refs_0_.refs_10_ = bf16[512,1024]{1,0:T(8,128)(2,1)S(1)} collective-permute-done((bf16[512,1024]{1,0:T(8,128)(2,1)S(1)}, bf16[512,1024]{1,0:T(8,128)(2,1)S(1)}, u32[]{:S(2)}, u32[]{:S(2)}) %collective-permute-start.7) | collective-permute-done | bytes 1048608 | tf_op jit(solution)/shard_map/ppermute | solution.py:33
  47.1 3.4 %collective-permute-done.8.refs_1_.refs_15_ = bf16[512,1024]{1,0:T(8,128)(2,1)S(1)} collective-permute-done((bf16[512,1024]{1,0:T(8,128)(2,1)S(1)}, bf16[512,1024]{1,0:T(8,128)(2,1)S(1)}, u32[]{:S(2)}, u32[]{:S(2)}) %collective-permute-start.8) | collective-permute-done | bytes 1048608 | tf_op jit(solution)/shard_map/ppermute | solution.py:33
  50.5 2.7 %collective-permute-start.11 = (bf16[512,1024]{1,0:T(8,128)(2,1)S(1)}, bf16[512,1024]{1,0:T(8,128)(2,1)S(1)}, u32[]{:S(2)}, u32[]{:S(2)}) collective-permute-start(bf16[512,1024]{1,0:T(8,128)(2,1)S(1)} %collective-permute-done.7.refs_0_.refs_10_), channel_id=1, source_target_pairs={{16,0},{3,1},{32,16},{19,17},{48,32},{35,33},{0,48},{51,49},{18,2}... | collective-permute-start | bytes 3145736 | tf_op jit(solution)/shard_map/ppermute | solution.py:33
  53.1 4.2 %scores.8 = (f32[2,512,512]{2,1,0:T(8,128)S(1)}, f32[2,512,512]{2,1,0:T(8,128)S(1)}, f32[4,1024]{1,0:T(4,128)S(1)}) custom-call(bf16[512,1024]{1,0:T(8,128)(2,1)S(1)} %copy-done, bf16[512,1024]{1,0:T(8,128)(2,1)} %collective-permute-done.6.other_ref, bf16[512,1024]{1,0:T(8,128)(2,1)S(1)} %collective-permute-done.7.refs_0_.refs_10_, ...), custom_call_target="tpu_custom_call" | custom-call | flops 4294967296 | bytes 8388608 | tf_op jit(solution)/shard_map/scores/pallas_call | solution.py:74
  57.3 4.4 %collective-permute-done.10.refs_1_.refs_14_ = bf16[512,1024]{1,0:T(8,128)(2,1)S(1)} collective-permute-done((bf16[512,1024]{1,0:T(8,128)(2,1)S(1)}, bf16[512,1024]{1,0:T(8,128)(2,1)S(1)}, u32[]{:S(2)}, u32[]{:S(2)}) %collective-permute-start.10) | collective-permute-done | bytes 1048608 | tf_op jit(solution)/shard_map/ppermute | solution.py:33
  61.7 4.2 %scores.9 = (f32[2,512,512]{2,1,0:T(8,128)S(1)}, f32[2,512,512]{2,1,0:T(8,128)S(1)}, f32[4,1024]{1,0:T(4,128)S(1)}) custom-call(bf16[512,1024]{1,0:T(8,128)(2,1)S(1)} %copy-done, bf16[512,1024]{1,0:T(8,128)(2,1)} %collective-permute-done.6.other_ref, bf16[512,1024]{1,0:T(8,128)(2,1)S(1)} %collective-permute-done.9.refs_0_.refs_11_, ...), custom_call_target="tpu_custom_call" | custom-call | flops 4294967296 | bytes 8388608 | tf_op jit(solution)/shard_map/scores/pallas_call | solution.py:74
  65.9 7.0 %collective-permute-done.12.refs_0_.refs_13_ = bf16[512,1024]{1,0:T(8,128)(2,1)S(1)} collective-permute-done((bf16[512,1024]{1,0:T(8,128)(2,1)S(1)}, bf16[512,1024]{1,0:T(8,128)(2,1)S(1)}, u32[]{:S(2)}, u32[]{:S(2)}) %collective-permute-start.12) | collective-permute-done | bytes 1048608 | tf_op jit(solution)/shard_map/ppermute | solution.py:33
  72.9 2.9 %scores.11 = (f32[2,512,512]{2,1,0:T(8,128)S(1)}, f32[4,512]{1,0:T(4,128)S(1)}) custom-call(bf16[512,1024]{1,0:T(8,128)(2,1)S(1)} %copy-done, bf16[512,1024]{1,0:T(8,128)(2,1)} %collective-permute-done.6.other_ref, bf16[512,1024]{1,0:T(8,128)(2,1)S(1)} %collective-permute-done.12.refs_0_.refs_13_), custom_call_target="tpu_custom_call" | custom-call | flops 2147483648 | bytes 5242880 | tf_op jit(solution)/shard_map/scores/pallas_call | solution.py:74
  75.8 2.9 %scores.10 = (f32[2,512,512]{2,1,0:T(8,128)S(1)}, f32[4,512]{1,0:T(4,128)S(1)}) custom-call(bf16[512,1024]{1,0:T(8,128)(2,1)S(1)} %copy-done, bf16[512,1024]{1,0:T(8,128)(2,1)} %collective-permute-done.6.other_ref, bf16[512,1024]{1,0:T(8,128)(2,1)S(1)} %collective-permute-done.11.refs_0_.refs_12_), custom_call_target="tpu_custom_call" | custom-call | flops 2147483648 | bytes 5242880 | tf_op jit(solution)/shard_map/scores/pallas_call | solution.py:74
  78.7 1.3 %first.1 = (f32[64,8,640]{2,1,0:T(8,128)S(1)}, f32[2,4096]{1,0:T(2,128)S(1)}) custom-call(s32[3]{0:T(128)S(1)} %broadcast_select_fusion.spot_ref, f32[1,128]{1,0:T(1,128)S(1)} %reshape_tile.3.ids_ref, f32[4,512]{1,0:T(4,128)S(1)} %get-tuple-element.37.refs_0_, f32[4,512]{1,0:T(4,128)S(1)} %get-tuple-element.39.refs_1_, ...), custom_call_target="tpu_custom_call" | custom-call | tf_op jit(solution)/shard_map/first/pallas_call | solution.py:275
  79.9 21.2 %all_to_all.5.all_ref = f32[64,8,640]{2,1,0:T(8,128)S(1)} all-to-all(f32[64,8,640]{2,1,0:T(8,128)S(1)} %get-tuple-element.48), channel_id=1, replica_groups={{0,8,64,72,2,10,66,74,4,12,68,76,6,14,70,78,16,24,80,88,18,26,82,90,20,..., dimensions={0} | all-to-all | bytes 2621440 | tf_op jit(solution)/shard_map/all_to_all | solution.py:294
  101.2 1.1 merge.1
  102.3 5.9 %sums.3 = f32[512,1152]{1,0:T(8,128)} custom-call(f32[1,4096]{1,0:T(1,128)S(1)} %get-tuple-element.49.lse_ref, f32[2,4096]{1,0:T(2,128)S(1)} %get-tuple-element.50.top_ref, f32[2,512,512]{2,1,0:T(8,128)S(1)} %get-tuple-element.51.refs_0_, f32[2,512,512]{2,1,0:T(8,128)S(1)} %get-tuple-element.52.refs_1_, f32[2,512,512]{2,1,0:T(8,128)S(1)} %get-tuple-element.53.refs_2_, ...), custom_call_target="tpu_custom_call" | custom-call | flops 4294967296 | bytes 18874368 | tf_op jit(solution)/shard_map/sums/pallas_call | solution.py:205
  108.3 5.2 %collective-permute-start.13 = (f32[512,1152]{1,0:T(8,128)}, f32[512,1152]{1,0:T(8,128)}, u32[]{:S(2)}, u32[]{:S(2)}) collective-permute-start(f32[512,1152]{1,0:T(8,128)} %sums.3), channel_id=1, source_target_pairs={{0,1},{1,0},{2,3},{3,2},{4,5},{5,4},{6,7},{7,6},{8,9},{9,8},{10,11... | collective-permute-start | bytes 7077896 | tf_op jit(solution)/shard_map/ppermute | solution.py:38
  113.7 4.5 %sums.2.ours_ref = f32[512,1152]{1,0:T(8,128)S(1)} custom-call(f32[1,4096]{1,0:T(1,128)S(1)} %get-tuple-element.49.lse_ref, f32[2,4096]{1,0:T(2,128)S(1)} %get-tuple-element.50.top_ref, f32[2,512,512]{2,1,0:T(8,128)S(1)} %get-tuple-element.51.refs_0_, f32[2,512,512]{2,1,0:T(8,128)S(1)} %get-tuple-element.52.refs_1_, ...), custom_call_target="tpu_custom_call" | custom-call | flops 4294967296 | bytes 18874368 | tf_op jit(solution)/shard_map/sums/pallas_call | solution.py:205
  118.2 0.8 route.1
  119.6 3.4 %final.1 = f32[512,1024]{1,0:T(8,128)} custom-call(f32[512,1152]{1,0:T(8,128)S(1)} %sums.2.ours_ref, f32[512,1152]{1,0:T(8,128)} %collective-permute-done.13.theirs_ref, bf16[512,1024]{1,0:T(8,128)(2,1)S(1)} %copy-done), custom_call_target="tpu_custom_call" | custom-call | tf_op jit(solution)/shard_map/final/pallas_call | solution.py:325
  (29 shorter events, 1.8 us)
Async XLA Ops:
  0.6 3.8 %copy-start.1 = (bf16[64,1024]{1,0:T(8,128)(2,1)S(1)}, bf16[64,1024]{1,0:T(8,128)(2,1)}, u32[]{:S(2)}) copy-start(bf16[64,1024]{1,0:T(8,128)(2,1)} %refs_0_.1) | copy-start | bytes 393220
  0.6 17.8 %copy-start.2 = (s32[64]{0:T(128)S(1)}, s32[64]{0:T(128)}, u32[]{:S(2)}) copy-start(s32[64]{0:T(128)} %param.4) | copy-start | bytes 772
  2.9 29.9 %collective-permute-start.6 = (bf16[512,1024]{1,0:T(8,128)(2,1)}, bf16[512,1024]{1,0:T(8,128)(2,1)}, u32[]{:S(2)}, u32[]{:S(2)}) collective-permute-start(bf16[512,1024]{1,0:T(8,128)(2,1)} %share.1.mine_ref), channel_id=1, source_target_pairs={{0,1},{1,0},{2,3},{3,2},{4,5},{5,4},{6,7},{7,6},{8,9},{9,8},{10,11... | collective-permute-start | bytes 3145736 | tf_op jit(solution)/shard_map/ppermute | solution.py:38
  4.4 7.2 %collective-permute-start = (bf16[64,1024]{1,0:T(8,128)(2,1)S(1)}, bf16[64,1024]{1,0:T(8,128)(2,1)S(1)}, u32[]{:S(2)}, u32[]{:S(2)}) collective-permute-start(bf16[64,1024]{1,0:T(8,128)(2,1)S(1)} %copy-done.1), channel_id=1, source_target_pairs={{8,0},{17,1},{24,16},{33,17},{40,32},{49,33},{56,48},{1,49},{10,2}... | collective-permute-start | bytes 393224 | tf_op jit(solution)/shard_map/ppermute | solution.py:33
  8.2 5.4 %collective-permute-start.1 = (bf16[64,1024]{1,0:T(8,128)(2,1)S(1)}, bf16[64,1024]{1,0:T(8,128)(2,1)S(1)}, u32[]{:S(2)}, u32[]{:S(2)}) collective-permute-start(bf16[64,1024]{1,0:T(8,128)(2,1)S(1)} %copy-done.1), channel_id=1, source_target_pairs={{64,0},{33,1},{80,16},{49,17},{96,32},{1,33},{112,48},{17,49},{66,... | collective-permute-start | bytes 393224 | tf_op jit(solution)/shard_map/ppermute | solution.py:33
  8.3 6.6 %collective-permute-start.2 = (bf16[64,1024]{1,0:T(8,128)(2,1)S(1)}, bf16[64,1024]{1,0:T(8,128)(2,1)S(1)}, u32[]{:S(2)}, u32[]{:S(2)}) collective-permute-start(bf16[64,1024]{1,0:T(8,128)(2,1)S(1)} %copy-done.1), channel_id=1, source_target_pairs={{72,0},{49,1},{88,16},{1,17},{104,32},{17,33},{120,48},{33,49},{74... | collective-permute-start | bytes 393224 | tf_op jit(solution)/shard_map/ppermute | solution.py:33
  14.9 14.2 %collective-permute-start.3 = (bf16[256,1024]{1,0:T(8,128)(2,1)S(1)}, bf16[256,1024]{1,0:T(8,128)(2,1)S(1)}, u32[]{:S(2)}, u32[]{:S(2)}) collective-permute-start(bf16[256,1024]{1,0:T(8,128)(2,1)S(1)} %join.3.refs_0_), channel_id=1, source_target_pairs={{2,0},{9,1},{18,16},{25,17},{34,32},{41,33},{50,48},{57,49},{4,2},... | collective-permute-start | bytes 1572872 | tf_op jit(solution)/shard_map/ppermute | solution.py:33
  17.3 11.8 %collective-permute-start.4 = (bf16[256,1024]{1,0:T(8,128)(2,1)S(1)}, bf16[256,1024]{1,0:T(8,128)(2,1)S(1)}, u32[]{:S(2)}, u32[]{:S(2)}) collective-permute-start(bf16[256,1024]{1,0:T(8,128)(2,1)S(1)} %join.3.refs_0_), channel_id=1, source_target_pairs={{4,0},{65,1},{20,16},{81,17},{36,32},{97,33},{52,48},{113,49},{6,2... | collective-permute-start | bytes 1572872 | tf_op jit(solution)/shard_map/ppermute | solution.py:33
  17.8 14.9 %collective-permute-start.5 = (bf16[256,1024]{1,0:T(8,128)(2,1)S(1)}, bf16[256,1024]{1,0:T(8,128)(2,1)S(1)}, u32[]{:S(2)}, u32[]{:S(2)}) collective-permute-start(bf16[256,1024]{1,0:T(8,128)(2,1)S(1)} %join.3.refs_0_), channel_id=1, source_target_pairs={{6,0},{73,1},{22,16},{89,17},{38,32},{105,33},{54,48},{121,49},{0,... | collective-permute-start | bytes 1572872 | tf_op jit(solution)/shard_map/ppermute | solution.py:33
  18.6 16.7 %copy-start = (bf16[512,1024]{1,0:T(8,128)(2,1)S(1)}, bf16[512,1024]{1,0:T(8,128)(2,1)}, u32[]{:S(2)}) copy-start(bf16[512,1024]{1,0:T(8,128)(2,1)} %share.1.mine_ref) | copy-start | bytes 3145732
  32.8 14.3 %collective-permute-start.7 = (bf16[512,1024]{1,0:T(8,128)(2,1)S(1)}, bf16[512,1024]{1,0:T(8,128)(2,1)S(1)}, u32[]{:S(2)}, u32[]{:S(2)}) collective-permute-start(bf16[512,1024]{1,0:T(8,128)(2,1)S(1)} %join.4.refs_0_.refs_8_), channel_id=1, source_target_pairs={{16,0},{3,1},{32,16},{19,17},{48,32},{35,33},{0,48},{51,49},{18,2}... | collective-permute-start | bytes 3145736 | tf_op jit(solution)/shard_map/ppermute | solution.py:33
  35.3 15.2 %collective-permute-start.8 = (bf16[512,1024]{1,0:T(8,128)(2,1)S(1)}, bf16[512,1024]{1,0:T(8,128)(2,1)S(1)}, u32[]{:S(2)}, u32[]{:S(2)}) collective-permute-start(bf16[512,1024]{1,0:T(8,128)(2,1)S(1)} %join.5.refs_0_.refs_9_), channel_id=1, source_target_pairs={{48,0},{7,1},{0,16},{23,17},{16,32},{39,33},{32,48},{55,49},{50,2}... | collective-permute-start | bytes 3145736 | tf_op jit(solution)/shard_map/ppermute | solution.py:33
  38.2 23.5 %collective-permute-start.10 = (bf16[512,1024]{1,0:T(8,128)(2,1)S(1)}, bf16[512,1024]{1,0:T(8,128)(2,1)S(1)}, u32[]{:S(2)}, u32[]{:S(2)}) collective-permute-start(bf16[512,1024]{1,0:T(8,128)(2,1)S(1)} %join.4.refs_0_.refs_8_), channel_id=1, source_target_pairs={{48,0},{7,1},{0,16},{23,17},{16,32},{39,33},{32,48},{55,49},{50,2}... | collective-permute-start | bytes 3145736 | tf_op jit(solution)/shard_map/ppermute | solution.py:33
  38.3 23.4 %collective-permute-start.9 = (bf16[512,1024]{1,0:T(8,128)(2,1)S(1)}, bf16[512,1024]{1,0:T(8,128)(2,1)S(1)}, u32[]{:S(2)}, u32[]{:S(2)}) collective-permute-start(bf16[512,1024]{1,0:T(8,128)(2,1)S(1)} %join.5.refs_0_.refs_9_), channel_id=1, source_target_pairs={{16,0},{3,1},{32,16},{19,17},{48,32},{35,33},{0,48},{51,49},{18,2}... | collective-permute-start | bytes 3145736 | tf_op jit(solution)/shard_map/ppermute | solution.py:33
  50.5 22.5 %collective-permute-start.12 = (bf16[512,1024]{1,0:T(8,128)(2,1)S(1)}, bf16[512,1024]{1,0:T(8,128)(2,1)S(1)}, u32[]{:S(2)}, u32[]{:S(2)}) collective-permute-start(bf16[512,1024]{1,0:T(8,128)(2,1)S(1)} %collective-permute-done.8.refs_1_.refs_15_), channel_id=1, source_target_pairs={{48,0},{7,1},{0,16},{23,17},{16,32},{39,33},{32,48},{55,49},{50,2}... | collective-permute-start | bytes 3145736 | tf_op jit(solution)/shard_map/ppermute | solution.py:33
  50.5 25.3 %collective-permute-start.11 = (bf16[512,1024]{1,0:T(8,128)(2,1)S(1)}, bf16[512,1024]{1,0:T(8,128)(2,1)S(1)}, u32[]{:S(2)}, u32[]{:S(2)}) collective-permute-start(bf16[512,1024]{1,0:T(8,128)(2,1)S(1)} %collective-permute-done.7.refs_0_.refs_10_), channel_id=1, source_target_pairs={{16,0},{3,1},{32,16},{19,17},{48,32},{35,33},{0,48},{51,49},{18,2}... | collective-permute-start | bytes 3145736 | tf_op jit(solution)/shard_map/ppermute | solution.py:33
  108.3 11.4 %collective-permute-start.13 = (f32[512,1152]{1,0:T(8,128)}, f32[512,1152]{1,0:T(8,128)}, u32[]{:S(2)}, u32[]{:S(2)}) collective-permute-start(f32[512,1152]{1,0:T(8,128)} %sums.3), channel_id=1, source_target_pairs={{0,1},{1,0},{2,3},{3,2},{4,5},{5,4},{6,7},{7,6},{8,9},{9,8},{10,11... | collective-permute-start | bytes 7077896 | tf_op jit(solution)/shard_map/ppermute | solution.py:38
  113.6 4.6 %collective-permute-start.14 = (f32[64,128]{1,0:T(8,128)S(1)}, f32[64,128]{1,0:T(8,128)S(1)}, u32[]{:S(2)}, u32[]{:S(2)}) collective-permute-start(f32[64,128]{1,0:T(8,128)S(1)} %pack.1.mine_ref), channel_id=1, source_target_pairs={{0,1},{1,0},{2,3},{3,2},{4,5},{5,4},{6,7},{7,6},{8,9},{9,8},{10,11... | collective-permute-start | bytes 98312 | tf_op jit(solution)/shard_map/ppermute | solution.py:38

commit v6 on v5

--- a/solution.py
+++ b/solution.py
@@ -13,7 +13,7 @@
 BOTH = ("samp", "cent")
 UNIT = 64
 X, Y, Z = 0, 1, 2
-ORDERS = ((X, Y, Z), (Z, X, Y))
+ORDERS = ((X, Y, Z), (X, Z, Y))
 
 
 def place(x, y, z, core):
@@ -35,6 +35,17 @@
 
 def swap_cores(value):
     pairs = [(i, i ^ 1) for i in range(128)]
+    return lax.ppermute(value, BOTH, pairs)
+
+
+def swap_sides(value):
+    pairs = []
+    for x in range(4):
+        for y in range(4):
+            for z in range(4):
+                for core in range(2):
+                    other = (x + (1 if x % 2 == core else 3)) % 4
+                    pairs.append((place(other, y, z, core), place(x, y, z, core)))
     return lax.ppermute(value, BOTH, pairs)
 
 
@@ -98,15 +109,15 @@
     return jnp.where(lane >= step * inner, ahead, back)
 
 
-def first_kernel(order, spot_ref, ids_ref, *refs):
+def first_kernel(swapped, spot_ref, ids_ref, *refs):
     *stats, out_ref, top_ref = refs
     parts = []
-    for k, (ref, piece) in enumerate(order):
-        lanes = slice(piece * 512, (piece + 1) * 512)
-        tops = stats[ref][0:2, lanes]
+    for k, ref in enumerate(stats):
+        tops = ref[0:2, :]
         top = jnp.max(tops, axis=0, keepdims=True)
-        total = jnp.sum(stats[ref][2:4, lanes] * jnp.exp2(tops - top), axis=0, keepdims=True)
-        parts.append(top + jnp.log2(total))
+        total = jnp.sum(ref[2:4, :] * jnp.exp2(tops - top), axis=0, keepdims=True)
+        part = top + jnp.log2(total)
+        parts.append(roll_within(part, 0, spot_ref[3]) if k in swapped else part)
         top_ref[:, k * 512 : (k + 1) * 512] = tops
     value = jnp.concatenate(parts, axis=1)
     for dim in range(3):
@@ -119,7 +130,7 @@
     out_ref[:, :, 512:640] = jnp.broadcast_to(ids.reshape(1, 1, 128), (64, 8, 128))
 
 
-def merge_kernel(spot_ref, all_ref, whole_ref, own_ref):
+def merge_kernel(swapped, spot_ref, all_ref, whole_ref, own_ref):
     values = all_ref[:, :, 0:512]
     top = jnp.max(values, axis=0)
     total = jnp.sum(jnp.exp2(values - top[None]), axis=0)
@@ -129,6 +140,9 @@
     for dim in range(3):
         value = roll_within(value, dim, (4 - spot_ref[dim]) % 4)
     own_ref[...] = value
+    for k in swapped:
+        lanes = slice(k * 512, (k + 1) * 512)
+        own_ref[:, lanes] = roll_within(value[:, lanes], 0, 4 - spot_ref[3])
 
 
 def pack_kernel(whole_ref, all_ref, out_ref):
@@ -147,7 +161,7 @@
         for line in range(32):
             hit = ref[32 + line : 33 + line, :] == rows
             total = total + jnp.where(hit, ref[line : line + 1, :], 0.0)
-    out_ref[...] = total
+    out_ref[...] = jnp.sum(total.T, axis=0, keepdims=True) * math.log(2.0)
 
 
 def join_kernel(*refs):
@@ -156,6 +170,18 @@
     for part in parts:
         out_ref[at : at + part.shape[0], :] = part[...]
         at += part.shape[0]
+
+
+def halves_kernel(spot_ref, *refs):
+    *parts, first_ref, second_ref = refs
+    rows = parts[0].shape[0]
+    for side in range(2):
+
+        @pl.when(spot_ref[4] == side)
+        def _():
+            for k, part in enumerate(parts):
+                out_ref = (first_ref, second_ref)[(k // 2 + side) % 2]
+                out_ref[k % 2 * rows : (k % 2 + 1) * rows, :] = part[...]
 
 
 def join(*parts):
@@ -206,7 +232,7 @@
         functools.partial(sums_kernel, half, count),
         out_shape=jax.ShapeDtypeStruct((512, width + 128), jnp.float32),
         in_specs=[vmem] * (2 + 2 * count),
-        compiler_params=pltpu.CompilerParams(vmem_limit_bytes=10 << 20),
+        compiler_params=pltpu.CompilerParams(vmem_limit_bytes=12 << 20),
         cost_estimate=pl.CostEstimate(
             flops=2 * 512 * 4096 * width, bytes_accessed=18 << 20, transcendentals=8192
         ),
@@ -224,9 +250,17 @@
 def share_kernel(at_ref, cents_ref, out_ref, sem):
     size = out_ref.shape[0]
     first = pl.multiple_of(at_ref[0] * size, size)
-    copy = pltpu.make_async_copy(cents_ref.at[pl.ds(first, size)], out_ref, sem)
-    copy.start()
-    copy.wait()
+    part = size // 8
+    copies = [
+        pltpu.make_async_copy(
+            cents_ref.at[pl.ds(first + k * part, part)], out_ref.at[pl.ds(k * part, part)], sem.at[k]
+        )
+        for k in range(8)
+    ]
+    for copy in copies:
+        copy.start()
+    for copy in copies:
+        copy.wait()
 
 
 def shards(embeddings, destination, centroids):
@@ -234,54 +268,64 @@
     core = lax.bitwise_and(cent, 1)
     x = lax.shift_right_logical(samp, 2) * 2 + lax.shift_right_logical(cent, 3)
     y, z = lax.bitwise_and(lax.shift_right_logical(cent, 1), 3), lax.bitwise_and(samp, 3)
-    spot = jnp.where(core == 0, jnp.stack([x, y, z]), jnp.stack([z, x, y])).astype(jnp.int32)
+    side = lax.bitwise_and(x, 1)
+    second = lax.bitwise_and(jnp.where(core == 0, y, z) + 2 * side, 3)
+    step = jnp.where(side == core, 1, 3)
+    spot = jnp.stack([x, second, jnp.where(core == 0, z, y), step, side]).astype(jnp.int32)
     share = centroids.shape[0] // 8
     width = embeddings.shape[1]
     smem = pl.BlockSpec(memory_space=pltpu.SMEM)
     vmem = pl.BlockSpec(memory_space=pltpu.VMEM)
     small = pltpu.CompilerParams(vmem_limit_bytes=8 << 20)
     line = join(embeddings, *[fetch(embeddings, 0, step) for step in (1, 2, 3)])
-    spot, destination, _ = lax.optimization_barrier((spot, destination, line))
+    near, across, back = [fetch(line, 1, step) for step in (1, 2, 3)]
+    destination, _ = lax.optimization_barrier((destination, line))
+    ids = jnp.tile(destination.astype(jnp.float32), 2).reshape(1, 128)
+    first, second = pl.pallas_call(
+        halves_kernel,
+        out_shape=[jax.ShapeDtypeStruct((512, width), embeddings.dtype)] * 2,
+        in_specs=[smem] + [vmem] * 4,
+        out_specs=[vmem] * 2,
+        compiler_params=small,
+        name="halves",
+    )(spot, line, near, across, back)
+    at_word = jnp.stack([samp, cent]).astype(jnp.int32)
+    first, second, ids, spot, at_word = lax.optimization_barrier((first, second, ids, spot, at_word))
+    far_first = fetch(first, 2, 2)
     mine = pl.pallas_call(
         share_kernel,
         out_shape=jax.ShapeDtypeStruct((share, width), centroids.dtype),
         in_specs=[smem, pl.BlockSpec(memory_space=pltpu.HBM)],
         out_specs=vmem,
-        scratch_shapes=[pltpu.SemaphoreType.DMA(())],
-        compiler_params=pltpu.CompilerParams(vmem_limit_bytes=56 << 20),
+        scratch_shapes=[pltpu.SemaphoreType.DMA((8,))],
+        compiler_params=pltpu.CompilerParams(vmem_limit_bytes=54 << 20),
         name="share",
-    )(samp.astype(jnp.int32).reshape(1), centroids)
+    )(at_word, centroids)
     other = swap_cores(mine)
-    ids = jnp.tile(destination.astype(jnp.float32), 2).reshape(1, 128)
-    near, across, back = [fetch(line, 1, step) for step in (1, 2, 3)]
-    upper, lower = join(line, near), join(across, back)
-    upper, lower, other, ids = lax.optimization_barrier((upper, lower, other, ids))
-    after_upper, before_lower = fetch(upper, 2, 1), fetch(lower, 2, 3)
-
-    p_upper, stat_upper = scores_call(mine, other, [upper])
-    upper_again, lower_again, _ = lax.optimization_barrier((upper, lower, stat_upper))
-    after_lower, before_upper = fetch(lower_again, 2, 1), fetch(upper_again, 2, 3)
-    p_lower, stat_lower = scores_call(mine, other, [lower])
-    passed_up, passed_down, _ = lax.optimization_barrier((after_upper, before_lower, stat_lower))
-    far_upper, far_lower = fetch(passed_up, 2, 1), fetch(passed_down, 2, 3)
-    p_first, stat_first = scores_call(mine, other, [after_upper, before_lower])
-    p_second, stat_second = scores_call(mine, other, [after_lower, before_upper])
-    p_third, stat_third = scores_call(mine, other, [far_upper])
-    p_fourth, stat_fourth = scores_call(mine, other, [far_lower])
-    chunks = [upper, lower, after_upper, after_lower, far_upper, far_lower, before_upper, before_lower]
-    ps = p_upper + p_lower + [p_first[0], p_second[0]] + p_third + p_fourth + [p_second[1], p_first[1]]
-    order = ((0, 0), (1, 0), (2, 0), (3, 0), (4, 0), (5, 0), (3, 1), (2, 1))
+    first_again, mine = lax.optimization_barrier((first, mine))
+    after_first, before_first = fetch(first_again, 2, 1), fetch(first_again, 2, 3)
+    score = functools.partial(scores_call, mine, other)
+    own_first = score([first])
+    second_again, _ = lax.optimization_barrier((second, own_first[1]))
+    own_second = score([second])
+    after_second, before_second = fetch(second_again, 2, 1), fetch(second_again, 2, 3)
+    far_second = swap_sides(far_first)
+    chunks = [first, second, after_first, after_second, far_first, far_second, before_first, before_second]
+    swapped = (5,)
+    pairs = [own_first, own_second] + [score([chunk]) for chunk in chunks[2:]]
+    ps = [p[0] for p, _ in pairs]
+    stats = [stat for _, stat in pairs]
 
     local, tops = pl.pallas_call(
-        functools.partial(first_kernel, order),
+        functools.partial(first_kernel, swapped),
         out_shape=(
             jax.ShapeDtypeStruct((64, 8, 640), jnp.float32),
             jax.ShapeDtypeStruct((2, 4096), jnp.float32),
         ),
-        in_specs=[smem] + [vmem] * 7,
+        in_specs=[smem] + [vmem] * 9,
         compiler_params=small,
         name="first",
-    )(spot, ids, stat_upper, stat_lower, stat_first, stat_second, stat_third, stat_fourth)
+    )(spot, ids, *stats)
     chips = []
     for side in range(2):
         group = []
@@ -293,7 +337,7 @@
         chips.append(group)
     shared = lax.all_to_all(local, BOTH, split_axis=0, concat_axis=0, tiled=True, axis_index_groups=chips)
     whole, lse = pl.pallas_call(
-        merge_kernel,
+        functools.partial(merge_kernel, swapped),
         out_shape=(
             jax.ShapeDtypeStruct((8, 512), jnp.float32),
             jax.ShapeDtypeStruct((1, 4096), jnp.float32),
@@ -314,19 +358,18 @@
     )(whole, shared)
     partner = swap_cores(pack)
     ours = sums_call(0, lse, tops, ps, chunks)
-    spread = pl.pallas_call(
+    row_lse = pl.pallas_call(
         route_kernel,
-        out_shape=jax.ShapeDtypeStruct((UNIT, 128), jnp.float32),
+        out_shape=jax.ShapeDtypeStruct((1, UNIT), jnp.float32),
         in_specs=[smem, vmem, vmem],
         compiler_params=small,
         name="route",
-    )(jnp.stack([samp, cent]).astype(jnp.int32), pack, partner)
-    row_lse = jnp.sum(spread, axis=1) * math.log(2.0)
+    )(at_word, pack, partner)
     new_centers = pl.pallas_call(
         final_kernel, out_shape=jax.ShapeDtypeStruct((share, width), jnp.float32), name="final",
         compiler_params=pltpu.CompilerParams(vmem_limit_bytes=8 << 20),
     )(ours, received, mine)
-    return new_centers, row_lse
+    return new_centers, row_lse.reshape(UNIT)
 
 
 def solution(mesh):

time: 123 us -> 125 us (1.016)
  Pallas kernels: 39.3 us -> 31.4 us
  waiting for transfers between devices: 38 us -> 44.4 us
  blocking collectives: 21.2 us -> 27 us
  starting transfers between devices: 22.9 us -> 17.9 us
  local copies, waits for them, and re-layouts: 0.1 us -> 2.31 us
    pallas_call x6 -> x8, Pallas kernels: 19.8 us -> 13 us  [scores_call(): pl.pallas_call(functools.partial(scores_kernel, factor, count), out_shape...]
    ppermute x12 -> x11, waiting for transfers between devices: 38 us -> 44.3 us  [fetch(): return lax.ppermute(value, BOTH, pairs)]
    all_to_all x1, blocking collectives: 21.2 us -> 27 us  [shards(): lax.all_to_all(local, BOTH, split_axis=0, concat_axis=0, tiled=True, axis...]
    ppermute x3, starting transfers between devices: 6.79 us -> 3.06 us  [swap_cores(): return lax.ppermute(value, BOTH, pairs)]
    unnamed x6 -> x8, local copies, waits for them, and re-layouts: 0.01 us -> 2.14 us
    pallas_call x1, Pallas kernels: 3.37 us -> 1.71 us  [shards(): pl.pallas_call(final_kernel, out_shape=jax.ShapeDtypeStruct((share, width...]
    ppermute x12 -> x11, starting transfers between devices: 16.1 us -> 14.6 us  [fetch(): return lax.ppermute(value, BOTH, pairs)]
    pallas_call x2, Pallas kernels: 10.4 us -> 8.98 us  [sums_call(): pl.pallas_call(functools.partial(sums_kernel, half, count), out_shape=jax...]
  transfers between devices with their start and end apart: 15 -> 15, of which waited for: 9 -> 8; matrix products, arithmetic and copies ran while one was open for 1% -> 1% of each run, Pallas kernels for 18% -> 14%
where the time goes in v6:
time: 125 us
  waiting for transfers between devices  44.4 us (36%)
  Pallas kernels  31.4 us (25%)
  blocking collectives  27 us (22%)
  starting transfers between devices  17.9 us (14%)
  local copies, waits for them, and re-layouts  2.31 us (2%)
  other arithmetic  1.26 us (1%)
    ppermute x11, waiting for transfers between devices, fetch(): return lax.ppermute(value, BOTH, pairs)  44.3 us
    all_to_all x1, blocking collectives, shards(): lax.all_to_all(local, BOTH, split_axis=0, concat_axis=0, tiled=True, axis...  27 us
    ppermute x11, starting transfers between devices, fetch(): return lax.ppermute(value, BOTH, pairs)  14.6 us
    pallas_call x8, Pallas kernels, scores_call(): pl.pallas_call(functools.partial(scores_kernel, factor, count), out_shape...  13 us
    pallas_call x2, Pallas kernels, sums_call(): pl.pallas_call(functools.partial(sums_kernel, half, count), out_shape=jax...  8.98 us
    ppermute x3, starting transfers between devices, swap_cores(): return lax.ppermute(value, BOTH, pairs)  3.06 us
    pallas_call x1, Pallas kernels, shards(): pl.pallas_call(share_kernel, out_shape=jax.ShapeDtypeStruct((share, width...  2.99 us
  transfers between devices with their start and end apart: 15, of which 8 were waited for; matrix products, arithmetic and copies ran while one was open for 1% of the time, Pallas kernels for 14%

profile of v6, /device:TPU:1, one launch (start us, length us, event | category | flops | bytes accessed | tf_op | source)
XLA Modules:
  0.0 125.0 jit_solution(12958014609977341020)
XLA Ops:
  0.6 3.4 %collective-permute-start = (bf16[64,1024]{1,0:T(8,128)(2,1)}, bf16[64,1024]{1,0:T(8,128)(2,1)S(1)}, u32[]{:S(2)}, u32[]{:S(2)}) collective-permute-start(bf16[64,1024]{1,0:T(8,128)(2,1)} %refs_0_.1), channel_id=1, source_target_pairs={{8,0},{9,1},{24,16},{25,17},{40,32},{41,33},{56,48},{57,49},{10,2}... | collective-permute-start | bytes 393224 | tf_op jit(solution)/shard_map/ppermute | solution.py:33
  5.1 4.2 %collective-permute-done.refs_1_ = bf16[64,1024]{1,0:T(8,128)(2,1)S(1)} collective-permute-done((bf16[64,1024]{1,0:T(8,128)(2,1)}, bf16[64,1024]{1,0:T(8,128)(2,1)S(1)}, u32[]{:S(2)}, u32[]{:S(2)}) %collective-permute-start) | collective-permute-done | bytes 131104 | tf_op jit(solution)/shard_map/ppermute | solution.py:33
  9.6 4.1 %collective-permute-done.2.refs_3_ = bf16[64,1024]{1,0:T(8,128)(2,1)S(1)} collective-permute-done((bf16[64,1024]{1,0:T(8,128)(2,1)}, bf16[64,1024]{1,0:T(8,128)(2,1)S(1)}, u32[]{:S(2)}, u32[]{:S(2)}) %collective-permute-start.2) | collective-permute-done | bytes 131104 | tf_op jit(solution)/shard_map/ppermute | solution.py:33
  13.8 0.9 copy-done.2
  14.7 3.8 %collective-permute-start.3 = (bf16[256,1024]{1,0:T(8,128)(2,1)S(1)}, bf16[256,1024]{1,0:T(8,128)(2,1)S(1)}, u32[]{:S(2)}, u32[]{:S(2)}) collective-permute-start(bf16[256,1024]{1,0:T(8,128)(2,1)S(1)} %join.1.refs_0_), channel_id=1, source_target_pairs={{2,0},{17,1},{18,16},{33,17},{34,32},{49,33},{50,48},{1,49},{4,2},... | collective-permute-start | bytes 1572872 | tf_op jit(solution)/shard_map/ppermute | solution.py:33
  20.7 9.6 %collective-permute-done.3.refs_1_ = bf16[256,1024]{1,0:T(8,128)(2,1)S(1)} collective-permute-done((bf16[256,1024]{1,0:T(8,128)(2,1)S(1)}, bf16[256,1024]{1,0:T(8,128)(2,1)S(1)}, u32[]{:S(2)}, u32[]{:S(2)}) %collective-permute-start.3) | collective-permute-done | bytes 524320 | tf_op jit(solution)/shard_map/ppermute | solution.py:33
  30.3 3.4 %collective-permute-done.5.refs_3_ = bf16[256,1024]{1,0:T(8,128)(2,1)S(1)} collective-permute-done((bf16[256,1024]{1,0:T(8,128)(2,1)S(1)}, bf16[256,1024]{1,0:T(8,128)(2,1)S(1)}, u32[]{:S(2)}, u32[]{:S(2)}) %collective-permute-start.5) | collective-permute-done | bytes 524320 | tf_op jit(solution)/shard_map/ppermute | solution.py:33
  34.4 3.0 %share.1.mine_ref = bf16[512,1024]{1,0:T(8,128)(2,1)} custom-call(s32[2]{0:T(128)} %pad_add_fusion.at_ref, bf16[4096,1024]{1,0:T(8,128)(2,1)} %cents_ref.1), custom_call_target="tpu_custom_call" | custom-call | tf_op jit(solution)/shard_map/share/pallas_call | solution.py:295
  37.4 1.2 collective-permute-start.6
  38.5 1.6 %collective-permute-start.9 = (bf16[512,1024]{1,0:T(8,128)(2,1)S(1)}, bf16[512,1024]{1,0:T(8,128)(2,1)S(1)}, u32[]{:S(2)}, u32[]{:S(2)}) collective-permute-start(bf16[512,1024]{1,0:T(8,128)(2,1)S(1)} %get-tuple-element.46.refs_0_.refs_8_), channel_id=1, source_target_pairs={{32,0},{5,1},{48,16},{21,17},{0,32},{37,33},{16,48},{53,49},{34,2}... | collective-permute-start | bytes 3145736 | tf_op jit(solution)/shard_map/ppermute | solution.py:33
  40.6 2.3 %collective-permute-start.7 = (bf16[512,1024]{1,0:T(8,128)(2,1)S(1)}, bf16[512,1024]{1,0:T(8,128)(2,1)S(1)}, u32[]{:S(2)}, u32[]{:S(2)}) collective-permute-start(bf16[512,1024]{1,0:T(8,128)(2,1)S(1)} %get-tuple-element.46.refs_0_.refs_8_), channel_id=1, source_target_pairs={{16,0},{3,1},{32,16},{19,17},{48,32},{35,33},{0,48},{51,49},{18,2}... | collective-permute-start | bytes 3145736 | tf_op jit(solution)/shard_map/ppermute | solution.py:33
  42.9 1.2 copy-done
  44.1 1.6 %scores.8 = (f32[2,512,512]{2,1,0:T(8,128)S(1)}, f32[4,512]{1,0:T(4,128)S(1)}) custom-call(bf16[512,1024]{1,0:T(8,128)(2,1)S(1)} %copy-done, bf16[512,1024]{1,0:T(8,128)(2,1)S(1)} %collective-permute-done.6.other_ref, bf16[512,1024]{1,0:T(8,128)(2,1)S(1)} %get-tuple-element.46.refs_0_.refs_8_), custom_call_target="tpu_custom_call" | custom-call | flops 2147483648 | bytes 5242880 | tf_op jit(solution)/shard_map/scores/pallas_call | solution.py:85
  45.8 8.2 %collective-permute-done.9.refs_0_.refs_12_ = bf16[512,1024]{1,0:T(8,128)(2,1)S(1)} collective-permute-done((bf16[512,1024]{1,0:T(8,128)(2,1)S(1)}, bf16[512,1024]{1,0:T(8,128)(2,1)S(1)}, u32[]{:S(2)}, u32[]{:S(2)}) %collective-permute-start.9) | collective-permute-done | bytes 1048608 | tf_op jit(solution)/shard_map/ppermute | solution.py:33
  54.3 1.2 collective-permute-start.8
  55.5 1.6 %scores.12 = (f32[2,512,512]{2,1,0:T(8,128)S(1)}, f32[4,512]{1,0:T(4,128)S(1)}) custom-call(bf16[512,1024]{1,0:T(8,128)(2,1)S(1)} %copy-done.1, bf16[512,1024]{1,0:T(8,128)(2,1)S(1)} %collective-permute-done.6.other_ref, bf16[512,1024]{1,0:T(8,128)(2,1)S(1)} %collective-permute-done.9.refs_0_.refs_12_), custom_call_target="tpu_custom_call" | custom-call | flops 2147483648 | bytes 5242880 | tf_op jit(solution)/shard_map/scores/pallas_call | solution.py:85
  57.1 1.6 %scores.9 = (f32[2,512,512]{2,1,0:T(8,128)S(1)}, f32[4,512]{1,0:T(4,128)S(1)}) custom-call(bf16[512,1024]{1,0:T(8,128)(2,1)S(1)} %copy-done.1, bf16[512,1024]{1,0:T(8,128)(2,1)S(1)} %collective-permute-done.6.other_ref, bf16[512,1024]{1,0:T(8,128)(2,1)S(1)} %get-tuple-element.48.refs_0_.refs_9_), custom_call_target="tpu_custom_call" | custom-call | flops 2147483648 | bytes 5242880 | tf_op jit(solution)/shard_map/scores/pallas_call | solution.py:85
  58.7 6.5 %collective-permute-done.11.refs_0_.refs_14_ = bf16[512,1024]{1,0:T(8,128)(2,1)S(1)} collective-permute-done((bf16[512,1024]{1,0:T(8,128)(2,1)S(1)}, bf16[512,1024]{1,0:T(8,128)(2,1)S(1)}, u32[]{:S(2)}, u32[]{:S(2)}) %collective-permute-start.11) | collective-permute-done | bytes 1048608 | tf_op jit(solution)/shard_map/ppermute | solution.py:33
  65.2 1.6 %scores.14 = (f32[2,512,512]{2,1,0:T(8,128)S(1)}, f32[4,512]{1,0:T(4,128)S(1)}) custom-call(bf16[512,1024]{1,0:T(8,128)(2,1)S(1)} %copy-done.1, bf16[512,1024]{1,0:T(8,128)(2,1)S(1)} %collective-permute-done.6.other_ref, bf16[512,1024]{1,0:T(8,128)(2,1)S(1)} %collective-permute-done.11.refs_0_.refs_14_), custom_call_target="tpu_custom_call" | custom-call | flops 2147483648 | bytes 5242880 | tf_op jit(solution)/shard_map/scores/pallas_call | solution.py:85
  66.9 1.6 %scores.10 = (f32[2,512,512]{2,1,0:T(8,128)S(1)}, f32[4,512]{1,0:T(4,128)S(1)}) custom-call(bf16[512,1024]{1,0:T(8,128)(2,1)S(1)} %copy-done.1, bf16[512,1024]{1,0:T(8,128)(2,1)S(1)} %collective-permute-done.6.other_ref, bf16[512,1024]{1,0:T(8,128)(2,1)S(1)} %collective-permute-done.7.refs_0_.refs_10_), custom_call_target="tpu_custom_call" | custom-call | flops 2147483648 | bytes 5242880 | tf_op jit(solution)/shard_map/scores/pallas_call | solution.py:85
  68.5 8.0 %collective-permute-done.12.refs_0_.refs_15_ = bf16[512,1024]{1,0:T(8,128)(2,1)S(1)} collective-permute-done((bf16[512,1024]{1,0:T(8,128)(2,1)S(1)}, bf16[512,1024]{1,0:T(8,128)(2,1)S(1)}, u32[]{:S(2)}, u32[]{:S(2)}) %collective-permute-start.12) | collective-permute-done | bytes 1048608 | tf_op jit(solution)/shard_map/ppermute | solution.py:33
  76.5 1.6 %scores.15 = (f32[2,512,512]{2,1,0:T(8,128)S(1)}, f32[4,512]{1,0:T(4,128)S(1)}) custom-call(bf16[512,1024]{1,0:T(8,128)(2,1)S(1)} %copy-done.1, bf16[512,1024]{1,0:T(8,128)(2,1)S(1)} %collective-permute-done.6.other_ref, bf16[512,1024]{1,0:T(8,128)(2,1)S(1)} %collective-permute-done.12.refs_0_.refs_15_), custom_call_target="tpu_custom_call" | custom-call | flops 2147483648 | bytes 5242880 | tf_op jit(solution)/shard_map/scores/pallas_call | solution.py:85
  78.1 1.6 %scores.13 = (f32[2,512,512]{2,1,0:T(8,128)S(1)}, f32[4,512]{1,0:T(4,128)S(1)}) custom-call(bf16[512,1024]{1,0:T(8,128)(2,1)S(1)} %copy-done.1, bf16[512,1024]{1,0:T(8,128)(2,1)S(1)} %collective-permute-done.6.other_ref, bf16[512,1024]{1,0:T(8,128)(2,1)S(1)} %collective-permute-done.10.refs_0_.refs_13_), custom_call_target="tpu_custom_call" | custom-call | flops 2147483648 | bytes 5242880 | tf_op jit(solution)/shard_map/scores/pallas_call | solution.py:85
  79.7 1.6 %scores.11 = (f32[2,512,512]{2,1,0:T(8,128)S(1)}, f32[4,512]{1,0:T(4,128)S(1)}) custom-call(bf16[512,1024]{1,0:T(8,128)(2,1)S(1)} %copy-done.1, bf16[512,1024]{1,0:T(8,128)(2,1)S(1)} %collective-permute-done.6.other_ref, bf16[512,1024]{1,0:T(8,128)(2,1)S(1)} %collective-permute-done.8.refs_0_.refs_11_), custom_call_target="tpu_custom_call" | custom-call | flops 2147483648 | bytes 5242880 | tf_op jit(solution)/shard_map/scores/pallas_call | solution.py:85
  81.4 1.3 %first.1 = (f32[64,8,640]{2,1,0:T(8,128)S(1)}, f32[2,4096]{1,0:T(2,128)S(1)}) custom-call(s32[5]{0:T(128)S(1)} %stack.32.spot_ref, f32[1,128]{1,0:T(1,128)S(1)} %reshape_tile.3.ids_ref, f32[4,512]{1,0:T(4,128)S(1)} %get-tuple-element.43.refs_0_, f32[4,512]{1,0:T(4,128)S(1)} %get-tuple-element.45.refs_1_, f32[4,512]{1,0:T(4,128)S(1)} %get-tuple-element.47.refs_2_, ...), custom_call_target="tpu_custom_call" | custom-call | tf_op jit(solution)/shard_map/first/pallas_call | solution.py:319
  82.7 27.0 %all_to_all.5.all_ref = f32[64,8,640]{2,1,0:T(8,128)S(1)} all-to-all(f32[64,8,640]{2,1,0:T(8,128)S(1)} %get-tuple-element.54), channel_id=1, replica_groups={{0,8,64,72,2,10,66,74,4,12,68,76,6,14,70,78,16,24,80,88,18,26,82,90,20,..., dimensions={0} | all-to-all | bytes 2621440 | tf_op jit(solution)/shard_map/all_to_all | solution.py:338
  109.7 1.2 merge.1
  110.9 4.5 %sums.3 = f32[512,1152]{1,0:T(8,128)S(1)} custom-call(f32[1,4096]{1,0:T(1,128)S(1)} %get-tuple-element.55.lse_ref, f32[2,4096]{1,0:T(2,128)S(1)} %get-tuple-element.56.top_ref, f32[2,512,512]{2,1,0:T(8,128)S(1)} %get-tuple-element.57.refs_0_, f32[2,512,512]{2,1,0:T(8,128)S(1)} %get-tuple-element.58.refs_1_, f32[2,512,512]{2,1,0:T(8,128)S(1)} %get-tuple-element.59.refs_2_, ...), custom_call_target="tpu_custom_call" | custom-call | flops 4294967296 | bytes 18874368 | tf_op jit(solution)/shard_map/sums/pallas_call | solution.py:231
  115.4 1.8 %collective-permute-start.13 = (f32[512,1152]{1,0:T(8,128)S(1)}, f32[512,1152]{1,0:T(8,128)S(1)}, u32[]{:S(2)}, u32[]{:S(2)}) collective-permute-start(f32[512,1152]{1,0:T(8,128)S(1)} %sums.3), channel_id=1, source_target_pairs={{0,1},{1,0},{2,3},{3,2},{4,5},{5,4},{6,7},{7,6},{8,9},{9,8},{10,11... | collective-permute-start | bytes 7077896 | tf_op jit(solution)/shard_map/ppermute | solution.py:38
  117.4 4.5 %sums.2.ours_ref = f32[512,1152]{1,0:T(8,128)S(1)} custom-call(f32[1,4096]{1,0:T(1,128)S(1)} %get-tuple-element.55.lse_ref, f32[2,4096]{1,0:T(2,128)S(1)} %get-tuple-element.56.top_ref, f32[2,512,512]{2,1,0:T(8,128)S(1)} %get-tuple-element.57.refs_0_, f32[2,512,512]{2,1,0:T(8,128)S(1)} %get-tuple-element.58.refs_1_, ...), custom_call_target="tpu_custom_call" | custom-call | flops 4294967296 | bytes 18874368 | tf_op jit(solution)/shard_map/sums/pallas_call | solution.py:231
  121.9 1.4 %route.1 = f32[1,64]{1,0:T(1,128)} custom-call(s32[2]{0:T(128)S(1)} %copy-done.3, f32[64,128]{1,0:T(8,128)S(1)} %pack.1.mine_ref, f32[64,128]{1,0:T(8,128)S(1)} %collective-permute-done.14.other_ref), custom_call_target="tpu_custom_call" | custom-call | tf_op jit(solution)/shard_map/route/pallas_call | solution.py:361
  123.3 1.7 %final.1 = f32[512,1024]{1,0:T(8,128)} custom-call(f32[512,1152]{1,0:T(8,128)S(1)} %sums.2.ours_ref, f32[512,1152]{1,0:T(8,128)S(1)} %collective-permute-done.13.theirs_ref, bf16[512,1024]{1,0:T(8,128)(2,1)S(1)} %copy-done.1), custom_call_target="tpu_custom_call" | custom-call | tf_op jit(solution)/shard_map/final/pallas_call | solution.py:368
  (30 shorter events, 5.2 us)
Async XLA Ops:
  0.6 8.7 %collective-permute-start = (bf16[64,1024]{1,0:T(8,128)(2,1)}, bf16[64,1024]{1,0:T(8,128)(2,1)S(1)}, u32[]{:S(2)}, u32[]{:S(2)}) collective-permute-start(bf16[64,1024]{1,0:T(8,128)(2,1)} %refs_0_.1), channel_id=1, source_target_pairs={{8,0},{9,1},{24,16},{25,17},{40,32},{41,33},{56,48},{57,49},{10,2}... | collective-permute-start | bytes 393224 | tf_op jit(solution)/shard_map/ppermute | solution.py:33
  4.0 5.6 %collective-permute-start.1 = (bf16[64,1024]{1,0:T(8,128)(2,1)}, bf16[64,1024]{1,0:T(8,128)(2,1)S(1)}, u32[]{:S(2)}, u32[]{:S(2)}) collective-permute-start(bf16[64,1024]{1,0:T(8,128)(2,1)} %refs_0_.1), channel_id=1, source_target_pairs={{64,0},{65,1},{80,16},{81,17},{96,32},{97,33},{112,48},{113,49},{6... | collective-permute-start | bytes 393224 | tf_op jit(solution)/shard_map/ppermute | solution.py:33
  4.5 9.2 %collective-permute-start.2 = (bf16[64,1024]{1,0:T(8,128)(2,1)}, bf16[64,1024]{1,0:T(8,128)(2,1)S(1)}, u32[]{:S(2)}, u32[]{:S(2)}) collective-permute-start(bf16[64,1024]{1,0:T(8,128)(2,1)} %refs_0_.1), channel_id=1, source_target_pairs={{72,0},{73,1},{88,16},{89,17},{104,32},{105,33},{120,48},{121,49},... | collective-permute-start | bytes 393224 | tf_op jit(solution)/shard_map/ppermute | solution.py:33
  13.8 0.9 copy-start.2
  14.7 15.6 %collective-permute-start.3 = (bf16[256,1024]{1,0:T(8,128)(2,1)S(1)}, bf16[256,1024]{1,0:T(8,128)(2,1)S(1)}, u32[]{:S(2)}, u32[]{:S(2)}) collective-permute-start(bf16[256,1024]{1,0:T(8,128)(2,1)S(1)} %join.1.refs_0_), channel_id=1, source_target_pairs={{2,0},{17,1},{18,16},{33,17},{34,32},{49,33},{50,48},{1,49},{4,2},... | collective-permute-start | bytes 1572872 | tf_op jit(solution)/shard_map/ppermute | solution.py:33
  18.5 11.7 %collective-permute-start.4 = (bf16[256,1024]{1,0:T(8,128)(2,1)S(1)}, bf16[256,1024]{1,0:T(8,128)(2,1)S(1)}, u32[]{:S(2)}, u32[]{:S(2)}) collective-permute-start(bf16[256,1024]{1,0:T(8,128)(2,1)S(1)} %join.1.refs_0_), channel_id=1, source_target_pairs={{4,0},{33,1},{20,16},{49,17},{36,32},{1,33},{52,48},{17,49},{6,2},... | collective-permute-start | bytes 1572872 | tf_op jit(solution)/shard_map/ppermute | solution.py:33
  18.5 15.2 %collective-permute-start.5 = (bf16[256,1024]{1,0:T(8,128)(2,1)S(1)}, bf16[256,1024]{1,0:T(8,128)(2,1)S(1)}, u32[]{:S(2)}, u32[]{:S(2)}) collective-permute-start(bf16[256,1024]{1,0:T(8,128)(2,1)S(1)} %join.1.refs_0_), channel_id=1, source_target_pairs={{6,0},{49,1},{22,16},{1,17},{38,32},{17,33},{54,48},{33,49},{0,2},... | collective-permute-start | bytes 1572872 | tf_op jit(solution)/shard_map/ppermute | solution.py:33
  37.4 5.5 %collective-permute-start.6 = (bf16[512,1024]{1,0:T(8,128)(2,1)}, bf16[512,1024]{1,0:T(8,128)(2,1)S(1)}, u32[]{:S(2)}, u32[]{:S(2)}) collective-permute-start(bf16[512,1024]{1,0:T(8,128)(2,1)} %share.1.mine_ref), channel_id=1, source_target_pairs={{0,1},{1,0},{2,3},{3,2},{4,5},{5,4},{6,7},{7,6},{8,9},{9,8},{10,11... | collective-permute-start | bytes 3145736 | tf_op jit(solution)/shard_map/ppermute | solution.py:38
  38.5 15.5 %collective-permute-start.9 = (bf16[512,1024]{1,0:T(8,128)(2,1)S(1)}, bf16[512,1024]{1,0:T(8,128)(2,1)S(1)}, u32[]{:S(2)}, u32[]{:S(2)}) collective-permute-start(bf16[512,1024]{1,0:T(8,128)(2,1)S(1)} %get-tuple-element.46.refs_0_.refs_8_), channel_id=1, source_target_pairs={{32,0},{5,1},{48,16},{21,17},{0,32},{37,33},{16,48},{53,49},{34,2}... | collective-permute-start | bytes 3145736 | tf_op jit(solution)/shard_map/ppermute | solution.py:33
  40.2 25.1 %collective-permute-start.11 = (bf16[512,1024]{1,0:T(8,128)(2,1)S(1)}, bf16[512,1024]{1,0:T(8,128)(2,1)S(1)}, u32[]{:S(2)}, u32[]{:S(2)}) collective-permute-start(bf16[512,1024]{1,0:T(8,128)(2,1)S(1)} %get-tuple-element.46.refs_0_.refs_8_), channel_id=1, source_target_pairs={{48,0},{7,1},{0,16},{23,17},{16,32},{39,33},{32,48},{55,49},{50,2}... | collective-permute-start | bytes 3145736 | tf_op jit(solution)/shard_map/ppermute | solution.py:33
  40.6 26.3 %collective-permute-start.7 = (bf16[512,1024]{1,0:T(8,128)(2,1)S(1)}, bf16[512,1024]{1,0:T(8,128)(2,1)S(1)}, u32[]{:S(2)}, u32[]{:S(2)}) collective-permute-start(bf16[512,1024]{1,0:T(8,128)(2,1)S(1)} %get-tuple-element.46.refs_0_.refs_8_), channel_id=1, source_target_pairs={{16,0},{3,1},{32,16},{19,17},{48,32},{35,33},{0,48},{51,49},{18,2}... | collective-permute-start | bytes 3145736 | tf_op jit(solution)/shard_map/ppermute | solution.py:33
  42.8 1.2 copy-start
  44.1 11.4 %copy-start.1 = (bf16[512,1024]{1,0:T(8,128)(2,1)S(1)}, bf16[512,1024]{1,0:T(8,128)(2,1)}, u32[]{:S(2)}) copy-start(bf16[512,1024]{1,0:T(8,128)(2,1)} %share.1.mine_ref) | copy-start | bytes 3145732
  45.7 30.8 %collective-permute-start.12 = (bf16[512,1024]{1,0:T(8,128)(2,1)S(1)}, bf16[512,1024]{1,0:T(8,128)(2,1)S(1)}, u32[]{:S(2)}, u32[]{:S(2)}) collective-permute-start(bf16[512,1024]{1,0:T(8,128)(2,1)S(1)} %get-tuple-element.48.refs_0_.refs_9_), channel_id=1, source_target_pairs={{48,0},{7,1},{0,16},{23,17},{16,32},{39,33},{32,48},{55,49},{50,2}... | collective-permute-start | bytes 3145736 | tf_op jit(solution)/shard_map/ppermute | solution.py:33
  54.0 24.1 %collective-permute-start.10 = (bf16[512,1024]{1,0:T(8,128)(2,1)S(1)}, bf16[512,1024]{1,0:T(8,128)(2,1)S(1)}, u32[]{:S(2)}, u32[]{:S(2)}) collective-permute-start(bf16[512,1024]{1,0:T(8,128)(2,1)S(1)} %collective-permute-done.9.refs_0_.refs_12_), channel_id=1, source_target_pairs={{8,0},{73,1},{24,16},{89,17},{40,32},{105,33},{56,48},{121,49},{10... | collective-permute-start | bytes 3145736 | tf_op jit(solution)/shard_map/ppermute | solution.py:49
  54.3 25.4 %collective-permute-start.8 = (bf16[512,1024]{1,0:T(8,128)(2,1)S(1)}, bf16[512,1024]{1,0:T(8,128)(2,1)S(1)}, u32[]{:S(2)}, u32[]{:S(2)}) collective-permute-start(bf16[512,1024]{1,0:T(8,128)(2,1)S(1)} %get-tuple-element.48.refs_0_.refs_9_), channel_id=1, source_target_pairs={{16,0},{3,1},{32,16},{19,17},{48,32},{35,33},{0,48},{51,49},{18,2}... | collective-permute-start | bytes 3145736 | tf_op jit(solution)/shard_map/ppermute | solution.py:33
  115.4 7.9 %collective-permute-start.13 = (f32[512,1152]{1,0:T(8,128)S(1)}, f32[512,1152]{1,0:T(8,128)S(1)}, u32[]{:S(2)}, u32[]{:S(2)}) collective-permute-start(f32[512,1152]{1,0:T(8,128)S(1)} %sums.3), channel_id=1, source_target_pairs={{0,1},{1,0},{2,3},{3,2},{4,5},{5,4},{6,7},{7,6},{8,9},{9,8},{10,11... | collective-permute-start | bytes 7077896 | tf_op jit(solution)/shard_map/ppermute | solution.py:38
  117.3 4.6 %copy-start.3 = (s32[2]{0:T(128)S(1)}, s32[2]{0:T(128)}, u32[]{:S(2)}) copy-start(s32[2]{0:T(128)} %pad_add_fusion.at_ref) | copy-start | bytes 28
  117.3 4.6 %collective-permute-start.14 = (f32[64,128]{1,0:T(8,128)S(1)}, f32[64,128]{1,0:T(8,128)S(1)}, u32[]{:S(2)}, u32[]{:S(2)}) collective-permute-start(f32[64,128]{1,0:T(8,128)S(1)} %pack.1.mine_ref), channel_id=1, source_target_pairs={{0,1},{1,0},{2,3},{3,2},{4,5},{5,4},{6,7},{7,6},{8,9},{9,8},{10,11... | collective-permute-start | bytes 98312 | tf_op jit(solution)/shard_map/ppermute | solution.py:38

commit v7 on v6

--- a/solution.py
+++ b/solution.py
@@ -145,11 +145,14 @@
         own_ref[:, lanes] = roll_within(value[:, lanes], 0, 4 - spot_ref[3])
 
 
-def pack_kernel(whole_ref, all_ref, out_ref):
+def pack_kernel(at_ref, whole_ref, all_ref, out_ref):
+    first_core = at_ref[1] % 2 == 0
     for line in range(32):
         tile = line % 4
         out_ref[line : line + 1, :] = whole_ref[line // 4 : line // 4 + 1, tile * 128 : (tile + 1) * 128]
-        pair = jnp.maximum(all_ref[2 * line, 0:1, 512:640], all_ref[2 * line + 1, 0:1, 512:640])
+        low, high = line // 2 % 4, line // 8
+        chip = line % 2 * 32 + jnp.where(first_core, low * 4 + high, high * 4 + low)
+        pair = jnp.maximum(all_ref[chip, 0:1, 512:640], all_ref[chip + 16, 0:1, 512:640])
         out_ref[32 + line : 33 + line, :] = pair
 
 
@@ -277,10 +280,11 @@
     smem = pl.BlockSpec(memory_space=pltpu.SMEM)
     vmem = pl.BlockSpec(memory_space=pltpu.VMEM)
     small = pltpu.CompilerParams(vmem_limit_bytes=8 << 20)
+    ids = jnp.tile(destination.astype(jnp.float32), 2).reshape(1, 128)
+    at_word = jnp.stack([samp, cent]).astype(jnp.int32)
     line = join(embeddings, *[fetch(embeddings, 0, step) for step in (1, 2, 3)])
+    spot, ids, at_word, line = lax.optimization_barrier((spot, ids, at_word, line))
     near, across, back = [fetch(line, 1, step) for step in (1, 2, 3)]
-    destination, _ = lax.optimization_barrier((destination, line))
-    ids = jnp.tile(destination.astype(jnp.float32), 2).reshape(1, 128)
     first, second = pl.pallas_call(
         halves_kernel,
         out_shape=[jax.ShapeDtypeStruct((512, width), embeddings.dtype)] * 2,
@@ -289,30 +293,25 @@
         compiler_params=small,
         name="halves",
     )(spot, line, near, across, back)
-    at_word = jnp.stack([samp, cent]).astype(jnp.int32)
-    first, second, ids, spot, at_word = lax.optimization_barrier((first, second, ids, spot, at_word))
     far_first = fetch(first, 2, 2)
+    after_first, before_first = fetch(first, 2, 1), fetch(first, 2, 3)
+    after_second, before_second = fetch(second, 2, 1), fetch(second, 2, 3)
+    at_word, first, second = lax.optimization_barrier((at_word, first, second))
     mine = pl.pallas_call(
         share_kernel,
         out_shape=jax.ShapeDtypeStruct((share, width), centroids.dtype),
         in_specs=[smem, pl.BlockSpec(memory_space=pltpu.HBM)],
         out_specs=vmem,
         scratch_shapes=[pltpu.SemaphoreType.DMA((8,))],
-        compiler_params=pltpu.CompilerParams(vmem_limit_bytes=54 << 20),
+        compiler_params=small,
         name="share",
     )(at_word, centroids)
     other = swap_cores(mine)
-    first_again, mine = lax.optimization_barrier((first, mine))
-    after_first, before_first = fetch(first_again, 2, 1), fetch(first_again, 2, 3)
     score = functools.partial(scores_call, mine, other)
-    own_first = score([first])
-    second_again, _ = lax.optimization_barrier((second, own_first[1]))
-    own_second = score([second])
-    after_second, before_second = fetch(second_again, 2, 1), fetch(second_again, 2, 3)
     far_second = swap_sides(far_first)
     chunks = [first, second, after_first, after_second, far_first, far_second, before_first, before_second]
     swapped = (5,)
-    pairs = [own_first, own_second] + [score([chunk]) for chunk in chunks[2:]]
+    pairs = [score([chunk]) for chunk in chunks]
     ps = [p[0] for p, _ in pairs]
     stats = [stat for _, stat in pairs]
 
@@ -326,15 +325,7 @@
         compiler_params=small,
         name="first",
     )(spot, ids, *stats)
-    chips = []
-    for side in range(2):
-        group = []
-        for i in range(64):
-            at = [0, 0, 0]
-            for dim in range(3):
-                at[ORDERS[side][dim]] = i // 4**dim % 4
-            group.append(place(*at, side))
-        chips.append(group)
+    chips = [[place(i // 16, i // 4 % 4, i % 4, side) for i in range(64)] for side in range(2)]
     shared = lax.all_to_all(local, BOTH, split_axis=0, concat_axis=0, tiled=True, axis_index_groups=chips)
     whole, lse = pl.pallas_call(
         functools.partial(merge_kernel, swapped),
@@ -352,10 +343,10 @@
     pack = pl.pallas_call(
         pack_kernel,
         out_shape=jax.ShapeDtypeStruct((64, 128), jnp.float32),
-        in_specs=[vmem] * 2,
+        in_specs=[smem] + [vmem] * 2,
         compiler_params=small,
         name="pack",
-    )(whole, shared)
+    )(at_word, whole, shared)
     partner = swap_cores(pack)
     ours = sums_call(0, lse, tops, ps, chunks)
     row_lse = pl.pallas_call(

time: 125 us -> 126 us (level)
  starting transfers between devices: 17.9 us -> 23.6 us
  blocking collectives: 27 us -> 23.5 us
  waiting for transfers between devices: 44.4 us -> 41.4 us
  local copies, waits for them, and re-layouts: 2.31 us -> 4.46 us
    ppermute x3, starting transfers between devices: 3.06 us -> 6.89 us  [swap_cores(): return lax.ppermute(value, BOTH, pairs)]
    all_to_all x1, blocking collectives: 27 us -> 23.5 us  [shards(): lax.all_to_all(local, BOTH, split_axis=0, concat_axis=0, tiled=True, axis...]
    ppermute x11, waiting for transfers between devices: 44.3 us -> 41.4 us  [fetch(): return lax.ppermute(value, BOTH, pairs)]
    unnamed x8 -> x4, local copies, waits for them, and re-layouts: 2.14 us -> 4.29 us
    ppermute x11, starting transfers between devices: 14.6 us -> 16.7 us  [fetch(): return lax.ppermute(value, BOTH, pairs)]
  transfers between devices with their start and end apart: 15 -> 15, of which waited for: 8 -> 8; matrix products, arithmetic and copies ran while one was open for 1% -> 1% of each run, Pallas kernels for 14% -> 16%
where the time goes in v7:
time: 126 us; the launch traced here: 125 us
  waiting for transfers between devices  41.4 us (33%)
  Pallas kernels  30.9 us (25%)
  starting transfers between devices  23.6 us (19%)
  blocking collectives  23.5 us (19%)
  local copies, waits for them, and re-layouts  4.46 us (4%)
    ppermute x11, waiting for transfers between devices, fetch(): return lax.ppermute(value, BOTH, pairs)  41.4 us
    all_to_all x1, blocking collectives, shards(): lax.all_to_all(local, BOTH, split_axis=0, concat_axis=0, tiled=True, axis...  23.5 us
    ppermute x11, starting transfers between devices, fetch(): return lax.ppermute(value, BOTH, pairs)  16.7 us
    pallas_call x8, Pallas kernels, scores_call(): pl.pallas_call(functools.partial(scores_kernel, factor, count), out_shape...  13 us
    pallas_call x2, Pallas kernels, sums_call(): pl.pallas_call(functools.partial(sums_kernel, half, count), out_shape=jax...  8.99 us
    ppermute x3, starting transfers between devices, swap_cores(): return lax.ppermute(value, BOTH, pairs)  6.89 us
    unnamed x4, local copies, waits for them, and re-layouts  4.29 us
  transfers between devices with their start and end apart: 15, of which 8 were waited for; matrix products, arithmetic and copies ran while one was open for 1% of the time, Pallas kernels for 16%

profile of v7, /device:TPU:1, one launch (start us, length us, event | category | flops | bytes accessed | tf_op | source)
XLA Modules:
  0.0 125.4 jit_solution(4582942982546686800)
XLA Ops:
  0.6 3.4 %collective-permute-start = (bf16[64,1024]{1,0:T(8,128)(2,1)}, bf16[64,1024]{1,0:T(8,128)(2,1)S(1)}, u32[]{:S(2)}, u32[]{:S(2)}) collective-permute-start(bf16[64,1024]{1,0:T(8,128)(2,1)} %refs_0_.1), channel_id=1, source_target_pairs={{8,0},{9,1},{24,16},{25,17},{40,32},{41,33},{56,48},{57,49},{10,2}... | collective-permute-start | bytes 393224 | tf_op jit(solution)/shard_map/ppermute | solution.py:33
  6.0 3.3 %collective-permute-done.refs_1_ = bf16[64,1024]{1,0:T(8,128)(2,1)S(1)} collective-permute-done((bf16[64,1024]{1,0:T(8,128)(2,1)}, bf16[64,1024]{1,0:T(8,128)(2,1)S(1)}, u32[]{:S(2)}, u32[]{:S(2)}) %collective-permute-start) | collective-permute-done | bytes 131104 | tf_op jit(solution)/shard_map/ppermute | solution.py:33
  9.6 4.1 %collective-permute-done.2.refs_3_ = bf16[64,1024]{1,0:T(8,128)(2,1)S(1)} collective-permute-done((bf16[64,1024]{1,0:T(8,128)(2,1)}, bf16[64,1024]{1,0:T(8,128)(2,1)S(1)}, u32[]{:S(2)}, u32[]{:S(2)}) %collective-permute-start.2) | collective-permute-done | bytes 131104 | tf_op jit(solution)/shard_map/ppermute | solution.py:33
  13.8 0.9 copy-done.1
  14.7 3.8 %collective-permute-start.3 = (bf16[256,1024]{1,0:T(8,128)(2,1)S(1)}, bf16[256,1024]{1,0:T(8,128)(2,1)S(1)}, u32[]{:S(2)}, u32[]{:S(2)}) collective-permute-start(bf16[256,1024]{1,0:T(8,128)(2,1)S(1)} %join.1.refs_0_), channel_id=1, source_target_pairs={{2,0},{17,1},{18,16},{33,17},{34,32},{49,33},{50,48},{1,49},{4,2},... | collective-permute-start | bytes 1572872 | tf_op jit(solution)/shard_map/ppermute | solution.py:33
  19.2 11.0 %collective-permute-done.3.refs_1_ = bf16[256,1024]{1,0:T(8,128)(2,1)S(1)} collective-permute-done((bf16[256,1024]{1,0:T(8,128)(2,1)S(1)}, bf16[256,1024]{1,0:T(8,128)(2,1)S(1)}, u32[]{:S(2)}, u32[]{:S(2)}) %collective-permute-start.3) | collective-permute-done | bytes 524320 | tf_op jit(solution)/shard_map/ppermute | solution.py:33
  30.3 3.4 %collective-permute-done.5.refs_3_ = bf16[256,1024]{1,0:T(8,128)(2,1)S(1)} collective-permute-done((bf16[256,1024]{1,0:T(8,128)(2,1)S(1)}, bf16[256,1024]{1,0:T(8,128)(2,1)S(1)}, u32[]{:S(2)}, u32[]{:S(2)}) %collective-permute-start.5) | collective-permute-done | bytes 524320 | tf_op jit(solution)/shard_map/ppermute | solution.py:33
  34.4 2.7 %collective-permute-start.9 = (bf16[512,1024]{1,0:T(8,128)(2,1)S(1)}, bf16[512,1024]{1,0:T(8,128)(2,1)S(1)}, u32[]{:S(2)}, u32[]{:S(2)}) collective-permute-start(bf16[512,1024]{1,0:T(8,128)(2,1)S(1)} %get-tuple-element.40.refs_0_.refs_8_), channel_id=1, source_target_pairs={{32,0},{5,1},{48,16},{21,17},{0,32},{37,33},{16,48},{53,49},{34,2}... | collective-permute-start | bytes 3145736 | tf_op jit(solution)/shard_map/ppermute | solution.py:33
  37.1 3.4 %copy-done = bf16[4096,1024]{1,0:T(8,128)(2,1)S(1)} copy-done((bf16[4096,1024]{1,0:T(8,128)(2,1)S(1)}, bf16[4096,1024]{1,0:T(8,128)(2,1)}, u32[]{:S(2)}) %copy-start) | copy-done | bytes 8388632
  40.5 2.0 %share.1.mine_ref = bf16[512,1024]{1,0:T(8,128)(2,1)S(1)} custom-call(s32[2]{0:T(128)S(1)} %pad_add_fusion.at_ref, bf16[4096,1024]{1,0:T(8,128)(2,1)S(1)} %copy-done), custom_call_target="tpu_custom_call" | custom-call | tf_op jit(solution)/shard_map/share/pallas_call | solution.py:300
  42.5 2.4 %collective-permute-start.6 = (bf16[512,1024]{1,0:T(8,128)(2,1)S(1)}, bf16[512,1024]{1,0:T(8,128)(2,1)S(1)}, u32[]{:S(2)}, u32[]{:S(2)}) collective-permute-start(bf16[512,1024]{1,0:T(8,128)(2,1)S(1)} %share.1.mine_ref), channel_id=1, source_target_pairs={{0,1},{1,0},{2,3},{3,2},{4,5},{5,4},{6,7},{7,6},{8,9},{9,8},{10,11... | collective-permute-start | bytes 3145736 | tf_op jit(solution)/shard_map/ppermute | solution.py:38
  44.9 2.7 %collective-permute-start.8 = (bf16[512,1024]{1,0:T(8,128)(2,1)S(1)}, bf16[512,1024]{1,0:T(8,128)(2,1)S(1)}, u32[]{:S(2)}, u32[]{:S(2)}) collective-permute-start(bf16[512,1024]{1,0:T(8,128)(2,1)S(1)} %get-tuple-element.42.refs_0_.refs_9_), channel_id=1, source_target_pairs={{16,0},{3,1},{32,16},{19,17},{48,32},{35,33},{0,48},{51,49},{18,2}... | collective-permute-start | bytes 3145736 | tf_op jit(solution)/shard_map/ppermute | solution.py:33
  47.6 2.3 %collective-permute-done.9.refs_0_.refs_12_ = bf16[512,1024]{1,0:T(8,128)(2,1)S(1)} collective-permute-done((bf16[512,1024]{1,0:T(8,128)(2,1)S(1)}, bf16[512,1024]{1,0:T(8,128)(2,1)S(1)}, u32[]{:S(2)}, u32[]{:S(2)}) %collective-permute-start.9) | collective-permute-done | bytes 1048608 | tf_op jit(solution)/shard_map/ppermute | solution.py:33
  49.9 2.3 %collective-permute-start.7 = (bf16[512,1024]{1,0:T(8,128)(2,1)S(1)}, bf16[512,1024]{1,0:T(8,128)(2,1)S(1)}, u32[]{:S(2)}, u32[]{:S(2)}) collective-permute-start(bf16[512,1024]{1,0:T(8,128)(2,1)S(1)} %get-tuple-element.40.refs_0_.refs_8_), channel_id=1, source_target_pairs={{16,0},{3,1},{32,16},{19,17},{48,32},{35,33},{0,48},{51,49},{18,2}... | collective-permute-start | bytes 3145736 | tf_op jit(solution)/shard_map/ppermute | solution.py:33
  52.2 1.6 %scores.12 = (f32[2,512,512]{2,1,0:T(8,128)S(1)}, f32[4,512]{1,0:T(4,128)S(1)}) custom-call(bf16[512,1024]{1,0:T(8,128)(2,1)S(1)} %share.1.mine_ref, bf16[512,1024]{1,0:T(8,128)(2,1)S(1)} %collective-permute-done.6.other_ref, bf16[512,1024]{1,0:T(8,128)(2,1)S(1)} %collective-permute-done.9.refs_0_.refs_12_), custom_call_target="tpu_custom_call" | custom-call | flops 2147483648 | bytes 5242880 | tf_op jit(solution)/shard_map/scores/pallas_call | solution.py:85
  53.8 7.3 %collective-permute-done.11.refs_0_.refs_14_ = bf16[512,1024]{1,0:T(8,128)(2,1)S(1)} collective-permute-done((bf16[512,1024]{1,0:T(8,128)(2,1)S(1)}, bf16[512,1024]{1,0:T(8,128)(2,1)S(1)}, u32[]{:S(2)}, u32[]{:S(2)}) %collective-permute-start.11) | collective-permute-done | bytes 1048608 | tf_op jit(solution)/shard_map/ppermute | solution.py:33
  61.1 1.6 %scores.14 = (f32[2,512,512]{2,1,0:T(8,128)S(1)}, f32[4,512]{1,0:T(4,128)S(1)}) custom-call(bf16[512,1024]{1,0:T(8,128)(2,1)S(1)} %share.1.mine_ref, bf16[512,1024]{1,0:T(8,128)(2,1)S(1)} %collective-permute-done.6.other_ref, bf16[512,1024]{1,0:T(8,128)(2,1)S(1)} %collective-permute-done.11.refs_0_.refs_14_), custom_call_target="tpu_custom_call" | custom-call | flops 2147483648 | bytes 5242880 | tf_op jit(solution)/shard_map/scores/pallas_call | solution.py:85
  62.8 9.6 %collective-permute-done.12.refs_0_.refs_15_ = bf16[512,1024]{1,0:T(8,128)(2,1)S(1)} collective-permute-done((bf16[512,1024]{1,0:T(8,128)(2,1)S(1)}, bf16[512,1024]{1,0:T(8,128)(2,1)S(1)}, u32[]{:S(2)}, u32[]{:S(2)}) %collective-permute-start.12) | collective-permute-done | bytes 1048608 | tf_op jit(solution)/shard_map/ppermute | solution.py:33
  72.4 1.6 %scores.15 = (f32[2,512,512]{2,1,0:T(8,128)S(1)}, f32[4,512]{1,0:T(4,128)S(1)}) custom-call(bf16[512,1024]{1,0:T(8,128)(2,1)S(1)} %share.1.mine_ref, bf16[512,1024]{1,0:T(8,128)(2,1)S(1)} %collective-permute-done.6.other_ref, bf16[512,1024]{1,0:T(8,128)(2,1)S(1)} %collective-permute-done.12.refs_0_.refs_15_), custom_call_target="tpu_custom_call" | custom-call | flops 2147483648 | bytes 5242880 | tf_op jit(solution)/shard_map/scores/pallas_call | solution.py:85
  74.0 1.6 %scores.11 = (f32[2,512,512]{2,1,0:T(8,128)S(1)}, f32[4,512]{1,0:T(4,128)S(1)}) custom-call(bf16[512,1024]{1,0:T(8,128)(2,1)S(1)} %share.1.mine_ref, bf16[512,1024]{1,0:T(8,128)(2,1)S(1)} %collective-permute-done.6.other_ref, bf16[512,1024]{1,0:T(8,128)(2,1)S(1)} %collective-permute-done.8.refs_0_.refs_11_), custom_call_target="tpu_custom_call" | custom-call | flops 2147483648 | bytes 5242880 | tf_op jit(solution)/shard_map/scores/pallas_call | solution.py:85
  75.7 1.6 %scores.10 = (f32[2,512,512]{2,1,0:T(8,128)S(1)}, f32[4,512]{1,0:T(4,128)S(1)}) custom-call(bf16[512,1024]{1,0:T(8,128)(2,1)S(1)} %share.1.mine_ref, bf16[512,1024]{1,0:T(8,128)(2,1)S(1)} %collective-permute-done.6.other_ref, bf16[512,1024]{1,0:T(8,128)(2,1)S(1)} %collective-permute-done.7.refs_0_.refs_10_), custom_call_target="tpu_custom_call" | custom-call | flops 2147483648 | bytes 5242880 | tf_op jit(solution)/shard_map/scores/pallas_call | solution.py:85
  77.3 1.6 %scores.9 = (f32[2,512,512]{2,1,0:T(8,128)S(1)}, f32[4,512]{1,0:T(4,128)S(1)}) custom-call(bf16[512,1024]{1,0:T(8,128)(2,1)S(1)} %share.1.mine_ref, bf16[512,1024]{1,0:T(8,128)(2,1)S(1)} %collective-permute-done.6.other_ref, bf16[512,1024]{1,0:T(8,128)(2,1)S(1)} %get-tuple-element.42.refs_0_.refs_9_), custom_call_target="tpu_custom_call" | custom-call | flops 2147483648 | bytes 5242880 | tf_op jit(solution)/shard_map/scores/pallas_call | solution.py:85
  78.9 1.6 %scores.8 = (f32[2,512,512]{2,1,0:T(8,128)S(1)}, f32[4,512]{1,0:T(4,128)S(1)}) custom-call(bf16[512,1024]{1,0:T(8,128)(2,1)S(1)} %share.1.mine_ref, bf16[512,1024]{1,0:T(8,128)(2,1)S(1)} %collective-permute-done.6.other_ref, bf16[512,1024]{1,0:T(8,128)(2,1)S(1)} %get-tuple-element.40.refs_0_.refs_8_), custom_call_target="tpu_custom_call" | custom-call | flops 2147483648 | bytes 5242880 | tf_op jit(solution)/shard_map/scores/pallas_call | solution.py:85
  80.6 1.6 %scores.13 = (f32[2,512,512]{2,1,0:T(8,128)S(1)}, f32[4,512]{1,0:T(4,128)S(1)}) custom-call(bf16[512,1024]{1,0:T(8,128)(2,1)S(1)} %share.1.mine_ref, bf16[512,1024]{1,0:T(8,128)(2,1)S(1)} %collective-permute-done.6.other_ref, bf16[512,1024]{1,0:T(8,128)(2,1)S(1)} %collective-permute-done.10.refs_0_.refs_13_), custom_call_target="tpu_custom_call" | custom-call | flops 2147483648 | bytes 5242880 | tf_op jit(solution)/shard_map/scores/pallas_call | solution.py:85
  82.2 1.3 %first.1 = (f32[64,8,640]{2,1,0:T(8,128)S(1)}, f32[2,4096]{1,0:T(2,128)S(1)}) custom-call(s32[5]{0:T(128)S(1)} %stack.32.spot_ref, f32[1,128]{1,0:T(1,128)S(1)} %reshape_tile.3.ids_ref, f32[4,512]{1,0:T(4,128)S(1)} %get-tuple-element.41.refs_0_, f32[4,512]{1,0:T(4,128)S(1)} %get-tuple-element.43.refs_1_, f32[4,512]{1,0:T(4,128)S(1)} %get-tuple-element.44.refs_2_, ...), custom_call_target="tpu_custom_call" | custom-call | tf_op jit(solution)/shard_map/first/pallas_call | solution.py:318
  83.5 23.5 %all_to_all.5.all_ref = f32[64,8,640]{2,1,0:T(8,128)S(1)} all-to-all(f32[64,8,640]{2,1,0:T(8,128)S(1)} %get-tuple-element.50), channel_id=1, replica_groups={{0,16,32,48,2,18,34,50,4,20,36,52,6,22,38,54,8,24,40,56,10,26,42,58,12,..., dimensions={0} | all-to-all | bytes 2621440 | tf_op jit(solution)/shard_map/all_to_all | solution.py:329
  107.0 1.2 merge.1
  108.2 4.5 %sums.3 = f32[512,1152]{1,0:T(8,128)S(1)} custom-call(f32[1,4096]{1,0:T(1,128)S(1)} %get-tuple-element.51.lse_ref, f32[2,4096]{1,0:T(2,128)S(1)} %get-tuple-element.52.top_ref, f32[2,512,512]{2,1,0:T(8,128)S(1)} %get-tuple-element.53.refs_0_, f32[2,512,512]{2,1,0:T(8,128)S(1)} %get-tuple-element.54.refs_1_, f32[2,512,512]{2,1,0:T(8,128)S(1)} %get-tuple-element.55.refs_2_, ...), custom_call_target="tpu_custom_call" | custom-call | flops 4294967296 | bytes 18874368 | tf_op jit(solution)/shard_map/sums/pallas_call | solution.py:234
  112.7 4.4 %collective-permute-start.13 = (f32[512,1152]{1,0:T(8,128)S(1)}, f32[512,1152]{1,0:T(8,128)S(1)}, u32[]{:S(2)}, u32[]{:S(2)}) collective-permute-start(f32[512,1152]{1,0:T(8,128)S(1)} %sums.3), channel_id=1, source_target_pairs={{0,1},{1,0},{2,3},{3,2},{4,5},{5,4},{6,7},{7,6},{8,9},{9,8},{10,11... | collective-permute-start | bytes 7077896 | tf_op jit(solution)/shard_map/ppermute | solution.py:38
  117.7 4.5 %sums.2.ours_ref = f32[512,1152]{1,0:T(8,128)S(1)} custom-call(f32[1,4096]{1,0:T(1,128)S(1)} %get-tuple-element.51.lse_ref, f32[2,4096]{1,0:T(2,128)S(1)} %get-tuple-element.52.top_ref, f32[2,512,512]{2,1,0:T(8,128)S(1)} %get-tuple-element.53.refs_0_, f32[2,512,512]{2,1,0:T(8,128)S(1)} %get-tuple-element.54.refs_1_, ...), custom_call_target="tpu_custom_call" | custom-call | flops 4294967296 | bytes 18874368 | tf_op jit(solution)/shard_map/sums/pallas_call | solution.py:234
  122.3 1.4 %route.1 = f32[1,64]{1,0:T(1,128)} custom-call(s32[2]{0:T(128)S(1)} %pad_add_fusion.at_ref, f32[64,128]{1,0:T(8,128)S(1)} %pack.1.mine_ref, f32[64,128]{1,0:T(8,128)S(1)} %collective-permute-done.14.other_ref), custom_call_target="tpu_custom_call" | custom-call | tf_op jit(solution)/shard_map/route/pallas_call | solution.py:352
  123.7 1.7 %final.1 = f32[512,1024]{1,0:T(8,128)} custom-call(f32[512,1152]{1,0:T(8,128)S(1)} %sums.2.ours_ref, f32[512,1152]{1,0:T(8,128)S(1)} %collective-permute-done.13.theirs_ref, bf16[512,1024]{1,0:T(8,128)(2,1)S(1)} %share.1.mine_ref), custom_call_target="tpu_custom_call" | custom-call | tf_op jit(solution)/shard_map/final/pallas_call | solution.py:359
  (26 shorter events, 4.5 us)
Async XLA Ops:
  0.6 8.7 %collective-permute-start = (bf16[64,1024]{1,0:T(8,128)(2,1)}, bf16[64,1024]{1,0:T(8,128)(2,1)S(1)}, u32[]{:S(2)}, u32[]{:S(2)}) collective-permute-start(bf16[64,1024]{1,0:T(8,128)(2,1)} %refs_0_.1), channel_id=1, source_target_pairs={{8,0},{9,1},{24,16},{25,17},{40,32},{41,33},{56,48},{57,49},{10,2}... | collective-permute-start | bytes 393224 | tf_op jit(solution)/shard_map/ppermute | solution.py:33
  4.0 5.6 %collective-permute-start.1 = (bf16[64,1024]{1,0:T(8,128)(2,1)}, bf16[64,1024]{1,0:T(8,128)(2,1)S(1)}, u32[]{:S(2)}, u32[]{:S(2)}) collective-permute-start(bf16[64,1024]{1,0:T(8,128)(2,1)} %refs_0_.1), channel_id=1, source_target_pairs={{64,0},{65,1},{80,16},{81,17},{96,32},{97,33},{112,48},{113,49},{6... | collective-permute-start | bytes 393224 | tf_op jit(solution)/shard_map/ppermute | solution.py:33
  4.5 9.2 %collective-permute-start.2 = (bf16[64,1024]{1,0:T(8,128)(2,1)}, bf16[64,1024]{1,0:T(8,128)(2,1)S(1)}, u32[]{:S(2)}, u32[]{:S(2)}) collective-permute-start(bf16[64,1024]{1,0:T(8,128)(2,1)} %refs_0_.1), channel_id=1, source_target_pairs={{72,0},{73,1},{88,16},{89,17},{104,32},{105,33},{120,48},{121,49},... | collective-permute-start | bytes 393224 | tf_op jit(solution)/shard_map/ppermute | solution.py:33
  13.8 0.9 copy-start.1
  14.7 15.6 %collective-permute-start.3 = (bf16[256,1024]{1,0:T(8,128)(2,1)S(1)}, bf16[256,1024]{1,0:T(8,128)(2,1)S(1)}, u32[]{:S(2)}, u32[]{:S(2)}) collective-permute-start(bf16[256,1024]{1,0:T(8,128)(2,1)S(1)} %join.1.refs_0_), channel_id=1, source_target_pairs={{2,0},{17,1},{18,16},{33,17},{34,32},{49,33},{50,48},{1,49},{4,2},... | collective-permute-start | bytes 1572872 | tf_op jit(solution)/shard_map/ppermute | solution.py:33
  18.5 11.7 %collective-permute-start.4 = (bf16[256,1024]{1,0:T(8,128)(2,1)S(1)}, bf16[256,1024]{1,0:T(8,128)(2,1)S(1)}, u32[]{:S(2)}, u32[]{:S(2)}) collective-permute-start(bf16[256,1024]{1,0:T(8,128)(2,1)S(1)} %join.1.refs_0_), channel_id=1, source_target_pairs={{4,0},{33,1},{20,16},{49,17},{36,32},{1,33},{52,48},{17,49},{6,2},... | collective-permute-start | bytes 1572872 | tf_op jit(solution)/shard_map/ppermute | solution.py:33
  18.5 15.2 %collective-permute-start.5 = (bf16[256,1024]{1,0:T(8,128)(2,1)S(1)}, bf16[256,1024]{1,0:T(8,128)(2,1)S(1)}, u32[]{:S(2)}, u32[]{:S(2)}) collective-permute-start(bf16[256,1024]{1,0:T(8,128)(2,1)S(1)} %join.1.refs_0_), channel_id=1, source_target_pairs={{6,0},{49,1},{22,16},{1,17},{38,32},{17,33},{54,48},{33,49},{0,2},... | collective-permute-start | bytes 1572872 | tf_op jit(solution)/shard_map/ppermute | solution.py:33
  34.4 15.5 %collective-permute-start.9 = (bf16[512,1024]{1,0:T(8,128)(2,1)S(1)}, bf16[512,1024]{1,0:T(8,128)(2,1)S(1)}, u32[]{:S(2)}, u32[]{:S(2)}) collective-permute-start(bf16[512,1024]{1,0:T(8,128)(2,1)S(1)} %get-tuple-element.40.refs_0_.refs_8_), channel_id=1, source_target_pairs={{32,0},{5,1},{48,16},{21,17},{0,32},{37,33},{16,48},{53,49},{34,2}... | collective-permute-start | bytes 3145736 | tf_op jit(solution)/shard_map/ppermute | solution.py:33
  37.1 3.4 %copy-start = (bf16[4096,1024]{1,0:T(8,128)(2,1)S(1)}, bf16[4096,1024]{1,0:T(8,128)(2,1)}, u32[]{:S(2)}) copy-start(bf16[4096,1024]{1,0:T(8,128)(2,1)} %cents_ref.1) | copy-start | bytes 25165828
  42.5 9.7 %collective-permute-start.6 = (bf16[512,1024]{1,0:T(8,128)(2,1)S(1)}, bf16[512,1024]{1,0:T(8,128)(2,1)S(1)}, u32[]{:S(2)}, u32[]{:S(2)}) collective-permute-start(bf16[512,1024]{1,0:T(8,128)(2,1)S(1)} %share.1.mine_ref), channel_id=1, source_target_pairs={{0,1},{1,0},{2,3},{3,2},{4,5},{5,4},{6,7},{7,6},{8,9},{9,8},{10,11... | collective-permute-start | bytes 3145736 | tf_op jit(solution)/shard_map/ppermute | solution.py:38
  44.9 16.3 %collective-permute-start.11 = (bf16[512,1024]{1,0:T(8,128)(2,1)S(1)}, bf16[512,1024]{1,0:T(8,128)(2,1)S(1)}, u32[]{:S(2)}, u32[]{:S(2)}) collective-permute-start(bf16[512,1024]{1,0:T(8,128)(2,1)S(1)} %get-tuple-element.40.refs_0_.refs_8_), channel_id=1, source_target_pairs={{48,0},{7,1},{0,16},{23,17},{16,32},{39,33},{32,48},{55,49},{50,2}... | collective-permute-start | bytes 3145736 | tf_op jit(solution)/shard_map/ppermute | solution.py:33
  44.9 27.5 %collective-permute-start.12 = (bf16[512,1024]{1,0:T(8,128)(2,1)S(1)}, bf16[512,1024]{1,0:T(8,128)(2,1)S(1)}, u32[]{:S(2)}, u32[]{:S(2)}) collective-permute-start(bf16[512,1024]{1,0:T(8,128)(2,1)S(1)} %get-tuple-element.42.refs_0_.refs_9_), channel_id=1, source_target_pairs={{48,0},{7,1},{0,16},{23,17},{16,32},{39,33},{32,48},{55,49},{50,2}... | collective-permute-start | bytes 3145736 | tf_op jit(solution)/shard_map/ppermute | solution.py:33
  44.9 29.1 %collective-permute-start.8 = (bf16[512,1024]{1,0:T(8,128)(2,1)S(1)}, bf16[512,1024]{1,0:T(8,128)(2,1)S(1)}, u32[]{:S(2)}, u32[]{:S(2)}) collective-permute-start(bf16[512,1024]{1,0:T(8,128)(2,1)S(1)} %get-tuple-element.42.refs_0_.refs_9_), channel_id=1, source_target_pairs={{16,0},{3,1},{32,16},{19,17},{48,32},{35,33},{0,48},{51,49},{18,2}... | collective-permute-start | bytes 3145736 | tf_op jit(solution)/shard_map/ppermute | solution.py:33
  49.9 25.7 %collective-permute-start.7 = (bf16[512,1024]{1,0:T(8,128)(2,1)S(1)}, bf16[512,1024]{1,0:T(8,128)(2,1)S(1)}, u32[]{:S(2)}, u32[]{:S(2)}) collective-permute-start(bf16[512,1024]{1,0:T(8,128)(2,1)S(1)} %get-tuple-element.40.refs_0_.refs_8_), channel_id=1, source_target_pairs={{16,0},{3,1},{32,16},{19,17},{48,32},{35,33},{0,48},{51,49},{18,2}... | collective-permute-start | bytes 3145736 | tf_op jit(solution)/shard_map/ppermute | solution.py:33
  52.2 28.4 %collective-permute-start.10 = (bf16[512,1024]{1,0:T(8,128)(2,1)S(1)}, bf16[512,1024]{1,0:T(8,128)(2,1)S(1)}, u32[]{:S(2)}, u32[]{:S(2)}) collective-permute-start(bf16[512,1024]{1,0:T(8,128)(2,1)S(1)} %collective-permute-done.9.refs_0_.refs_12_), channel_id=1, source_target_pairs={{8,0},{73,1},{24,16},{89,17},{40,32},{105,33},{56,48},{121,49},{10... | collective-permute-start | bytes 3145736 | tf_op jit(solution)/shard_map/ppermute | solution.py:49
  112.7 11.0 %collective-permute-start.13 = (f32[512,1152]{1,0:T(8,128)S(1)}, f32[512,1152]{1,0:T(8,128)S(1)}, u32[]{:S(2)}, u32[]{:S(2)}) collective-permute-start(f32[512,1152]{1,0:T(8,128)S(1)} %sums.3), channel_id=1, source_target_pairs={{0,1},{1,0},{2,3},{3,2},{4,5},{5,4},{6,7},{7,6},{8,9},{9,8},{10,11... | collective-permute-start | bytes 7077896 | tf_op jit(solution)/shard_map/ppermute | solution.py:38
  117.6 4.6 %collective-permute-start.14 = (f32[64,128]{1,0:T(8,128)S(1)}, f32[64,128]{1,0:T(8,128)S(1)}, u32[]{:S(2)}, u32[]{:S(2)}) collective-permute-start(f32[64,128]{1,0:T(8,128)S(1)} %pack.1.mine_ref), channel_id=1, source_target_pairs={{0,1},{1,0},{2,3},{3,2},{4,5},{5,4},{6,7},{7,6},{8,9},{9,8},{10,11... | collective-permute-start | bytes 98312 | tf_op jit(solution)/shard_map/ppermute | solution.py:38

commit v8 on v7

--- a/solution.py
+++ b/solution.py
@@ -109,13 +109,14 @@
     return jnp.where(lane >= step * inner, ahead, back)
 
 
-def first_kernel(swapped, spot_ref, ids_ref, *refs):
+def first_kernel(swapped, order, spot_ref, ids_ref, *refs):
     *stats, out_ref, top_ref = refs
     parts = []
-    for k, ref in enumerate(stats):
-        tops = ref[0:2, :]
+    for k, (ref, piece) in enumerate(order):
+        lanes = slice(piece * 512, (piece + 1) * 512)
+        tops = stats[ref][0:2, lanes]
         top = jnp.max(tops, axis=0, keepdims=True)
-        total = jnp.sum(ref[2:4, :] * jnp.exp2(tops - top), axis=0, keepdims=True)
+        total = jnp.sum(stats[ref][2:4, lanes] * jnp.exp2(tops - top), axis=0, keepdims=True)
         part = top + jnp.log2(total)
         parts.append(roll_within(part, 0, spot_ref[3]) if k in swapped else part)
         top_ref[:, k * 512 : (k + 1) * 512] = tops
@@ -151,8 +152,9 @@
         tile = line % 4
         out_ref[line : line + 1, :] = whole_ref[line // 4 : line // 4 + 1, tile * 128 : (tile + 1) * 128]
         low, high = line // 2 % 4, line // 8
-        chip = line % 2 * 32 + jnp.where(first_core, low * 4 + high, high * 4 + low)
-        pair = jnp.maximum(all_ref[chip, 0:1, 512:640], all_ref[chip + 16, 0:1, 512:640])
+        even = jnp.where(first_core, 2 * line, high * 16 + line % 2 * 8 + low)
+        odd = jnp.where(first_core, 2 * line + 1, high * 16 + line % 2 * 8 + 4 + low)
+        pair = jnp.maximum(all_ref[even, 0:1, 512:640], all_ref[odd, 0:1, 512:640])
         out_ref[32 + line : 33 + line, :] = pair
 
 
@@ -311,21 +313,27 @@
     far_second = swap_sides(far_first)
     chunks = [first, second, after_first, after_second, far_first, far_second, before_first, before_second]
     swapped = (5,)
-    pairs = [score([chunk]) for chunk in chunks]
-    ps = [p[0] for p, _ in pairs]
-    stats = [stat for _, stat in pairs]
+    early_ps, early_stat = score([far_first, first, second])
+    chunks[3], _ = lax.optimization_barrier((chunks[3], early_stat))
+    calls = {k: score([chunks[k]]) for k in (2, 3, 5, 6, 7)}
+    ps = early_ps[1:] + [calls[2][0][0], calls[3][0][0], early_ps[0]] + [calls[k][0][0] for k in (5, 6, 7)]
+    stats = [early_stat] + [calls[k][1] for k in (2, 3, 5, 6, 7)]
+    order = ((0, 1), (0, 2), (1, 0), (2, 0), (0, 0), (3, 0), (4, 0), (5, 0))
 
     local, tops = pl.pallas_call(
-        functools.partial(first_kernel, swapped),
+        functools.partial(first_kernel, swapped, order),
         out_shape=(
             jax.ShapeDtypeStruct((64, 8, 640), jnp.float32),
             jax.ShapeDtypeStruct((2, 4096), jnp.float32),
         ),
-        in_specs=[smem] + [vmem] * 9,
+        in_specs=[smem] + [vmem] * 7,
         compiler_params=small,
         name="first",
     )(spot, ids, *stats)
-    chips = [[place(i // 16, i // 4 % 4, i % 4, side) for i in range(64)] for side in range(2)]
+    chips = [
+        [place(i % 4, i // 4 % 4, i // 16, 0) for i in range(64)],
+        [place(i // 4 % 4, i // 16, i % 4, 1) for i in range(64)],
+    ]
     shared = lax.all_to_all(local, BOTH, split_axis=0, concat_axis=0, tiled=True, axis_index_groups=chips)
     whole, lse = pl.pallas_call(
         functools.partial(merge_kernel, swapped),

time: 126 us -> 121 us (0.960)
  waiting for transfers between devices: 41.4 us -> 38.4 us
    ppermute x11, waiting for transfers between devices: 41.4 us -> 38.3 us  [fetch(): return lax.ppermute(value, BOTH, pairs)]
    pallas_call x8 -> x6, Pallas kernels: 13 us -> 12.5 us  [scores_call(): pl.pallas_call(functools.partial(scores_kernel, factor, count), out_shape...]
where the time goes in v8:
time: 121 us
  waiting for transfers between devices  38.4 us (32%)
  Pallas kernels  30.5 us (25%)
  blocking collectives  23.6 us (20%)
  starting transfers between devices  22.4 us (19%)
  local copies, waits for them, and re-layouts  4.46 us (4%)
    ppermute x11, waiting for transfers between devices, fetch(): return lax.ppermute(value, BOTH, pairs)  38.3 us
    all_to_all x1, blocking collectives, shards(): lax.all_to_all(local, BOTH, split_axis=0, concat_axis=0, tiled=True, axis...  23.6 us
    ppermute x11, starting transfers between devices, fetch(): return lax.ppermute(value, BOTH, pairs)  15.5 us
    pallas_call x6, Pallas kernels, scores_call(): pl.pallas_call(functools.partial(scores_kernel, factor, count), out_shape...  12.5 us
    pallas_call x2, Pallas kernels, sums_call(): pl.pallas_call(functools.partial(sums_kernel, half, count), out_shape=jax...  9.05 us
    ppermute x3, starting transfers between devices, swap_cores(): return lax.ppermute(value, BOTH, pairs)  6.91 us
    unnamed x4, local copies, waits for them, and re-layouts  4.29 us
  transfers between devices with their start and end apart: 15, of which 8 were waited for; matrix products, arithmetic and copies ran while one was open for 1% of the time, Pallas kernels for 16%

profile of v8, /device:TPU:1, one launch (start us, length us, event | category | flops | bytes accessed | tf_op | source)
XLA Modules:
  0.0 120.8 jit_solution(9011388865644719994)
XLA Ops:
  0.6 3.4 %collective-permute-start = (bf16[64,1024]{1,0:T(8,128)(2,1)}, bf16[64,1024]{1,0:T(8,128)(2,1)S(1)}, u32[]{:S(2)}, u32[]{:S(2)}) collective-permute-start(bf16[64,1024]{1,0:T(8,128)(2,1)} %refs_0_.1), channel_id=1, source_target_pairs={{8,0},{9,1},{24,16},{25,17},{40,32},{41,33},{56,48},{57,49},{10,2}... | collective-permute-start | bytes 393224 | tf_op jit(solution)/shard_map/ppermute | solution.py:33
  6.0 3.3 %collective-permute-done.refs_1_ = bf16[64,1024]{1,0:T(8,128)(2,1)S(1)} collective-permute-done((bf16[64,1024]{1,0:T(8,128)(2,1)}, bf16[64,1024]{1,0:T(8,128)(2,1)S(1)}, u32[]{:S(2)}, u32[]{:S(2)}) %collective-permute-start) | collective-permute-done | bytes 131104 | tf_op jit(solution)/shard_map/ppermute | solution.py:33
  9.6 4.1 %collective-permute-done.2.refs_3_ = bf16[64,1024]{1,0:T(8,128)(2,1)S(1)} collective-permute-done((bf16[64,1024]{1,0:T(8,128)(2,1)}, bf16[64,1024]{1,0:T(8,128)(2,1)S(1)}, u32[]{:S(2)}, u32[]{:S(2)}) %collective-permute-start.2) | collective-permute-done | bytes 131104 | tf_op jit(solution)/shard_map/ppermute | solution.py:33
  13.8 0.9 copy-done.1
  14.7 3.8 %collective-permute-start.3 = (bf16[256,1024]{1,0:T(8,128)(2,1)S(1)}, bf16[256,1024]{1,0:T(8,128)(2,1)S(1)}, u32[]{:S(2)}, u32[]{:S(2)}) collective-permute-start(bf16[256,1024]{1,0:T(8,128)(2,1)S(1)} %join.1.refs_0_), channel_id=1, source_target_pairs={{2,0},{17,1},{18,16},{33,17},{34,32},{49,33},{50,48},{1,49},{4,2},... | collective-permute-start | bytes 1572872 | tf_op jit(solution)/shard_map/ppermute | solution.py:33
  18.5 0.7 collective-permute-start.5
  19.2 11.0 %collective-permute-done.3.refs_1_ = bf16[256,1024]{1,0:T(8,128)(2,1)S(1)} collective-permute-done((bf16[256,1024]{1,0:T(8,128)(2,1)S(1)}, bf16[256,1024]{1,0:T(8,128)(2,1)S(1)}, u32[]{:S(2)}, u32[]{:S(2)}) %collective-permute-start.3) | collective-permute-done | bytes 524320 | tf_op jit(solution)/shard_map/ppermute | solution.py:33
  30.3 3.4 %collective-permute-done.5.refs_3_ = bf16[256,1024]{1,0:T(8,128)(2,1)S(1)} collective-permute-done((bf16[256,1024]{1,0:T(8,128)(2,1)S(1)}, bf16[256,1024]{1,0:T(8,128)(2,1)S(1)}, u32[]{:S(2)}, u32[]{:S(2)}) %collective-permute-start.5) | collective-permute-done | bytes 524320 | tf_op jit(solution)/shard_map/ppermute | solution.py:33
  33.7 0.7 halves.1
  34.4 2.7 %collective-permute-start.7 = (bf16[512,1024]{1,0:T(8,128)(2,1)S(1)}, bf16[512,1024]{1,0:T(8,128)(2,1)S(1)}, u32[]{:S(2)}, u32[]{:S(2)}) collective-permute-start(bf16[512,1024]{1,0:T(8,128)(2,1)S(1)} %get-tuple-element.39.refs_1_.refs_8_), channel_id=1, source_target_pairs={{32,0},{5,1},{48,16},{21,17},{0,32},{37,33},{16,48},{53,49},{34,2}... | collective-permute-start | bytes 3145736 | tf_op jit(solution)/shard_map/ppermute | solution.py:33
  37.1 3.4 %copy-done = bf16[4096,1024]{1,0:T(8,128)(2,1)S(1)} copy-done((bf16[4096,1024]{1,0:T(8,128)(2,1)S(1)}, bf16[4096,1024]{1,0:T(8,128)(2,1)}, u32[]{:S(2)}) %copy-start) | copy-done | bytes 8388632
  40.5 2.0 %share.1.mine_ref = bf16[512,1024]{1,0:T(8,128)(2,1)S(1)} custom-call(s32[2]{0:T(128)S(1)} %pad_add_fusion.at_ref, bf16[4096,1024]{1,0:T(8,128)(2,1)S(1)} %copy-done), custom_call_target="tpu_custom_call" | custom-call | tf_op jit(solution)/shard_map/share/pallas_call | solution.py:302
  42.5 2.4 %collective-permute-start.6 = (bf16[512,1024]{1,0:T(8,128)(2,1)S(1)}, bf16[512,1024]{1,0:T(8,128)(2,1)S(1)}, u32[]{:S(2)}, u32[]{:S(2)}) collective-permute-start(bf16[512,1024]{1,0:T(8,128)(2,1)S(1)} %share.1.mine_ref), channel_id=1, source_target_pairs={{0,1},{1,0},{2,3},{3,2},{4,5},{5,4},{6,7},{7,6},{8,9},{9,8},{10,11... | collective-permute-start | bytes 3145736 | tf_op jit(solution)/shard_map/ppermute | solution.py:38
  45.2 1.1 collective-permute-start.11
  46.4 3.5 %collective-permute-done.7.refs_0_.refs_12_ = bf16[512,1024]{1,0:T(8,128)(2,1)S(1)} collective-permute-done((bf16[512,1024]{1,0:T(8,128)(2,1)S(1)}, bf16[512,1024]{1,0:T(8,128)(2,1)S(1)}, u32[]{:S(2)}, u32[]{:S(2)}) %collective-permute-start.7) | collective-permute-done | bytes 1048608 | tf_op jit(solution)/shard_map/ppermute | solution.py:33
  49.9 2.3 %collective-permute-start.8 = (bf16[512,1024]{1,0:T(8,128)(2,1)S(1)}, bf16[512,1024]{1,0:T(8,128)(2,1)S(1)}, u32[]{:S(2)}, u32[]{:S(2)}) collective-permute-start(bf16[512,1024]{1,0:T(8,128)(2,1)S(1)} %get-tuple-element.39.refs_1_.refs_8_), channel_id=1, source_target_pairs={{16,0},{3,1},{32,16},{19,17},{48,32},{35,33},{0,48},{51,49},{18,2}... | collective-permute-start | bytes 3145736 | tf_op jit(solution)/shard_map/ppermute | solution.py:33
  52.2 4.3 %scores.6 = (f32[2,512,512]{2,1,0:T(8,128)S(1)}, f32[2,512,512]{2,1,0:T(8,128)S(1)}, f32[2,512,512]{2,1,0:T(8,128)S(1)}, f32[4,1536]{1,0:T(4,128)S(1)}) custom-call(bf16[512,1024]{1,0:T(8,128)(2,1)S(1)} %share.1.mine_ref, bf16[512,1024]{1,0:T(8,128)(2,1)S(1)} %collective-permute-done.6.other_ref, ...), custom_call_target="tpu_custom_call" | custom-call | flops 6442450944 | bytes 11534336 | tf_op jit(solution)/shard_map/scores/pallas_call | solution.py:85
  56.5 4.8 %collective-permute-done.9.refs_0_.refs_11_ = bf16[512,1024]{1,0:T(8,128)(2,1)S(1)} collective-permute-done((bf16[512,1024]{1,0:T(8,128)(2,1)S(1)}, bf16[512,1024]{1,0:T(8,128)(2,1)S(1)}, u32[]{:S(2)}, u32[]{:S(2)}) %collective-permute-start.9) | collective-permute-done | bytes 1048608 | tf_op jit(solution)/shard_map/ppermute | solution.py:33
  61.2 1.6 %scores.8 = (f32[2,512,512]{2,1,0:T(8,128)S(1)}, f32[4,512]{1,0:T(4,128)S(1)}) custom-call(bf16[512,1024]{1,0:T(8,128)(2,1)S(1)} %share.1.mine_ref, bf16[512,1024]{1,0:T(8,128)(2,1)S(1)} %collective-permute-done.6.other_ref, bf16[512,1024]{1,0:T(8,128)(2,1)S(1)} %collective-permute-done.9.refs_0_.refs_11_), custom_call_target="tpu_custom_call" | custom-call | flops 2147483648 | bytes 5242880 | tf_op jit(solution)/shard_map/scores/pallas_call | solution.py:85
  62.9 1.6 %scores.10 = (f32[2,512,512]{2,1,0:T(8,128)S(1)}, f32[4,512]{1,0:T(4,128)S(1)}) custom-call(bf16[512,1024]{1,0:T(8,128)(2,1)S(1)} %share.1.mine_ref, bf16[512,1024]{1,0:T(8,128)(2,1)S(1)} %collective-permute-done.6.other_ref, bf16[512,1024]{1,0:T(8,128)(2,1)S(1)} %collective-permute-done.11.refs_0_.refs_14_), custom_call_target="tpu_custom_call" | custom-call | flops 2147483648 | bytes 5242880 | tf_op jit(solution)/shard_map/scores/pallas_call | solution.py:85
  64.5 7.9 %collective-permute-done.12.refs_0_.refs_15_ = bf16[512,1024]{1,0:T(8,128)(2,1)S(1)} collective-permute-done((bf16[512,1024]{1,0:T(8,128)(2,1)S(1)}, bf16[512,1024]{1,0:T(8,128)(2,1)S(1)}, u32[]{:S(2)}, u32[]{:S(2)}) %collective-permute-start.12) | collective-permute-done | bytes 1048608 | tf_op jit(solution)/shard_map/ppermute | solution.py:33
  72.4 1.6 %scores.11 = (f32[2,512,512]{2,1,0:T(8,128)S(1)}, f32[4,512]{1,0:T(4,128)S(1)}) custom-call(bf16[512,1024]{1,0:T(8,128)(2,1)S(1)} %share.1.mine_ref, bf16[512,1024]{1,0:T(8,128)(2,1)S(1)} %collective-permute-done.6.other_ref, bf16[512,1024]{1,0:T(8,128)(2,1)S(1)} %collective-permute-done.12.refs_0_.refs_15_), custom_call_target="tpu_custom_call" | custom-call | flops 2147483648 | bytes 5242880 | tf_op jit(solution)/shard_map/scores/pallas_call | solution.py:85
  74.0 1.6 %scores.7 = (f32[2,512,512]{2,1,0:T(8,128)S(1)}, f32[4,512]{1,0:T(4,128)S(1)}) custom-call(bf16[512,1024]{1,0:T(8,128)(2,1)S(1)} %share.1.mine_ref, bf16[512,1024]{1,0:T(8,128)(2,1)S(1)} %collective-permute-done.6.other_ref, bf16[512,1024]{1,0:T(8,128)(2,1)S(1)} %collective-permute-done.8.refs_0_.refs_10_), custom_call_target="tpu_custom_call" | custom-call | flops 2147483648 | bytes 5242880 | tf_op jit(solution)/shard_map/scores/pallas_call | solution.py:85
  75.7 1.6 %scores.9 = (f32[2,512,512]{2,1,0:T(8,128)S(1)}, f32[4,512]{1,0:T(4,128)S(1)}) custom-call(bf16[512,1024]{1,0:T(8,128)(2,1)S(1)} %share.1.mine_ref, bf16[512,1024]{1,0:T(8,128)(2,1)S(1)} %collective-permute-done.6.other_ref, bf16[512,1024]{1,0:T(8,128)(2,1)S(1)} %collective-permute-done.10.refs_0_.refs_13_), custom_call_target="tpu_custom_call" | custom-call | flops 2147483648 | bytes 5242880 | tf_op jit(solution)/shard_map/scores/pallas_call | solution.py:85
  77.3 1.3 %first.1 = (f32[64,8,640]{2,1,0:T(8,128)S(1)}, f32[2,4096]{1,0:T(2,128)S(1)}) custom-call(s32[5]{0:T(128)S(1)} %stack.32.spot_ref, f32[1,128]{1,0:T(1,128)S(1)} %reshape_tile.3.ids_ref, f32[4,1536]{1,0:T(4,128)S(1)} %get-tuple-element.41.refs_0_, f32[4,512]{1,0:T(4,128)S(1)} %get-tuple-element.42.refs_1_, f32[4,512]{1,0:T(4,128)S(1)} %get-tuple-element.44.refs_2_, ...), custom_call_target="tpu_custom_call" | custom-call | tf_op jit(solution)/shard_map/first/pallas_call | solution.py:323
  78.6 23.6 %all_to_all.5.all_ref = f32[64,8,640]{2,1,0:T(8,128)S(1)} all-to-all(f32[64,8,640]{2,1,0:T(8,128)S(1)} %get-tuple-element.48), channel_id=1, replica_groups={{0,8,64,72,2,10,66,74,4,12,68,76,6,14,70,78,16,24,80,88,18,26,82,90,20,..., dimensions={0} | all-to-all | bytes 2621440 | tf_op jit(solution)/shard_map/all_to_all | solution.py:337
  102.2 1.2 %merge.1 = (f32[8,512]{1,0:T(8,128)S(1)}, f32[1,4096]{1,0:T(1,128)S(1)}) custom-call(s32[5]{0:T(128)S(1)} %stack.32.spot_ref, f32[64,8,640]{2,1,0:T(8,128)S(1)} %all_to_all.5.all_ref), custom_call_target="tpu_custom_call" | custom-call | tf_op jit(solution)/shard_map/merge/pallas_call | solution.py:338
  103.5 4.5 %sums.3 = f32[512,1152]{1,0:T(8,128)S(1)} custom-call(f32[1,4096]{1,0:T(1,128)S(1)} %get-tuple-element.49.lse_ref, f32[2,4096]{1,0:T(2,128)S(1)} %get-tuple-element.50.top_ref, f32[2,512,512]{2,1,0:T(8,128)S(1)} %get-tuple-element.51.refs_0_, f32[2,512,512]{2,1,0:T(8,128)S(1)} %get-tuple-element.52.refs_1_, f32[2,512,512]{2,1,0:T(8,128)S(1)} %get-tuple-element.53.refs_2_, ...), custom_call_target="tpu_custom_call" | custom-call | flops 4294967296 | bytes 18874368 | tf_op jit(solution)/shard_map/sums/pallas_call | solution.py:236
  108.0 4.4 %collective-permute-start.13 = (f32[512,1152]{1,0:T(8,128)S(1)}, f32[512,1152]{1,0:T(8,128)S(1)}, u32[]{:S(2)}, u32[]{:S(2)}) collective-permute-start(f32[512,1152]{1,0:T(8,128)S(1)} %sums.3), channel_id=1, source_target_pairs={{0,1},{1,0},{2,3},{3,2},{4,5},{5,4},{6,7},{7,6},{8,9},{9,8},{10,11... | collective-permute-start | bytes 7077896 | tf_op jit(solution)/shard_map/ppermute | solution.py:38
  113.1 4.5 %sums.2.ours_ref = f32[512,1152]{1,0:T(8,128)S(1)} custom-call(f32[1,4096]{1,0:T(1,128)S(1)} %get-tuple-element.49.lse_ref, f32[2,4096]{1,0:T(2,128)S(1)} %get-tuple-element.50.top_ref, f32[2,512,512]{2,1,0:T(8,128)S(1)} %get-tuple-element.51.refs_0_, f32[2,512,512]{2,1,0:T(8,128)S(1)} %get-tuple-element.52.refs_1_, ...), custom_call_target="tpu_custom_call" | custom-call | flops 4294967296 | bytes 18874368 | tf_op jit(solution)/shard_map/sums/pallas_call | solution.py:236
  117.6 1.4 %route.1 = f32[1,64]{1,0:T(1,128)} custom-call(s32[2]{0:T(128)S(1)} %pad_add_fusion.at_ref, f32[64,128]{1,0:T(8,128)S(1)} %pack.1.mine_ref, f32[64,128]{1,0:T(8,128)S(1)} %collective-permute-done.14.other_ref), custom_call_target="tpu_custom_call" | custom-call | tf_op jit(solution)/shard_map/route/pallas_call | solution.py:360
  119.1 1.7 %final.1 = f32[512,1024]{1,0:T(8,128)} custom-call(f32[512,1152]{1,0:T(8,128)S(1)} %sums.2.ours_ref, f32[512,1152]{1,0:T(8,128)S(1)} %collective-permute-done.13.theirs_ref, bf16[512,1024]{1,0:T(8,128)(2,1)S(1)} %share.1.mine_ref), custom_call_target="tpu_custom_call" | custom-call | tf_op jit(solution)/shard_map/final/pallas_call | solution.py:367
  (24 shorter events, 3.5 us)
Async XLA Ops:
  0.6 8.7 %collective-permute-start = (bf16[64,1024]{1,0:T(8,128)(2,1)}, bf16[64,1024]{1,0:T(8,128)(2,1)S(1)}, u32[]{:S(2)}, u32[]{:S(2)}) collective-permute-start(bf16[64,1024]{1,0:T(8,128)(2,1)} %refs_0_.1), channel_id=1, source_target_pairs={{8,0},{9,1},{24,16},{25,17},{40,32},{41,33},{56,48},{57,49},{10,2}... | collective-permute-start | bytes 393224 | tf_op jit(solution)/shard_map/ppermute | solution.py:33
  4.0 5.6 %collective-permute-start.1 = (bf16[64,1024]{1,0:T(8,128)(2,1)}, bf16[64,1024]{1,0:T(8,128)(2,1)S(1)}, u32[]{:S(2)}, u32[]{:S(2)}) collective-permute-start(bf16[64,1024]{1,0:T(8,128)(2,1)} %refs_0_.1), channel_id=1, source_target_pairs={{64,0},{65,1},{80,16},{81,17},{96,32},{97,33},{112,48},{113,49},{6... | collective-permute-start | bytes 393224 | tf_op jit(solution)/shard_map/ppermute | solution.py:33
  4.5 9.2 %collective-permute-start.2 = (bf16[64,1024]{1,0:T(8,128)(2,1)}, bf16[64,1024]{1,0:T(8,128)(2,1)S(1)}, u32[]{:S(2)}, u32[]{:S(2)}) collective-permute-start(bf16[64,1024]{1,0:T(8,128)(2,1)} %refs_0_.1), channel_id=1, source_target_pairs={{72,0},{73,1},{88,16},{89,17},{104,32},{105,33},{120,48},{121,49},... | collective-permute-start | bytes 393224 | tf_op jit(solution)/shard_map/ppermute | solution.py:33
  13.8 0.9 copy-start.1
  14.7 15.6 %collective-permute-start.3 = (bf16[256,1024]{1,0:T(8,128)(2,1)S(1)}, bf16[256,1024]{1,0:T(8,128)(2,1)S(1)}, u32[]{:S(2)}, u32[]{:S(2)}) collective-permute-start(bf16[256,1024]{1,0:T(8,128)(2,1)S(1)} %join.1.refs_0_), channel_id=1, source_target_pairs={{2,0},{17,1},{18,16},{33,17},{34,32},{49,33},{50,48},{1,49},{4,2},... | collective-permute-start | bytes 1572872 | tf_op jit(solution)/shard_map/ppermute | solution.py:33
  18.5 11.7 %collective-permute-start.4 = (bf16[256,1024]{1,0:T(8,128)(2,1)S(1)}, bf16[256,1024]{1,0:T(8,128)(2,1)S(1)}, u32[]{:S(2)}, u32[]{:S(2)}) collective-permute-start(bf16[256,1024]{1,0:T(8,128)(2,1)S(1)} %join.1.refs_0_), channel_id=1, source_target_pairs={{4,0},{33,1},{20,16},{49,17},{36,32},{1,33},{52,48},{17,49},{6,2},... | collective-permute-start | bytes 1572872 | tf_op jit(solution)/shard_map/ppermute | solution.py:33
  18.5 15.2 %collective-permute-start.5 = (bf16[256,1024]{1,0:T(8,128)(2,1)S(1)}, bf16[256,1024]{1,0:T(8,128)(2,1)S(1)}, u32[]{:S(2)}, u32[]{:S(2)}) collective-permute-start(bf16[256,1024]{1,0:T(8,128)(2,1)S(1)} %join.1.refs_0_), channel_id=1, source_target_pairs={{6,0},{49,1},{22,16},{1,17},{38,32},{17,33},{54,48},{33,49},{0,2},... | collective-permute-start | bytes 1572872 | tf_op jit(solution)/shard_map/ppermute | solution.py:33
  34.4 15.5 %collective-permute-start.7 = (bf16[512,1024]{1,0:T(8,128)(2,1)S(1)}, bf16[512,1024]{1,0:T(8,128)(2,1)S(1)}, u32[]{:S(2)}, u32[]{:S(2)}) collective-permute-start(bf16[512,1024]{1,0:T(8,128)(2,1)S(1)} %get-tuple-element.39.refs_1_.refs_8_), channel_id=1, source_target_pairs={{32,0},{5,1},{48,16},{21,17},{0,32},{37,33},{16,48},{53,49},{34,2}... | collective-permute-start | bytes 3145736 | tf_op jit(solution)/shard_map/ppermute | solution.py:33
  37.1 3.4 %copy-start = (bf16[4096,1024]{1,0:T(8,128)(2,1)S(1)}, bf16[4096,1024]{1,0:T(8,128)(2,1)}, u32[]{:S(2)}) copy-start(bf16[4096,1024]{1,0:T(8,128)(2,1)} %cents_ref.1) | copy-start | bytes 25165828
  42.5 9.7 %collective-permute-start.6 = (bf16[512,1024]{1,0:T(8,128)(2,1)S(1)}, bf16[512,1024]{1,0:T(8,128)(2,1)S(1)}, u32[]{:S(2)}, u32[]{:S(2)}) collective-permute-start(bf16[512,1024]{1,0:T(8,128)(2,1)S(1)} %share.1.mine_ref), channel_id=1, source_target_pairs={{0,1},{1,0},{2,3},{3,2},{4,5},{5,4},{6,7},{7,6},{8,9},{9,8},{10,11... | collective-permute-start | bytes 3145736 | tf_op jit(solution)/shard_map/ppermute | solution.py:38
  44.9 16.4 %collective-permute-start.9 = (bf16[512,1024]{1,0:T(8,128)(2,1)S(1)}, bf16[512,1024]{1,0:T(8,128)(2,1)S(1)}, u32[]{:S(2)}, u32[]{:S(2)}) collective-permute-start(bf16[512,1024]{1,0:T(8,128)(2,1)S(1)} %get-tuple-element.40.refs_2_.refs_9_), channel_id=1, source_target_pairs={{16,0},{3,1},{32,16},{19,17},{48,32},{35,33},{0,48},{51,49},{18,2}... | collective-permute-start | bytes 3145736 | tf_op jit(solution)/shard_map/ppermute | solution.py:33
  45.2 17.7 %collective-permute-start.11 = (bf16[512,1024]{1,0:T(8,128)(2,1)S(1)}, bf16[512,1024]{1,0:T(8,128)(2,1)S(1)}, u32[]{:S(2)}, u32[]{:S(2)}) collective-permute-start(bf16[512,1024]{1,0:T(8,128)(2,1)S(1)} %get-tuple-element.39.refs_1_.refs_8_), channel_id=1, source_target_pairs={{48,0},{7,1},{0,16},{23,17},{16,32},{39,33},{32,48},{55,49},{50,2}... | collective-permute-start | bytes 3145736 | tf_op jit(solution)/shard_map/ppermute | solution.py:33
  46.3 26.0 %collective-permute-start.12 = (bf16[512,1024]{1,0:T(8,128)(2,1)S(1)}, bf16[512,1024]{1,0:T(8,128)(2,1)S(1)}, u32[]{:S(2)}, u32[]{:S(2)}) collective-permute-start(bf16[512,1024]{1,0:T(8,128)(2,1)S(1)} %get-tuple-element.40.refs_2_.refs_9_), channel_id=1, source_target_pairs={{48,0},{7,1},{0,16},{23,17},{16,32},{39,33},{32,48},{55,49},{50,2}... | collective-permute-start | bytes 3145736 | tf_op jit(solution)/shard_map/ppermute | solution.py:33
  49.9 24.1 %collective-permute-start.8 = (bf16[512,1024]{1,0:T(8,128)(2,1)S(1)}, bf16[512,1024]{1,0:T(8,128)(2,1)S(1)}, u32[]{:S(2)}, u32[]{:S(2)}) collective-permute-start(bf16[512,1024]{1,0:T(8,128)(2,1)S(1)} %get-tuple-element.39.refs_1_.refs_8_), channel_id=1, source_target_pairs={{16,0},{3,1},{32,16},{19,17},{48,32},{35,33},{0,48},{51,49},{18,2}... | collective-permute-start | bytes 3145736 | tf_op jit(solution)/shard_map/ppermute | solution.py:33
  52.2 23.5 %collective-permute-start.10 = (bf16[512,1024]{1,0:T(8,128)(2,1)S(1)}, bf16[512,1024]{1,0:T(8,128)(2,1)S(1)}, u32[]{:S(2)}, u32[]{:S(2)}) collective-permute-start(bf16[512,1024]{1,0:T(8,128)(2,1)S(1)} %collective-permute-done.7.refs_0_.refs_12_), channel_id=1, source_target_pairs={{8,0},{73,1},{24,16},{89,17},{40,32},{105,33},{56,48},{121,49},{10... | collective-permute-start | bytes 3145736 | tf_op jit(solution)/shard_map/ppermute | solution.py:49
  108.0 11.1 %collective-permute-start.13 = (f32[512,1152]{1,0:T(8,128)S(1)}, f32[512,1152]{1,0:T(8,128)S(1)}, u32[]{:S(2)}, u32[]{:S(2)}) collective-permute-start(f32[512,1152]{1,0:T(8,128)S(1)} %sums.3), channel_id=1, source_target_pairs={{0,1},{1,0},{2,3},{3,2},{4,5},{5,4},{6,7},{7,6},{8,9},{9,8},{10,11... | collective-permute-start | bytes 7077896 | tf_op jit(solution)/shard_map/ppermute | solution.py:38
  113.0 4.6 %collective-permute-start.14 = (f32[64,128]{1,0:T(8,128)S(1)}, f32[64,128]{1,0:T(8,128)S(1)}, u32[]{:S(2)}, u32[]{:S(2)}) collective-permute-start(f32[64,128]{1,0:T(8,128)S(1)} %pack.1.mine_ref), channel_id=1, source_target_pairs={{0,1},{1,0},{2,3},{3,2},{4,5},{5,4},{6,7},{7,6},{8,9},{9,8},{10,11... | collective-permute-start | bytes 98312 | tf_op jit(solution)/shard_map/ppermute | solution.py:38

commit v9 on v8

--- a/solution.py
+++ b/solution.py
@@ -125,37 +125,39 @@
         value = roll_within(value, dim, spot_ref[dim])
     for line in range(8):
         piece = value[:, line * 512 : (line + 1) * 512]
-        out_ref[:, line, 0:512] = jnp.broadcast_to(piece, (64, 512))
+        out_ref[:, line, 0:512] = jnp.broadcast_to(piece, (16, 512))
     lane = lax.broadcasted_iota(jnp.int32, (1, 128), 1)
     ids = jnp.where(lane // UNIT == spot_ref[0] % 2, ids_ref[...], -1.0)
-    out_ref[:, :, 512:640] = jnp.broadcast_to(ids.reshape(1, 1, 128), (64, 8, 128))
-
-
-def merge_kernel(swapped, spot_ref, all_ref, whole_ref, own_ref):
-    values = all_ref[:, :, 0:512]
-    top = jnp.max(values, axis=0)
-    total = jnp.sum(jnp.exp2(values - top[None]), axis=0)
-    lse = top + jnp.log2(total)
-    whole_ref[...] = lse
+    out_ref[:, :, 512:640] = jnp.broadcast_to(ids.reshape(1, 1, 128), (16, 8, 128))
+
+
+def combine(values):
+    top = functools.reduce(jnp.maximum, values)
+    return top + jnp.log2(sum(jnp.exp2(value - top) for value in values))
+
+
+def plane_kernel(all_ref, out_ref):
+    out_ref[:, 0:512] = combine([all_ref[k, :, 0:512] for k in range(16)])
+    for line in range(8):
+        pair = jnp.maximum(all_ref[2 * line, 0:1, 512:640], all_ref[2 * line + 1, 0:1, 512:640])
+        out_ref[line : line + 1, 512:640] = pair
+
+
+def merge_kernel(swapped, spot_ref, *refs):
+    *planes, pack_ref, own_ref = refs
+    lse = combine([plane[:, 0:512] for plane in planes])
     value = jnp.concatenate([lse[line : line + 1, :] for line in range(8)], axis=1)
+    for tile in range(32):
+        pack_ref[tile : tile + 1, :] = value[:, tile * 128 : (tile + 1) * 128]
+    for k, plane in enumerate(planes):
+        first = pl.multiple_of(32 + (spot_ref[2] + k) % 4 * 8, 8)
+        pack_ref[pl.ds(first, 8), :] = plane[:, 512:640]
     for dim in range(3):
         value = roll_within(value, dim, (4 - spot_ref[dim]) % 4)
     own_ref[...] = value
     for k in swapped:
         lanes = slice(k * 512, (k + 1) * 512)
         own_ref[:, lanes] = roll_within(value[:, lanes], 0, 4 - spot_ref[3])
-
-
-def pack_kernel(at_ref, whole_ref, all_ref, out_ref):
-    first_core = at_ref[1] % 2 == 0
-    for line in range(32):
-        tile = line % 4
-        out_ref[line : line + 1, :] = whole_ref[line // 4 : line // 4 + 1, tile * 128 : (tile + 1) * 128]
-        low, high = line // 2 % 4, line // 8
-        even = jnp.where(first_core, 2 * line, high * 16 + line % 2 * 8 + low)
-        odd = jnp.where(first_core, 2 * line + 1, high * 16 + line % 2 * 8 + 4 + low)
-        pair = jnp.maximum(all_ref[even, 0:1, 512:640], all_ref[odd, 0:1, 512:640])
-        out_ref[32 + line : 33 + line, :] = pair
 
 
 def route_kernel(at_ref, mine_ref, other_ref, out_ref):
@@ -323,38 +325,36 @@
     local, tops = pl.pallas_call(
         functools.partial(first_kernel, swapped, order),
         out_shape=(
-            jax.ShapeDtypeStruct((64, 8, 640), jnp.float32),
+            jax.ShapeDtypeStruct((16, 8, 640), jnp.float32),
             jax.ShapeDtypeStruct((2, 4096), jnp.float32),
         ),
         in_specs=[smem] + [vmem] * 7,
         compiler_params=small,
         name="first",
     )(spot, ids, *stats)
-    chips = [
-        [place(i % 4, i // 4 % 4, i // 16, 0) for i in range(64)],
-        [place(i // 4 % 4, i // 16, i % 4, 1) for i in range(64)],
-    ]
-    shared = lax.all_to_all(local, BOTH, split_axis=0, concat_axis=0, tiled=True, axis_index_groups=chips)
-    whole, lse = pl.pallas_call(
+    planes = [[place(i % 4, i // 4, z, 0) for i in range(16)] for z in range(4)]
+    planes += [[place(i % 4, y, i // 4, 1) for i in range(16)] for y in range(4)]
+    shared = lax.all_to_all(local, BOTH, split_axis=0, concat_axis=0, tiled=True, axis_index_groups=planes)
+    plane = pl.pallas_call(
+        plane_kernel,
+        out_shape=jax.ShapeDtypeStruct((8, 640), jnp.float32),
+        in_specs=[vmem],
+        out_specs=vmem,
+        compiler_params=small,
+        name="plane",
+    )(shared)
+    pack, lse = pl.pallas_call(
         functools.partial(merge_kernel, swapped),
         out_shape=(
-            jax.ShapeDtypeStruct((8, 512), jnp.float32),
+            jax.ShapeDtypeStruct((64, 128), jnp.float32),
             jax.ShapeDtypeStruct((1, 4096), jnp.float32),
         ),
-        in_specs=[smem, vmem],
+        in_specs=[smem] + [vmem] * 4,
         compiler_params=small,
         name="merge",
-    )(spot, shared)
+    )(spot, plane, *[fetch(plane, 2, offset) for offset in (1, 2, 3)])
     theirs = sums_call(1, lse, tops, ps, chunks)
     received = swap_cores(theirs)
-    whole, shared, _ = lax.optimization_barrier((whole, shared, theirs))
-    pack = pl.pallas_call(
-        pack_kernel,
-        out_shape=jax.ShapeDtypeStruct((64, 128), jnp.float32),
-        in_specs=[smem] + [vmem] * 2,
-        compiler_params=small,
-        name="pack",
-    )(at_word, whole, shared)
     partner = swap_cores(pack)
     ours = sums_call(0, lse, tops, ps, chunks)
     row_lse = pl.pallas_call(

time: 121 us -> 123 us (1.017)
  blocking collectives: 23.6 us -> 14.5 us
  starting transfers between devices: 22.4 us -> 29.2 us
  waiting for transfers between devices: 38.4 us -> 43.7 us
    all_to_all x1, blocking collectives: 23.6 us -> 14.5 us  [shards(): lax.all_to_all(local, BOTH, split_axis=0, concat_axis=0, tiled=True, axis...]
    ppermute x11 -> x14, starting transfers between devices: 15.5 us -> 20.9 us  [fetch(): return lax.ppermute(value, BOTH, pairs)]
    ppermute x11 -> x14, waiting for transfers between devices: 38.3 us -> 43.7 us  [fetch(): return lax.ppermute(value, BOTH, pairs)]
    ppermute x1, starting transfers between devices: 0.01 us -> 1.69 us  [swap_sides(): return lax.ppermute(value, BOTH, pairs)]
  transfers between devices with their start and end apart: 15 -> 18, of which waited for: 8 -> 9; matrix products, arithmetic and copies ran while one was open for 1% -> 1% of each run, Pallas kernels for 16% -> 14%
where the time goes in v9:
time: 123 us
  waiting for transfers between devices  43.7 us (36%)
  Pallas kernels  29.6 us (24%)
  starting transfers between devices  29.2 us (24%)
  blocking collectives  14.5 us (12%)
  local copies, waits for them, and re-layouts  4.45 us (4%)
    ppermute x14, waiting for transfers between devices, fetch(): return lax.ppermute(value, BOTH, pairs)  43.7 us
    ppermute x14, starting transfers between devices, fetch(): return lax.ppermute(value, BOTH, pairs)  20.9 us
    all_to_all x1, blocking collectives, shards(): lax.all_to_all(local, BOTH, split_axis=0, concat_axis=0, tiled=True, axis...  14.5 us
    pallas_call x6, Pallas kernels, scores_call(): pl.pallas_call(functools.partial(scores_kernel, factor, count), out_shape...  12.5 us
    pallas_call x2, Pallas kernels, sums_call(): pl.pallas_call(functools.partial(sums_kernel, half, count), out_shape=jax...  8.98 us
    ppermute x3, starting transfers between devices, swap_cores(): return lax.ppermute(value, BOTH, pairs)  6.59 us
    unnamed x4, local copies, waits for them, and re-layouts  4.28 us
  transfers between devices with their start and end apart: 18, of which 9 were waited for; matrix products, arithmetic and copies ran while one was open for 1% of the time, Pallas kernels for 14%

profile of v9, /device:TPU:1, one launch (start us, length us, event | category | flops | bytes accessed | tf_op | source)
XLA Modules:
  0.0 123.0 jit_solution(11958863674220475568)
XLA Ops:
  0.6 3.7 %collective-permute-start.1 = (bf16[64,1024]{1,0:T(8,128)(2,1)}, bf16[64,1024]{1,0:T(8,128)(2,1)S(1)}, u32[]{:S(2)}, u32[]{:S(2)}) collective-permute-start(bf16[64,1024]{1,0:T(8,128)(2,1)} %refs_0_.1), channel_id=1, source_target_pairs={{64,0},{65,1},{80,16},{81,17},{96,32},{97,33},{112,48},{113,49},{6... | collective-permute-start | bytes 393224 | tf_op jit(solution)/shard_map/ppermute | solution.py:33
  7.2 3.3 %collective-permute-done.refs_1_ = bf16[64,1024]{1,0:T(8,128)(2,1)S(1)} collective-permute-done((bf16[64,1024]{1,0:T(8,128)(2,1)}, bf16[64,1024]{1,0:T(8,128)(2,1)S(1)}, u32[]{:S(2)}, u32[]{:S(2)}) %collective-permute-start) | collective-permute-done | bytes 131104 | tf_op jit(solution)/shard_map/ppermute | solution.py:33
  11.5 1.8 %collective-permute-start.5 = (bf16[256,1024]{1,0:T(8,128)(2,1)S(1)}, bf16[256,1024]{1,0:T(8,128)(2,1)S(1)}, u32[]{:S(2)}, u32[]{:S(2)}) collective-permute-start(bf16[256,1024]{1,0:T(8,128)(2,1)S(1)} %join.1.refs_0_), channel_id=1, source_target_pairs={{6,0},{49,1},{22,16},{1,17},{38,32},{17,33},{54,48},{33,49},{0,2},... | collective-permute-start | bytes 1572872 | tf_op jit(solution)/shard_map/ppermute | solution.py:33
  13.2 3.3 %collective-permute-start.4 = (bf16[256,1024]{1,0:T(8,128)(2,1)S(1)}, bf16[256,1024]{1,0:T(8,128)(2,1)S(1)}, u32[]{:S(2)}, u32[]{:S(2)}) collective-permute-start(bf16[256,1024]{1,0:T(8,128)(2,1)S(1)} %join.1.refs_0_), channel_id=1, source_target_pairs={{4,0},{33,1},{20,16},{49,17},{36,32},{1,33},{52,48},{17,49},{6,2},... | collective-permute-start | bytes 1572872 | tf_op jit(solution)/shard_map/ppermute | solution.py:33
  17.3 5.0 %collective-permute-done.5.refs_3_ = bf16[256,1024]{1,0:T(8,128)(2,1)S(1)} collective-permute-done((bf16[256,1024]{1,0:T(8,128)(2,1)S(1)}, bf16[256,1024]{1,0:T(8,128)(2,1)S(1)}, u32[]{:S(2)}, u32[]{:S(2)}) %collective-permute-start.5) | collective-permute-done | bytes 524320 | tf_op jit(solution)/shard_map/ppermute | solution.py:33
  22.2 6.8 %collective-permute-done.4.refs_2_ = bf16[256,1024]{1,0:T(8,128)(2,1)S(1)} collective-permute-done((bf16[256,1024]{1,0:T(8,128)(2,1)S(1)}, bf16[256,1024]{1,0:T(8,128)(2,1)S(1)}, u32[]{:S(2)}, u32[]{:S(2)}) %collective-permute-start.4) | collective-permute-done | bytes 524320 | tf_op jit(solution)/shard_map/ppermute | solution.py:33
  29.7 3.4 %copy-done = bf16[4096,1024]{1,0:T(8,128)(2,1)S(1)} copy-done((bf16[4096,1024]{1,0:T(8,128)(2,1)S(1)}, bf16[4096,1024]{1,0:T(8,128)(2,1)}, u32[]{:S(2)}) %copy-start) | copy-done | bytes 8388632
  33.1 2.0 %share.1.mine_ref = bf16[512,1024]{1,0:T(8,128)(2,1)S(1)} custom-call(s32[2]{0:T(128)S(1)} %pad_add_fusion.at_ref, bf16[4096,1024]{1,0:T(8,128)(2,1)S(1)} %copy-done), custom_call_target="tpu_custom_call" | custom-call | tf_op jit(solution)/shard_map/share/pallas_call | solution.py:304
  35.1 2.1 %collective-permute-start.6 = (bf16[512,1024]{1,0:T(8,128)(2,1)S(1)}, bf16[512,1024]{1,0:T(8,128)(2,1)S(1)}, u32[]{:S(2)}, u32[]{:S(2)}) collective-permute-start(bf16[512,1024]{1,0:T(8,128)(2,1)S(1)} %share.1.mine_ref), channel_id=1, source_target_pairs={{0,1},{1,0},{2,3},{3,2},{4,5},{5,4},{6,7},{7,6},{8,9},{9,8},{10,11... | collective-permute-start | bytes 3145736 | tf_op jit(solution)/shard_map/ppermute | solution.py:38
  37.2 2.6 %collective-permute-start.7 = (bf16[512,1024]{1,0:T(8,128)(2,1)S(1)}, bf16[512,1024]{1,0:T(8,128)(2,1)S(1)}, u32[]{:S(2)}, u32[]{:S(2)}) collective-permute-start(bf16[512,1024]{1,0:T(8,128)(2,1)S(1)} %get-tuple-element.37.refs_1_.refs_8_), channel_id=1, source_target_pairs={{32,0},{5,1},{48,16},{21,17},{0,32},{37,33},{16,48},{53,49},{34,2}... | collective-permute-start | bytes 3145736 | tf_op jit(solution)/shard_map/ppermute | solution.py:33
  39.8 1.2 collective-permute-start.9
  41.0 1.4 %collective-permute-start.11 = (bf16[512,1024]{1,0:T(8,128)(2,1)S(1)}, bf16[512,1024]{1,0:T(8,128)(2,1)S(1)}, u32[]{:S(2)}, u32[]{:S(2)}) collective-permute-start(bf16[512,1024]{1,0:T(8,128)(2,1)S(1)} %get-tuple-element.37.refs_1_.refs_8_), channel_id=1, source_target_pairs={{48,0},{7,1},{0,16},{23,17},{16,32},{39,33},{32,48},{55,49},{50,2}... | collective-permute-start | bytes 3145736 | tf_op jit(solution)/shard_map/ppermute | solution.py:33
  42.7 10.0 %collective-permute-done.7.refs_0_.refs_12_ = bf16[512,1024]{1,0:T(8,128)(2,1)S(1)} collective-permute-done((bf16[512,1024]{1,0:T(8,128)(2,1)S(1)}, bf16[512,1024]{1,0:T(8,128)(2,1)S(1)}, u32[]{:S(2)}, u32[]{:S(2)}) %collective-permute-start.7) | collective-permute-done | bytes 1048608 | tf_op jit(solution)/shard_map/ppermute | solution.py:33
  52.7 1.7 %collective-permute-start.10 = (bf16[512,1024]{1,0:T(8,128)(2,1)S(1)}, bf16[512,1024]{1,0:T(8,128)(2,1)S(1)}, u32[]{:S(2)}, u32[]{:S(2)}) collective-permute-start(bf16[512,1024]{1,0:T(8,128)(2,1)S(1)} %collective-permute-done.7.refs_0_.refs_12_), channel_id=1, source_target_pairs={{8,0},{73,1},{24,16},{89,17},{40,32},{105,33},{56,48},{121,49},{10... | collective-permute-start | bytes 3145736 | tf_op jit(solution)/shard_map/ppermute | solution.py:49
  54.4 4.3 %scores.6 = (f32[2,512,512]{2,1,0:T(8,128)S(1)}, f32[2,512,512]{2,1,0:T(8,128)S(1)}, f32[2,512,512]{2,1,0:T(8,128)S(1)}, f32[4,1536]{1,0:T(4,128)S(1)}) custom-call(bf16[512,1024]{1,0:T(8,128)(2,1)S(1)} %share.1.mine_ref, bf16[512,1024]{1,0:T(8,128)(2,1)S(1)} %collective-permute-done.6.other_ref, ...), custom_call_target="tpu_custom_call" | custom-call | flops 6442450944 | bytes 11534336 | tf_op jit(solution)/shard_map/scores/pallas_call | solution.py:85
  58.7 4.8 %collective-permute-done.9.refs_0_.refs_11_ = bf16[512,1024]{1,0:T(8,128)(2,1)S(1)} collective-permute-done((bf16[512,1024]{1,0:T(8,128)(2,1)S(1)}, bf16[512,1024]{1,0:T(8,128)(2,1)S(1)}, u32[]{:S(2)}, u32[]{:S(2)}) %collective-permute-start.9) | collective-permute-done | bytes 1048608 | tf_op jit(solution)/shard_map/ppermute | solution.py:33
  63.5 11.2 %collective-permute-done.8.refs_0_.refs_10_ = bf16[512,1024]{1,0:T(8,128)(2,1)S(1)} collective-permute-done((bf16[512,1024]{1,0:T(8,128)(2,1)S(1)}, bf16[512,1024]{1,0:T(8,128)(2,1)S(1)}, u32[]{:S(2)}, u32[]{:S(2)}) %collective-permute-start.8) | collective-permute-done | bytes 1048608 | tf_op jit(solution)/shard_map/ppermute | solution.py:33
  74.8 1.6 %scores.7 = (f32[2,512,512]{2,1,0:T(8,128)S(1)}, f32[4,512]{1,0:T(4,128)S(1)}) custom-call(bf16[512,1024]{1,0:T(8,128)(2,1)S(1)} %share.1.mine_ref, bf16[512,1024]{1,0:T(8,128)(2,1)S(1)} %collective-permute-done.6.other_ref, bf16[512,1024]{1,0:T(8,128)(2,1)S(1)} %collective-permute-done.8.refs_0_.refs_10_), custom_call_target="tpu_custom_call" | custom-call | flops 2147483648 | bytes 5242880 | tf_op jit(solution)/shard_map/scores/pallas_call | solution.py:85
  76.4 1.6 %scores.10 = (f32[2,512,512]{2,1,0:T(8,128)S(1)}, f32[4,512]{1,0:T(4,128)S(1)}) custom-call(bf16[512,1024]{1,0:T(8,128)(2,1)S(1)} %share.1.mine_ref, bf16[512,1024]{1,0:T(8,128)(2,1)S(1)} %collective-permute-done.6.other_ref, bf16[512,1024]{1,0:T(8,128)(2,1)S(1)} %collective-permute-done.11.refs_0_.refs_14_), custom_call_target="tpu_custom_call" | custom-call | flops 2147483648 | bytes 5242880 | tf_op jit(solution)/shard_map/scores/pallas_call | solution.py:85
  78.1 1.6 %scores.11 = (f32[2,512,512]{2,1,0:T(8,128)S(1)}, f32[4,512]{1,0:T(4,128)S(1)}) custom-call(bf16[512,1024]{1,0:T(8,128)(2,1)S(1)} %share.1.mine_ref, bf16[512,1024]{1,0:T(8,128)(2,1)S(1)} %collective-permute-done.6.other_ref, bf16[512,1024]{1,0:T(8,128)(2,1)S(1)} %collective-permute-done.12.refs_0_.refs_15_), custom_call_target="tpu_custom_call" | custom-call | flops 2147483648 | bytes 5242880 | tf_op jit(solution)/shard_map/scores/pallas_call | solution.py:85
  79.7 1.6 %scores.8 = (f32[2,512,512]{2,1,0:T(8,128)S(1)}, f32[4,512]{1,0:T(4,128)S(1)}) custom-call(bf16[512,1024]{1,0:T(8,128)(2,1)S(1)} %share.1.mine_ref, bf16[512,1024]{1,0:T(8,128)(2,1)S(1)} %collective-permute-done.6.other_ref, bf16[512,1024]{1,0:T(8,128)(2,1)S(1)} %collective-permute-done.9.refs_0_.refs_11_), custom_call_target="tpu_custom_call" | custom-call | flops 2147483648 | bytes 5242880 | tf_op jit(solution)/shard_map/scores/pallas_call | solution.py:85
  81.4 1.6 %scores.9 = (f32[2,512,512]{2,1,0:T(8,128)S(1)}, f32[4,512]{1,0:T(4,128)S(1)}) custom-call(bf16[512,1024]{1,0:T(8,128)(2,1)S(1)} %share.1.mine_ref, bf16[512,1024]{1,0:T(8,128)(2,1)S(1)} %collective-permute-done.6.other_ref, bf16[512,1024]{1,0:T(8,128)(2,1)S(1)} %collective-permute-done.10.refs_0_.refs_13_), custom_call_target="tpu_custom_call" | custom-call | flops 2147483648 | bytes 5242880 | tf_op jit(solution)/shard_map/scores/pallas_call | solution.py:85
  83.0 1.1 first.1
  84.1 14.5 %all_to_all.5.all_ref = f32[16,8,640]{2,1,0:T(8,128)S(1)} all-to-all(f32[16,8,640]{2,1,0:T(8,128)S(1)} %get-tuple-element.46), channel_id=1, replica_groups={{0,8,64,72,2,10,66,74,4,12,68,76,6,14,70,78},{16,24,80,88,18,26,82,90,2..., dimensions={0} | all-to-all | bytes 655360 | tf_op jit(solution)/shard_map/all_to_all | solution.py:337
  98.7 1.7 %collective-permute-start.15 = (f32[8,640]{1,0:T(8,128)S(1)}, f32[8,640]{1,0:T(8,128)S(1)}, u32[]{:S(2)}, u32[]{:S(2)}) collective-permute-start(f32[8,640]{1,0:T(8,128)S(1)} %plane.1.refs_0_), channel_id=1, source_target_pairs={{48,0},{7,1},{0,16},{23,17},{16,32},{39,33},{32,48},{55,49},{50,2}... | collective-permute-start | bytes 61448 | tf_op jit(solution)/shard_map/ppermute | solution.py:33
  100.4 2.2 %collective-permute-start.14 = (f32[8,640]{1,0:T(8,128)S(1)}, f32[8,640]{1,0:T(8,128)S(1)}, u32[]{:S(2)}, u32[]{:S(2)}) collective-permute-start(f32[8,640]{1,0:T(8,128)S(1)} %plane.1.refs_0_), channel_id=1, source_target_pairs={{32,0},{5,1},{48,16},{21,17},{0,32},{37,33},{16,48},{53,49},{34,2}... | collective-permute-start | bytes 61448 | tf_op jit(solution)/shard_map/ppermute | solution.py:33
  103.2 1.4 %collective-permute-done.14.refs_2_ = f32[8,640]{1,0:T(8,128)S(1)} collective-permute-done((f32[8,640]{1,0:T(8,128)S(1)}, f32[8,640]{1,0:T(8,128)S(1)}, u32[]{:S(2)}, u32[]{:S(2)}) %collective-permute-start.14) | collective-permute-done | bytes 20512 | tf_op jit(solution)/shard_map/ppermute | solution.py:33
  106.3 4.5 %sums.3 = f32[512,1152]{1,0:T(8,128)S(1)} custom-call(f32[1,4096]{1,0:T(1,128)S(1)} %get-tuple-element.47.lse_ref, f32[2,4096]{1,0:T(2,128)S(1)} %get-tuple-element.48.top_ref, f32[2,512,512]{2,1,0:T(8,128)S(1)} %get-tuple-element.49.refs_0_, f32[2,512,512]{2,1,0:T(8,128)S(1)} %get-tuple-element.50.refs_1_, f32[2,512,512]{2,1,0:T(8,128)S(1)} %get-tuple-element.51.refs_2_, ...), custom_call_target="tpu_custom_call" | custom-call | flops 4294967296 | bytes 18874368 | tf_op jit(solution)/shard_map/sums/pallas_call | solution.py:238
  110.8 4.4 %collective-permute-start.16 = (f32[512,1152]{1,0:T(8,128)S(1)}, f32[512,1152]{1,0:T(8,128)S(1)}, u32[]{:S(2)}, u32[]{:S(2)}) collective-permute-start(f32[512,1152]{1,0:T(8,128)S(1)} %sums.3), channel_id=1, source_target_pairs={{0,1},{1,0},{2,3},{3,2},{4,5},{5,4},{6,7},{7,6},{8,9},{9,8},{10,11... | collective-permute-start | bytes 7077896 | tf_op jit(solution)/shard_map/ppermute | solution.py:38
  115.3 4.5 %sums.2.ours_ref = f32[512,1152]{1,0:T(8,128)S(1)} custom-call(f32[1,4096]{1,0:T(1,128)S(1)} %get-tuple-element.47.lse_ref, f32[2,4096]{1,0:T(2,128)S(1)} %get-tuple-element.48.top_ref, f32[2,512,512]{2,1,0:T(8,128)S(1)} %get-tuple-element.49.refs_0_, f32[2,512,512]{2,1,0:T(8,128)S(1)} %get-tuple-element.50.refs_1_, ...), custom_call_target="tpu_custom_call" | custom-call | flops 4294967296 | bytes 18874368 | tf_op jit(solution)/shard_map/sums/pallas_call | solution.py:238
  119.8 1.4 %route.1 = f32[1,64]{1,0:T(1,128)} custom-call(s32[2]{0:T(128)S(1)} %pad_add_fusion.at_ref, f32[64,128]{1,0:T(8,128)S(1)} %get-tuple-element.57.mine_ref, f32[64,128]{1,0:T(8,128)S(1)} %collective-permute-done.17.other_ref), custom_call_target="tpu_custom_call" | custom-call | tf_op jit(solution)/shard_map/route/pallas_call | solution.py:360
  121.2 1.8 %final.1 = f32[512,1024]{1,0:T(8,128)} custom-call(f32[512,1152]{1,0:T(8,128)S(1)} %sums.2.ours_ref, f32[512,1152]{1,0:T(8,128)S(1)} %collective-permute-done.16.theirs_ref, bf16[512,1024]{1,0:T(8,128)(2,1)S(1)} %share.1.mine_ref), custom_call_target="tpu_custom_call" | custom-call | tf_op jit(solution)/shard_map/final/pallas_call | solution.py:367
  (30 shorter events, 8.1 us)
Async XLA Ops:
  0.6 6.6 %collective-permute-start.1 = (bf16[64,1024]{1,0:T(8,128)(2,1)}, bf16[64,1024]{1,0:T(8,128)(2,1)S(1)}, u32[]{:S(2)}, u32[]{:S(2)}) collective-permute-start(bf16[64,1024]{1,0:T(8,128)(2,1)} %refs_0_.1), channel_id=1, source_target_pairs={{64,0},{65,1},{80,16},{81,17},{96,32},{97,33},{112,48},{113,49},{6... | collective-permute-start | bytes 393224 | tf_op jit(solution)/shard_map/ppermute | solution.py:33
  4.3 6.2 %collective-permute-start = (bf16[64,1024]{1,0:T(8,128)(2,1)}, bf16[64,1024]{1,0:T(8,128)(2,1)S(1)}, u32[]{:S(2)}, u32[]{:S(2)}) collective-permute-start(bf16[64,1024]{1,0:T(8,128)(2,1)} %refs_0_.1), channel_id=1, source_target_pairs={{8,0},{9,1},{24,16},{25,17},{40,32},{41,33},{56,48},{57,49},{10,2}... | collective-permute-start | bytes 393224 | tf_op jit(solution)/shard_map/ppermute | solution.py:33
  5.1 5.4 %collective-permute-start.2 = (bf16[64,1024]{1,0:T(8,128)(2,1)}, bf16[64,1024]{1,0:T(8,128)(2,1)S(1)}, u32[]{:S(2)}, u32[]{:S(2)}) collective-permute-start(bf16[64,1024]{1,0:T(8,128)(2,1)} %refs_0_.1), channel_id=1, source_target_pairs={{72,0},{73,1},{88,16},{89,17},{104,32},{105,33},{120,48},{121,49},... | collective-permute-start | bytes 393224 | tf_op jit(solution)/shard_map/ppermute | solution.py:33
  10.5 0.9 copy-start.1
  11.5 10.8 %collective-permute-start.5 = (bf16[256,1024]{1,0:T(8,128)(2,1)S(1)}, bf16[256,1024]{1,0:T(8,128)(2,1)S(1)}, u32[]{:S(2)}, u32[]{:S(2)}) collective-permute-start(bf16[256,1024]{1,0:T(8,128)(2,1)S(1)} %join.1.refs_0_), channel_id=1, source_target_pairs={{6,0},{49,1},{22,16},{1,17},{38,32},{17,33},{54,48},{33,49},{0,2},... | collective-permute-start | bytes 1572872 | tf_op jit(solution)/shard_map/ppermute | solution.py:33
  13.2 15.8 %collective-permute-start.4 = (bf16[256,1024]{1,0:T(8,128)(2,1)S(1)}, bf16[256,1024]{1,0:T(8,128)(2,1)S(1)}, u32[]{:S(2)}, u32[]{:S(2)}) collective-permute-start(bf16[256,1024]{1,0:T(8,128)(2,1)S(1)} %join.1.refs_0_), channel_id=1, source_target_pairs={{4,0},{33,1},{20,16},{49,17},{36,32},{1,33},{52,48},{17,49},{6,2},... | collective-permute-start | bytes 1572872 | tf_op jit(solution)/shard_map/ppermute | solution.py:33
  16.5 12.5 %collective-permute-start.3 = (bf16[256,1024]{1,0:T(8,128)(2,1)S(1)}, bf16[256,1024]{1,0:T(8,128)(2,1)S(1)}, u32[]{:S(2)}, u32[]{:S(2)}) collective-permute-start(bf16[256,1024]{1,0:T(8,128)(2,1)S(1)} %join.1.refs_0_), channel_id=1, source_target_pairs={{2,0},{17,1},{18,16},{33,17},{34,32},{49,33},{50,48},{1,49},{4,2},... | collective-permute-start | bytes 1572872 | tf_op jit(solution)/shard_map/ppermute | solution.py:33
  29.7 3.4 %copy-start = (bf16[4096,1024]{1,0:T(8,128)(2,1)S(1)}, bf16[4096,1024]{1,0:T(8,128)(2,1)}, u32[]{:S(2)}) copy-start(bf16[4096,1024]{1,0:T(8,128)(2,1)} %cents_ref.1) | copy-start | bytes 25165828
  35.1 7.3 %collective-permute-start.6 = (bf16[512,1024]{1,0:T(8,128)(2,1)S(1)}, bf16[512,1024]{1,0:T(8,128)(2,1)S(1)}, u32[]{:S(2)}, u32[]{:S(2)}) collective-permute-start(bf16[512,1024]{1,0:T(8,128)(2,1)S(1)} %share.1.mine_ref), channel_id=1, source_target_pairs={{0,1},{1,0},{2,3},{3,2},{4,5},{5,4},{6,7},{7,6},{8,9},{9,8},{10,11... | collective-permute-start | bytes 3145736 | tf_op jit(solution)/shard_map/ppermute | solution.py:38
  37.2 15.5 %collective-permute-start.7 = (bf16[512,1024]{1,0:T(8,128)(2,1)S(1)}, bf16[512,1024]{1,0:T(8,128)(2,1)S(1)}, u32[]{:S(2)}, u32[]{:S(2)}) collective-permute-start(bf16[512,1024]{1,0:T(8,128)(2,1)S(1)} %get-tuple-element.37.refs_1_.refs_8_), channel_id=1, source_target_pairs={{32,0},{5,1},{48,16},{21,17},{0,32},{37,33},{16,48},{53,49},{34,2}... | collective-permute-start | bytes 3145736 | tf_op jit(solution)/shard_map/ppermute | solution.py:33
  39.8 23.8 %collective-permute-start.9 = (bf16[512,1024]{1,0:T(8,128)(2,1)S(1)}, bf16[512,1024]{1,0:T(8,128)(2,1)S(1)}, u32[]{:S(2)}, u32[]{:S(2)}) collective-permute-start(bf16[512,1024]{1,0:T(8,128)(2,1)S(1)} %get-tuple-element.38.refs_2_.refs_9_), channel_id=1, source_target_pairs={{16,0},{3,1},{32,16},{19,17},{48,32},{35,33},{0,48},{51,49},{18,2}... | collective-permute-start | bytes 3145736 | tf_op jit(solution)/shard_map/ppermute | solution.py:33
  40.9 33.8 %collective-permute-start.8 = (bf16[512,1024]{1,0:T(8,128)(2,1)S(1)}, bf16[512,1024]{1,0:T(8,128)(2,1)S(1)}, u32[]{:S(2)}, u32[]{:S(2)}) collective-permute-start(bf16[512,1024]{1,0:T(8,128)(2,1)S(1)} %get-tuple-element.37.refs_1_.refs_8_), channel_id=1, source_target_pairs={{16,0},{3,1},{32,16},{19,17},{48,32},{35,33},{0,48},{51,49},{18,2}... | collective-permute-start | bytes 3145736 | tf_op jit(solution)/shard_map/ppermute | solution.py:33
  41.0 35.4 %collective-permute-start.11 = (bf16[512,1024]{1,0:T(8,128)(2,1)S(1)}, bf16[512,1024]{1,0:T(8,128)(2,1)S(1)}, u32[]{:S(2)}, u32[]{:S(2)}) collective-permute-start(bf16[512,1024]{1,0:T(8,128)(2,1)S(1)} %get-tuple-element.37.refs_1_.refs_8_), channel_id=1, source_target_pairs={{48,0},{7,1},{0,16},{23,17},{16,32},{39,33},{32,48},{55,49},{50,2}... | collective-permute-start | bytes 3145736 | tf_op jit(solution)/shard_map/ppermute | solution.py:33
  42.4 35.6 %collective-permute-start.12 = (bf16[512,1024]{1,0:T(8,128)(2,1)S(1)}, bf16[512,1024]{1,0:T(8,128)(2,1)S(1)}, u32[]{:S(2)}, u32[]{:S(2)}) collective-permute-start(bf16[512,1024]{1,0:T(8,128)(2,1)S(1)} %get-tuple-element.38.refs_2_.refs_9_), channel_id=1, source_target_pairs={{48,0},{7,1},{0,16},{23,17},{16,32},{39,33},{32,48},{55,49},{50,2}... | collective-permute-start | bytes 3145736 | tf_op jit(solution)/shard_map/ppermute | solution.py:33
  52.7 28.7 %collective-permute-start.10 = (bf16[512,1024]{1,0:T(8,128)(2,1)S(1)}, bf16[512,1024]{1,0:T(8,128)(2,1)S(1)}, u32[]{:S(2)}, u32[]{:S(2)}) collective-permute-start(bf16[512,1024]{1,0:T(8,128)(2,1)S(1)} %collective-permute-done.7.refs_0_.refs_12_), channel_id=1, source_target_pairs={{8,0},{73,1},{24,16},{89,17},{40,32},{105,33},{56,48},{121,49},{10... | collective-permute-start | bytes 3145736 | tf_op jit(solution)/shard_map/ppermute | solution.py:49
  98.7 4.4 %collective-permute-start.15 = (f32[8,640]{1,0:T(8,128)S(1)}, f32[8,640]{1,0:T(8,128)S(1)}, u32[]{:S(2)}, u32[]{:S(2)}) collective-permute-start(f32[8,640]{1,0:T(8,128)S(1)} %plane.1.refs_0_), channel_id=1, source_target_pairs={{48,0},{7,1},{0,16},{23,17},{16,32},{39,33},{32,48},{55,49},{50,2}... | collective-permute-start | bytes 61448 | tf_op jit(solution)/shard_map/ppermute | solution.py:33
  100.4 4.1 %collective-permute-start.14 = (f32[8,640]{1,0:T(8,128)S(1)}, f32[8,640]{1,0:T(8,128)S(1)}, u32[]{:S(2)}, u32[]{:S(2)}) collective-permute-start(f32[8,640]{1,0:T(8,128)S(1)} %plane.1.refs_0_), channel_id=1, source_target_pairs={{32,0},{5,1},{48,16},{21,17},{0,32},{37,33},{16,48},{53,49},{34,2}... | collective-permute-start | bytes 61448 | tf_op jit(solution)/shard_map/ppermute | solution.py:33
  102.6 2.6 %collective-permute-start.13 = (f32[8,640]{1,0:T(8,128)S(1)}, f32[8,640]{1,0:T(8,128)S(1)}, u32[]{:S(2)}, u32[]{:S(2)}) collective-permute-start(f32[8,640]{1,0:T(8,128)S(1)} %plane.1.refs_0_), channel_id=1, source_target_pairs={{16,0},{3,1},{32,16},{19,17},{48,32},{35,33},{0,48},{51,49},{18,2}... | collective-permute-start | bytes 61448 | tf_op jit(solution)/shard_map/ppermute | solution.py:33
  110.8 10.4 %collective-permute-start.16 = (f32[512,1152]{1,0:T(8,128)S(1)}, f32[512,1152]{1,0:T(8,128)S(1)}, u32[]{:S(2)}, u32[]{:S(2)}) collective-permute-start(f32[512,1152]{1,0:T(8,128)S(1)} %sums.3), channel_id=1, source_target_pairs={{0,1},{1,0},{2,3},{3,2},{4,5},{5,4},{6,7},{7,6},{8,9},{9,8},{10,11... | collective-permute-start | bytes 7077896 | tf_op jit(solution)/shard_map/ppermute | solution.py:38
  115.2 4.6 %collective-permute-start.17 = (f32[64,128]{1,0:T(8,128)S(1)}, f32[64,128]{1,0:T(8,128)S(1)}, u32[]{:S(2)}, u32[]{:S(2)}) collective-permute-start(f32[64,128]{1,0:T(8,128)S(1)} %get-tuple-element.57.mine_ref), channel_id=1, source_target_pairs={{0,1},{1,0},{2,3},{3,2},{4,5},{5,4},{6,7},{7,6},{8,9},{9,8},{10,11... | collective-permute-start | bytes 98312 | tf_op jit(solution)/shard_map/ppermute | solution.py:38

commit v10 on v9

--- a/solution.py
+++ b/solution.py
@@ -316,8 +316,11 @@
     chunks = [first, second, after_first, after_second, far_first, far_second, before_first, before_second]
     swapped = (5,)
     early_ps, early_stat = score([far_first, first, second])
-    chunks[3], _ = lax.optimization_barrier((chunks[3], early_stat))
-    calls = {k: score([chunks[k]]) for k in (2, 3, 5, 6, 7)}
+    calls, last = {}, early_stat
+    for k in (3, 6, 5, 7, 2):
+        chunks[k], _ = lax.optimization_barrier((chunks[k], last))
+        calls[k] = score([chunks[k]])
+        last = calls[k][1]
     ps = early_ps[1:] + [calls[2][0][0], calls[3][0][0], early_ps[0]] + [calls[k][0][0] for k in (5, 6, 7)]
     stats = [early_stat] + [calls[k][1] for k in (2, 3, 5, 6, 7)]
     order = ((0, 1), (0, 2), (1, 0), (2, 0), (0, 0), (3, 0), (4, 0), (5, 0))

time: 123 us -> 112 us (0.911)
  waiting for transfers between devices: 43.7 us -> 27.9 us
  starting transfers between devices: 29.2 us -> 35.8 us
  blocking collectives: 14.5 us -> 12.2 us
    ppermute x14, waiting for transfers between devices: 43.7 us -> 26.9 us  [fetch(): return lax.ppermute(value, BOTH, pairs)]
    ppermute x3, starting transfers between devices: 6.59 us -> 9.2 us  [swap_cores(): return lax.ppermute(value, BOTH, pairs)]
    ppermute x14, starting transfers between devices: 20.9 us -> 23.5 us  [fetch(): return lax.ppermute(value, BOTH, pairs)]
    all_to_all x1, blocking collectives: 14.5 us -> 12.2 us  [shards(): lax.all_to_all(local, BOTH, split_axis=0, concat_axis=0, tiled=True, axis...]
    ppermute x1, starting transfers between devices: 1.69 us -> 3.17 us  [swap_sides(): return lax.ppermute(value, BOTH, pairs)]
  transfers between devices with their start and end apart: 18 -> 18, of which waited for: 9 -> 11; matrix products, arithmetic and copies ran while one was open for 1% -> 1% of each run, Pallas kernels for 14% -> 17%
where the time goes in v10:
time: 112 us; the launch traced here: 111 us
  starting transfers between devices  35.8 us (32%)
  Pallas kernels  29.5 us (26%)
  waiting for transfers between devices  27.9 us (25%)
  blocking collectives  12.2 us (11%)
  local copies, waits for them, and re-layouts  4.46 us (4%)
    ppermute x14, waiting for transfers between devices, fetch(): return lax.ppermute(value, BOTH, pairs)  26.9 us
    ppermute x14, starting transfers between devices, fetch(): return lax.ppermute(value, BOTH, pairs)  23.5 us
    pallas_call x6, Pallas kernels, scores_call(): pl.pallas_call(functools.partial(scores_kernel, factor, count), out_shape...  12.5 us
    all_to_all x1, blocking collectives, shards(): lax.all_to_all(local, BOTH, split_axis=0, concat_axis=0, tiled=True, axis...  12.2 us
    ppermute x3, starting transfers between devices, swap_cores(): return lax.ppermute(value, BOTH, pairs)  9.2 us
    pallas_call x2, Pallas kernels, sums_call(): pl.pallas_call(functools.partial(sums_kernel, half, count), out_shape=jax...  9.04 us
    unnamed x4, local copies, waits for them, and re-layouts  4.29 us
    ppermute x1, starting transfers between devices, swap_sides(): return lax.ppermute(value, BOTH, pairs)  3.17 us
  transfers between devices with their start and end apart: 18, of which 11 were waited for; matrix products, arithmetic and copies ran while one was open for 1% of the time, Pallas kernels for 17%

profile of v10, /device:TPU:1, one launch (start us, length us, event | category | flops | bytes accessed | tf_op | source)
XLA Modules:
  0.0 111.4 jit_solution(8477836544666026884)
XLA Ops:
  0.6 3.7 %collective-permute-start.1 = (bf16[64,1024]{1,0:T(8,128)(2,1)}, bf16[64,1024]{1,0:T(8,128)(2,1)S(1)}, u32[]{:S(2)}, u32[]{:S(2)}) collective-permute-start(bf16[64,1024]{1,0:T(8,128)(2,1)} %refs_0_.1), channel_id=1, source_target_pairs={{64,0},{65,1},{80,16},{81,17},{96,32},{97,33},{112,48},{113,49},{6... | collective-permute-start | bytes 393224 | tf_op jit(solution)/shard_map/ppermute | solution.py:33
  7.2 3.3 %collective-permute-done.refs_1_ = bf16[64,1024]{1,0:T(8,128)(2,1)S(1)} collective-permute-done((bf16[64,1024]{1,0:T(8,128)(2,1)}, bf16[64,1024]{1,0:T(8,128)(2,1)S(1)}, u32[]{:S(2)}, u32[]{:S(2)}) %collective-permute-start) | collective-permute-done | bytes 131104 | tf_op jit(solution)/shard_map/ppermute | solution.py:33
  11.5 1.8 %collective-permute-start.5 = (bf16[256,1024]{1,0:T(8,128)(2,1)S(1)}, bf16[256,1024]{1,0:T(8,128)(2,1)S(1)}, u32[]{:S(2)}, u32[]{:S(2)}) collective-permute-start(bf16[256,1024]{1,0:T(8,128)(2,1)S(1)} %join.1.refs_0_), channel_id=1, source_target_pairs={{6,0},{49,1},{22,16},{1,17},{38,32},{17,33},{54,48},{33,49},{0,2},... | collective-permute-start | bytes 1572872 | tf_op jit(solution)/shard_map/ppermute | solution.py:33
  13.2 3.3 %collective-permute-start.4 = (bf16[256,1024]{1,0:T(8,128)(2,1)S(1)}, bf16[256,1024]{1,0:T(8,128)(2,1)S(1)}, u32[]{:S(2)}, u32[]{:S(2)}) collective-permute-start(bf16[256,1024]{1,0:T(8,128)(2,1)S(1)} %join.1.refs_0_), channel_id=1, source_target_pairs={{4,0},{33,1},{20,16},{49,17},{36,32},{1,33},{52,48},{17,49},{6,2},... | collective-permute-start | bytes 1572872 | tf_op jit(solution)/shard_map/ppermute | solution.py:33
  17.3 5.0 %collective-permute-done.5.refs_3_ = bf16[256,1024]{1,0:T(8,128)(2,1)S(1)} collective-permute-done((bf16[256,1024]{1,0:T(8,128)(2,1)S(1)}, bf16[256,1024]{1,0:T(8,128)(2,1)S(1)}, u32[]{:S(2)}, u32[]{:S(2)}) %collective-permute-start.5) | collective-permute-done | bytes 524320 | tf_op jit(solution)/shard_map/ppermute | solution.py:33
  22.2 6.8 %collective-permute-done.4.refs_2_ = bf16[256,1024]{1,0:T(8,128)(2,1)S(1)} collective-permute-done((bf16[256,1024]{1,0:T(8,128)(2,1)S(1)}, bf16[256,1024]{1,0:T(8,128)(2,1)S(1)}, u32[]{:S(2)}, u32[]{:S(2)}) %collective-permute-start.4) | collective-permute-done | bytes 524320 | tf_op jit(solution)/shard_map/ppermute | solution.py:33
  29.7 2.7 %collective-permute-start.7 = (bf16[512,1024]{1,0:T(8,128)(2,1)S(1)}, bf16[512,1024]{1,0:T(8,128)(2,1)S(1)}, u32[]{:S(2)}, u32[]{:S(2)}) collective-permute-start(bf16[512,1024]{1,0:T(8,128)(2,1)S(1)} %get-tuple-element.41.refs_1_.refs_8_), channel_id=1, source_target_pairs={{32,0},{5,1},{48,16},{21,17},{0,32},{37,33},{16,48},{53,49},{34,2}... | collective-permute-start | bytes 3145736 | tf_op jit(solution)/shard_map/ppermute | solution.py:33
  32.4 3.4 %copy-done = bf16[4096,1024]{1,0:T(8,128)(2,1)S(1)} copy-done((bf16[4096,1024]{1,0:T(8,128)(2,1)S(1)}, bf16[4096,1024]{1,0:T(8,128)(2,1)}, u32[]{:S(2)}) %copy-start) | copy-done | bytes 8388632
  35.8 2.0 %share.1.mine_ref = bf16[512,1024]{1,0:T(8,128)(2,1)S(1)} custom-call(s32[2]{0:T(128)S(1)} %pad_add_fusion.at_ref, bf16[4096,1024]{1,0:T(8,128)(2,1)S(1)} %copy-done), custom_call_target="tpu_custom_call" | custom-call | tf_op jit(solution)/shard_map/share/pallas_call | solution.py:304
  37.8 3.3 %collective-permute-start.6 = (bf16[512,1024]{1,0:T(8,128)(2,1)S(1)}, bf16[512,1024]{1,0:T(8,128)(2,1)S(1)}, u32[]{:S(2)}, u32[]{:S(2)}) collective-permute-start(bf16[512,1024]{1,0:T(8,128)(2,1)S(1)} %share.1.mine_ref), channel_id=1, source_target_pairs={{0,1},{1,0},{2,3},{3,2},{4,5},{5,4},{6,7},{7,6},{8,9},{9,8},{10,11... | collective-permute-start | bytes 3145736 | tf_op jit(solution)/shard_map/ppermute | solution.py:38
  41.1 2.0 %collective-permute-start.12 = (bf16[512,1024]{1,0:T(8,128)(2,1)S(1)}, bf16[512,1024]{1,0:T(8,128)(2,1)S(1)}, u32[]{:S(2)}, u32[]{:S(2)}) collective-permute-start(bf16[512,1024]{1,0:T(8,128)(2,1)S(1)} %get-tuple-element.42.refs_2_.refs_9_), channel_id=1, source_target_pairs={{16,0},{3,1},{32,16},{19,17},{48,32},{35,33},{0,48},{51,49},{18,2}... | collective-permute-start | bytes 3145736 | tf_op jit(solution)/shard_map/ppermute | solution.py:33
  43.2 2.1 %collective-permute-done.7.refs_0_.refs_12_ = bf16[512,1024]{1,0:T(8,128)(2,1)S(1)} collective-permute-done((bf16[512,1024]{1,0:T(8,128)(2,1)S(1)}, bf16[512,1024]{1,0:T(8,128)(2,1)S(1)}, u32[]{:S(2)}, u32[]{:S(2)}) %collective-permute-start.7) | collective-permute-done | bytes 1048608 | tf_op jit(solution)/shard_map/ppermute | solution.py:33
  45.3 3.2 %collective-permute-start.10 = (bf16[512,1024]{1,0:T(8,128)(2,1)S(1)}, bf16[512,1024]{1,0:T(8,128)(2,1)S(1)}, u32[]{:S(2)}, u32[]{:S(2)}) collective-permute-start(bf16[512,1024]{1,0:T(8,128)(2,1)S(1)} %collective-permute-done.7.refs_0_.refs_12_), channel_id=1, source_target_pairs={{8,0},{73,1},{24,16},{89,17},{40,32},{105,33},{56,48},{121,49},{10... | collective-permute-start | bytes 3145736 | tf_op jit(solution)/shard_map/ppermute | solution.py:49
  49.5 1.6 %collective-permute-start.8 = (bf16[512,1024]{1,0:T(8,128)(2,1)S(1)}, bf16[512,1024]{1,0:T(8,128)(2,1)S(1)}, u32[]{:S(2)}, u32[]{:S(2)}) collective-permute-start(bf16[512,1024]{1,0:T(8,128)(2,1)S(1)} %get-tuple-element.41.refs_1_.refs_8_), channel_id=1, source_target_pairs={{16,0},{3,1},{32,16},{19,17},{48,32},{35,33},{0,48},{51,49},{18,2}... | collective-permute-start | bytes 3145736 | tf_op jit(solution)/shard_map/ppermute | solution.py:33
  51.1 4.3 %scores.6 = (f32[2,512,512]{2,1,0:T(8,128)S(1)}, f32[2,512,512]{2,1,0:T(8,128)S(1)}, f32[2,512,512]{2,1,0:T(8,128)S(1)}, f32[4,1536]{1,0:T(4,128)S(1)}) custom-call(bf16[512,1024]{1,0:T(8,128)(2,1)S(1)} %share.1.mine_ref, bf16[512,1024]{1,0:T(8,128)(2,1)S(1)} %collective-permute-done.6.other_ref, ...), custom_call_target="tpu_custom_call" | custom-call | flops 6442450944 | bytes 11534336 | tf_op jit(solution)/shard_map/scores/pallas_call | solution.py:85
  55.4 1.1 %collective-permute-done.12.refs_0_.refs_11_ = bf16[512,1024]{1,0:T(8,128)(2,1)S(1)} collective-permute-done((bf16[512,1024]{1,0:T(8,128)(2,1)S(1)}, bf16[512,1024]{1,0:T(8,128)(2,1)S(1)}, u32[]{:S(2)}, u32[]{:S(2)}) %collective-permute-start.12) | collective-permute-done | bytes 1048608 | tf_op jit(solution)/shard_map/ppermute | solution.py:33
  56.5 1.6 %scores.7 = (f32[2,512,512]{2,1,0:T(8,128)S(1)}, f32[4,512]{1,0:T(4,128)S(1)}) custom-call(bf16[512,1024]{1,0:T(8,128)(2,1)S(1)} %share.1.mine_ref, bf16[512,1024]{1,0:T(8,128)(2,1)S(1)} %collective-permute-done.6.other_ref, bf16[512,1024]{1,0:T(8,128)(2,1)S(1)} %collective-permute-done.12.refs_0_.refs_11_), custom_call_target="tpu_custom_call" | custom-call | flops 2147483648 | bytes 5242880 | tf_op jit(solution)/shard_map/scores/pallas_call | solution.py:85
  58.3 1.6 %scores.8 = (f32[2,512,512]{2,1,0:T(8,128)S(1)}, f32[4,512]{1,0:T(4,128)S(1)}) custom-call(bf16[512,1024]{1,0:T(8,128)(2,1)S(1)} %share.1.mine_ref, bf16[512,1024]{1,0:T(8,128)(2,1)S(1)} %collective-permute-done.6.other_ref, bf16[512,1024]{1,0:T(8,128)(2,1)S(1)} %collective-permute-done.11.refs_0_.refs_14_), custom_call_target="tpu_custom_call" | custom-call | flops 2147483648 | bytes 5242880 | tf_op jit(solution)/shard_map/scores/pallas_call | solution.py:85
  60.9 1.6 %scores.9 = (f32[2,512,512]{2,1,0:T(8,128)S(1)}, f32[4,512]{1,0:T(4,128)S(1)}) custom-call(bf16[512,1024]{1,0:T(8,128)(2,1)S(1)} %share.1.mine_ref, bf16[512,1024]{1,0:T(8,128)(2,1)S(1)} %collective-permute-done.6.other_ref, bf16[512,1024]{1,0:T(8,128)(2,1)S(1)} %collective-permute-done.10.refs_0_.refs_13_), custom_call_target="tpu_custom_call" | custom-call | flops 2147483648 | bytes 5242880 | tf_op jit(solution)/shard_map/scores/pallas_call | solution.py:85
  62.5 7.0 %collective-permute-done.9.refs_0_.refs_15_ = bf16[512,1024]{1,0:T(8,128)(2,1)S(1)} collective-permute-done((bf16[512,1024]{1,0:T(8,128)(2,1)S(1)}, bf16[512,1024]{1,0:T(8,128)(2,1)S(1)}, u32[]{:S(2)}, u32[]{:S(2)}) %collective-permute-start.9) | collective-permute-done | bytes 1048608 | tf_op jit(solution)/shard_map/ppermute | solution.py:33
  69.5 1.6 %scores.10 = (f32[2,512,512]{2,1,0:T(8,128)S(1)}, f32[4,512]{1,0:T(4,128)S(1)}) custom-call(bf16[512,1024]{1,0:T(8,128)(2,1)S(1)} %share.1.mine_ref, bf16[512,1024]{1,0:T(8,128)(2,1)S(1)} %collective-permute-done.6.other_ref, bf16[512,1024]{1,0:T(8,128)(2,1)S(1)} %collective-permute-done.9.refs_0_.refs_15_), custom_call_target="tpu_custom_call" | custom-call | flops 2147483648 | bytes 5242880 | tf_op jit(solution)/shard_map/scores/pallas_call | solution.py:85
  71.2 1.6 %scores.11 = (f32[2,512,512]{2,1,0:T(8,128)S(1)}, f32[4,512]{1,0:T(4,128)S(1)}) custom-call(bf16[512,1024]{1,0:T(8,128)(2,1)S(1)} %share.1.mine_ref, bf16[512,1024]{1,0:T(8,128)(2,1)S(1)} %collective-permute-done.6.other_ref, bf16[512,1024]{1,0:T(8,128)(2,1)S(1)} %collective-permute-done.8.refs_0_.refs_10_), custom_call_target="tpu_custom_call" | custom-call | flops 2147483648 | bytes 5242880 | tf_op jit(solution)/shard_map/scores/pallas_call | solution.py:85
  72.8 1.1 first.1
  73.9 12.2 %all_to_all.5.all_ref = f32[16,8,640]{2,1,0:T(8,128)S(1)} all-to-all(f32[16,8,640]{2,1,0:T(8,128)S(1)} %get-tuple-element.54), channel_id=1, replica_groups={{0,8,64,72,2,10,66,74,4,12,68,76,6,14,70,78},{16,24,80,88,18,26,82,90,2..., dimensions={0} | all-to-all | bytes 655360 | tf_op jit(solution)/shard_map/all_to_all | solution.py:340
  86.3 1.6 %collective-permute-start.15 = (f32[8,640]{1,0:T(8,128)S(1)}, f32[8,640]{1,0:T(8,128)S(1)}, u32[]{:S(2)}, u32[]{:S(2)}) collective-permute-start(f32[8,640]{1,0:T(8,128)S(1)} %plane.1.refs_0_), channel_id=1, source_target_pairs={{48,0},{7,1},{0,16},{23,17},{16,32},{39,33},{32,48},{55,49},{50,2}... | collective-permute-start | bytes 61448 | tf_op jit(solution)/shard_map/ppermute | solution.py:33
  87.9 1.6 %collective-permute-start.14 = (f32[8,640]{1,0:T(8,128)S(1)}, f32[8,640]{1,0:T(8,128)S(1)}, u32[]{:S(2)}, u32[]{:S(2)}) collective-permute-start(f32[8,640]{1,0:T(8,128)S(1)} %plane.1.refs_0_), channel_id=1, source_target_pairs={{32,0},{5,1},{48,16},{21,17},{0,32},{37,33},{16,48},{53,49},{34,2}... | collective-permute-start | bytes 61448 | tf_op jit(solution)/shard_map/ppermute | solution.py:33
  89.4 2.0 %collective-permute-start.13 = (f32[8,640]{1,0:T(8,128)S(1)}, f32[8,640]{1,0:T(8,128)S(1)}, u32[]{:S(2)}, u32[]{:S(2)}) collective-permute-start(f32[8,640]{1,0:T(8,128)S(1)} %plane.1.refs_0_), channel_id=1, source_target_pairs={{16,0},{3,1},{32,16},{19,17},{48,32},{35,33},{0,48},{51,49},{18,2}... | collective-permute-start | bytes 61448 | tf_op jit(solution)/shard_map/ppermute | solution.py:33
  93.4 4.5 %sums.3 = f32[512,1152]{1,0:T(8,128)S(1)} custom-call(f32[1,4096]{1,0:T(1,128)S(1)} %get-tuple-element.55.lse_ref, f32[2,4096]{1,0:T(2,128)S(1)} %get-tuple-element.56.top_ref, f32[2,512,512]{2,1,0:T(8,128)S(1)} %get-tuple-element.57.refs_0_, f32[2,512,512]{2,1,0:T(8,128)S(1)} %get-tuple-element.58.refs_1_, f32[2,512,512]{2,1,0:T(8,128)S(1)} %get-tuple-element.59.refs_2_, ...), custom_call_target="tpu_custom_call" | custom-call | flops 4294967296 | bytes 18874368 | tf_op jit(solution)/shard_map/sums/pallas_call | solution.py:238
  97.9 5.8 %collective-permute-start.16 = (f32[512,1152]{1,0:T(8,128)S(1)}, f32[512,1152]{1,0:T(8,128)S(1)}, u32[]{:S(2)}, u32[]{:S(2)}) collective-permute-start(f32[512,1152]{1,0:T(8,128)S(1)} %sums.3), channel_id=1, source_target_pairs={{0,1},{1,0},{2,3},{3,2},{4,5},{5,4},{6,7},{7,6},{8,9},{9,8},{10,11... | collective-permute-start | bytes 7077896 | tf_op jit(solution)/shard_map/ppermute | solution.py:38
  103.8 4.5 %sums.2.ours_ref = f32[512,1152]{1,0:T(8,128)S(1)} custom-call(f32[1,4096]{1,0:T(1,128)S(1)} %get-tuple-element.55.lse_ref, f32[2,4096]{1,0:T(2,128)S(1)} %get-tuple-element.56.top_ref, f32[2,512,512]{2,1,0:T(8,128)S(1)} %get-tuple-element.57.refs_0_, f32[2,512,512]{2,1,0:T(8,128)S(1)} %get-tuple-element.58.refs_1_, ...), custom_call_target="tpu_custom_call" | custom-call | flops 4294967296 | bytes 18874368 | tf_op jit(solution)/shard_map/sums/pallas_call | solution.py:238
  108.3 1.4 %route.1 = f32[1,64]{1,0:T(1,128)} custom-call(s32[2]{0:T(128)S(1)} %pad_add_fusion.at_ref, f32[64,128]{1,0:T(8,128)S(1)} %get-tuple-element.65.mine_ref, f32[64,128]{1,0:T(8,128)S(1)} %collective-permute-done.17.other_ref), custom_call_target="tpu_custom_call" | custom-call | tf_op jit(solution)/shard_map/route/pallas_call | solution.py:363
  109.7 1.7 %final.1 = f32[512,1024]{1,0:T(8,128)} custom-call(f32[512,1152]{1,0:T(8,128)S(1)} %sums.2.ours_ref, f32[512,1152]{1,0:T(8,128)S(1)} %collective-permute-done.16.theirs_ref, bf16[512,1024]{1,0:T(8,128)(2,1)S(1)} %share.1.mine_ref), custom_call_target="tpu_custom_call" | custom-call | tf_op jit(solution)/shard_map/final/pallas_call | solution.py:370
  (30 shorter events, 9.6 us)
Async XLA Ops:
  0.6 6.6 %collective-permute-start.1 = (bf16[64,1024]{1,0:T(8,128)(2,1)}, bf16[64,1024]{1,0:T(8,128)(2,1)S(1)}, u32[]{:S(2)}, u32[]{:S(2)}) collective-permute-start(bf16[64,1024]{1,0:T(8,128)(2,1)} %refs_0_.1), channel_id=1, source_target_pairs={{64,0},{65,1},{80,16},{81,17},{96,32},{97,33},{112,48},{113,49},{6... | collective-permute-start | bytes 393224 | tf_op jit(solution)/shard_map/ppermute | solution.py:33
  4.3 6.2 %collective-permute-start = (bf16[64,1024]{1,0:T(8,128)(2,1)}, bf16[64,1024]{1,0:T(8,128)(2,1)S(1)}, u32[]{:S(2)}, u32[]{:S(2)}) collective-permute-start(bf16[64,1024]{1,0:T(8,128)(2,1)} %refs_0_.1), channel_id=1, source_target_pairs={{8,0},{9,1},{24,16},{25,17},{40,32},{41,33},{56,48},{57,49},{10,2}... | collective-permute-start | bytes 393224 | tf_op jit(solution)/shard_map/ppermute | solution.py:33
  5.1 5.4 %collective-permute-start.2 = (bf16[64,1024]{1,0:T(8,128)(2,1)}, bf16[64,1024]{1,0:T(8,128)(2,1)S(1)}, u32[]{:S(2)}, u32[]{:S(2)}) collective-permute-start(bf16[64,1024]{1,0:T(8,128)(2,1)} %refs_0_.1), channel_id=1, source_target_pairs={{72,0},{73,1},{88,16},{89,17},{104,32},{105,33},{120,48},{121,49},... | collective-permute-start | bytes 393224 | tf_op jit(solution)/shard_map/ppermute | solution.py:33
  10.5 0.9 copy-start.1
  11.5 10.8 %collective-permute-start.5 = (bf16[256,1024]{1,0:T(8,128)(2,1)S(1)}, bf16[256,1024]{1,0:T(8,128)(2,1)S(1)}, u32[]{:S(2)}, u32[]{:S(2)}) collective-permute-start(bf16[256,1024]{1,0:T(8,128)(2,1)S(1)} %join.1.refs_0_), channel_id=1, source_target_pairs={{6,0},{49,1},{22,16},{1,17},{38,32},{17,33},{54,48},{33,49},{0,2},... | collective-permute-start | bytes 1572872 | tf_op jit(solution)/shard_map/ppermute | solution.py:33
  13.2 15.8 %collective-permute-start.4 = (bf16[256,1024]{1,0:T(8,128)(2,1)S(1)}, bf16[256,1024]{1,0:T(8,128)(2,1)S(1)}, u32[]{:S(2)}, u32[]{:S(2)}) collective-permute-start(bf16[256,1024]{1,0:T(8,128)(2,1)S(1)} %join.1.refs_0_), channel_id=1, source_target_pairs={{4,0},{33,1},{20,16},{49,17},{36,32},{1,33},{52,48},{17,49},{6,2},... | collective-permute-start | bytes 1572872 | tf_op jit(solution)/shard_map/ppermute | solution.py:33
  16.5 12.5 %collective-permute-start.3 = (bf16[256,1024]{1,0:T(8,128)(2,1)S(1)}, bf16[256,1024]{1,0:T(8,128)(2,1)S(1)}, u32[]{:S(2)}, u32[]{:S(2)}) collective-permute-start(bf16[256,1024]{1,0:T(8,128)(2,1)S(1)} %join.1.refs_0_), channel_id=1, source_target_pairs={{2,0},{17,1},{18,16},{33,17},{34,32},{49,33},{50,48},{1,49},{4,2},... | collective-permute-start | bytes 1572872 | tf_op jit(solution)/shard_map/ppermute | solution.py:33
  29.7 15.5 %collective-permute-start.7 = (bf16[512,1024]{1,0:T(8,128)(2,1)S(1)}, bf16[512,1024]{1,0:T(8,128)(2,1)S(1)}, u32[]{:S(2)}, u32[]{:S(2)}) collective-permute-start(bf16[512,1024]{1,0:T(8,128)(2,1)S(1)} %get-tuple-element.41.refs_1_.refs_8_), channel_id=1, source_target_pairs={{32,0},{5,1},{48,16},{21,17},{0,32},{37,33},{16,48},{53,49},{34,2}... | collective-permute-start | bytes 3145736 | tf_op jit(solution)/shard_map/ppermute | solution.py:33
  32.4 3.4 %copy-start = (bf16[4096,1024]{1,0:T(8,128)(2,1)S(1)}, bf16[4096,1024]{1,0:T(8,128)(2,1)}, u32[]{:S(2)}) copy-start(bf16[4096,1024]{1,0:T(8,128)(2,1)} %cents_ref.1) | copy-start | bytes 25165828
  37.8 11.7 %collective-permute-start.6 = (bf16[512,1024]{1,0:T(8,128)(2,1)S(1)}, bf16[512,1024]{1,0:T(8,128)(2,1)S(1)}, u32[]{:S(2)}, u32[]{:S(2)}) collective-permute-start(bf16[512,1024]{1,0:T(8,128)(2,1)S(1)} %share.1.mine_ref), channel_id=1, source_target_pairs={{0,1},{1,0},{2,3},{3,2},{4,5},{5,4},{6,7},{7,6},{8,9},{9,8},{10,11... | collective-permute-start | bytes 3145736 | tf_op jit(solution)/shard_map/ppermute | solution.py:38
  41.1 15.4 %collective-permute-start.12 = (bf16[512,1024]{1,0:T(8,128)(2,1)S(1)}, bf16[512,1024]{1,0:T(8,128)(2,1)S(1)}, u32[]{:S(2)}, u32[]{:S(2)}) collective-permute-start(bf16[512,1024]{1,0:T(8,128)(2,1)S(1)} %get-tuple-element.42.refs_2_.refs_9_), channel_id=1, source_target_pairs={{16,0},{3,1},{32,16},{19,17},{48,32},{35,33},{0,48},{51,49},{18,2}... | collective-permute-start | bytes 3145736 | tf_op jit(solution)/shard_map/ppermute | solution.py:33
  43.1 15.2 %collective-permute-start.11 = (bf16[512,1024]{1,0:T(8,128)(2,1)S(1)}, bf16[512,1024]{1,0:T(8,128)(2,1)S(1)}, u32[]{:S(2)}, u32[]{:S(2)}) collective-permute-start(bf16[512,1024]{1,0:T(8,128)(2,1)S(1)} %get-tuple-element.41.refs_1_.refs_8_), channel_id=1, source_target_pairs={{48,0},{7,1},{0,16},{23,17},{16,32},{39,33},{32,48},{55,49},{50,2}... | collective-permute-start | bytes 3145736 | tf_op jit(solution)/shard_map/ppermute | solution.py:33
  45.3 15.7 %collective-permute-start.10 = (bf16[512,1024]{1,0:T(8,128)(2,1)S(1)}, bf16[512,1024]{1,0:T(8,128)(2,1)S(1)}, u32[]{:S(2)}, u32[]{:S(2)}) collective-permute-start(bf16[512,1024]{1,0:T(8,128)(2,1)S(1)} %collective-permute-done.7.refs_0_.refs_12_), channel_id=1, source_target_pairs={{8,0},{73,1},{24,16},{89,17},{40,32},{105,33},{56,48},{121,49},{10... | collective-permute-start | bytes 3145736 | tf_op jit(solution)/shard_map/ppermute | solution.py:49
  48.4 21.1 %collective-permute-start.9 = (bf16[512,1024]{1,0:T(8,128)(2,1)S(1)}, bf16[512,1024]{1,0:T(8,128)(2,1)S(1)}, u32[]{:S(2)}, u32[]{:S(2)}) collective-permute-start(bf16[512,1024]{1,0:T(8,128)(2,1)S(1)} %get-tuple-element.42.refs_2_.refs_9_), channel_id=1, source_target_pairs={{48,0},{7,1},{0,16},{23,17},{16,32},{39,33},{32,48},{55,49},{50,2}... | collective-permute-start | bytes 3145736 | tf_op jit(solution)/shard_map/ppermute | solution.py:33
  49.5 21.7 %collective-permute-start.8 = (bf16[512,1024]{1,0:T(8,128)(2,1)S(1)}, bf16[512,1024]{1,0:T(8,128)(2,1)S(1)}, u32[]{:S(2)}, u32[]{:S(2)}) collective-permute-start(bf16[512,1024]{1,0:T(8,128)(2,1)S(1)} %get-tuple-element.41.refs_1_.refs_8_), channel_id=1, source_target_pairs={{16,0},{3,1},{32,16},{19,17},{48,32},{35,33},{0,48},{51,49},{18,2}... | collective-permute-start | bytes 3145736 | tf_op jit(solution)/shard_map/ppermute | solution.py:33
  86.3 5.2 %collective-permute-start.15 = (f32[8,640]{1,0:T(8,128)S(1)}, f32[8,640]{1,0:T(8,128)S(1)}, u32[]{:S(2)}, u32[]{:S(2)}) collective-permute-start(f32[8,640]{1,0:T(8,128)S(1)} %plane.1.refs_0_), channel_id=1, source_target_pairs={{48,0},{7,1},{0,16},{23,17},{16,32},{39,33},{32,48},{55,49},{50,2}... | collective-permute-start | bytes 61448 | tf_op jit(solution)/shard_map/ppermute | solution.py:33
  87.9 4.1 %collective-permute-start.14 = (f32[8,640]{1,0:T(8,128)S(1)}, f32[8,640]{1,0:T(8,128)S(1)}, u32[]{:S(2)}, u32[]{:S(2)}) collective-permute-start(f32[8,640]{1,0:T(8,128)S(1)} %plane.1.refs_0_), channel_id=1, source_target_pairs={{32,0},{5,1},{48,16},{21,17},{0,32},{37,33},{16,48},{53,49},{34,2}... | collective-permute-start | bytes 61448 | tf_op jit(solution)/shard_map/ppermute | solution.py:33
  89.4 2.9 %collective-permute-start.13 = (f32[8,640]{1,0:T(8,128)S(1)}, f32[8,640]{1,0:T(8,128)S(1)}, u32[]{:S(2)}, u32[]{:S(2)}) collective-permute-start(f32[8,640]{1,0:T(8,128)S(1)} %plane.1.refs_0_), channel_id=1, source_target_pairs={{16,0},{3,1},{32,16},{19,17},{48,32},{35,33},{0,48},{51,49},{18,2}... | collective-permute-start | bytes 61448 | tf_op jit(solution)/shard_map/ppermute | solution.py:33
  97.9 11.8 %collective-permute-start.16 = (f32[512,1152]{1,0:T(8,128)S(1)}, f32[512,1152]{1,0:T(8,128)S(1)}, u32[]{:S(2)}, u32[]{:S(2)}) collective-permute-start(f32[512,1152]{1,0:T(8,128)S(1)} %sums.3), channel_id=1, source_target_pairs={{0,1},{1,0},{2,3},{3,2},{4,5},{5,4},{6,7},{7,6},{8,9},{9,8},{10,11... | collective-permute-start | bytes 7077896 | tf_op jit(solution)/shard_map/ppermute | solution.py:38
  103.7 4.6 %collective-permute-start.17 = (f32[64,128]{1,0:T(8,128)S(1)}, f32[64,128]{1,0:T(8,128)S(1)}, u32[]{:S(2)}, u32[]{:S(2)}) collective-permute-start(f32[64,128]{1,0:T(8,128)S(1)} %get-tuple-element.65.mine_ref), channel_id=1, source_target_pairs={{0,1},{1,0},{2,3},{3,2},{4,5},{5,4},{6,7},{7,6},{8,9},{9,8},{10,11... | collective-permute-start | bytes 98312 | tf_op jit(solution)/shard_map/ppermute | solution.py:38

commit v11 on v10

--- a/solution.py
+++ b/solution.py
@@ -163,11 +163,12 @@
 def route_kernel(at_ref, mine_ref, other_ref, out_ref):
     first = (at_ref[0] * 16 + at_ref[1]) * UNIT
     rows = (lax.broadcasted_iota(jnp.int32, (UNIT, 128), 0) + first).astype(jnp.float32)
-    total = jnp.zeros((UNIT, 128), jnp.float32)
+    totals = [jnp.zeros((UNIT, 128), jnp.float32)] * 4
     for ref in (mine_ref, other_ref):
         for line in range(32):
             hit = ref[32 + line : 33 + line, :] == rows
-            total = total + jnp.where(hit, ref[line : line + 1, :], 0.0)
+            totals[line % 4] = totals[line % 4] + jnp.where(hit, ref[line : line + 1, :], 0.0)
+    total = (totals[0] + totals[1]) + (totals[2] + totals[3])
     out_ref[...] = jnp.sum(total.T, axis=0, keepdims=True) * math.log(2.0)
 
 
@@ -241,17 +242,40 @@
         in_specs=[vmem] * (2 + 2 * count),
         compiler_params=pltpu.CompilerParams(vmem_limit_bytes=12 << 20),
         cost_estimate=pl.CostEstimate(
-            flops=2 * 512 * 4096 * width, bytes_accessed=18 << 20, transcendentals=8192
+            flops=2 * 512 * 512 * count * width, bytes_accessed=18 << 20, transcendentals=8192
         ),
         name="sums",
     )(lse, tops, *ps, *rows)
 
 
-def final_kernel(ours_ref, theirs_ref, mine_ref, out_ref):
-    width = out_ref.shape[1]
-    mass = jnp.sum(ours_ref[:, width:] + theirs_ref[:, width:], axis=1, keepdims=True) + prior_mass
-    total = ours_ref[:, :width] + theirs_ref[:, :width] + prior_mass * mine_ref[...].astype(jnp.float32)
-    out_ref[...] = total * (1.0 / mass)
+def final_kernel(skip, count, lse_ref, top_ref, ours_ref, theirs_ref, mine_ref, *refs):
+    ps = refs[:count]
+    rows = refs[count : 2 * count]
+    out_ref, buf, sems = refs[2 * count :]
+    n, width = rows[0].shape
+    mass = ours_ref[:, width:] + theirs_ref[:, width:]
+    ws = []
+    for k in range(count):
+        lanes = slice((skip + k) * n, (skip + k + 1) * n)
+        f = jnp.exp2(top_ref[0:1, lanes] - lse_ref[:, lanes])
+        w = (ps[k][0] * f).astype(jnp.bfloat16)
+        wide = w.astype(jnp.float32)
+        mass = mass + sum(wide[:, c : c + 128] for c in range(0, n, 128))
+        ws.append(w)
+    inverse = 1.0 / (jnp.sum(mass, axis=1, keepdims=True) + prior_mass)
+    copies = []
+    for block in range(4):
+        columns = slice(block * width // 4, (block + 1) * width // 4)
+        total = ours_ref[:, columns] + theirs_ref[:, columns]
+        total = total + prior_mass * mine_ref[:, columns].astype(jnp.float32)
+        for k in range(count):
+            total = total + jnp.dot(ws[k], rows[k][:, columns], preferred_element_type=jnp.float32)
+        buf[:, columns] = total * inverse
+        copy = pltpu.make_async_copy(buf.at[:, columns], out_ref.at[:, columns], sems.at[block])
+        copy.start()
+        copies.append(copy)
+    for copy in copies:
+        copy.wait()
 
 
 def share_kernel(at_ref, cents_ref, out_ref, sem):
@@ -359,7 +383,7 @@
     theirs = sums_call(1, lse, tops, ps, chunks)
     received = swap_cores(theirs)
     partner = swap_cores(pack)
-    ours = sums_call(0, lse, tops, ps, chunks)
+    ours = sums_call(0, lse, tops, ps[:6], chunks[:6])
     row_lse = pl.pallas_call(
         route_kernel,
         out_shape=jax.ShapeDtypeStruct((1, UNIT), jnp.float32),
@@ -368,9 +392,14 @@
         name="route",
     )(at_word, pack, partner)
     new_centers = pl.pallas_call(
-        final_kernel, out_shape=jax.ShapeDtypeStruct((share, width), jnp.float32), name="final",
-        compiler_params=pltpu.CompilerParams(vmem_limit_bytes=8 << 20),
-    )(ours, received, mine)
+        functools.partial(final_kernel, 6, 2),
+        out_shape=jax.ShapeDtypeStruct((share, width), jnp.float32),
+        in_specs=[vmem] * 9,
+        out_specs=pl.BlockSpec(memory_space=pl.ANY),
+        scratch_shapes=[pltpu.VMEM((share, width), jnp.float32), pltpu.SemaphoreType.DMA((4,))],
+        compiler_params=pltpu.CompilerParams(vmem_limit_bytes=12 << 20),
+        name="final",
+    )(lse, tops, ours, received, mine, *ps[6:], *chunks[6:])
     return new_centers, row_lse.reshape(UNIT)
 
 

time: 112 us -> 112 us (level)
  transfers between devices with their start and end apart: 18 -> 18, of which waited for: 11 -> 12; matrix products, arithmetic and copies ran while one was open for 1% -> 1% of each run, Pallas kernels for 17% -> 16%
where the time goes in v11:
time: 112 us
  starting transfers between devices  35.8 us (32%)
  Pallas kernels  29.2 us (26%)
  waiting for transfers between devices  28.5 us (25%)
  blocking collectives  12.3 us (11%)
  local copies, waits for them, and re-layouts  4.46 us (4%)
    ppermute x14, waiting for transfers between devices, fetch(): return lax.ppermute(value, BOTH, pairs)  26.9 us
    ppermute x14, starting transfers between devices, fetch(): return lax.ppermute(value, BOTH, pairs)  23.5 us
    pallas_call x6, Pallas kernels, scores_call(): pl.pallas_call(functools.partial(scores_kernel, factor, count), out_shape...  12.5 us
    all_to_all x1, blocking collectives, shards(): lax.all_to_all(local, BOTH, split_axis=0, concat_axis=0, tiled=True, axis...  12.3 us
    ppermute x3, starting transfers between devices, swap_cores(): return lax.ppermute(value, BOTH, pairs)  9.21 us
    pallas_call x2, Pallas kernels, sums_call(): pl.pallas_call(functools.partial(sums_kernel, half, count), out_shape=jax...  7.94 us
    unnamed x4, local copies, waits for them, and re-layouts  4.29 us
    ppermute x1, starting transfers between devices, swap_sides(): return lax.ppermute(value, BOTH, pairs)  3.17 us
  transfers between devices with their start and end apart: 18, of which 12 were waited for; matrix products, arithmetic and copies ran while one was open for 1% of the time, Pallas kernels for 16%

profile of v11, /device:TPU:1, one launch (start us, length us, event | category | flops | bytes accessed | tf_op | source)
XLA Modules:
  0.0 111.9 jit_solution(12605988709719578144)
XLA Ops:
  0.6 3.7 %collective-permute-start.1 = (bf16[64,1024]{1,0:T(8,128)(2,1)}, bf16[64,1024]{1,0:T(8,128)(2,1)S(1)}, u32[]{:S(2)}, u32[]{:S(2)}) collective-permute-start(bf16[64,1024]{1,0:T(8,128)(2,1)} %refs_0_.1), channel_id=1, source_target_pairs={{64,0},{65,1},{80,16},{81,17},{96,32},{97,33},{112,48},{113,49},{6... | collective-permute-start | bytes 393224 | tf_op jit(solution)/shard_map/ppermute | solution.py:33
  7.2 3.3 %collective-permute-done.refs_1_ = bf16[64,1024]{1,0:T(8,128)(2,1)S(1)} collective-permute-done((bf16[64,1024]{1,0:T(8,128)(2,1)}, bf16[64,1024]{1,0:T(8,128)(2,1)S(1)}, u32[]{:S(2)}, u32[]{:S(2)}) %collective-permute-start) | collective-permute-done | bytes 131104 | tf_op jit(solution)/shard_map/ppermute | solution.py:33
  11.5 1.8 %collective-permute-start.5 = (bf16[256,1024]{1,0:T(8,128)(2,1)S(1)}, bf16[256,1024]{1,0:T(8,128)(2,1)S(1)}, u32[]{:S(2)}, u32[]{:S(2)}) collective-permute-start(bf16[256,1024]{1,0:T(8,128)(2,1)S(1)} %join.1.refs_0_), channel_id=1, source_target_pairs={{6,0},{49,1},{22,16},{1,17},{38,32},{17,33},{54,48},{33,49},{0,2},... | collective-permute-start | bytes 1572872 | tf_op jit(solution)/shard_map/ppermute | solution.py:33
  13.2 3.3 %collective-permute-start.4 = (bf16[256,1024]{1,0:T(8,128)(2,1)S(1)}, bf16[256,1024]{1,0:T(8,128)(2,1)S(1)}, u32[]{:S(2)}, u32[]{:S(2)}) collective-permute-start(bf16[256,1024]{1,0:T(8,128)(2,1)S(1)} %join.1.refs_0_), channel_id=1, source_target_pairs={{4,0},{33,1},{20,16},{49,17},{36,32},{1,33},{52,48},{17,49},{6,2},... | collective-permute-start | bytes 1572872 | tf_op jit(solution)/shard_map/ppermute | solution.py:33
  17.3 5.0 %collective-permute-done.5.refs_3_ = bf16[256,1024]{1,0:T(8,128)(2,1)S(1)} collective-permute-done((bf16[256,1024]{1,0:T(8,128)(2,1)S(1)}, bf16[256,1024]{1,0:T(8,128)(2,1)S(1)}, u32[]{:S(2)}, u32[]{:S(2)}) %collective-permute-start.5) | collective-permute-done | bytes 524320 | tf_op jit(solution)/shard_map/ppermute | solution.py:33
  22.2 6.8 %collective-permute-done.4.refs_2_ = bf16[256,1024]{1,0:T(8,128)(2,1)S(1)} collective-permute-done((bf16[256,1024]{1,0:T(8,128)(2,1)S(1)}, bf16[256,1024]{1,0:T(8,128)(2,1)S(1)}, u32[]{:S(2)}, u32[]{:S(2)}) %collective-permute-start.4) | collective-permute-done | bytes 524320 | tf_op jit(solution)/shard_map/ppermute | solution.py:33
  29.7 2.7 %collective-permute-start.7 = (bf16[512,1024]{1,0:T(8,128)(2,1)S(1)}, bf16[512,1024]{1,0:T(8,128)(2,1)S(1)}, u32[]{:S(2)}, u32[]{:S(2)}) collective-permute-start(bf16[512,1024]{1,0:T(8,128)(2,1)S(1)} %get-tuple-element.41.refs_1_.refs_6_.refs_8_), channel_id=1, source_target_pairs={{32,0},{5,1},{48,16},{21,17},{0,32},{37,33},{16,48},{53,49},{34,2}... | collective-permute-start | bytes 3145736 | tf_op jit(solution)/shard_map/ppermute | solution.py:33
  32.4 3.4 %copy-done = bf16[4096,1024]{1,0:T(8,128)(2,1)S(1)} copy-done((bf16[4096,1024]{1,0:T(8,128)(2,1)S(1)}, bf16[4096,1024]{1,0:T(8,128)(2,1)}, u32[]{:S(2)}) %copy-start) | copy-done | bytes 8388632
  35.8 2.0 %share.1.mine_ref = bf16[512,1024]{1,0:T(8,128)(2,1)S(1)} custom-call(s32[2]{0:T(128)S(1)} %pad_add_fusion.at_ref, bf16[4096,1024]{1,0:T(8,128)(2,1)S(1)} %copy-done), custom_call_target="tpu_custom_call" | custom-call | tf_op jit(solution)/shard_map/share/pallas_call | solution.py:328
  37.8 3.3 %collective-permute-start.6 = (bf16[512,1024]{1,0:T(8,128)(2,1)S(1)}, bf16[512,1024]{1,0:T(8,128)(2,1)S(1)}, u32[]{:S(2)}, u32[]{:S(2)}) collective-permute-start(bf16[512,1024]{1,0:T(8,128)(2,1)S(1)} %share.1.mine_ref), channel_id=1, source_target_pairs={{0,1},{1,0},{2,3},{3,2},{4,5},{5,4},{6,7},{7,6},{8,9},{9,8},{10,11... | collective-permute-start | bytes 3145736 | tf_op jit(solution)/shard_map/ppermute | solution.py:38
  41.1 2.0 %collective-permute-start.12 = (bf16[512,1024]{1,0:T(8,128)(2,1)S(1)}, bf16[512,1024]{1,0:T(8,128)(2,1)S(1)}, u32[]{:S(2)}, u32[]{:S(2)}) collective-permute-start(bf16[512,1024]{1,0:T(8,128)(2,1)S(1)} %get-tuple-element.42.refs_2_.refs_7_.refs_9_), channel_id=1, source_target_pairs={{16,0},{3,1},{32,16},{19,17},{48,32},{35,33},{0,48},{51,49},{18,2}... | collective-permute-start | bytes 3145736 | tf_op jit(solution)/shard_map/ppermute | solution.py:33
  43.2 2.1 %collective-permute-done.7.refs_0_.refs_10_.refs_12_ = bf16[512,1024]{1,0:T(8,128)(2,1)S(1)} collective-permute-done((bf16[512,1024]{1,0:T(8,128)(2,1)S(1)}, bf16[512,1024]{1,0:T(8,128)(2,1)S(1)}, u32[]{:S(2)}, u32[]{:S(2)}) %collective-permute-start.7) | collective-permute-done | bytes 1048608 | tf_op jit(solution)/shard_map/ppermute | solution.py:33
  45.3 3.2 %collective-permute-start.10 = (bf16[512,1024]{1,0:T(8,128)(2,1)S(1)}, bf16[512,1024]{1,0:T(8,128)(2,1)S(1)}, u32[]{:S(2)}, u32[]{:S(2)}) collective-permute-start(bf16[512,1024]{1,0:T(8,128)(2,1)S(1)} %collective-permute-done.7.refs_0_.refs_10_.refs_12_), channel_id=1, source_target_pairs={{8,0},{73,1},{24,16},{89,17},{40,32},{105,33},{56,48},{121,49},{10... | collective-permute-start | bytes 3145736 | tf_op jit(solution)/shard_map/ppermute | solution.py:49
  49.5 1.6 %collective-permute-start.8 = (bf16[512,1024]{1,0:T(8,128)(2,1)S(1)}, bf16[512,1024]{1,0:T(8,128)(2,1)S(1)}, u32[]{:S(2)}, u32[]{:S(2)}) collective-permute-start(bf16[512,1024]{1,0:T(8,128)(2,1)S(1)} %get-tuple-element.41.refs_1_.refs_6_.refs_8_), channel_id=1, source_target_pairs={{16,0},{3,1},{32,16},{19,17},{48,32},{35,33},{0,48},{51,49},{18,2}... | collective-permute-start | bytes 3145736 | tf_op jit(solution)/shard_map/ppermute | solution.py:33
  51.1 4.3 %scores.6 = (f32[2,512,512]{2,1,0:T(8,128)S(1)}, f32[2,512,512]{2,1,0:T(8,128)S(1)}, f32[2,512,512]{2,1,0:T(8,128)S(1)}, f32[4,1536]{1,0:T(4,128)S(1)}) custom-call(bf16[512,1024]{1,0:T(8,128)(2,1)S(1)} %share.1.mine_ref, bf16[512,1024]{1,0:T(8,128)(2,1)S(1)} %collective-permute-done.6.other_ref, ...), custom_call_target="tpu_custom_call" | custom-call | flops 6442450944 | bytes 11534336 | tf_op jit(solution)/shard_map/scores/pallas_call | solution.py:85
  55.4 1.1 collective-permute-done.12.refs_0_.refs_9_.refs_11_
  56.5 1.6 %scores.7 = (f32[2,512,512]{2,1,0:T(8,128)S(1)}, f32[4,512]{1,0:T(4,128)S(1)}) custom-call(bf16[512,1024]{1,0:T(8,128)(2,1)S(1)} %share.1.mine_ref, bf16[512,1024]{1,0:T(8,128)(2,1)S(1)} %collective-permute-done.6.other_ref, bf16[512,1024]{1,0:T(8,128)(2,1)S(1)} %collective-permute-done.12.refs_0_.refs_9_.refs_11_), custom_call_target="tpu_custom_call" | custom-call | flops 2147483648 | bytes 5242880 | tf_op jit(solution)/shard_map/scores/pallas_call | solution.py:85
  58.3 1.6 %scores.8 = (f32[2,512,512]{2,1,0:T(8,128)S(1)}, f32[4,512]{1,0:T(4,128)S(1)}) custom-call(bf16[512,1024]{1,0:T(8,128)(2,1)S(1)} %share.1.mine_ref, bf16[512,1024]{1,0:T(8,128)(2,1)S(1)} %collective-permute-done.6.other_ref, bf16[512,1024]{1,0:T(8,128)(2,1)S(1)} %collective-permute-done.11.refs_0_.refs_14_.refs_2_), custom_call_target="tpu_custom_call" | custom-call | flops 2147483648 | bytes 5242880 | tf_op jit(solution)/shard_map/scores/pallas_call | solution.py:85
  60.9 1.6 %scores.9 = (f32[2,512,512]{2,1,0:T(8,128)S(1)}, f32[4,512]{1,0:T(4,128)S(1)}) custom-call(bf16[512,1024]{1,0:T(8,128)(2,1)S(1)} %share.1.mine_ref, bf16[512,1024]{1,0:T(8,128)(2,1)S(1)} %collective-permute-done.6.other_ref, bf16[512,1024]{1,0:T(8,128)(2,1)S(1)} %collective-permute-done.10.refs_0_.refs_11_.refs_13_), custom_call_target="tpu_custom_call" | custom-call | flops 2147483648 | bytes 5242880 | tf_op jit(solution)/shard_map/scores/pallas_call | solution.py:85
  62.5 7.0 %collective-permute-done.9.refs_0_.refs_15_.refs_3_ = bf16[512,1024]{1,0:T(8,128)(2,1)S(1)} collective-permute-done((bf16[512,1024]{1,0:T(8,128)(2,1)S(1)}, bf16[512,1024]{1,0:T(8,128)(2,1)S(1)}, u32[]{:S(2)}, u32[]{:S(2)}) %collective-permute-start.9) | collective-permute-done | bytes 1048608 | tf_op jit(solution)/shard_map/ppermute | solution.py:33
  69.5 1.6 %scores.10 = (f32[2,512,512]{2,1,0:T(8,128)S(1)}, f32[4,512]{1,0:T(4,128)S(1)}) custom-call(bf16[512,1024]{1,0:T(8,128)(2,1)S(1)} %share.1.mine_ref, bf16[512,1024]{1,0:T(8,128)(2,1)S(1)} %collective-permute-done.6.other_ref, bf16[512,1024]{1,0:T(8,128)(2,1)S(1)} %collective-permute-done.9.refs_0_.refs_15_.refs_3_), custom_call_target="tpu_custom_call" | custom-call | flops 2147483648 | bytes 5242880 | tf_op jit(solution)/shard_map/scores/pallas_call | solution.py:85
  71.2 1.6 %scores.11 = (f32[2,512,512]{2,1,0:T(8,128)S(1)}, f32[4,512]{1,0:T(4,128)S(1)}) custom-call(bf16[512,1024]{1,0:T(8,128)(2,1)S(1)} %share.1.mine_ref, bf16[512,1024]{1,0:T(8,128)(2,1)S(1)} %collective-permute-done.6.other_ref, bf16[512,1024]{1,0:T(8,128)(2,1)S(1)} %collective-permute-done.8.refs_0_.refs_8_.refs_10_), custom_call_target="tpu_custom_call" | custom-call | flops 2147483648 | bytes 5242880 | tf_op jit(solution)/shard_map/scores/pallas_call | solution.py:85
  72.8 1.1 first.1
  74.0 12.3 %all_to_all.5.all_ref = f32[16,8,640]{2,1,0:T(8,128)S(1)} all-to-all(f32[16,8,640]{2,1,0:T(8,128)S(1)} %get-tuple-element.54), channel_id=1, replica_groups={{0,8,64,72,2,10,66,74,4,12,68,76,6,14,70,78},{16,24,80,88,18,26,82,90,2..., dimensions={0} | all-to-all | bytes 655360 | tf_op jit(solution)/shard_map/all_to_all | solution.py:364
  86.3 1.6 %collective-permute-start.15 = (f32[8,640]{1,0:T(8,128)S(1)}, f32[8,640]{1,0:T(8,128)S(1)}, u32[]{:S(2)}, u32[]{:S(2)}) collective-permute-start(f32[8,640]{1,0:T(8,128)S(1)} %plane.1.refs_0_), channel_id=1, source_target_pairs={{48,0},{7,1},{0,16},{23,17},{16,32},{39,33},{32,48},{55,49},{50,2}... | collective-permute-start | bytes 61448 | tf_op jit(solution)/shard_map/ppermute | solution.py:33
  87.9 1.6 %collective-permute-start.14 = (f32[8,640]{1,0:T(8,128)S(1)}, f32[8,640]{1,0:T(8,128)S(1)}, u32[]{:S(2)}, u32[]{:S(2)}) collective-permute-start(f32[8,640]{1,0:T(8,128)S(1)} %plane.1.refs_0_), channel_id=1, source_target_pairs={{32,0},{5,1},{48,16},{21,17},{0,32},{37,33},{16,48},{53,49},{34,2}... | collective-permute-start | bytes 61448 | tf_op jit(solution)/shard_map/ppermute | solution.py:33
  89.5 2.0 %collective-permute-start.13 = (f32[8,640]{1,0:T(8,128)S(1)}, f32[8,640]{1,0:T(8,128)S(1)}, u32[]{:S(2)}, u32[]{:S(2)}) collective-permute-start(f32[8,640]{1,0:T(8,128)S(1)} %plane.1.refs_0_), channel_id=1, source_target_pairs={{16,0},{3,1},{32,16},{19,17},{48,32},{35,33},{0,48},{51,49},{18,2}... | collective-permute-start | bytes 61448 | tf_op jit(solution)/shard_map/ppermute | solution.py:33
  93.4 4.5 %sums.3 = f32[512,1152]{1,0:T(8,128)S(1)} custom-call(f32[1,4096]{1,0:T(1,128)S(1)} %get-tuple-element.55.lse_ref, f32[2,4096]{1,0:T(2,128)S(1)} %get-tuple-element.56.top_ref, f32[2,512,512]{2,1,0:T(8,128)S(1)} %get-tuple-element.57.refs_0_, f32[2,512,512]{2,1,0:T(8,128)S(1)} %get-tuple-element.58.refs_1_, f32[2,512,512]{2,1,0:T(8,128)S(1)} %get-tuple-element.59.refs_2_, ...), custom_call_target="tpu_custom_call" | custom-call | flops 4294967296 | bytes 18874368 | tf_op jit(solution)/shard_map/sums/pallas_call | solution.py:239
  97.9 5.8 %collective-permute-start.16 = (f32[512,1152]{1,0:T(8,128)S(1)}, f32[512,1152]{1,0:T(8,128)S(1)}, u32[]{:S(2)}, u32[]{:S(2)}) collective-permute-start(f32[512,1152]{1,0:T(8,128)S(1)} %sums.3), channel_id=1, source_target_pairs={{0,1},{1,0},{2,3},{3,2},{4,5},{5,4},{6,7},{7,6},{8,9},{9,8},{10,11... | collective-permute-start | bytes 7077896 | tf_op jit(solution)/shard_map/ppermute | solution.py:38
  103.8 3.4 %sums.2.ours_ref = f32[512,1152]{1,0:T(8,128)S(1)} custom-call(f32[1,4096]{1,0:T(1,128)S(1)} %get-tuple-element.55.lse_ref, f32[2,4096]{1,0:T(2,128)S(1)} %get-tuple-element.56.top_ref, f32[2,512,512]{2,1,0:T(8,128)S(1)} %get-tuple-element.57.refs_0_, f32[2,512,512]{2,1,0:T(8,128)S(1)} %get-tuple-element.58.refs_1_, ...), custom_call_target="tpu_custom_call" | custom-call | flops 3221225472 | bytes 18874368 | tf_op jit(solution)/shard_map/sums/pallas_call | solution.py:239
  107.9 1.4 %route.1 = f32[1,64]{1,0:T(1,128)} custom-call(s32[2]{0:T(128)S(1)} %pad_add_fusion.at_ref, f32[64,128]{1,0:T(8,128)S(1)} %get-tuple-element.65.mine_ref, f32[64,128]{1,0:T(8,128)S(1)} %collective-permute-done.17.other_ref), custom_call_target="tpu_custom_call" | custom-call | tf_op jit(solution)/shard_map/route/pallas_call | solution.py:387
  109.3 2.4 %final.1 = f32[512,1024]{1,0:T(8,128)} custom-call(f32[1,4096]{1,0:T(1,128)S(1)} %get-tuple-element.55.lse_ref, f32[2,4096]{1,0:T(2,128)S(1)} %get-tuple-element.56.top_ref, f32[512,1152]{1,0:T(8,128)S(1)} %sums.2.ours_ref, f32[512,1152]{1,0:T(8,128)S(1)} %collective-permute-done.16.theirs_ref, bf16[512,1024]{1,0:T(8,128)(2,1)S(1)} %share.1.mine_ref, ...), custom_call_target="tpu_custom_call" | custom-call | tf_op jit(solution)/shard_map/final/pallas_call | solution.py:394
  (30 shorter events, 10.2 us)
Async XLA Ops:
  0.6 6.6 %collective-permute-start.1 = (bf16[64,1024]{1,0:T(8,128)(2,1)}, bf16[64,1024]{1,0:T(8,128)(2,1)S(1)}, u32[]{:S(2)}, u32[]{:S(2)}) collective-permute-start(bf16[64,1024]{1,0:T(8,128)(2,1)} %refs_0_.1), channel_id=1, source_target_pairs={{64,0},{65,1},{80,16},{81,17},{96,32},{97,33},{112,48},{113,49},{6... | collective-permute-start | bytes 393224 | tf_op jit(solution)/shard_map/ppermute | solution.py:33
  4.3 6.2 %collective-permute-start = (bf16[64,1024]{1,0:T(8,128)(2,1)}, bf16[64,1024]{1,0:T(8,128)(2,1)S(1)}, u32[]{:S(2)}, u32[]{:S(2)}) collective-permute-start(bf16[64,1024]{1,0:T(8,128)(2,1)} %refs_0_.1), channel_id=1, source_target_pairs={{8,0},{9,1},{24,16},{25,17},{40,32},{41,33},{56,48},{57,49},{10,2}... | collective-permute-start | bytes 393224 | tf_op jit(solution)/shard_map/ppermute | solution.py:33
  5.1 5.4 %collective-permute-start.2 = (bf16[64,1024]{1,0:T(8,128)(2,1)}, bf16[64,1024]{1,0:T(8,128)(2,1)S(1)}, u32[]{:S(2)}, u32[]{:S(2)}) collective-permute-start(bf16[64,1024]{1,0:T(8,128)(2,1)} %refs_0_.1), channel_id=1, source_target_pairs={{72,0},{73,1},{88,16},{89,17},{104,32},{105,33},{120,48},{121,49},... | collective-permute-start | bytes 393224 | tf_op jit(solution)/shard_map/ppermute | solution.py:33
  10.5 0.9 copy-start.1
  11.5 10.8 %collective-permute-start.5 = (bf16[256,1024]{1,0:T(8,128)(2,1)S(1)}, bf16[256,1024]{1,0:T(8,128)(2,1)S(1)}, u32[]{:S(2)}, u32[]{:S(2)}) collective-permute-start(bf16[256,1024]{1,0:T(8,128)(2,1)S(1)} %join.1.refs_0_), channel_id=1, source_target_pairs={{6,0},{49,1},{22,16},{1,17},{38,32},{17,33},{54,48},{33,49},{0,2},... | collective-permute-start | bytes 1572872 | tf_op jit(solution)/shard_map/ppermute | solution.py:33
  13.2 15.8 %collective-permute-start.4 = (bf16[256,1024]{1,0:T(8,128)(2,1)S(1)}, bf16[256,1024]{1,0:T(8,128)(2,1)S(1)}, u32[]{:S(2)}, u32[]{:S(2)}) collective-permute-start(bf16[256,1024]{1,0:T(8,128)(2,1)S(1)} %join.1.refs_0_), channel_id=1, source_target_pairs={{4,0},{33,1},{20,16},{49,17},{36,32},{1,33},{52,48},{17,49},{6,2},... | collective-permute-start | bytes 1572872 | tf_op jit(solution)/shard_map/ppermute | solution.py:33
  16.5 12.5 %collective-permute-start.3 = (bf16[256,1024]{1,0:T(8,128)(2,1)S(1)}, bf16[256,1024]{1,0:T(8,128)(2,1)S(1)}, u32[]{:S(2)}, u32[]{:S(2)}) collective-permute-start(bf16[256,1024]{1,0:T(8,128)(2,1)S(1)} %join.1.refs_0_), channel_id=1, source_target_pairs={{2,0},{17,1},{18,16},{33,17},{34,32},{49,33},{50,48},{1,49},{4,2},... | collective-permute-start | bytes 1572872 | tf_op jit(solution)/shard_map/ppermute | solution.py:33
  29.7 15.5 %collective-permute-start.7 = (bf16[512,1024]{1,0:T(8,128)(2,1)S(1)}, bf16[512,1024]{1,0:T(8,128)(2,1)S(1)}, u32[]{:S(2)}, u32[]{:S(2)}) collective-permute-start(bf16[512,1024]{1,0:T(8,128)(2,1)S(1)} %get-tuple-element.41.refs_1_.refs_6_.refs_8_), channel_id=1, source_target_pairs={{32,0},{5,1},{48,16},{21,17},{0,32},{37,33},{16,48},{53,49},{34,2}... | collective-permute-start | bytes 3145736 | tf_op jit(solution)/shard_map/ppermute | solution.py:33
  32.4 3.4 %copy-start = (bf16[4096,1024]{1,0:T(8,128)(2,1)S(1)}, bf16[4096,1024]{1,0:T(8,128)(2,1)}, u32[]{:S(2)}) copy-start(bf16[4096,1024]{1,0:T(8,128)(2,1)} %cents_ref.1) | copy-start | bytes 25165828
  37.8 11.7 %collective-permute-start.6 = (bf16[512,1024]{1,0:T(8,128)(2,1)S(1)}, bf16[512,1024]{1,0:T(8,128)(2,1)S(1)}, u32[]{:S(2)}, u32[]{:S(2)}) collective-permute-start(bf16[512,1024]{1,0:T(8,128)(2,1)S(1)} %share.1.mine_ref), channel_id=1, source_target_pairs={{0,1},{1,0},{2,3},{3,2},{4,5},{5,4},{6,7},{7,6},{8,9},{9,8},{10,11... | collective-permute-start | bytes 3145736 | tf_op jit(solution)/shard_map/ppermute | solution.py:38
  41.1 15.4 %collective-permute-start.12 = (bf16[512,1024]{1,0:T(8,128)(2,1)S(1)}, bf16[512,1024]{1,0:T(8,128)(2,1)S(1)}, u32[]{:S(2)}, u32[]{:S(2)}) collective-permute-start(bf16[512,1024]{1,0:T(8,128)(2,1)S(1)} %get-tuple-element.42.refs_2_.refs_7_.refs_9_), channel_id=1, source_target_pairs={{16,0},{3,1},{32,16},{19,17},{48,32},{35,33},{0,48},{51,49},{18,2}... | collective-permute-start | bytes 3145736 | tf_op jit(solution)/shard_map/ppermute | solution.py:33
  43.1 15.2 %collective-permute-start.11 = (bf16[512,1024]{1,0:T(8,128)(2,1)S(1)}, bf16[512,1024]{1,0:T(8,128)(2,1)S(1)}, u32[]{:S(2)}, u32[]{:S(2)}) collective-permute-start(bf16[512,1024]{1,0:T(8,128)(2,1)S(1)} %get-tuple-element.41.refs_1_.refs_6_.refs_8_), channel_id=1, source_target_pairs={{48,0},{7,1},{0,16},{23,17},{16,32},{39,33},{32,48},{55,49},{50,2}... | collective-permute-start | bytes 3145736 | tf_op jit(solution)/shard_map/ppermute | solution.py:33
  45.3 15.7 %collective-permute-start.10 = (bf16[512,1024]{1,0:T(8,128)(2,1)S(1)}, bf16[512,1024]{1,0:T(8,128)(2,1)S(1)}, u32[]{:S(2)}, u32[]{:S(2)}) collective-permute-start(bf16[512,1024]{1,0:T(8,128)(2,1)S(1)} %collective-permute-done.7.refs_0_.refs_10_.refs_12_), channel_id=1, source_target_pairs={{8,0},{73,1},{24,16},{89,17},{40,32},{105,33},{56,48},{121,49},{10... | collective-permute-start | bytes 3145736 | tf_op jit(solution)/shard_map/ppermute | solution.py:49
  48.4 21.1 %collective-permute-start.9 = (bf16[512,1024]{1,0:T(8,128)(2,1)S(1)}, bf16[512,1024]{1,0:T(8,128)(2,1)S(1)}, u32[]{:S(2)}, u32[]{:S(2)}) collective-permute-start(bf16[512,1024]{1,0:T(8,128)(2,1)S(1)} %get-tuple-element.42.refs_2_.refs_7_.refs_9_), channel_id=1, source_target_pairs={{48,0},{7,1},{0,16},{23,17},{16,32},{39,33},{32,48},{55,49},{50,2}... | collective-permute-start | bytes 3145736 | tf_op jit(solution)/shard_map/ppermute | solution.py:33
  49.5 21.7 %collective-permute-start.8 = (bf16[512,1024]{1,0:T(8,128)(2,1)S(1)}, bf16[512,1024]{1,0:T(8,128)(2,1)S(1)}, u32[]{:S(2)}, u32[]{:S(2)}) collective-permute-start(bf16[512,1024]{1,0:T(8,128)(2,1)S(1)} %get-tuple-element.41.refs_1_.refs_6_.refs_8_), channel_id=1, source_target_pairs={{16,0},{3,1},{32,16},{19,17},{48,32},{35,33},{0,48},{51,49},{18,2}... | collective-permute-start | bytes 3145736 | tf_op jit(solution)/shard_map/ppermute | solution.py:33
  86.3 5.2 %collective-permute-start.15 = (f32[8,640]{1,0:T(8,128)S(1)}, f32[8,640]{1,0:T(8,128)S(1)}, u32[]{:S(2)}, u32[]{:S(2)}) collective-permute-start(f32[8,640]{1,0:T(8,128)S(1)} %plane.1.refs_0_), channel_id=1, source_target_pairs={{48,0},{7,1},{0,16},{23,17},{16,32},{39,33},{32,48},{55,49},{50,2}... | collective-permute-start | bytes 61448 | tf_op jit(solution)/shard_map/ppermute | solution.py:33
  87.9 4.1 %collective-permute-start.14 = (f32[8,640]{1,0:T(8,128)S(1)}, f32[8,640]{1,0:T(8,128)S(1)}, u32[]{:S(2)}, u32[]{:S(2)}) collective-permute-start(f32[8,640]{1,0:T(8,128)S(1)} %plane.1.refs_0_), channel_id=1, source_target_pairs={{32,0},{5,1},{48,16},{21,17},{0,32},{37,33},{16,48},{53,49},{34,2}... | collective-permute-start | bytes 61448 | tf_op jit(solution)/shard_map/ppermute | solution.py:33
  89.5 2.9 %collective-permute-start.13 = (f32[8,640]{1,0:T(8,128)S(1)}, f32[8,640]{1,0:T(8,128)S(1)}, u32[]{:S(2)}, u32[]{:S(2)}) collective-permute-start(f32[8,640]{1,0:T(8,128)S(1)} %plane.1.refs_0_), channel_id=1, source_target_pairs={{16,0},{3,1},{32,16},{19,17},{48,32},{35,33},{0,48},{51,49},{18,2}... | collective-permute-start | bytes 61448 | tf_op jit(solution)/shard_map/ppermute | solution.py:33
  97.9 11.4 %collective-permute-start.16 = (f32[512,1152]{1,0:T(8,128)S(1)}, f32[512,1152]{1,0:T(8,128)S(1)}, u32[]{:S(2)}, u32[]{:S(2)}) collective-permute-start(f32[512,1152]{1,0:T(8,128)S(1)} %sums.3), channel_id=1, source_target_pairs={{0,1},{1,0},{2,3},{3,2},{4,5},{5,4},{6,7},{7,6},{8,9},{9,8},{10,11... | collective-permute-start | bytes 7077896 | tf_op jit(solution)/shard_map/ppermute | solution.py:38
  103.7 4.2 %collective-permute-start.17 = (f32[64,128]{1,0:T(8,128)S(1)}, f32[64,128]{1,0:T(8,128)S(1)}, u32[]{:S(2)}, u32[]{:S(2)}) collective-permute-start(f32[64,128]{1,0:T(8,128)S(1)} %get-tuple-element.65.mine_ref), channel_id=1, source_target_pairs={{0,1},{1,0},{2,3},{3,2},{4,5},{5,4},{6,7},{7,6},{8,9},{9,8},{10,11... | collective-permute-start | bytes 98312 | tf_op jit(solution)/shard_map/ppermute | solution.py:38

commit v12 on v11

--- a/solution.py
+++ b/solution.py
@@ -160,18 +160,6 @@
         own_ref[:, lanes] = roll_within(value[:, lanes], 0, 4 - spot_ref[3])
 
 
-def route_kernel(at_ref, mine_ref, other_ref, out_ref):
-    first = (at_ref[0] * 16 + at_ref[1]) * UNIT
-    rows = (lax.broadcasted_iota(jnp.int32, (UNIT, 128), 0) + first).astype(jnp.float32)
-    totals = [jnp.zeros((UNIT, 128), jnp.float32)] * 4
-    for ref in (mine_ref, other_ref):
-        for line in range(32):
-            hit = ref[32 + line : 33 + line, :] == rows
-            totals[line % 4] = totals[line % 4] + jnp.where(hit, ref[line : line + 1, :], 0.0)
-    total = (totals[0] + totals[1]) + (totals[2] + totals[3])
-    out_ref[...] = jnp.sum(total.T, axis=0, keepdims=True) * math.log(2.0)
-
-
 def join_kernel(*refs):
     *parts, out_ref = refs
     at = 0
@@ -248,10 +236,10 @@
     )(lse, tops, *ps, *rows)
 
 
-def final_kernel(skip, count, lse_ref, top_ref, ours_ref, theirs_ref, mine_ref, *refs):
+def final_kernel(skip, count, at_ref, lse_ref, top_ref, ours_ref, theirs_ref, mine_ref, pack_ref, other_ref, *refs):
     ps = refs[:count]
     rows = refs[count : 2 * count]
-    out_ref, buf, sems = refs[2 * count :]
+    out_ref, row_ref, buf, sems = refs[2 * count :]
     n, width = rows[0].shape
     mass = ours_ref[:, width:] + theirs_ref[:, width:]
     ws = []
@@ -263,8 +251,17 @@
         mass = mass + sum(wide[:, c : c + 128] for c in range(0, n, 128))
         ws.append(w)
     inverse = 1.0 / (jnp.sum(mass, axis=1, keepdims=True) + prior_mass)
+    base = (at_ref[0] * 16 + at_ref[1]) * UNIT
+    logical = (lax.broadcasted_iota(jnp.int32, (UNIT, 128), 0) + base).astype(jnp.float32)
+    routed = []
     copies = []
     for block in range(4):
+        found = jnp.zeros((UNIT, 128), jnp.float32)
+        for line in range(block * 8, block * 8 + 8):
+            for ref in (pack_ref, other_ref):
+                hit = ref[32 + line : 33 + line, :] == logical
+                found = found + jnp.where(hit, ref[line : line + 1, :], 0.0)
+        routed.append(found)
         columns = slice(block * width // 4, (block + 1) * width // 4)
         total = ours_ref[:, columns] + theirs_ref[:, columns]
         total = total + prior_mass * mine_ref[:, columns].astype(jnp.float32)
@@ -274,6 +271,8 @@
         copy = pltpu.make_async_copy(buf.at[:, columns], out_ref.at[:, columns], sems.at[block])
         copy.start()
         copies.append(copy)
+    found = (routed[0] + routed[1]) + (routed[2] + routed[3])
+    row_ref[...] = jnp.sum(found.T, axis=0, keepdims=True) * math.log(2.0)
     for copy in copies:
         copy.wait()
 
@@ -383,23 +382,19 @@
     theirs = sums_call(1, lse, tops, ps, chunks)
     received = swap_cores(theirs)
     partner = swap_cores(pack)
-    ours = sums_call(0, lse, tops, ps[:6], chunks[:6])
-    row_lse = pl.pallas_call(
-        route_kernel,
-        out_shape=jax.ShapeDtypeStruct((1, UNIT), jnp.float32),
-        in_specs=[smem, vmem, vmem],
-        compiler_params=small,
-        name="route",
-    )(at_word, pack, partner)
-    new_centers = pl.pallas_call(
-        functools.partial(final_kernel, 6, 2),
-        out_shape=jax.ShapeDtypeStruct((share, width), jnp.float32),
-        in_specs=[vmem] * 9,
-        out_specs=pl.BlockSpec(memory_space=pl.ANY),
+    ours = sums_call(0, lse, tops, ps[:7], chunks[:7])
+    new_centers, row_lse = pl.pallas_call(
+        functools.partial(final_kernel, 7, 1),
+        out_shape=(
+            jax.ShapeDtypeStruct((share, width), jnp.float32),
+            jax.ShapeDtypeStruct((1, UNIT), jnp.float32),
+        ),
+        in_specs=[smem] + [vmem] * 9,
+        out_specs=(pl.BlockSpec(memory_space=pl.ANY), vmem),
         scratch_shapes=[pltpu.VMEM((share, width), jnp.float32), pltpu.SemaphoreType.DMA((4,))],
         compiler_params=pltpu.CompilerParams(vmem_limit_bytes=12 << 20),
         name="final",
-    )(lse, tops, ours, received, mine, *ps[6:], *chunks[6:])
+    )(at_word, lse, tops, ours, received, mine, pack, partner, *ps[7:], *chunks[7:])
     return new_centers, row_lse.reshape(UNIT)
 
 

time: 112 us -> 114 us (1.018)
  waiting for transfers between devices: 28.5 us -> 40.2 us
  starting transfers between devices: 35.8 us -> 27.6 us
  blocking collectives: 12.3 us -> 10.5 us
    ppermute x14, waiting for transfers between devices: 26.9 us -> 39.5 us  [fetch(): return lax.ppermute(value, BOTH, pairs)]
    ppermute x14, starting transfers between devices: 23.5 us -> 19 us  [fetch(): return lax.ppermute(value, BOTH, pairs)]
    ppermute x1, starting transfers between devices: 3.17 us -> 0.01 us  [swap_sides(): return lax.ppermute(value, BOTH, pairs)]
    all_to_all x1, blocking collectives: 12.3 us -> 10.5 us  [shards(): lax.all_to_all(local, BOTH, split_axis=0, concat_axis=0, tiled=True, axis...]
    pallas_call x2 -> x1, Pallas kernels: 3.83 us -> 3.11 us  [shards(): pl.pallas_call(functools.partial(final_kernel, 7, 1), out_shape=(jax.Shap...]
  transfers between devices with their start and end apart: 18 -> 18, of which waited for: 12 -> 12; matrix products, arithmetic and copies ran while one was open for 1% -> 1% of each run, Pallas kernels for 16% -> 15%
where the time goes in v12:
time: 114 us; the launch traced here: 113 us
  waiting for transfers between devices  40.2 us (35%)
  Pallas kernels  29 us (25%)
  starting transfers between devices  27.6 us (24%)
  blocking collectives  10.5 us (9%)
  local copies, waits for them, and re-layouts  4.46 us (4%)
    ppermute x14, waiting for transfers between devices, fetch(): return lax.ppermute(value, BOTH, pairs)  39.5 us
    ppermute x14, starting transfers between devices, fetch(): return lax.ppermute(value, BOTH, pairs)  19 us
    pallas_call x6, Pallas kernels, scores_call(): pl.pallas_call(functools.partial(scores_kernel, factor, count), out_shape...  12.5 us
    all_to_all x1, blocking collectives, shards(): lax.all_to_all(local, BOTH, split_axis=0, concat_axis=0, tiled=True, axis...  10.5 us
    ppermute x3, starting transfers between devices, swap_cores(): return lax.ppermute(value, BOTH, pairs)  8.57 us
    pallas_call x2, Pallas kernels, sums_call(): pl.pallas_call(functools.partial(sums_kernel, half, count), out_shape=jax...  8.5 us
    unnamed x4, local copies, waits for them, and re-layouts  4.29 us
    pallas_call x1, Pallas kernels, shards(): pl.pallas_call(functools.partial(final_kernel, 7, 1), out_shape=(jax.Shap...  3.11 us
  transfers between devices with their start and end apart: 18, of which 12 were waited for; matrix products, arithmetic and copies ran while one was open for 1% of the time, Pallas kernels for 15%

profile of v12, /device:TPU:1, one launch (start us, length us, event | category | flops | bytes accessed | tf_op | source)
XLA Modules:
  0.0 113.3 jit_solution(2064778210232654170)
XLA Ops:
  0.6 3.4 %collective-permute-start = (bf16[64,1024]{1,0:T(8,128)(2,1)}, bf16[64,1024]{1,0:T(8,128)(2,1)S(1)}, u32[]{:S(2)}, u32[]{:S(2)}) collective-permute-start(bf16[64,1024]{1,0:T(8,128)(2,1)} %refs_0_.1), channel_id=1, source_target_pairs={{8,0},{9,1},{24,16},{25,17},{40,32},{41,33},{56,48},{57,49},{10,2}... | collective-permute-start | bytes 393224 | tf_op jit(solution)/shard_map/ppermute | solution.py:33
  6.0 3.3 %collective-permute-done.refs_1_ = bf16[64,1024]{1,0:T(8,128)(2,1)S(1)} collective-permute-done((bf16[64,1024]{1,0:T(8,128)(2,1)}, bf16[64,1024]{1,0:T(8,128)(2,1)S(1)}, u32[]{:S(2)}, u32[]{:S(2)}) %collective-permute-start) | collective-permute-done | bytes 131104 | tf_op jit(solution)/shard_map/ppermute | solution.py:33
  9.6 4.1 %collective-permute-done.2.refs_3_ = bf16[64,1024]{1,0:T(8,128)(2,1)S(1)} collective-permute-done((bf16[64,1024]{1,0:T(8,128)(2,1)}, bf16[64,1024]{1,0:T(8,128)(2,1)S(1)}, u32[]{:S(2)}, u32[]{:S(2)}) %collective-permute-start.2) | collective-permute-done | bytes 131104 | tf_op jit(solution)/shard_map/ppermute | solution.py:33
  13.8 0.9 copy-done.1
  14.7 3.8 %collective-permute-start.3 = (bf16[256,1024]{1,0:T(8,128)(2,1)S(1)}, bf16[256,1024]{1,0:T(8,128)(2,1)S(1)}, u32[]{:S(2)}, u32[]{:S(2)}) collective-permute-start(bf16[256,1024]{1,0:T(8,128)(2,1)S(1)} %join.1.refs_0_), channel_id=1, source_target_pairs={{2,0},{17,1},{18,16},{33,17},{34,32},{49,33},{50,48},{1,49},{4,2},... | collective-permute-start | bytes 1572872 | tf_op jit(solution)/shard_map/ppermute | solution.py:33
  19.2 11.0 %collective-permute-done.3.refs_1_ = bf16[256,1024]{1,0:T(8,128)(2,1)S(1)} collective-permute-done((bf16[256,1024]{1,0:T(8,128)(2,1)S(1)}, bf16[256,1024]{1,0:T(8,128)(2,1)S(1)}, u32[]{:S(2)}, u32[]{:S(2)}) %collective-permute-start.3) | collective-permute-done | bytes 524320 | tf_op jit(solution)/shard_map/ppermute | solution.py:33
  30.3 3.4 %collective-permute-done.5.refs_3_ = bf16[256,1024]{1,0:T(8,128)(2,1)S(1)} collective-permute-done((bf16[256,1024]{1,0:T(8,128)(2,1)S(1)}, bf16[256,1024]{1,0:T(8,128)(2,1)S(1)}, u32[]{:S(2)}, u32[]{:S(2)}) %collective-permute-start.5) | collective-permute-done | bytes 524320 | tf_op jit(solution)/shard_map/ppermute | solution.py:33
  34.4 2.7 %collective-permute-start.7 = (bf16[512,1024]{1,0:T(8,128)(2,1)S(1)}, bf16[512,1024]{1,0:T(8,128)(2,1)S(1)}, u32[]{:S(2)}, u32[]{:S(2)}) collective-permute-start(bf16[512,1024]{1,0:T(8,128)(2,1)S(1)} %get-tuple-element.43.refs_1_.refs_7_.refs_8_), channel_id=1, source_target_pairs={{32,0},{5,1},{48,16},{21,17},{0,32},{37,33},{16,48},{53,49},{34,2}... | collective-permute-start | bytes 3145736 | tf_op jit(solution)/shard_map/ppermute | solution.py:33
  37.1 3.4 %copy-done = bf16[4096,1024]{1,0:T(8,128)(2,1)S(1)} copy-done((bf16[4096,1024]{1,0:T(8,128)(2,1)S(1)}, bf16[4096,1024]{1,0:T(8,128)(2,1)}, u32[]{:S(2)}) %copy-start) | copy-done | bytes 8388632
  40.5 2.0 %share.1.mine_ref = bf16[512,1024]{1,0:T(8,128)(2,1)S(1)} custom-call(s32[2]{0:T(128)S(1)} %pad_add_fusion.at_ref, bf16[4096,1024]{1,0:T(8,128)(2,1)S(1)} %copy-done), custom_call_target="tpu_custom_call" | custom-call | tf_op jit(solution)/shard_map/share/pallas_call | solution.py:327
  42.5 2.4 %collective-permute-start.6 = (bf16[512,1024]{1,0:T(8,128)(2,1)S(1)}, bf16[512,1024]{1,0:T(8,128)(2,1)S(1)}, u32[]{:S(2)}, u32[]{:S(2)}) collective-permute-start(bf16[512,1024]{1,0:T(8,128)(2,1)S(1)} %share.1.mine_ref), channel_id=1, source_target_pairs={{0,1},{1,0},{2,3},{3,2},{4,5},{5,4},{6,7},{7,6},{8,9},{9,8},{10,11... | collective-permute-start | bytes 3145736 | tf_op jit(solution)/shard_map/ppermute | solution.py:38
  45.2 1.1 %collective-permute-start.11 = (bf16[512,1024]{1,0:T(8,128)(2,1)S(1)}, bf16[512,1024]{1,0:T(8,128)(2,1)S(1)}, u32[]{:S(2)}, u32[]{:S(2)}) collective-permute-start(bf16[512,1024]{1,0:T(8,128)(2,1)S(1)} %get-tuple-element.43.refs_1_.refs_7_.refs_8_), channel_id=1, source_target_pairs={{48,0},{7,1},{0,16},{23,17},{16,32},{39,33},{32,48},{55,49},{50,2}... | collective-permute-start | bytes 3145736 | tf_op jit(solution)/shard_map/ppermute | solution.py:33
  46.3 3.6 %collective-permute-done.7.refs_0_.refs_11_.refs_12_ = bf16[512,1024]{1,0:T(8,128)(2,1)S(1)} collective-permute-done((bf16[512,1024]{1,0:T(8,128)(2,1)S(1)}, bf16[512,1024]{1,0:T(8,128)(2,1)S(1)}, u32[]{:S(2)}, u32[]{:S(2)}) %collective-permute-start.7) | collective-permute-done | bytes 1048608 | tf_op jit(solution)/shard_map/ppermute | solution.py:33
  49.9 2.3 %collective-permute-start.8 = (bf16[512,1024]{1,0:T(8,128)(2,1)S(1)}, bf16[512,1024]{1,0:T(8,128)(2,1)S(1)}, u32[]{:S(2)}, u32[]{:S(2)}) collective-permute-start(bf16[512,1024]{1,0:T(8,128)(2,1)S(1)} %get-tuple-element.43.refs_1_.refs_7_.refs_8_), channel_id=1, source_target_pairs={{16,0},{3,1},{32,16},{19,17},{48,32},{35,33},{0,48},{51,49},{18,2}... | collective-permute-start | bytes 3145736 | tf_op jit(solution)/shard_map/ppermute | solution.py:33
  52.2 4.3 %scores.6 = (f32[2,512,512]{2,1,0:T(8,128)S(1)}, f32[2,512,512]{2,1,0:T(8,128)S(1)}, f32[2,512,512]{2,1,0:T(8,128)S(1)}, f32[4,1536]{1,0:T(4,128)S(1)}) custom-call(bf16[512,1024]{1,0:T(8,128)(2,1)S(1)} %share.1.mine_ref, bf16[512,1024]{1,0:T(8,128)(2,1)S(1)} %collective-permute-done.6.other_ref, ...), custom_call_target="tpu_custom_call" | custom-call | flops 6442450944 | bytes 11534336 | tf_op jit(solution)/shard_map/scores/pallas_call | solution.py:85
  56.5 4.8 %collective-permute-done.12.refs_0_.refs_10_.refs_11_ = bf16[512,1024]{1,0:T(8,128)(2,1)S(1)} collective-permute-done((bf16[512,1024]{1,0:T(8,128)(2,1)S(1)}, bf16[512,1024]{1,0:T(8,128)(2,1)S(1)}, u32[]{:S(2)}, u32[]{:S(2)}) %collective-permute-start.12) | collective-permute-done | bytes 1048608 | tf_op jit(solution)/shard_map/ppermute | solution.py:33
  61.2 1.6 %scores.7 = (f32[2,512,512]{2,1,0:T(8,128)S(1)}, f32[4,512]{1,0:T(4,128)S(1)}) custom-call(bf16[512,1024]{1,0:T(8,128)(2,1)S(1)} %share.1.mine_ref, bf16[512,1024]{1,0:T(8,128)(2,1)S(1)} %collective-permute-done.6.other_ref, bf16[512,1024]{1,0:T(8,128)(2,1)S(1)} %collective-permute-done.12.refs_0_.refs_10_.refs_11_), custom_call_target="tpu_custom_call" | custom-call | flops 2147483648 | bytes 5242880 | tf_op jit(solution)/shard_map/scores/pallas_call | solution.py:85
  62.9 1.6 %scores.8 = (f32[2,512,512]{2,1,0:T(8,128)S(1)}, f32[4,512]{1,0:T(4,128)S(1)}) custom-call(bf16[512,1024]{1,0:T(8,128)(2,1)S(1)} %share.1.mine_ref, bf16[512,1024]{1,0:T(8,128)(2,1)S(1)} %collective-permute-done.6.other_ref, bf16[512,1024]{1,0:T(8,128)(2,1)S(1)} %collective-permute-done.11.refs_0_.refs_13_.refs_14_), custom_call_target="tpu_custom_call" | custom-call | flops 2147483648 | bytes 5242880 | tf_op jit(solution)/shard_map/scores/pallas_call | solution.py:85
  65.1 1.6 %scores.9 = (f32[2,512,512]{2,1,0:T(8,128)S(1)}, f32[4,512]{1,0:T(4,128)S(1)}) custom-call(bf16[512,1024]{1,0:T(8,128)(2,1)S(1)} %share.1.mine_ref, bf16[512,1024]{1,0:T(8,128)(2,1)S(1)} %collective-permute-done.6.other_ref, bf16[512,1024]{1,0:T(8,128)(2,1)S(1)} %collective-permute-done.10.refs_0_.refs_12_.refs_13_), custom_call_target="tpu_custom_call" | custom-call | flops 2147483648 | bytes 5242880 | tf_op jit(solution)/shard_map/scores/pallas_call | solution.py:85
  66.7 5.7 %collective-permute-done.9.refs_0_.refs_15_.refs_1_ = bf16[512,1024]{1,0:T(8,128)(2,1)S(1)} collective-permute-done((bf16[512,1024]{1,0:T(8,128)(2,1)S(1)}, bf16[512,1024]{1,0:T(8,128)(2,1)S(1)}, u32[]{:S(2)}, u32[]{:S(2)}) %collective-permute-start.9) | collective-permute-done | bytes 1048608 | tf_op jit(solution)/shard_map/ppermute | solution.py:33
  72.4 1.6 %scores.10 = (f32[2,512,512]{2,1,0:T(8,128)S(1)}, f32[4,512]{1,0:T(4,128)S(1)}) custom-call(bf16[512,1024]{1,0:T(8,128)(2,1)S(1)} %share.1.mine_ref, bf16[512,1024]{1,0:T(8,128)(2,1)S(1)} %collective-permute-done.6.other_ref, bf16[512,1024]{1,0:T(8,128)(2,1)S(1)} %collective-permute-done.9.refs_0_.refs_15_.refs_1_), custom_call_target="tpu_custom_call" | custom-call | flops 2147483648 | bytes 5242880 | tf_op jit(solution)/shard_map/scores/pallas_call | solution.py:85
  74.0 1.6 %scores.11 = (f32[2,512,512]{2,1,0:T(8,128)S(1)}, f32[4,512]{1,0:T(4,128)S(1)}) custom-call(bf16[512,1024]{1,0:T(8,128)(2,1)S(1)} %share.1.mine_ref, bf16[512,1024]{1,0:T(8,128)(2,1)S(1)} %collective-permute-done.6.other_ref, bf16[512,1024]{1,0:T(8,128)(2,1)S(1)} %collective-permute-done.8.refs_0_.refs_9_.refs_10_), custom_call_target="tpu_custom_call" | custom-call | flops 2147483648 | bytes 5242880 | tf_op jit(solution)/shard_map/scores/pallas_call | solution.py:85
  75.6 1.1 first.1
  76.8 10.5 %all_to_all.5.all_ref = f32[16,8,640]{2,1,0:T(8,128)S(1)} all-to-all(f32[16,8,640]{2,1,0:T(8,128)S(1)} %get-tuple-element.56), channel_id=1, replica_groups={{0,8,64,72,2,10,66,74,4,12,68,76,6,14,70,78},{16,24,80,88,18,26,82,90,2..., dimensions={0} | all-to-all | bytes 655360 | tf_op jit(solution)/shard_map/all_to_all | solution.py:363
  88.0 2.3 %collective-permute-start.14 = (f32[8,640]{1,0:T(8,128)S(1)}, f32[8,640]{1,0:T(8,128)S(1)}, u32[]{:S(2)}, u32[]{:S(2)}) collective-permute-start(f32[8,640]{1,0:T(8,128)S(1)} %plane.1.refs_0_), channel_id=1, source_target_pairs={{32,0},{5,1},{48,16},{21,17},{0,32},{37,33},{16,48},{53,49},{34,2}... | collective-permute-start | bytes 61448 | tf_op jit(solution)/shard_map/ppermute | solution.py:33
  90.9 1.3 %collective-permute-done.14.refs_2_ = f32[8,640]{1,0:T(8,128)S(1)} collective-permute-done((f32[8,640]{1,0:T(8,128)S(1)}, f32[8,640]{1,0:T(8,128)S(1)}, u32[]{:S(2)}, u32[]{:S(2)}) %collective-permute-start.14) | collective-permute-done | bytes 20512 | tf_op jit(solution)/shard_map/ppermute | solution.py:33
  92.1 2.0 %collective-permute-done.15.refs_3_ = f32[8,640]{1,0:T(8,128)S(1)} collective-permute-done((f32[8,640]{1,0:T(8,128)S(1)}, f32[8,640]{1,0:T(8,128)S(1)}, u32[]{:S(2)}, u32[]{:S(2)}) %collective-permute-start.15) | collective-permute-done | bytes 20512 | tf_op jit(solution)/shard_map/ppermute | solution.py:33
  94.2 1.0 merge.1
  95.2 4.5 %sums.3 = f32[512,1152]{1,0:T(8,128)S(1)} custom-call(f32[1,4096]{1,0:T(1,128)S(1)} %get-tuple-element.57.lse_ref, f32[2,4096]{1,0:T(2,128)S(1)} %get-tuple-element.58.top_ref, f32[2,512,512]{2,1,0:T(8,128)S(1)} %get-tuple-element.59.refs_0_, f32[2,512,512]{2,1,0:T(8,128)S(1)} %get-tuple-element.60.refs_1_, f32[2,512,512]{2,1,0:T(8,128)S(1)} %get-tuple-element.61.refs_2_, ...), custom_call_target="tpu_custom_call" | custom-call | flops 4294967296 | bytes 18874368 | tf_op jit(solution)/shard_map/sums/pallas_call | solution.py:227
  99.8 6.1 %collective-permute-start.16 = (f32[512,1152]{1,0:T(8,128)S(1)}, f32[512,1152]{1,0:T(8,128)S(1)}, u32[]{:S(2)}, u32[]{:S(2)}) collective-permute-start(f32[512,1152]{1,0:T(8,128)S(1)} %sums.3), channel_id=1, source_target_pairs={{0,1},{1,0},{2,3},{3,2},{4,5},{5,4},{6,7},{7,6},{8,9},{9,8},{10,11... | collective-permute-start | bytes 7077896 | tf_op jit(solution)/shard_map/ppermute | solution.py:38
  105.9 4.0 %sums.2.ours_ref = f32[512,1152]{1,0:T(8,128)S(1)} custom-call(f32[1,4096]{1,0:T(1,128)S(1)} %get-tuple-element.57.lse_ref, f32[2,4096]{1,0:T(2,128)S(1)} %get-tuple-element.58.top_ref, f32[2,512,512]{2,1,0:T(8,128)S(1)} %get-tuple-element.59.refs_0_, f32[2,512,512]{2,1,0:T(8,128)S(1)} %get-tuple-element.60.refs_1_, ...), custom_call_target="tpu_custom_call" | custom-call | flops 3758096384 | bytes 18874368 | tf_op jit(solution)/shard_map/sums/pallas_call | solution.py:227
  110.0 3.1 %final.1 = (f32[512,1024]{1,0:T(8,128)}, f32[1,64]{1,0:T(1,128)}) custom-call(s32[2]{0:T(128)S(1)} %pad_add_fusion.at_ref, f32[1,4096]{1,0:T(1,128)S(1)} %get-tuple-element.57.lse_ref, f32[2,4096]{1,0:T(2,128)S(1)} %get-tuple-element.58.top_ref, f32[512,1152]{1,0:T(8,128)S(1)} %sums.2.ours_ref, f32[512,1152]{1,0:T(8,128)S(1)} %collective-permute-done.16.theirs_ref, ...), custom_call_target="tpu_custom_call" | custom-call | tf_op jit(solution)/shard_map/final/pallas_call | solution.py:386
  (29 shorter events, 6.2 us)
Async XLA Ops:
  0.6 8.7 %collective-permute-start = (bf16[64,1024]{1,0:T(8,128)(2,1)}, bf16[64,1024]{1,0:T(8,128)(2,1)S(1)}, u32[]{:S(2)}, u32[]{:S(2)}) collective-permute-start(bf16[64,1024]{1,0:T(8,128)(2,1)} %refs_0_.1), channel_id=1, source_target_pairs={{8,0},{9,1},{24,16},{25,17},{40,32},{41,33},{56,48},{57,49},{10,2}... | collective-permute-start | bytes 393224 | tf_op jit(solution)/shard_map/ppermute | solution.py:33
  4.0 5.6 %collective-permute-start.1 = (bf16[64,1024]{1,0:T(8,128)(2,1)}, bf16[64,1024]{1,0:T(8,128)(2,1)S(1)}, u32[]{:S(2)}, u32[]{:S(2)}) collective-permute-start(bf16[64,1024]{1,0:T(8,128)(2,1)} %refs_0_.1), channel_id=1, source_target_pairs={{64,0},{65,1},{80,16},{81,17},{96,32},{97,33},{112,48},{113,49},{6... | collective-permute-start | bytes 393224 | tf_op jit(solution)/shard_map/ppermute | solution.py:33
  4.5 9.2 %collective-permute-start.2 = (bf16[64,1024]{1,0:T(8,128)(2,1)}, bf16[64,1024]{1,0:T(8,128)(2,1)S(1)}, u32[]{:S(2)}, u32[]{:S(2)}) collective-permute-start(bf16[64,1024]{1,0:T(8,128)(2,1)} %refs_0_.1), channel_id=1, source_target_pairs={{72,0},{73,1},{88,16},{89,17},{104,32},{105,33},{120,48},{121,49},... | collective-permute-start | bytes 393224 | tf_op jit(solution)/shard_map/ppermute | solution.py:33
  13.8 0.9 copy-start.1
  14.7 15.6 %collective-permute-start.3 = (bf16[256,1024]{1,0:T(8,128)(2,1)S(1)}, bf16[256,1024]{1,0:T(8,128)(2,1)S(1)}, u32[]{:S(2)}, u32[]{:S(2)}) collective-permute-start(bf16[256,1024]{1,0:T(8,128)(2,1)S(1)} %join.1.refs_0_), channel_id=1, source_target_pairs={{2,0},{17,1},{18,16},{33,17},{34,32},{49,33},{50,48},{1,49},{4,2},... | collective-permute-start | bytes 1572872 | tf_op jit(solution)/shard_map/ppermute | solution.py:33
  18.5 11.7 %collective-permute-start.4 = (bf16[256,1024]{1,0:T(8,128)(2,1)S(1)}, bf16[256,1024]{1,0:T(8,128)(2,1)S(1)}, u32[]{:S(2)}, u32[]{:S(2)}) collective-permute-start(bf16[256,1024]{1,0:T(8,128)(2,1)S(1)} %join.1.refs_0_), channel_id=1, source_target_pairs={{4,0},{33,1},{20,16},{49,17},{36,32},{1,33},{52,48},{17,49},{6,2},... | collective-permute-start | bytes 1572872 | tf_op jit(solution)/shard_map/ppermute | solution.py:33
  18.5 15.2 %collective-permute-start.5 = (bf16[256,1024]{1,0:T(8,128)(2,1)S(1)}, bf16[256,1024]{1,0:T(8,128)(2,1)S(1)}, u32[]{:S(2)}, u32[]{:S(2)}) collective-permute-start(bf16[256,1024]{1,0:T(8,128)(2,1)S(1)} %join.1.refs_0_), channel_id=1, source_target_pairs={{6,0},{49,1},{22,16},{1,17},{38,32},{17,33},{54,48},{33,49},{0,2},... | collective-permute-start | bytes 1572872 | tf_op jit(solution)/shard_map/ppermute | solution.py:33
  34.4 15.5 %collective-permute-start.7 = (bf16[512,1024]{1,0:T(8,128)(2,1)S(1)}, bf16[512,1024]{1,0:T(8,128)(2,1)S(1)}, u32[]{:S(2)}, u32[]{:S(2)}) collective-permute-start(bf16[512,1024]{1,0:T(8,128)(2,1)S(1)} %get-tuple-element.43.refs_1_.refs_7_.refs_8_), channel_id=1, source_target_pairs={{32,0},{5,1},{48,16},{21,17},{0,32},{37,33},{16,48},{53,49},{34,2}... | collective-permute-start | bytes 3145736 | tf_op jit(solution)/shard_map/ppermute | solution.py:33
  37.1 3.4 %copy-start = (bf16[4096,1024]{1,0:T(8,128)(2,1)S(1)}, bf16[4096,1024]{1,0:T(8,128)(2,1)}, u32[]{:S(2)}) copy-start(bf16[4096,1024]{1,0:T(8,128)(2,1)} %cents_ref.1) | copy-start | bytes 25165828
  42.5 9.7 %collective-permute-start.6 = (bf16[512,1024]{1,0:T(8,128)(2,1)S(1)}, bf16[512,1024]{1,0:T(8,128)(2,1)S(1)}, u32[]{:S(2)}, u32[]{:S(2)}) collective-permute-start(bf16[512,1024]{1,0:T(8,128)(2,1)S(1)} %share.1.mine_ref), channel_id=1, source_target_pairs={{0,1},{1,0},{2,3},{3,2},{4,5},{5,4},{6,7},{7,6},{8,9},{9,8},{10,11... | collective-permute-start | bytes 3145736 | tf_op jit(solution)/shard_map/ppermute | solution.py:38
  44.9 16.4 %collective-permute-start.12 = (bf16[512,1024]{1,0:T(8,128)(2,1)S(1)}, bf16[512,1024]{1,0:T(8,128)(2,1)S(1)}, u32[]{:S(2)}, u32[]{:S(2)}) collective-permute-start(bf16[512,1024]{1,0:T(8,128)(2,1)S(1)} %get-tuple-element.44.refs_2_.refs_8_.refs_9_), channel_id=1, source_target_pairs={{16,0},{3,1},{32,16},{19,17},{48,32},{35,33},{0,48},{51,49},{18,2}... | collective-permute-start | bytes 3145736 | tf_op jit(solution)/shard_map/ppermute | solution.py:33
  45.2 17.7 %collective-permute-start.11 = (bf16[512,1024]{1,0:T(8,128)(2,1)S(1)}, bf16[512,1024]{1,0:T(8,128)(2,1)S(1)}, u32[]{:S(2)}, u32[]{:S(2)}) collective-permute-start(bf16[512,1024]{1,0:T(8,128)(2,1)S(1)} %get-tuple-element.43.refs_1_.refs_7_.refs_8_), channel_id=1, source_target_pairs={{48,0},{7,1},{0,16},{23,17},{16,32},{39,33},{32,48},{55,49},{50,2}... | collective-permute-start | bytes 3145736 | tf_op jit(solution)/shard_map/ppermute | solution.py:33
  49.9 15.2 %collective-permute-start.10 = (bf16[512,1024]{1,0:T(8,128)(2,1)S(1)}, bf16[512,1024]{1,0:T(8,128)(2,1)S(1)}, u32[]{:S(2)}, u32[]{:S(2)}) collective-permute-start(bf16[512,1024]{1,0:T(8,128)(2,1)S(1)} %collective-permute-done.7.refs_0_.refs_11_.refs_12_), channel_id=1, source_target_pairs={{8,0},{73,1},{24,16},{89,17},{40,32},{105,33},{56,48},{121,49},{10... | collective-permute-start | bytes 3145736 | tf_op jit(solution)/shard_map/ppermute | solution.py:49
  49.9 24.1 %collective-permute-start.8 = (bf16[512,1024]{1,0:T(8,128)(2,1)S(1)}, bf16[512,1024]{1,0:T(8,128)(2,1)S(1)}, u32[]{:S(2)}, u32[]{:S(2)}) collective-permute-start(bf16[512,1024]{1,0:T(8,128)(2,1)S(1)} %get-tuple-element.43.refs_1_.refs_7_.refs_8_), channel_id=1, source_target_pairs={{16,0},{3,1},{32,16},{19,17},{48,32},{35,33},{0,48},{51,49},{18,2}... | collective-permute-start | bytes 3145736 | tf_op jit(solution)/shard_map/ppermute | solution.py:33
  52.2 20.2 %collective-permute-start.9 = (bf16[512,1024]{1,0:T(8,128)(2,1)S(1)}, bf16[512,1024]{1,0:T(8,128)(2,1)S(1)}, u32[]{:S(2)}, u32[]{:S(2)}) collective-permute-start(bf16[512,1024]{1,0:T(8,128)(2,1)S(1)} %get-tuple-element.44.refs_2_.refs_8_.refs_9_), channel_id=1, source_target_pairs={{48,0},{7,1},{0,16},{23,17},{16,32},{39,33},{32,48},{55,49},{50,2}... | collective-permute-start | bytes 3145736 | tf_op jit(solution)/shard_map/ppermute | solution.py:33
  87.3 3.6 %collective-permute-start.13 = (f32[8,640]{1,0:T(8,128)S(1)}, f32[8,640]{1,0:T(8,128)S(1)}, u32[]{:S(2)}, u32[]{:S(2)}) collective-permute-start(f32[8,640]{1,0:T(8,128)S(1)} %plane.1.refs_0_), channel_id=1, source_target_pairs={{16,0},{3,1},{32,16},{19,17},{48,32},{35,33},{0,48},{51,49},{18,2}... | collective-permute-start | bytes 61448 | tf_op jit(solution)/shard_map/ppermute | solution.py:33
  88.0 4.1 %collective-permute-start.14 = (f32[8,640]{1,0:T(8,128)S(1)}, f32[8,640]{1,0:T(8,128)S(1)}, u32[]{:S(2)}, u32[]{:S(2)}) collective-permute-start(f32[8,640]{1,0:T(8,128)S(1)} %plane.1.refs_0_), channel_id=1, source_target_pairs={{32,0},{5,1},{48,16},{21,17},{0,32},{37,33},{16,48},{53,49},{34,2}... | collective-permute-start | bytes 61448 | tf_op jit(solution)/shard_map/ppermute | solution.py:33
  90.3 3.8 %collective-permute-start.15 = (f32[8,640]{1,0:T(8,128)S(1)}, f32[8,640]{1,0:T(8,128)S(1)}, u32[]{:S(2)}, u32[]{:S(2)}) collective-permute-start(f32[8,640]{1,0:T(8,128)S(1)} %plane.1.refs_0_), channel_id=1, source_target_pairs={{48,0},{7,1},{0,16},{23,17},{16,32},{39,33},{32,48},{55,49},{50,2}... | collective-permute-start | bytes 61448 | tf_op jit(solution)/shard_map/ppermute | solution.py:33
  99.8 10.3 %collective-permute-start.16 = (f32[512,1152]{1,0:T(8,128)S(1)}, f32[512,1152]{1,0:T(8,128)S(1)}, u32[]{:S(2)}, u32[]{:S(2)}) collective-permute-start(f32[512,1152]{1,0:T(8,128)S(1)} %sums.3), channel_id=1, source_target_pairs={{0,1},{1,0},{2,3},{3,2},{4,5},{5,4},{6,7},{7,6},{8,9},{9,8},{10,11... | collective-permute-start | bytes 7077896 | tf_op jit(solution)/shard_map/ppermute | solution.py:38
  105.8 4.2 %collective-permute-start.17 = (f32[64,128]{1,0:T(8,128)S(1)}, f32[64,128]{1,0:T(8,128)S(1)}, u32[]{:S(2)}, u32[]{:S(2)}) collective-permute-start(f32[64,128]{1,0:T(8,128)S(1)} %get-tuple-element.67.pack_ref), channel_id=1, source_target_pairs={{0,1},{1,0},{2,3},{3,2},{4,5},{5,4},{6,7},{7,6},{8,9},{9,8},{10,11... | collective-permute-start | bytes 98312 | tf_op jit(solution)/shard_map/ppermute | solution.py:38

commit v13 on v12

--- a/solution.py
+++ b/solution.py
@@ -149,8 +149,8 @@
     value = jnp.concatenate([lse[line : line + 1, :] for line in range(8)], axis=1)
     for tile in range(32):
         pack_ref[tile : tile + 1, :] = value[:, tile * 128 : (tile + 1) * 128]
-    for k, plane in enumerate(planes):
-        first = pl.multiple_of(32 + (spot_ref[2] + k) % 4 * 8, 8)
+    for offset, plane in zip((0, 3, 2, 1), planes):
+        first = pl.multiple_of(32 + (spot_ref[2] + offset) % 4 * 8, 8)
         pack_ref[pl.ds(first, 8), :] = plane[:, 512:640]
     for dim in range(3):
         value = roll_within(value, dim, (4 - spot_ref[dim]) % 4)
@@ -160,16 +160,16 @@
         own_ref[:, lanes] = roll_within(value[:, lanes], 0, 4 - spot_ref[3])
 
 
-def join_kernel(*refs):
+def join_kernel(slots, *refs):
     *parts, out_ref = refs
-    at = 0
-    for part in parts:
-        out_ref[at : at + part.shape[0], :] = part[...]
-        at += part.shape[0]
+    rows = parts[0].shape[0]
+    for slot, part in zip(slots, parts):
+        out_ref[slot * rows : (slot + 1) * rows, :] = part[...]
 
 
 def halves_kernel(spot_ref, *refs):
-    *parts, first_ref, second_ref = refs
+    line, back, across, near, first_ref, second_ref = refs
+    parts = (line, near, across, back)
     rows = parts[0].shape[0]
     for side in range(2):
 
@@ -180,11 +180,11 @@
                 out_ref[k % 2 * rows : (k % 2 + 1) * rows, :] = part[...]
 
 
-def join(*parts):
+def join(slots, *parts):
     vmem = pl.BlockSpec(memory_space=pltpu.VMEM)
     shape = (sum(part.shape[0] for part in parts), parts[0].shape[1])
     return pl.pallas_call(
-        join_kernel,
+        functools.partial(join_kernel, slots),
         out_shape=jax.ShapeDtypeStruct(shape, parts[0].dtype),
         in_specs=[vmem] * len(parts),
         out_specs=vmem,
@@ -309,9 +309,9 @@
     small = pltpu.CompilerParams(vmem_limit_bytes=8 << 20)
     ids = jnp.tile(destination.astype(jnp.float32), 2).reshape(1, 128)
     at_word = jnp.stack([samp, cent]).astype(jnp.int32)
-    line = join(embeddings, *[fetch(embeddings, 0, step) for step in (1, 2, 3)])
+    line = join((0, 2, 1, 3), embeddings, *[fetch(embeddings, 0, step) for step in (2, 1, 3)])
     spot, ids, at_word, line = lax.optimization_barrier((spot, ids, at_word, line))
-    near, across, back = [fetch(line, 1, step) for step in (1, 2, 3)]
+    back, across, near = [fetch(line, 1, step) for step in (3, 2, 1)]
     first, second = pl.pallas_call(
         halves_kernel,
         out_shape=[jax.ShapeDtypeStruct((512, width), embeddings.dtype)] * 2,
@@ -319,7 +319,7 @@
         out_specs=[vmem] * 2,
         compiler_params=small,
         name="halves",
-    )(spot, line, near, across, back)
+    )(spot, line, back, across, near)
     far_first = fetch(first, 2, 2)
     after_first, before_first = fetch(first, 2, 1), fetch(first, 2, 3)
     after_second, before_second = fetch(second, 2, 1), fetch(second, 2, 3)
@@ -378,7 +378,7 @@
         in_specs=[smem] + [vmem] * 4,
         compiler_params=small,
         name="merge",
-    )(spot, plane, *[fetch(plane, 2, offset) for offset in (1, 2, 3)])
+    )(spot, plane, *[fetch(plane, 2, offset) for offset in (3, 2, 1)])
     theirs = sums_call(1, lse, tops, ps, chunks)
     received = swap_cores(theirs)
     partner = swap_cores(pack)

time: 114 us -> 111 us (0.974)
  waiting for transfers between devices: 40.2 us -> 28.2 us
  starting transfers between devices: 27.6 us -> 35.7 us
  blocking collectives: 10.5 us -> 12.3 us
    ppermute x14, waiting for transfers between devices: 39.5 us -> 27.1 us  [fetch(): return lax.ppermute(value, BOTH, pairs)]
    ppermute x14, starting transfers between devices: 19 us -> 23.3 us  [fetch(): return lax.ppermute(value, BOTH, pairs)]
    ppermute x1, starting transfers between devices: 0.01 us -> 3.17 us  [swap_sides(): return lax.ppermute(value, BOTH, pairs)]
    all_to_all x1, blocking collectives: 10.5 us -> 12.3 us  [shards(): lax.all_to_all(local, BOTH, split_axis=0, concat_axis=0, tiled=True, axis...]
where the time goes in v13:
time: 111 us
  starting transfers between devices  35.7 us (32%)
  Pallas kernels  29 us (26%)
  waiting for transfers between devices  28.2 us (25%)
  blocking collectives  12.3 us (11%)
  local copies, waits for them, and re-layouts  4.46 us (4%)
    ppermute x14, waiting for transfers between devices, fetch(): return lax.ppermute(value, BOTH, pairs)  27.1 us
    ppermute x14, starting transfers between devices, fetch(): return lax.ppermute(value, BOTH, pairs)  23.3 us
    pallas_call x6, Pallas kernels, scores_call(): pl.pallas_call(functools.partial(scores_kernel, factor, count), out_shape...  12.5 us
    all_to_all x1, blocking collectives, shards(): lax.all_to_all(local, BOTH, split_axis=0, concat_axis=0, tiled=True, axis...  12.3 us
    ppermute x3, starting transfers between devices, swap_cores(): return lax.ppermute(value, BOTH, pairs)  9.21 us
    pallas_call x2, Pallas kernels, sums_call(): pl.pallas_call(functools.partial(sums_kernel, half, count), out_shape=jax...  8.5 us
    unnamed x4, local copies, waits for them, and re-layouts  4.29 us
    ppermute x1, starting transfers between devices, swap_sides(): return lax.ppermute(value, BOTH, pairs)  3.17 us
  transfers between devices with their start and end apart: 18, of which 12 were waited for; matrix products, arithmetic and copies ran while one was open for 1% of the time, Pallas kernels for 15%

profile of v13, /device:TPU:1, one launch (start us, length us, event | category | flops | bytes accessed | tf_op | source)
XLA Modules:
  0.0 111.2 jit_solution(3705288636140619164)
XLA Ops:
  0.6 3.7 %collective-permute-start = (bf16[64,1024]{1,0:T(8,128)(2,1)}, bf16[64,1024]{1,0:T(8,128)(2,1)S(1)}, u32[]{:S(2)}, u32[]{:S(2)}) collective-permute-start(bf16[64,1024]{1,0:T(8,128)(2,1)} %refs_0_.1), channel_id=1, source_target_pairs={{64,0},{65,1},{80,16},{81,17},{96,32},{97,33},{112,48},{113,49},{6... | collective-permute-start | bytes 393224 | tf_op jit(solution)/shard_map/ppermute | solution.py:33
  7.2 3.3 %collective-permute-done.1.refs_2_ = bf16[64,1024]{1,0:T(8,128)(2,1)S(1)} collective-permute-done((bf16[64,1024]{1,0:T(8,128)(2,1)}, bf16[64,1024]{1,0:T(8,128)(2,1)S(1)}, u32[]{:S(2)}, u32[]{:S(2)}) %collective-permute-start.1) | collective-permute-done | bytes 131104 | tf_op jit(solution)/shard_map/ppermute | solution.py:33
  11.5 1.8 %collective-permute-start.3 = (bf16[256,1024]{1,0:T(8,128)(2,1)S(1)}, bf16[256,1024]{1,0:T(8,128)(2,1)S(1)}, u32[]{:S(2)}, u32[]{:S(2)}) collective-permute-start(bf16[256,1024]{1,0:T(8,128)(2,1)S(1)} %join.1.refs_0_), channel_id=1, source_target_pairs={{6,0},{49,1},{22,16},{1,17},{38,32},{17,33},{54,48},{33,49},{0,2},... | collective-permute-start | bytes 1572872 | tf_op jit(solution)/shard_map/ppermute | solution.py:33
  13.2 3.3 %collective-permute-start.4 = (bf16[256,1024]{1,0:T(8,128)(2,1)S(1)}, bf16[256,1024]{1,0:T(8,128)(2,1)S(1)}, u32[]{:S(2)}, u32[]{:S(2)}) collective-permute-start(bf16[256,1024]{1,0:T(8,128)(2,1)S(1)} %join.1.refs_0_), channel_id=1, source_target_pairs={{4,0},{33,1},{20,16},{49,17},{36,32},{1,33},{52,48},{17,49},{6,2},... | collective-permute-start | bytes 1572872 | tf_op jit(solution)/shard_map/ppermute | solution.py:33
  17.3 5.0 %collective-permute-done.3.refs_1_ = bf16[256,1024]{1,0:T(8,128)(2,1)S(1)} collective-permute-done((bf16[256,1024]{1,0:T(8,128)(2,1)S(1)}, bf16[256,1024]{1,0:T(8,128)(2,1)S(1)}, u32[]{:S(2)}, u32[]{:S(2)}) %collective-permute-start.3) | collective-permute-done | bytes 524320 | tf_op jit(solution)/shard_map/ppermute | solution.py:33
  22.2 6.8 %collective-permute-done.4.refs_2_ = bf16[256,1024]{1,0:T(8,128)(2,1)S(1)} collective-permute-done((bf16[256,1024]{1,0:T(8,128)(2,1)S(1)}, bf16[256,1024]{1,0:T(8,128)(2,1)S(1)}, u32[]{:S(2)}, u32[]{:S(2)}) %collective-permute-start.4) | collective-permute-done | bytes 524320 | tf_op jit(solution)/shard_map/ppermute | solution.py:33
  29.7 2.7 %collective-permute-start.7 = (bf16[512,1024]{1,0:T(8,128)(2,1)S(1)}, bf16[512,1024]{1,0:T(8,128)(2,1)S(1)}, u32[]{:S(2)}, u32[]{:S(2)}) collective-permute-start(bf16[512,1024]{1,0:T(8,128)(2,1)S(1)} %get-tuple-element.43.refs_1_.refs_7_.refs_8_), channel_id=1, source_target_pairs={{32,0},{5,1},{48,16},{21,17},{0,32},{37,33},{16,48},{53,49},{34,2}... | collective-permute-start | bytes 3145736 | tf_op jit(solution)/shard_map/ppermute | solution.py:33
  32.4 3.4 %copy-done = bf16[4096,1024]{1,0:T(8,128)(2,1)S(1)} copy-done((bf16[4096,1024]{1,0:T(8,128)(2,1)S(1)}, bf16[4096,1024]{1,0:T(8,128)(2,1)}, u32[]{:S(2)}) %copy-start) | copy-done | bytes 8388632
  35.8 2.0 %share.1.mine_ref = bf16[512,1024]{1,0:T(8,128)(2,1)S(1)} custom-call(s32[2]{0:T(128)S(1)} %pad_add_fusion.at_ref, bf16[4096,1024]{1,0:T(8,128)(2,1)S(1)} %copy-done), custom_call_target="tpu_custom_call" | custom-call | tf_op jit(solution)/shard_map/share/pallas_call | solution.py:327
  37.8 3.3 %collective-permute-start.6 = (bf16[512,1024]{1,0:T(8,128)(2,1)S(1)}, bf16[512,1024]{1,0:T(8,128)(2,1)S(1)}, u32[]{:S(2)}, u32[]{:S(2)}) collective-permute-start(bf16[512,1024]{1,0:T(8,128)(2,1)S(1)} %share.1.mine_ref), channel_id=1, source_target_pairs={{0,1},{1,0},{2,3},{3,2},{4,5},{5,4},{6,7},{7,6},{8,9},{9,8},{10,11... | collective-permute-start | bytes 3145736 | tf_op jit(solution)/shard_map/ppermute | solution.py:38
  41.1 2.0 %collective-permute-start.12 = (bf16[512,1024]{1,0:T(8,128)(2,1)S(1)}, bf16[512,1024]{1,0:T(8,128)(2,1)S(1)}, u32[]{:S(2)}, u32[]{:S(2)}) collective-permute-start(bf16[512,1024]{1,0:T(8,128)(2,1)S(1)} %get-tuple-element.44.refs_2_.refs_8_.refs_9_), channel_id=1, source_target_pairs={{16,0},{3,1},{32,16},{19,17},{48,32},{35,33},{0,48},{51,49},{18,2}... | collective-permute-start | bytes 3145736 | tf_op jit(solution)/shard_map/ppermute | solution.py:33
  43.2 2.1 %collective-permute-done.7.refs_0_.refs_11_.refs_12_ = bf16[512,1024]{1,0:T(8,128)(2,1)S(1)} collective-permute-done((bf16[512,1024]{1,0:T(8,128)(2,1)S(1)}, bf16[512,1024]{1,0:T(8,128)(2,1)S(1)}, u32[]{:S(2)}, u32[]{:S(2)}) %collective-permute-start.7) | collective-permute-done | bytes 1048608 | tf_op jit(solution)/shard_map/ppermute | solution.py:33
  45.3 3.2 %collective-permute-start.10 = (bf16[512,1024]{1,0:T(8,128)(2,1)S(1)}, bf16[512,1024]{1,0:T(8,128)(2,1)S(1)}, u32[]{:S(2)}, u32[]{:S(2)}) collective-permute-start(bf16[512,1024]{1,0:T(8,128)(2,1)S(1)} %collective-permute-done.7.refs_0_.refs_11_.refs_12_), channel_id=1, source_target_pairs={{8,0},{73,1},{24,16},{89,17},{40,32},{105,33},{56,48},{121,49},{10... | collective-permute-start | bytes 3145736 | tf_op jit(solution)/shard_map/ppermute | solution.py:49
  48.4 2.5 %collective-permute-start.8 = (bf16[512,1024]{1,0:T(8,128)(2,1)S(1)}, bf16[512,1024]{1,0:T(8,128)(2,1)S(1)}, u32[]{:S(2)}, u32[]{:S(2)}) collective-permute-start(bf16[512,1024]{1,0:T(8,128)(2,1)S(1)} %get-tuple-element.43.refs_1_.refs_7_.refs_8_), channel_id=1, source_target_pairs={{16,0},{3,1},{32,16},{19,17},{48,32},{35,33},{0,48},{51,49},{18,2}... | collective-permute-start | bytes 3145736 | tf_op jit(solution)/shard_map/ppermute | solution.py:33
  50.9 4.3 %scores.6 = (f32[2,512,512]{2,1,0:T(8,128)S(1)}, f32[2,512,512]{2,1,0:T(8,128)S(1)}, f32[2,512,512]{2,1,0:T(8,128)S(1)}, f32[4,1536]{1,0:T(4,128)S(1)}) custom-call(bf16[512,1024]{1,0:T(8,128)(2,1)S(1)} %share.1.mine_ref, bf16[512,1024]{1,0:T(8,128)(2,1)S(1)} %collective-permute-done.6.other_ref, ...), custom_call_target="tpu_custom_call" | custom-call | flops 6442450944 | bytes 11534336 | tf_op jit(solution)/shard_map/scores/pallas_call | solution.py:85
  55.2 1.3 %collective-permute-done.12.refs_0_.refs_10_.refs_11_ = bf16[512,1024]{1,0:T(8,128)(2,1)S(1)} collective-permute-done((bf16[512,1024]{1,0:T(8,128)(2,1)S(1)}, bf16[512,1024]{1,0:T(8,128)(2,1)S(1)}, u32[]{:S(2)}, u32[]{:S(2)}) %collective-permute-start.12) | collective-permute-done | bytes 1048608 | tf_op jit(solution)/shard_map/ppermute | solution.py:33
  56.5 1.6 %scores.7 = (f32[2,512,512]{2,1,0:T(8,128)S(1)}, f32[4,512]{1,0:T(4,128)S(1)}) custom-call(bf16[512,1024]{1,0:T(8,128)(2,1)S(1)} %share.1.mine_ref, bf16[512,1024]{1,0:T(8,128)(2,1)S(1)} %collective-permute-done.6.other_ref, bf16[512,1024]{1,0:T(8,128)(2,1)S(1)} %collective-permute-done.12.refs_0_.refs_10_.refs_11_), custom_call_target="tpu_custom_call" | custom-call | flops 2147483648 | bytes 5242880 | tf_op jit(solution)/shard_map/scores/pallas_call | solution.py:85
  58.3 1.6 %scores.8 = (f32[2,512,512]{2,1,0:T(8,128)S(1)}, f32[4,512]{1,0:T(4,128)S(1)}) custom-call(bf16[512,1024]{1,0:T(8,128)(2,1)S(1)} %share.1.mine_ref, bf16[512,1024]{1,0:T(8,128)(2,1)S(1)} %collective-permute-done.6.other_ref, bf16[512,1024]{1,0:T(8,128)(2,1)S(1)} %collective-permute-done.11.refs_0_.refs_13_.refs_14_), custom_call_target="tpu_custom_call" | custom-call | flops 2147483648 | bytes 5242880 | tf_op jit(solution)/shard_map/scores/pallas_call | solution.py:85
  60.9 1.6 %scores.9 = (f32[2,512,512]{2,1,0:T(8,128)S(1)}, f32[4,512]{1,0:T(4,128)S(1)}) custom-call(bf16[512,1024]{1,0:T(8,128)(2,1)S(1)} %share.1.mine_ref, bf16[512,1024]{1,0:T(8,128)(2,1)S(1)} %collective-permute-done.6.other_ref, bf16[512,1024]{1,0:T(8,128)(2,1)S(1)} %collective-permute-done.10.refs_0_.refs_12_.refs_13_), custom_call_target="tpu_custom_call" | custom-call | flops 2147483648 | bytes 5242880 | tf_op jit(solution)/shard_map/scores/pallas_call | solution.py:85
  62.5 7.0 %collective-permute-done.9.refs_0_.refs_15_.refs_1_ = bf16[512,1024]{1,0:T(8,128)(2,1)S(1)} collective-permute-done((bf16[512,1024]{1,0:T(8,128)(2,1)S(1)}, bf16[512,1024]{1,0:T(8,128)(2,1)S(1)}, u32[]{:S(2)}, u32[]{:S(2)}) %collective-permute-start.9) | collective-permute-done | bytes 1048608 | tf_op jit(solution)/shard_map/ppermute | solution.py:33
  69.5 1.6 %scores.10 = (f32[2,512,512]{2,1,0:T(8,128)S(1)}, f32[4,512]{1,0:T(4,128)S(1)}) custom-call(bf16[512,1024]{1,0:T(8,128)(2,1)S(1)} %share.1.mine_ref, bf16[512,1024]{1,0:T(8,128)(2,1)S(1)} %collective-permute-done.6.other_ref, bf16[512,1024]{1,0:T(8,128)(2,1)S(1)} %collective-permute-done.9.refs_0_.refs_15_.refs_1_), custom_call_target="tpu_custom_call" | custom-call | flops 2147483648 | bytes 5242880 | tf_op jit(solution)/shard_map/scores/pallas_call | solution.py:85
  71.2 1.6 %scores.11 = (f32[2,512,512]{2,1,0:T(8,128)S(1)}, f32[4,512]{1,0:T(4,128)S(1)}) custom-call(bf16[512,1024]{1,0:T(8,128)(2,1)S(1)} %share.1.mine_ref, bf16[512,1024]{1,0:T(8,128)(2,1)S(1)} %collective-permute-done.6.other_ref, bf16[512,1024]{1,0:T(8,128)(2,1)S(1)} %collective-permute-done.8.refs_0_.refs_9_.refs_10_), custom_call_target="tpu_custom_call" | custom-call | flops 2147483648 | bytes 5242880 | tf_op jit(solution)/shard_map/scores/pallas_call | solution.py:85
  72.8 1.1 first.1
  73.9 12.3 %all_to_all.5.all_ref = f32[16,8,640]{2,1,0:T(8,128)S(1)} all-to-all(f32[16,8,640]{2,1,0:T(8,128)S(1)} %get-tuple-element.56), channel_id=1, replica_groups={{0,8,64,72,2,10,66,74,4,12,68,76,6,14,70,78},{16,24,80,88,18,26,82,90,2..., dimensions={0} | all-to-all | bytes 655360 | tf_op jit(solution)/shard_map/all_to_all | solution.py:363
  86.3 1.6 %collective-permute-start.13 = (f32[8,640]{1,0:T(8,128)S(1)}, f32[8,640]{1,0:T(8,128)S(1)}, u32[]{:S(2)}, u32[]{:S(2)}) collective-permute-start(f32[8,640]{1,0:T(8,128)S(1)} %plane.1.refs_0_), channel_id=1, source_target_pairs={{48,0},{7,1},{0,16},{23,17},{16,32},{39,33},{32,48},{55,49},{50,2}... | collective-permute-start | bytes 61448 | tf_op jit(solution)/shard_map/ppermute | solution.py:33
  87.9 1.6 %collective-permute-start.14 = (f32[8,640]{1,0:T(8,128)S(1)}, f32[8,640]{1,0:T(8,128)S(1)}, u32[]{:S(2)}, u32[]{:S(2)}) collective-permute-start(f32[8,640]{1,0:T(8,128)S(1)} %plane.1.refs_0_), channel_id=1, source_target_pairs={{32,0},{5,1},{48,16},{21,17},{0,32},{37,33},{16,48},{53,49},{34,2}... | collective-permute-start | bytes 61448 | tf_op jit(solution)/shard_map/ppermute | solution.py:33
  89.4 2.0 %collective-permute-start.15 = (f32[8,640]{1,0:T(8,128)S(1)}, f32[8,640]{1,0:T(8,128)S(1)}, u32[]{:S(2)}, u32[]{:S(2)}) collective-permute-start(f32[8,640]{1,0:T(8,128)S(1)} %plane.1.refs_0_), channel_id=1, source_target_pairs={{16,0},{3,1},{32,16},{19,17},{48,32},{35,33},{0,48},{51,49},{18,2}... | collective-permute-start | bytes 61448 | tf_op jit(solution)/shard_map/ppermute | solution.py:33
  92.3 1.0 merge.1
  93.4 4.5 %sums.3 = f32[512,1152]{1,0:T(8,128)S(1)} custom-call(f32[1,4096]{1,0:T(1,128)S(1)} %get-tuple-element.57.lse_ref, f32[2,4096]{1,0:T(2,128)S(1)} %get-tuple-element.58.top_ref, f32[2,512,512]{2,1,0:T(8,128)S(1)} %get-tuple-element.59.refs_0_, f32[2,512,512]{2,1,0:T(8,128)S(1)} %get-tuple-element.60.refs_1_, f32[2,512,512]{2,1,0:T(8,128)S(1)} %get-tuple-element.61.refs_2_, ...), custom_call_target="tpu_custom_call" | custom-call | flops 4294967296 | bytes 18874368 | tf_op jit(solution)/shard_map/sums/pallas_call | solution.py:227
  97.9 5.8 %collective-permute-start.16 = (f32[512,1152]{1,0:T(8,128)S(1)}, f32[512,1152]{1,0:T(8,128)S(1)}, u32[]{:S(2)}, u32[]{:S(2)}) collective-permute-start(f32[512,1152]{1,0:T(8,128)S(1)} %sums.3), channel_id=1, source_target_pairs={{0,1},{1,0},{2,3},{3,2},{4,5},{5,4},{6,7},{7,6},{8,9},{9,8},{10,11... | collective-permute-start | bytes 7077896 | tf_op jit(solution)/shard_map/ppermute | solution.py:38
  103.8 4.0 %sums.2.ours_ref = f32[512,1152]{1,0:T(8,128)S(1)} custom-call(f32[1,4096]{1,0:T(1,128)S(1)} %get-tuple-element.57.lse_ref, f32[2,4096]{1,0:T(2,128)S(1)} %get-tuple-element.58.top_ref, f32[2,512,512]{2,1,0:T(8,128)S(1)} %get-tuple-element.59.refs_0_, f32[2,512,512]{2,1,0:T(8,128)S(1)} %get-tuple-element.60.refs_1_, ...), custom_call_target="tpu_custom_call" | custom-call | flops 3758096384 | bytes 18874368 | tf_op jit(solution)/shard_map/sums/pallas_call | solution.py:227
  107.9 3.1 %final.1 = (f32[512,1024]{1,0:T(8,128)}, f32[1,64]{1,0:T(1,128)}) custom-call(s32[2]{0:T(128)S(1)} %pad_add_fusion.at_ref, f32[1,4096]{1,0:T(1,128)S(1)} %get-tuple-element.57.lse_ref, f32[2,4096]{1,0:T(2,128)S(1)} %get-tuple-element.58.top_ref, f32[512,1152]{1,0:T(8,128)S(1)} %sums.2.ours_ref, f32[512,1152]{1,0:T(8,128)S(1)} %collective-permute-done.16.theirs_ref, ...), custom_call_target="tpu_custom_call" | custom-call | tf_op jit(solution)/shard_map/final/pallas_call | solution.py:386
  (29 shorter events, 7.6 us)
Async XLA Ops:
  0.6 6.6 %collective-permute-start = (bf16[64,1024]{1,0:T(8,128)(2,1)}, bf16[64,1024]{1,0:T(8,128)(2,1)S(1)}, u32[]{:S(2)}, u32[]{:S(2)}) collective-permute-start(bf16[64,1024]{1,0:T(8,128)(2,1)} %refs_0_.1), channel_id=1, source_target_pairs={{64,0},{65,1},{80,16},{81,17},{96,32},{97,33},{112,48},{113,49},{6... | collective-permute-start | bytes 393224 | tf_op jit(solution)/shard_map/ppermute | solution.py:33
  4.3 6.2 %collective-permute-start.1 = (bf16[64,1024]{1,0:T(8,128)(2,1)}, bf16[64,1024]{1,0:T(8,128)(2,1)S(1)}, u32[]{:S(2)}, u32[]{:S(2)}) collective-permute-start(bf16[64,1024]{1,0:T(8,128)(2,1)} %refs_0_.1), channel_id=1, source_target_pairs={{8,0},{9,1},{24,16},{25,17},{40,32},{41,33},{56,48},{57,49},{10,2}... | collective-permute-start | bytes 393224 | tf_op jit(solution)/shard_map/ppermute | solution.py:33
  5.1 5.4 %collective-permute-start.2 = (bf16[64,1024]{1,0:T(8,128)(2,1)}, bf16[64,1024]{1,0:T(8,128)(2,1)S(1)}, u32[]{:S(2)}, u32[]{:S(2)}) collective-permute-start(bf16[64,1024]{1,0:T(8,128)(2,1)} %refs_0_.1), channel_id=1, source_target_pairs={{72,0},{73,1},{88,16},{89,17},{104,32},{105,33},{120,48},{121,49},... | collective-permute-start | bytes 393224 | tf_op jit(solution)/shard_map/ppermute | solution.py:33
  10.5 0.9 copy-start.1
  11.5 10.8 %collective-permute-start.3 = (bf16[256,1024]{1,0:T(8,128)(2,1)S(1)}, bf16[256,1024]{1,0:T(8,128)(2,1)S(1)}, u32[]{:S(2)}, u32[]{:S(2)}) collective-permute-start(bf16[256,1024]{1,0:T(8,128)(2,1)S(1)} %join.1.refs_0_), channel_id=1, source_target_pairs={{6,0},{49,1},{22,16},{1,17},{38,32},{17,33},{54,48},{33,49},{0,2},... | collective-permute-start | bytes 1572872 | tf_op jit(solution)/shard_map/ppermute | solution.py:33
  13.2 15.8 %collective-permute-start.4 = (bf16[256,1024]{1,0:T(8,128)(2,1)S(1)}, bf16[256,1024]{1,0:T(8,128)(2,1)S(1)}, u32[]{:S(2)}, u32[]{:S(2)}) collective-permute-start(bf16[256,1024]{1,0:T(8,128)(2,1)S(1)} %join.1.refs_0_), channel_id=1, source_target_pairs={{4,0},{33,1},{20,16},{49,17},{36,32},{1,33},{52,48},{17,49},{6,2},... | collective-permute-start | bytes 1572872 | tf_op jit(solution)/shard_map/ppermute | solution.py:33
  16.5 12.5 %collective-permute-start.5 = (bf16[256,1024]{1,0:T(8,128)(2,1)S(1)}, bf16[256,1024]{1,0:T(8,128)(2,1)S(1)}, u32[]{:S(2)}, u32[]{:S(2)}) collective-permute-start(bf16[256,1024]{1,0:T(8,128)(2,1)S(1)} %join.1.refs_0_), channel_id=1, source_target_pairs={{2,0},{17,1},{18,16},{33,17},{34,32},{49,33},{50,48},{1,49},{4,2},... | collective-permute-start | bytes 1572872 | tf_op jit(solution)/shard_map/ppermute | solution.py:33
  29.7 15.5 %collective-permute-start.7 = (bf16[512,1024]{1,0:T(8,128)(2,1)S(1)}, bf16[512,1024]{1,0:T(8,128)(2,1)S(1)}, u32[]{:S(2)}, u32[]{:S(2)}) collective-permute-start(bf16[512,1024]{1,0:T(8,128)(2,1)S(1)} %get-tuple-element.43.refs_1_.refs_7_.refs_8_), channel_id=1, source_target_pairs={{32,0},{5,1},{48,16},{21,17},{0,32},{37,33},{16,48},{53,49},{34,2}... | collective-permute-start | bytes 3145736 | tf_op jit(solution)/shard_map/ppermute | solution.py:33
  32.4 3.4 %copy-start = (bf16[4096,1024]{1,0:T(8,128)(2,1)S(1)}, bf16[4096,1024]{1,0:T(8,128)(2,1)}, u32[]{:S(2)}) copy-start(bf16[4096,1024]{1,0:T(8,128)(2,1)} %cents_ref.1) | copy-start | bytes 25165828
  37.8 13.1 %collective-permute-start.6 = (bf16[512,1024]{1,0:T(8,128)(2,1)S(1)}, bf16[512,1024]{1,0:T(8,128)(2,1)S(1)}, u32[]{:S(2)}, u32[]{:S(2)}) collective-permute-start(bf16[512,1024]{1,0:T(8,128)(2,1)S(1)} %share.1.mine_ref), channel_id=1, source_target_pairs={{0,1},{1,0},{2,3},{3,2},{4,5},{5,4},{6,7},{7,6},{8,9},{9,8},{10,11... | collective-permute-start | bytes 3145736 | tf_op jit(solution)/shard_map/ppermute | solution.py:38
  41.1 15.4 %collective-permute-start.12 = (bf16[512,1024]{1,0:T(8,128)(2,1)S(1)}, bf16[512,1024]{1,0:T(8,128)(2,1)S(1)}, u32[]{:S(2)}, u32[]{:S(2)}) collective-permute-start(bf16[512,1024]{1,0:T(8,128)(2,1)S(1)} %get-tuple-element.44.refs_2_.refs_8_.refs_9_), channel_id=1, source_target_pairs={{16,0},{3,1},{32,16},{19,17},{48,32},{35,33},{0,48},{51,49},{18,2}... | collective-permute-start | bytes 3145736 | tf_op jit(solution)/shard_map/ppermute | solution.py:33
  43.1 15.2 %collective-permute-start.11 = (bf16[512,1024]{1,0:T(8,128)(2,1)S(1)}, bf16[512,1024]{1,0:T(8,128)(2,1)S(1)}, u32[]{:S(2)}, u32[]{:S(2)}) collective-permute-start(bf16[512,1024]{1,0:T(8,128)(2,1)S(1)} %get-tuple-element.43.refs_1_.refs_7_.refs_8_), channel_id=1, source_target_pairs={{48,0},{7,1},{0,16},{23,17},{16,32},{39,33},{32,48},{55,49},{50,2}... | collective-permute-start | bytes 3145736 | tf_op jit(solution)/shard_map/ppermute | solution.py:33
  45.3 15.7 %collective-permute-start.10 = (bf16[512,1024]{1,0:T(8,128)(2,1)S(1)}, bf16[512,1024]{1,0:T(8,128)(2,1)S(1)}, u32[]{:S(2)}, u32[]{:S(2)}) collective-permute-start(bf16[512,1024]{1,0:T(8,128)(2,1)S(1)} %collective-permute-done.7.refs_0_.refs_11_.refs_12_), channel_id=1, source_target_pairs={{8,0},{73,1},{24,16},{89,17},{40,32},{105,33},{56,48},{121,49},{10... | collective-permute-start | bytes 3145736 | tf_op jit(solution)/shard_map/ppermute | solution.py:49
  48.4 22.7 %collective-permute-start.8 = (bf16[512,1024]{1,0:T(8,128)(2,1)S(1)}, bf16[512,1024]{1,0:T(8,128)(2,1)S(1)}, u32[]{:S(2)}, u32[]{:S(2)}) collective-permute-start(bf16[512,1024]{1,0:T(8,128)(2,1)S(1)} %get-tuple-element.43.refs_1_.refs_7_.refs_8_), channel_id=1, source_target_pairs={{16,0},{3,1},{32,16},{19,17},{48,32},{35,33},{0,48},{51,49},{18,2}... | collective-permute-start | bytes 3145736 | tf_op jit(solution)/shard_map/ppermute | solution.py:33
  50.9 18.6 %collective-permute-start.9 = (bf16[512,1024]{1,0:T(8,128)(2,1)S(1)}, bf16[512,1024]{1,0:T(8,128)(2,1)S(1)}, u32[]{:S(2)}, u32[]{:S(2)}) collective-permute-start(bf16[512,1024]{1,0:T(8,128)(2,1)S(1)} %get-tuple-element.44.refs_2_.refs_8_.refs_9_), channel_id=1, source_target_pairs={{48,0},{7,1},{0,16},{23,17},{16,32},{39,33},{32,48},{55,49},{50,2}... | collective-permute-start | bytes 3145736 | tf_op jit(solution)/shard_map/ppermute | solution.py:33
  86.3 5.2 %collective-permute-start.13 = (f32[8,640]{1,0:T(8,128)S(1)}, f32[8,640]{1,0:T(8,128)S(1)}, u32[]{:S(2)}, u32[]{:S(2)}) collective-permute-start(f32[8,640]{1,0:T(8,128)S(1)} %plane.1.refs_0_), channel_id=1, source_target_pairs={{48,0},{7,1},{0,16},{23,17},{16,32},{39,33},{32,48},{55,49},{50,2}... | collective-permute-start | bytes 61448 | tf_op jit(solution)/shard_map/ppermute | solution.py:33
  87.9 4.1 %collective-permute-start.14 = (f32[8,640]{1,0:T(8,128)S(1)}, f32[8,640]{1,0:T(8,128)S(1)}, u32[]{:S(2)}, u32[]{:S(2)}) collective-permute-start(f32[8,640]{1,0:T(8,128)S(1)} %plane.1.refs_0_), channel_id=1, source_target_pairs={{32,0},{5,1},{48,16},{21,17},{0,32},{37,33},{16,48},{53,49},{34,2}... | collective-permute-start | bytes 61448 | tf_op jit(solution)/shard_map/ppermute | solution.py:33
  89.4 2.9 %collective-permute-start.15 = (f32[8,640]{1,0:T(8,128)S(1)}, f32[8,640]{1,0:T(8,128)S(1)}, u32[]{:S(2)}, u32[]{:S(2)}) collective-permute-start(f32[8,640]{1,0:T(8,128)S(1)} %plane.1.refs_0_), channel_id=1, source_target_pairs={{16,0},{3,1},{32,16},{19,17},{48,32},{35,33},{0,48},{51,49},{18,2}... | collective-permute-start | bytes 61448 | tf_op jit(solution)/shard_map/ppermute | solution.py:33
  97.9 10.0 %collective-permute-start.16 = (f32[512,1152]{1,0:T(8,128)S(1)}, f32[512,1152]{1,0:T(8,128)S(1)}, u32[]{:S(2)}, u32[]{:S(2)}) collective-permute-start(f32[512,1152]{1,0:T(8,128)S(1)} %sums.3), channel_id=1, source_target_pairs={{0,1},{1,0},{2,3},{3,2},{4,5},{5,4},{6,7},{7,6},{8,9},{9,8},{10,11... | collective-permute-start | bytes 7077896 | tf_op jit(solution)/shard_map/ppermute | solution.py:38
  103.7 4.2 %collective-permute-start.17 = (f32[64,128]{1,0:T(8,128)S(1)}, f32[64,128]{1,0:T(8,128)S(1)}, u32[]{:S(2)}, u32[]{:S(2)}) collective-permute-start(f32[64,128]{1,0:T(8,128)S(1)} %get-tuple-element.67.pack_ref), channel_id=1, source_target_pairs={{0,1},{1,0},{2,3},{3,2},{4,5},{5,4},{6,7},{7,6},{8,9},{9,8},{10,11... | collective-permute-start | bytes 98312 | tf_op jit(solution)/shard_map/ppermute | solution.py:38

commit v14 on v13

--- a/solution.py
+++ b/solution.py
@@ -149,7 +149,7 @@
     value = jnp.concatenate([lse[line : line + 1, :] for line in range(8)], axis=1)
     for tile in range(32):
         pack_ref[tile : tile + 1, :] = value[:, tile * 128 : (tile + 1) * 128]
-    for offset, plane in zip((0, 3, 2, 1), planes):
+    for offset, plane in zip((0, 2, 1, 3), planes):
         first = pl.multiple_of(32 + (spot_ref[2] + offset) % 4 * 8, 8)
         pack_ref[pl.ds(first, 8), :] = plane[:, 512:640]
     for dim in range(3):
@@ -168,7 +168,7 @@
 
 
 def halves_kernel(spot_ref, *refs):
-    line, back, across, near, first_ref, second_ref = refs
+    line, across, near, back, first_ref, second_ref = refs
     parts = (line, near, across, back)
     rows = parts[0].shape[0]
     for side in range(2):
@@ -319,7 +319,7 @@
         out_specs=[vmem] * 2,
         compiler_params=small,
         name="halves",
-    )(spot, line, back, across, near)
+    )(spot, line, across, near, back)
     far_first = fetch(first, 2, 2)
     after_first, before_first = fetch(first, 2, 1), fetch(first, 2, 3)
     after_second, before_second = fetch(second, 2, 1), fetch(second, 2, 3)
@@ -378,7 +378,7 @@
         in_specs=[smem] + [vmem] * 4,
         compiler_params=small,
         name="merge",
-    )(spot, plane, *[fetch(plane, 2, offset) for offset in (3, 2, 1)])
+    )(spot, plane, *[fetch(plane, 2, offset) for offset in (2, 1, 3)])
     theirs = sums_call(1, lse, tops, ps, chunks)
     received = swap_cores(theirs)
     partner = swap_cores(pack)

time: 111 us -> 113 us (1.018)
  waiting for transfers between devices: 28.2 us -> 30.9 us
  starting transfers between devices: 35.7 us -> 34.2 us
    ppermute x14, waiting for transfers between devices: 27.1 us -> 30.2 us  [fetch(): return lax.ppermute(value, BOTH, pairs)]
where the time goes in v14:
time: 113 us
  starting transfers between devices  34.2 us (30%)
  waiting for transfers between devices  30.9 us (27%)
  Pallas kernels  29 us (26%)
  blocking collectives  12.4 us (11%)
  local copies, waits for them, and re-layouts  4.46 us (4%)
    ppermute x14, waiting for transfers between devices, fetch(): return lax.ppermute(value, BOTH, pairs)  30.2 us
    ppermute x14, starting transfers between devices, fetch(): return lax.ppermute(value, BOTH, pairs)  22.5 us
    pallas_call x6, Pallas kernels, scores_call(): pl.pallas_call(functools.partial(scores_kernel, factor, count), out_shape...  12.4 us
    all_to_all x1, blocking collectives, shards(): lax.all_to_all(local, BOTH, split_axis=0, concat_axis=0, tiled=True, axis...  12.4 us
    pallas_call x2, Pallas kernels, sums_call(): pl.pallas_call(functools.partial(sums_kernel, half, count), out_shape=jax...  8.5 us
    ppermute x3, starting transfers between devices, swap_cores(): return lax.ppermute(value, BOTH, pairs)  8.48 us
    unnamed x4, local copies, waits for them, and re-layouts  4.29 us
    ppermute x1, starting transfers between devices, swap_sides(): return lax.ppermute(value, BOTH, pairs)  3.17 us
  transfers between devices with their start and end apart: 18, of which 12 were waited for; matrix products, arithmetic and copies ran while one was open for 1% of the time, Pallas kernels for 15%

profile of v14, /device:TPU:1, one launch (start us, length us, event | category | flops | bytes accessed | tf_op | source)
XLA Modules:
  0.0 112.5 jit_solution(4840073849384440281)
XLA Ops:
  0.6 3.7 %collective-permute-start = (bf16[64,1024]{1,0:T(8,128)(2,1)}, bf16[64,1024]{1,0:T(8,128)(2,1)S(1)}, u32[]{:S(2)}, u32[]{:S(2)}) collective-permute-start(bf16[64,1024]{1,0:T(8,128)(2,1)} %refs_0_.1), channel_id=1, source_target_pairs={{64,0},{65,1},{80,16},{81,17},{96,32},{97,33},{112,48},{113,49},{6... | collective-permute-start | bytes 393224 | tf_op jit(solution)/shard_map/ppermute | solution.py:33
  7.2 3.3 %collective-permute-done.1.refs_2_ = bf16[64,1024]{1,0:T(8,128)(2,1)S(1)} collective-permute-done((bf16[64,1024]{1,0:T(8,128)(2,1)}, bf16[64,1024]{1,0:T(8,128)(2,1)S(1)}, u32[]{:S(2)}, u32[]{:S(2)}) %collective-permute-start.1) | collective-permute-done | bytes 131104 | tf_op jit(solution)/shard_map/ppermute | solution.py:33
  11.5 3.8 %collective-permute-start.3 = (bf16[256,1024]{1,0:T(8,128)(2,1)S(1)}, bf16[256,1024]{1,0:T(8,128)(2,1)S(1)}, u32[]{:S(2)}, u32[]{:S(2)}) collective-permute-start(bf16[256,1024]{1,0:T(8,128)(2,1)S(1)} %join.1.refs_0_), channel_id=1, source_target_pairs={{4,0},{33,1},{20,16},{49,17},{36,32},{1,33},{52,48},{17,49},{6,2},... | collective-permute-start | bytes 1572872 | tf_op jit(solution)/shard_map/ppermute | solution.py:33
  15.7 1.0 collective-permute-start.5
  16.7 5.4 %collective-permute-done.3.refs_1_ = bf16[256,1024]{1,0:T(8,128)(2,1)S(1)} collective-permute-done((bf16[256,1024]{1,0:T(8,128)(2,1)S(1)}, bf16[256,1024]{1,0:T(8,128)(2,1)S(1)}, u32[]{:S(2)}, u32[]{:S(2)}) %collective-permute-start.3) | collective-permute-done | bytes 524320 | tf_op jit(solution)/shard_map/ppermute | solution.py:33
  22.1 6.3 %collective-permute-done.4.refs_2_ = bf16[256,1024]{1,0:T(8,128)(2,1)S(1)} collective-permute-done((bf16[256,1024]{1,0:T(8,128)(2,1)S(1)}, bf16[256,1024]{1,0:T(8,128)(2,1)S(1)}, u32[]{:S(2)}, u32[]{:S(2)}) %collective-permute-start.4) | collective-permute-done | bytes 524320 | tf_op jit(solution)/shard_map/ppermute | solution.py:33
  29.2 3.0 %collective-permute-start.7 = (bf16[512,1024]{1,0:T(8,128)(2,1)S(1)}, bf16[512,1024]{1,0:T(8,128)(2,1)S(1)}, u32[]{:S(2)}, u32[]{:S(2)}) collective-permute-start(bf16[512,1024]{1,0:T(8,128)(2,1)S(1)} %get-tuple-element.43.refs_1_.refs_7_.refs_8_), channel_id=1, source_target_pairs={{32,0},{5,1},{48,16},{21,17},{0,32},{37,33},{16,48},{53,49},{34,2}... | collective-permute-start | bytes 3145736 | tf_op jit(solution)/shard_map/ppermute | solution.py:33
  32.2 3.4 %copy-done = bf16[4096,1024]{1,0:T(8,128)(2,1)S(1)} copy-done((bf16[4096,1024]{1,0:T(8,128)(2,1)S(1)}, bf16[4096,1024]{1,0:T(8,128)(2,1)}, u32[]{:S(2)}) %copy-start) | copy-done | bytes 8388632
  35.6 2.0 %share.1.mine_ref = bf16[512,1024]{1,0:T(8,128)(2,1)S(1)} custom-call(s32[2]{0:T(128)S(1)} %pad_add_fusion.at_ref, bf16[4096,1024]{1,0:T(8,128)(2,1)S(1)} %copy-done), custom_call_target="tpu_custom_call" | custom-call | tf_op jit(solution)/shard_map/share/pallas_call | solution.py:327
  37.5 3.0 %collective-permute-start.6 = (bf16[512,1024]{1,0:T(8,128)(2,1)S(1)}, bf16[512,1024]{1,0:T(8,128)(2,1)S(1)}, u32[]{:S(2)}, u32[]{:S(2)}) collective-permute-start(bf16[512,1024]{1,0:T(8,128)(2,1)S(1)} %share.1.mine_ref), channel_id=1, source_target_pairs={{0,1},{1,0},{2,3},{3,2},{4,5},{5,4},{6,7},{7,6},{8,9},{9,8},{10,11... | collective-permute-start | bytes 3145736 | tf_op jit(solution)/shard_map/ppermute | solution.py:38
  40.6 2.3 %collective-permute-start.12 = (bf16[512,1024]{1,0:T(8,128)(2,1)S(1)}, bf16[512,1024]{1,0:T(8,128)(2,1)S(1)}, u32[]{:S(2)}, u32[]{:S(2)}) collective-permute-start(bf16[512,1024]{1,0:T(8,128)(2,1)S(1)} %get-tuple-element.44.refs_2_.refs_8_.refs_9_), channel_id=1, source_target_pairs={{16,0},{3,1},{32,16},{19,17},{48,32},{35,33},{0,48},{51,49},{18,2}... | collective-permute-start | bytes 3145736 | tf_op jit(solution)/shard_map/ppermute | solution.py:33
  42.9 1.8 %collective-permute-done.7.refs_0_.refs_11_.refs_12_ = bf16[512,1024]{1,0:T(8,128)(2,1)S(1)} collective-permute-done((bf16[512,1024]{1,0:T(8,128)(2,1)S(1)}, bf16[512,1024]{1,0:T(8,128)(2,1)S(1)}, u32[]{:S(2)}, u32[]{:S(2)}) %collective-permute-start.7) | collective-permute-done | bytes 1048608 | tf_op jit(solution)/shard_map/ppermute | solution.py:33
  44.7 3.2 %collective-permute-start.10 = (bf16[512,1024]{1,0:T(8,128)(2,1)S(1)}, bf16[512,1024]{1,0:T(8,128)(2,1)S(1)}, u32[]{:S(2)}, u32[]{:S(2)}) collective-permute-start(bf16[512,1024]{1,0:T(8,128)(2,1)S(1)} %collective-permute-done.7.refs_0_.refs_11_.refs_12_), channel_id=1, source_target_pairs={{8,0},{73,1},{24,16},{89,17},{40,32},{105,33},{56,48},{121,49},{10... | collective-permute-start | bytes 3145736 | tf_op jit(solution)/shard_map/ppermute | solution.py:49
  47.9 2.5 %collective-permute-start.8 = (bf16[512,1024]{1,0:T(8,128)(2,1)S(1)}, bf16[512,1024]{1,0:T(8,128)(2,1)S(1)}, u32[]{:S(2)}, u32[]{:S(2)}) collective-permute-start(bf16[512,1024]{1,0:T(8,128)(2,1)S(1)} %get-tuple-element.43.refs_1_.refs_7_.refs_8_), channel_id=1, source_target_pairs={{16,0},{3,1},{32,16},{19,17},{48,32},{35,33},{0,48},{51,49},{18,2}... | collective-permute-start | bytes 3145736 | tf_op jit(solution)/shard_map/ppermute | solution.py:33
  50.4 4.3 %scores.6 = (f32[2,512,512]{2,1,0:T(8,128)S(1)}, f32[2,512,512]{2,1,0:T(8,128)S(1)}, f32[2,512,512]{2,1,0:T(8,128)S(1)}, f32[4,1536]{1,0:T(4,128)S(1)}) custom-call(bf16[512,1024]{1,0:T(8,128)(2,1)S(1)} %share.1.mine_ref, bf16[512,1024]{1,0:T(8,128)(2,1)S(1)} %collective-permute-done.6.other_ref, ...), custom_call_target="tpu_custom_call" | custom-call | flops 6442450944 | bytes 11534336 | tf_op jit(solution)/shard_map/scores/pallas_call | solution.py:85
  54.7 1.6 %collective-permute-done.12.refs_0_.refs_10_.refs_11_ = bf16[512,1024]{1,0:T(8,128)(2,1)S(1)} collective-permute-done((bf16[512,1024]{1,0:T(8,128)(2,1)S(1)}, bf16[512,1024]{1,0:T(8,128)(2,1)S(1)}, u32[]{:S(2)}, u32[]{:S(2)}) %collective-permute-start.12) | collective-permute-done | bytes 1048608 | tf_op jit(solution)/shard_map/ppermute | solution.py:33
  56.3 1.6 %scores.7 = (f32[2,512,512]{2,1,0:T(8,128)S(1)}, f32[4,512]{1,0:T(4,128)S(1)}) custom-call(bf16[512,1024]{1,0:T(8,128)(2,1)S(1)} %share.1.mine_ref, bf16[512,1024]{1,0:T(8,128)(2,1)S(1)} %collective-permute-done.6.other_ref, bf16[512,1024]{1,0:T(8,128)(2,1)S(1)} %collective-permute-done.12.refs_0_.refs_10_.refs_11_), custom_call_target="tpu_custom_call" | custom-call | flops 2147483648 | bytes 5242880 | tf_op jit(solution)/shard_map/scores/pallas_call | solution.py:85
  58.1 1.6 %scores.8 = (f32[2,512,512]{2,1,0:T(8,128)S(1)}, f32[4,512]{1,0:T(4,128)S(1)}) custom-call(bf16[512,1024]{1,0:T(8,128)(2,1)S(1)} %share.1.mine_ref, bf16[512,1024]{1,0:T(8,128)(2,1)S(1)} %collective-permute-done.6.other_ref, bf16[512,1024]{1,0:T(8,128)(2,1)S(1)} %collective-permute-done.11.refs_0_.refs_13_.refs_14_), custom_call_target="tpu_custom_call" | custom-call | flops 2147483648 | bytes 5242880 | tf_op jit(solution)/shard_map/scores/pallas_call | solution.py:85
  60.4 1.6 %scores.9 = (f32[2,512,512]{2,1,0:T(8,128)S(1)}, f32[4,512]{1,0:T(4,128)S(1)}) custom-call(bf16[512,1024]{1,0:T(8,128)(2,1)S(1)} %share.1.mine_ref, bf16[512,1024]{1,0:T(8,128)(2,1)S(1)} %collective-permute-done.6.other_ref, bf16[512,1024]{1,0:T(8,128)(2,1)S(1)} %collective-permute-done.10.refs_0_.refs_12_.refs_13_), custom_call_target="tpu_custom_call" | custom-call | flops 2147483648 | bytes 5242880 | tf_op jit(solution)/shard_map/scores/pallas_call | solution.py:85
  62.0 7.3 %collective-permute-done.9.refs_0_.refs_15_.refs_1_ = bf16[512,1024]{1,0:T(8,128)(2,1)S(1)} collective-permute-done((bf16[512,1024]{1,0:T(8,128)(2,1)S(1)}, bf16[512,1024]{1,0:T(8,128)(2,1)S(1)}, u32[]{:S(2)}, u32[]{:S(2)}) %collective-permute-start.9) | collective-permute-done | bytes 1048608 | tf_op jit(solution)/shard_map/ppermute | solution.py:33
  69.3 1.6 %scores.10 = (f32[2,512,512]{2,1,0:T(8,128)S(1)}, f32[4,512]{1,0:T(4,128)S(1)}) custom-call(bf16[512,1024]{1,0:T(8,128)(2,1)S(1)} %share.1.mine_ref, bf16[512,1024]{1,0:T(8,128)(2,1)S(1)} %collective-permute-done.6.other_ref, bf16[512,1024]{1,0:T(8,128)(2,1)S(1)} %collective-permute-done.9.refs_0_.refs_15_.refs_1_), custom_call_target="tpu_custom_call" | custom-call | flops 2147483648 | bytes 5242880 | tf_op jit(solution)/shard_map/scores/pallas_call | solution.py:85
  71.0 1.6 %scores.11 = (f32[2,512,512]{2,1,0:T(8,128)S(1)}, f32[4,512]{1,0:T(4,128)S(1)}) custom-call(bf16[512,1024]{1,0:T(8,128)(2,1)S(1)} %share.1.mine_ref, bf16[512,1024]{1,0:T(8,128)(2,1)S(1)} %collective-permute-done.6.other_ref, bf16[512,1024]{1,0:T(8,128)(2,1)S(1)} %collective-permute-done.8.refs_0_.refs_9_.refs_10_), custom_call_target="tpu_custom_call" | custom-call | flops 2147483648 | bytes 5242880 | tf_op jit(solution)/shard_map/scores/pallas_call | solution.py:85
  72.6 1.1 first.1
  73.7 12.4 %all_to_all.5.all_ref = f32[16,8,640]{2,1,0:T(8,128)S(1)} all-to-all(f32[16,8,640]{2,1,0:T(8,128)S(1)} %get-tuple-element.56), channel_id=1, replica_groups={{0,8,64,72,2,10,66,74,4,12,68,76,6,14,70,78},{16,24,80,88,18,26,82,90,2..., dimensions={0} | all-to-all | bytes 655360 | tf_op jit(solution)/shard_map/all_to_all | solution.py:363
  86.2 2.8 %collective-permute-start.13 = (f32[8,640]{1,0:T(8,128)S(1)}, f32[8,640]{1,0:T(8,128)S(1)}, u32[]{:S(2)}, u32[]{:S(2)}) collective-permute-start(f32[8,640]{1,0:T(8,128)S(1)} %plane.1.refs_0_), channel_id=1, source_target_pairs={{32,0},{5,1},{48,16},{21,17},{0,32},{37,33},{16,48},{53,49},{34,2}... | collective-permute-start | bytes 61448 | tf_op jit(solution)/shard_map/ppermute | solution.py:33
  90.5 1.2 %collective-permute-done.14.refs_2_ = f32[8,640]{1,0:T(8,128)S(1)} collective-permute-done((f32[8,640]{1,0:T(8,128)S(1)}, f32[8,640]{1,0:T(8,128)S(1)}, u32[]{:S(2)}, u32[]{:S(2)}) %collective-permute-start.14) | collective-permute-done | bytes 20512 | tf_op jit(solution)/shard_map/ppermute | solution.py:33
  91.6 2.4 %collective-permute-done.15.refs_3_ = f32[8,640]{1,0:T(8,128)S(1)} collective-permute-done((f32[8,640]{1,0:T(8,128)S(1)}, f32[8,640]{1,0:T(8,128)S(1)}, u32[]{:S(2)}, u32[]{:S(2)}) %collective-permute-start.15) | collective-permute-done | bytes 20512 | tf_op jit(solution)/shard_map/ppermute | solution.py:33
  94.1 1.0 merge.1
  95.1 4.5 %sums.3 = f32[512,1152]{1,0:T(8,128)S(1)} custom-call(f32[1,4096]{1,0:T(1,128)S(1)} %get-tuple-element.57.lse_ref, f32[2,4096]{1,0:T(2,128)S(1)} %get-tuple-element.58.top_ref, f32[2,512,512]{2,1,0:T(8,128)S(1)} %get-tuple-element.59.refs_0_, f32[2,512,512]{2,1,0:T(8,128)S(1)} %get-tuple-element.60.refs_1_, f32[2,512,512]{2,1,0:T(8,128)S(1)} %get-tuple-element.61.refs_2_, ...), custom_call_target="tpu_custom_call" | custom-call | flops 4294967296 | bytes 18874368 | tf_op jit(solution)/shard_map/sums/pallas_call | solution.py:227
  99.7 5.3 %collective-permute-start.16 = (f32[512,1152]{1,0:T(8,128)S(1)}, f32[512,1152]{1,0:T(8,128)S(1)}, u32[]{:S(2)}, u32[]{:S(2)}) collective-permute-start(f32[512,1152]{1,0:T(8,128)S(1)} %sums.3), channel_id=1, source_target_pairs={{0,1},{1,0},{2,3},{3,2},{4,5},{5,4},{6,7},{7,6},{8,9},{9,8},{10,11... | collective-permute-start | bytes 7077896 | tf_op jit(solution)/shard_map/ppermute | solution.py:38
  105.1 4.0 %sums.2.ours_ref = f32[512,1152]{1,0:T(8,128)S(1)} custom-call(f32[1,4096]{1,0:T(1,128)S(1)} %get-tuple-element.57.lse_ref, f32[2,4096]{1,0:T(2,128)S(1)} %get-tuple-element.58.top_ref, f32[2,512,512]{2,1,0:T(8,128)S(1)} %get-tuple-element.59.refs_0_, f32[2,512,512]{2,1,0:T(8,128)S(1)} %get-tuple-element.60.refs_1_, ...), custom_call_target="tpu_custom_call" | custom-call | flops 3758096384 | bytes 18874368 | tf_op jit(solution)/shard_map/sums/pallas_call | solution.py:227
  109.2 3.1 %final.1 = (f32[512,1024]{1,0:T(8,128)}, f32[1,64]{1,0:T(1,128)}) custom-call(s32[2]{0:T(128)S(1)} %pad_add_fusion.at_ref, f32[1,4096]{1,0:T(1,128)S(1)} %get-tuple-element.57.lse_ref, f32[2,4096]{1,0:T(2,128)S(1)} %get-tuple-element.58.top_ref, f32[512,1152]{1,0:T(8,128)S(1)} %sums.2.ours_ref, f32[512,1152]{1,0:T(8,128)S(1)} %collective-permute-done.16.theirs_ref, ...), custom_call_target="tpu_custom_call" | custom-call | tf_op jit(solution)/shard_map/final/pallas_call | solution.py:386
  (29 shorter events, 7.6 us)
Async XLA Ops:
  0.6 6.6 %collective-permute-start = (bf16[64,1024]{1,0:T(8,128)(2,1)}, bf16[64,1024]{1,0:T(8,128)(2,1)S(1)}, u32[]{:S(2)}, u32[]{:S(2)}) collective-permute-start(bf16[64,1024]{1,0:T(8,128)(2,1)} %refs_0_.1), channel_id=1, source_target_pairs={{64,0},{65,1},{80,16},{81,17},{96,32},{97,33},{112,48},{113,49},{6... | collective-permute-start | bytes 393224 | tf_op jit(solution)/shard_map/ppermute | solution.py:33
  4.3 6.2 %collective-permute-start.1 = (bf16[64,1024]{1,0:T(8,128)(2,1)}, bf16[64,1024]{1,0:T(8,128)(2,1)S(1)}, u32[]{:S(2)}, u32[]{:S(2)}) collective-permute-start(bf16[64,1024]{1,0:T(8,128)(2,1)} %refs_0_.1), channel_id=1, source_target_pairs={{8,0},{9,1},{24,16},{25,17},{40,32},{41,33},{56,48},{57,49},{10,2}... | collective-permute-start | bytes 393224 | tf_op jit(solution)/shard_map/ppermute | solution.py:33
  5.1 5.4 %collective-permute-start.2 = (bf16[64,1024]{1,0:T(8,128)(2,1)}, bf16[64,1024]{1,0:T(8,128)(2,1)S(1)}, u32[]{:S(2)}, u32[]{:S(2)}) collective-permute-start(bf16[64,1024]{1,0:T(8,128)(2,1)} %refs_0_.1), channel_id=1, source_target_pairs={{72,0},{73,1},{88,16},{89,17},{104,32},{105,33},{120,48},{121,49},... | collective-permute-start | bytes 393224 | tf_op jit(solution)/shard_map/ppermute | solution.py:33
  10.5 0.9 copy-start.1
  11.5 10.7 %collective-permute-start.3 = (bf16[256,1024]{1,0:T(8,128)(2,1)S(1)}, bf16[256,1024]{1,0:T(8,128)(2,1)S(1)}, u32[]{:S(2)}, u32[]{:S(2)}) collective-permute-start(bf16[256,1024]{1,0:T(8,128)(2,1)S(1)} %join.1.refs_0_), channel_id=1, source_target_pairs={{4,0},{33,1},{20,16},{49,17},{36,32},{1,33},{52,48},{17,49},{6,2},... | collective-permute-start | bytes 1572872 | tf_op jit(solution)/shard_map/ppermute | solution.py:33
  15.2 13.3 %collective-permute-start.4 = (bf16[256,1024]{1,0:T(8,128)(2,1)S(1)}, bf16[256,1024]{1,0:T(8,128)(2,1)S(1)}, u32[]{:S(2)}, u32[]{:S(2)}) collective-permute-start(bf16[256,1024]{1,0:T(8,128)(2,1)S(1)} %join.1.refs_0_), channel_id=1, source_target_pairs={{2,0},{17,1},{18,16},{33,17},{34,32},{49,33},{50,48},{1,49},{4,2},... | collective-permute-start | bytes 1572872 | tf_op jit(solution)/shard_map/ppermute | solution.py:33
  15.7 12.8 %collective-permute-start.5 = (bf16[256,1024]{1,0:T(8,128)(2,1)S(1)}, bf16[256,1024]{1,0:T(8,128)(2,1)S(1)}, u32[]{:S(2)}, u32[]{:S(2)}) collective-permute-start(bf16[256,1024]{1,0:T(8,128)(2,1)S(1)} %join.1.refs_0_), channel_id=1, source_target_pairs={{6,0},{49,1},{22,16},{1,17},{38,32},{17,33},{54,48},{33,49},{0,2},... | collective-permute-start | bytes 1572872 | tf_op jit(solution)/shard_map/ppermute | solution.py:33
  29.2 15.5 %collective-permute-start.7 = (bf16[512,1024]{1,0:T(8,128)(2,1)S(1)}, bf16[512,1024]{1,0:T(8,128)(2,1)S(1)}, u32[]{:S(2)}, u32[]{:S(2)}) collective-permute-start(bf16[512,1024]{1,0:T(8,128)(2,1)S(1)} %get-tuple-element.43.refs_1_.refs_7_.refs_8_), channel_id=1, source_target_pairs={{32,0},{5,1},{48,16},{21,17},{0,32},{37,33},{16,48},{53,49},{34,2}... | collective-permute-start | bytes 3145736 | tf_op jit(solution)/shard_map/ppermute | solution.py:33
  32.2 3.4 %copy-start = (bf16[4096,1024]{1,0:T(8,128)(2,1)S(1)}, bf16[4096,1024]{1,0:T(8,128)(2,1)}, u32[]{:S(2)}) copy-start(bf16[4096,1024]{1,0:T(8,128)(2,1)} %cents_ref.1) | copy-start | bytes 25165828
  37.5 12.8 %collective-permute-start.6 = (bf16[512,1024]{1,0:T(8,128)(2,1)S(1)}, bf16[512,1024]{1,0:T(8,128)(2,1)S(1)}, u32[]{:S(2)}, u32[]{:S(2)}) collective-permute-start(bf16[512,1024]{1,0:T(8,128)(2,1)S(1)} %share.1.mine_ref), channel_id=1, source_target_pairs={{0,1},{1,0},{2,3},{3,2},{4,5},{5,4},{6,7},{7,6},{8,9},{9,8},{10,11... | collective-permute-start | bytes 3145736 | tf_op jit(solution)/shard_map/ppermute | solution.py:38
  40.6 15.7 %collective-permute-start.12 = (bf16[512,1024]{1,0:T(8,128)(2,1)S(1)}, bf16[512,1024]{1,0:T(8,128)(2,1)S(1)}, u32[]{:S(2)}, u32[]{:S(2)}) collective-permute-start(bf16[512,1024]{1,0:T(8,128)(2,1)S(1)} %get-tuple-element.44.refs_2_.refs_8_.refs_9_), channel_id=1, source_target_pairs={{16,0},{3,1},{32,16},{19,17},{48,32},{35,33},{0,48},{51,49},{18,2}... | collective-permute-start | bytes 3145736 | tf_op jit(solution)/shard_map/ppermute | solution.py:33
  42.9 15.2 %collective-permute-start.11 = (bf16[512,1024]{1,0:T(8,128)(2,1)S(1)}, bf16[512,1024]{1,0:T(8,128)(2,1)S(1)}, u32[]{:S(2)}, u32[]{:S(2)}) collective-permute-start(bf16[512,1024]{1,0:T(8,128)(2,1)S(1)} %get-tuple-element.43.refs_1_.refs_7_.refs_8_), channel_id=1, source_target_pairs={{48,0},{7,1},{0,16},{23,17},{16,32},{39,33},{32,48},{55,49},{50,2}... | collective-permute-start | bytes 3145736 | tf_op jit(solution)/shard_map/ppermute | solution.py:33
  44.7 15.7 %collective-permute-start.10 = (bf16[512,1024]{1,0:T(8,128)(2,1)S(1)}, bf16[512,1024]{1,0:T(8,128)(2,1)S(1)}, u32[]{:S(2)}, u32[]{:S(2)}) collective-permute-start(bf16[512,1024]{1,0:T(8,128)(2,1)S(1)} %collective-permute-done.7.refs_0_.refs_11_.refs_12_), channel_id=1, source_target_pairs={{8,0},{73,1},{24,16},{89,17},{40,32},{105,33},{56,48},{121,49},{10... | collective-permute-start | bytes 3145736 | tf_op jit(solution)/shard_map/ppermute | solution.py:49
  47.9 23.1 %collective-permute-start.8 = (bf16[512,1024]{1,0:T(8,128)(2,1)S(1)}, bf16[512,1024]{1,0:T(8,128)(2,1)S(1)}, u32[]{:S(2)}, u32[]{:S(2)}) collective-permute-start(bf16[512,1024]{1,0:T(8,128)(2,1)S(1)} %get-tuple-element.43.refs_1_.refs_7_.refs_8_), channel_id=1, source_target_pairs={{16,0},{3,1},{32,16},{19,17},{48,32},{35,33},{0,48},{51,49},{18,2}... | collective-permute-start | bytes 3145736 | tf_op jit(solution)/shard_map/ppermute | solution.py:33
  50.4 18.9 %collective-permute-start.9 = (bf16[512,1024]{1,0:T(8,128)(2,1)S(1)}, bf16[512,1024]{1,0:T(8,128)(2,1)S(1)}, u32[]{:S(2)}, u32[]{:S(2)}) collective-permute-start(bf16[512,1024]{1,0:T(8,128)(2,1)S(1)} %get-tuple-element.44.refs_2_.refs_8_.refs_9_), channel_id=1, source_target_pairs={{48,0},{7,1},{0,16},{23,17},{16,32},{39,33},{32,48},{55,49},{50,2}... | collective-permute-start | bytes 3145736 | tf_op jit(solution)/shard_map/ppermute | solution.py:33
  86.2 4.3 %collective-permute-start.13 = (f32[8,640]{1,0:T(8,128)S(1)}, f32[8,640]{1,0:T(8,128)S(1)}, u32[]{:S(2)}, u32[]{:S(2)}) collective-permute-start(f32[8,640]{1,0:T(8,128)S(1)} %plane.1.refs_0_), channel_id=1, source_target_pairs={{32,0},{5,1},{48,16},{21,17},{0,32},{37,33},{16,48},{53,49},{34,2}... | collective-permute-start | bytes 61448 | tf_op jit(solution)/shard_map/ppermute | solution.py:33
  89.0 2.6 %collective-permute-start.14 = (f32[8,640]{1,0:T(8,128)S(1)}, f32[8,640]{1,0:T(8,128)S(1)}, u32[]{:S(2)}, u32[]{:S(2)}) collective-permute-start(f32[8,640]{1,0:T(8,128)S(1)} %plane.1.refs_0_), channel_id=1, source_target_pairs={{16,0},{3,1},{32,16},{19,17},{48,32},{35,33},{0,48},{51,49},{18,2}... | collective-permute-start | bytes 61448 | tf_op jit(solution)/shard_map/ppermute | solution.py:33
  89.9 4.1 %collective-permute-start.15 = (f32[8,640]{1,0:T(8,128)S(1)}, f32[8,640]{1,0:T(8,128)S(1)}, u32[]{:S(2)}, u32[]{:S(2)}) collective-permute-start(f32[8,640]{1,0:T(8,128)S(1)} %plane.1.refs_0_), channel_id=1, source_target_pairs={{48,0},{7,1},{0,16},{23,17},{16,32},{39,33},{32,48},{55,49},{50,2}... | collective-permute-start | bytes 61448 | tf_op jit(solution)/shard_map/ppermute | solution.py:33
  99.7 9.6 %collective-permute-start.16 = (f32[512,1152]{1,0:T(8,128)S(1)}, f32[512,1152]{1,0:T(8,128)S(1)}, u32[]{:S(2)}, u32[]{:S(2)}) collective-permute-start(f32[512,1152]{1,0:T(8,128)S(1)} %sums.3), channel_id=1, source_target_pairs={{0,1},{1,0},{2,3},{3,2},{4,5},{5,4},{6,7},{7,6},{8,9},{9,8},{10,11... | collective-permute-start | bytes 7077896 | tf_op jit(solution)/shard_map/ppermute | solution.py:38
  105.0 4.2 %collective-permute-start.17 = (f32[64,128]{1,0:T(8,128)S(1)}, f32[64,128]{1,0:T(8,128)S(1)}, u32[]{:S(2)}, u32[]{:S(2)}) collective-permute-start(f32[64,128]{1,0:T(8,128)S(1)} %get-tuple-element.67.pack_ref), channel_id=1, source_target_pairs={{0,1},{1,0},{2,3},{3,2},{4,5},{5,4},{6,7},{7,6},{8,9},{9,8},{10,11... | collective-permute-start | bytes 98312 | tf_op jit(solution)/shard_map/ppermute | solution.py:38

commit v15 on v14

--- a/solution.py
+++ b/solution.py
@@ -149,7 +149,7 @@
     value = jnp.concatenate([lse[line : line + 1, :] for line in range(8)], axis=1)
     for tile in range(32):
         pack_ref[tile : tile + 1, :] = value[:, tile * 128 : (tile + 1) * 128]
-    for offset, plane in zip((0, 2, 1, 3), planes):
+    for offset, plane in zip((0, 3, 2, 1), planes):
         first = pl.multiple_of(32 + (spot_ref[2] + offset) % 4 * 8, 8)
         pack_ref[pl.ds(first, 8), :] = plane[:, 512:640]
     for dim in range(3):
@@ -378,7 +378,7 @@
         in_specs=[smem] + [vmem] * 4,
         compiler_params=small,
         name="merge",
-    )(spot, plane, *[fetch(plane, 2, offset) for offset in (2, 1, 3)])
+    )(spot, plane, *[fetch(plane, 2, offset) for offset in (3, 2, 1)])
     theirs = sums_call(1, lse, tops, ps, chunks)
     received = swap_cores(theirs)
     partner = swap_cores(pack)

time: 113 us -> 111 us (0.982)
  waiting for transfers between devices: 30.9 us -> 28.2 us
    ppermute x14, waiting for transfers between devices: 30.2 us -> 27.5 us  [fetch(): return lax.ppermute(value, BOTH, pairs)]
where the time goes in v15:
time: 111 us; the launch traced here: 110 us
  starting transfers between devices  34.8 us (31%)
  Pallas kernels  29 us (26%)
  waiting for transfers between devices  28.2 us (25%)
  blocking collectives  12.4 us (11%)
  local copies, waits for them, and re-layouts  4.46 us (4%)
    ppermute x14, waiting for transfers between devices, fetch(): return lax.ppermute(value, BOTH, pairs)  27.5 us
    ppermute x14, starting transfers between devices, fetch(): return lax.ppermute(value, BOTH, pairs)  23.1 us
    pallas_call x6, Pallas kernels, scores_call(): pl.pallas_call(functools.partial(scores_kernel, factor, count), out_shape...  12.4 us
    all_to_all x1, blocking collectives, shards(): lax.all_to_all(local, BOTH, split_axis=0, concat_axis=0, tiled=True, axis...  12.4 us
    pallas_call x2, Pallas kernels, sums_call(): pl.pallas_call(functools.partial(sums_kernel, half, count), out_shape=jax...  8.5 us
    ppermute x3, starting transfers between devices, swap_cores(): return lax.ppermute(value, BOTH, pairs)  8.48 us
    unnamed x4, local copies, waits for them, and re-layouts  4.29 us
    ppermute x1, starting transfers between devices, swap_sides(): return lax.ppermute(value, BOTH, pairs)  3.17 us
  transfers between devices with their start and end apart: 18, of which 12 were waited for; matrix products, arithmetic and copies ran while one was open for 1% of the time, Pallas kernels for 15%

profile of v15, /device:TPU:1, one launch (start us, length us, event | category | flops | bytes accessed | tf_op | source)
XLA Modules:
  0.0 110.4 jit_solution(13873336712426746122)
XLA Ops:
  0.6 3.7 %collective-permute-start = (bf16[64,1024]{1,0:T(8,128)(2,1)}, bf16[64,1024]{1,0:T(8,128)(2,1)S(1)}, u32[]{:S(2)}, u32[]{:S(2)}) collective-permute-start(bf16[64,1024]{1,0:T(8,128)(2,1)} %refs_0_.1), channel_id=1, source_target_pairs={{64,0},{65,1},{80,16},{81,17},{96,32},{97,33},{112,48},{113,49},{6... | collective-permute-start | bytes 393224 | tf_op jit(solution)/shard_map/ppermute | solution.py:33
  7.2 3.3 %collective-permute-done.1.refs_2_ = bf16[64,1024]{1,0:T(8,128)(2,1)S(1)} collective-permute-done((bf16[64,1024]{1,0:T(8,128)(2,1)}, bf16[64,1024]{1,0:T(8,128)(2,1)S(1)}, u32[]{:S(2)}, u32[]{:S(2)}) %collective-permute-start.1) | collective-permute-done | bytes 131104 | tf_op jit(solution)/shard_map/ppermute | solution.py:33
  11.5 3.8 %collective-permute-start.3 = (bf16[256,1024]{1,0:T(8,128)(2,1)S(1)}, bf16[256,1024]{1,0:T(8,128)(2,1)S(1)}, u32[]{:S(2)}, u32[]{:S(2)}) collective-permute-start(bf16[256,1024]{1,0:T(8,128)(2,1)S(1)} %join.1.refs_0_), channel_id=1, source_target_pairs={{4,0},{33,1},{20,16},{49,17},{36,32},{1,33},{52,48},{17,49},{6,2},... | collective-permute-start | bytes 1572872 | tf_op jit(solution)/shard_map/ppermute | solution.py:33
  15.7 1.0 collective-permute-start.5
  16.7 5.4 %collective-permute-done.3.refs_1_ = bf16[256,1024]{1,0:T(8,128)(2,1)S(1)} collective-permute-done((bf16[256,1024]{1,0:T(8,128)(2,1)S(1)}, bf16[256,1024]{1,0:T(8,128)(2,1)S(1)}, u32[]{:S(2)}, u32[]{:S(2)}) %collective-permute-start.3) | collective-permute-done | bytes 524320 | tf_op jit(solution)/shard_map/ppermute | solution.py:33
  22.1 6.3 %collective-permute-done.4.refs_2_ = bf16[256,1024]{1,0:T(8,128)(2,1)S(1)} collective-permute-done((bf16[256,1024]{1,0:T(8,128)(2,1)S(1)}, bf16[256,1024]{1,0:T(8,128)(2,1)S(1)}, u32[]{:S(2)}, u32[]{:S(2)}) %collective-permute-start.4) | collective-permute-done | bytes 524320 | tf_op jit(solution)/shard_map/ppermute | solution.py:33
  29.2 3.0 %collective-permute-start.7 = (bf16[512,1024]{1,0:T(8,128)(2,1)S(1)}, bf16[512,1024]{1,0:T(8,128)(2,1)S(1)}, u32[]{:S(2)}, u32[]{:S(2)}) collective-permute-start(bf16[512,1024]{1,0:T(8,128)(2,1)S(1)} %get-tuple-element.43.refs_1_.refs_7_.refs_8_), channel_id=1, source_target_pairs={{32,0},{5,1},{48,16},{21,17},{0,32},{37,33},{16,48},{53,49},{34,2}... | collective-permute-start | bytes 3145736 | tf_op jit(solution)/shard_map/ppermute | solution.py:33
  32.2 3.4 %copy-done = bf16[4096,1024]{1,0:T(8,128)(2,1)S(1)} copy-done((bf16[4096,1024]{1,0:T(8,128)(2,1)S(1)}, bf16[4096,1024]{1,0:T(8,128)(2,1)}, u32[]{:S(2)}) %copy-start) | copy-done | bytes 8388632
  35.6 2.0 %share.1.mine_ref = bf16[512,1024]{1,0:T(8,128)(2,1)S(1)} custom-call(s32[2]{0:T(128)S(1)} %pad_add_fusion.at_ref, bf16[4096,1024]{1,0:T(8,128)(2,1)S(1)} %copy-done), custom_call_target="tpu_custom_call" | custom-call | tf_op jit(solution)/shard_map/share/pallas_call | solution.py:327
  37.5 3.0 %collective-permute-start.6 = (bf16[512,1024]{1,0:T(8,128)(2,1)S(1)}, bf16[512,1024]{1,0:T(8,128)(2,1)S(1)}, u32[]{:S(2)}, u32[]{:S(2)}) collective-permute-start(bf16[512,1024]{1,0:T(8,128)(2,1)S(1)} %share.1.mine_ref), channel_id=1, source_target_pairs={{0,1},{1,0},{2,3},{3,2},{4,5},{5,4},{6,7},{7,6},{8,9},{9,8},{10,11... | collective-permute-start | bytes 3145736 | tf_op jit(solution)/shard_map/ppermute | solution.py:38
  40.6 2.3 %collective-permute-start.12 = (bf16[512,1024]{1,0:T(8,128)(2,1)S(1)}, bf16[512,1024]{1,0:T(8,128)(2,1)S(1)}, u32[]{:S(2)}, u32[]{:S(2)}) collective-permute-start(bf16[512,1024]{1,0:T(8,128)(2,1)S(1)} %get-tuple-element.44.refs_2_.refs_8_.refs_9_), channel_id=1, source_target_pairs={{16,0},{3,1},{32,16},{19,17},{48,32},{35,33},{0,48},{51,49},{18,2}... | collective-permute-start | bytes 3145736 | tf_op jit(solution)/shard_map/ppermute | solution.py:33
  42.9 1.8 %collective-permute-done.7.refs_0_.refs_11_.refs_12_ = bf16[512,1024]{1,0:T(8,128)(2,1)S(1)} collective-permute-done((bf16[512,1024]{1,0:T(8,128)(2,1)S(1)}, bf16[512,1024]{1,0:T(8,128)(2,1)S(1)}, u32[]{:S(2)}, u32[]{:S(2)}) %collective-permute-start.7) | collective-permute-done | bytes 1048608 | tf_op jit(solution)/shard_map/ppermute | solution.py:33
  44.7 3.2 %collective-permute-start.10 = (bf16[512,1024]{1,0:T(8,128)(2,1)S(1)}, bf16[512,1024]{1,0:T(8,128)(2,1)S(1)}, u32[]{:S(2)}, u32[]{:S(2)}) collective-permute-start(bf16[512,1024]{1,0:T(8,128)(2,1)S(1)} %collective-permute-done.7.refs_0_.refs_11_.refs_12_), channel_id=1, source_target_pairs={{8,0},{73,1},{24,16},{89,17},{40,32},{105,33},{56,48},{121,49},{10... | collective-permute-start | bytes 3145736 | tf_op jit(solution)/shard_map/ppermute | solution.py:49
  47.9 2.5 %collective-permute-start.8 = (bf16[512,1024]{1,0:T(8,128)(2,1)S(1)}, bf16[512,1024]{1,0:T(8,128)(2,1)S(1)}, u32[]{:S(2)}, u32[]{:S(2)}) collective-permute-start(bf16[512,1024]{1,0:T(8,128)(2,1)S(1)} %get-tuple-element.43.refs_1_.refs_7_.refs_8_), channel_id=1, source_target_pairs={{16,0},{3,1},{32,16},{19,17},{48,32},{35,33},{0,48},{51,49},{18,2}... | collective-permute-start | bytes 3145736 | tf_op jit(solution)/shard_map/ppermute | solution.py:33
  50.4 4.3 %scores.6 = (f32[2,512,512]{2,1,0:T(8,128)S(1)}, f32[2,512,512]{2,1,0:T(8,128)S(1)}, f32[2,512,512]{2,1,0:T(8,128)S(1)}, f32[4,1536]{1,0:T(4,128)S(1)}) custom-call(bf16[512,1024]{1,0:T(8,128)(2,1)S(1)} %share.1.mine_ref, bf16[512,1024]{1,0:T(8,128)(2,1)S(1)} %collective-permute-done.6.other_ref, ...), custom_call_target="tpu_custom_call" | custom-call | flops 6442450944 | bytes 11534336 | tf_op jit(solution)/shard_map/scores/pallas_call | solution.py:85
  54.7 1.6 %collective-permute-done.12.refs_0_.refs_10_.refs_11_ = bf16[512,1024]{1,0:T(8,128)(2,1)S(1)} collective-permute-done((bf16[512,1024]{1,0:T(8,128)(2,1)S(1)}, bf16[512,1024]{1,0:T(8,128)(2,1)S(1)}, u32[]{:S(2)}, u32[]{:S(2)}) %collective-permute-start.12) | collective-permute-done | bytes 1048608 | tf_op jit(solution)/shard_map/ppermute | solution.py:33
  56.3 1.6 %scores.7 = (f32[2,512,512]{2,1,0:T(8,128)S(1)}, f32[4,512]{1,0:T(4,128)S(1)}) custom-call(bf16[512,1024]{1,0:T(8,128)(2,1)S(1)} %share.1.mine_ref, bf16[512,1024]{1,0:T(8,128)(2,1)S(1)} %collective-permute-done.6.other_ref, bf16[512,1024]{1,0:T(8,128)(2,1)S(1)} %collective-permute-done.12.refs_0_.refs_10_.refs_11_), custom_call_target="tpu_custom_call" | custom-call | flops 2147483648 | bytes 5242880 | tf_op jit(solution)/shard_map/scores/pallas_call | solution.py:85
  58.1 1.6 %scores.8 = (f32[2,512,512]{2,1,0:T(8,128)S(1)}, f32[4,512]{1,0:T(4,128)S(1)}) custom-call(bf16[512,1024]{1,0:T(8,128)(2,1)S(1)} %share.1.mine_ref, bf16[512,1024]{1,0:T(8,128)(2,1)S(1)} %collective-permute-done.6.other_ref, bf16[512,1024]{1,0:T(8,128)(2,1)S(1)} %collective-permute-done.11.refs_0_.refs_13_.refs_14_), custom_call_target="tpu_custom_call" | custom-call | flops 2147483648 | bytes 5242880 | tf_op jit(solution)/shard_map/scores/pallas_call | solution.py:85
  60.4 1.6 %scores.9 = (f32[2,512,512]{2,1,0:T(8,128)S(1)}, f32[4,512]{1,0:T(4,128)S(1)}) custom-call(bf16[512,1024]{1,0:T(8,128)(2,1)S(1)} %share.1.mine_ref, bf16[512,1024]{1,0:T(8,128)(2,1)S(1)} %collective-permute-done.6.other_ref, bf16[512,1024]{1,0:T(8,128)(2,1)S(1)} %collective-permute-done.10.refs_0_.refs_12_.refs_13_), custom_call_target="tpu_custom_call" | custom-call | flops 2147483648 | bytes 5242880 | tf_op jit(solution)/shard_map/scores/pallas_call | solution.py:85
  62.0 7.3 %collective-permute-done.9.refs_0_.refs_15_.refs_1_ = bf16[512,1024]{1,0:T(8,128)(2,1)S(1)} collective-permute-done((bf16[512,1024]{1,0:T(8,128)(2,1)S(1)}, bf16[512,1024]{1,0:T(8,128)(2,1)S(1)}, u32[]{:S(2)}, u32[]{:S(2)}) %collective-permute-start.9) | collective-permute-done | bytes 1048608 | tf_op jit(solution)/shard_map/ppermute | solution.py:33
  69.3 1.6 %scores.10 = (f32[2,512,512]{2,1,0:T(8,128)S(1)}, f32[4,512]{1,0:T(4,128)S(1)}) custom-call(bf16[512,1024]{1,0:T(8,128)(2,1)S(1)} %share.1.mine_ref, bf16[512,1024]{1,0:T(8,128)(2,1)S(1)} %collective-permute-done.6.other_ref, bf16[512,1024]{1,0:T(8,128)(2,1)S(1)} %collective-permute-done.9.refs_0_.refs_15_.refs_1_), custom_call_target="tpu_custom_call" | custom-call | flops 2147483648 | bytes 5242880 | tf_op jit(solution)/shard_map/scores/pallas_call | solution.py:85
  71.0 1.6 %scores.11 = (f32[2,512,512]{2,1,0:T(8,128)S(1)}, f32[4,512]{1,0:T(4,128)S(1)}) custom-call(bf16[512,1024]{1,0:T(8,128)(2,1)S(1)} %share.1.mine_ref, bf16[512,1024]{1,0:T(8,128)(2,1)S(1)} %collective-permute-done.6.other_ref, bf16[512,1024]{1,0:T(8,128)(2,1)S(1)} %collective-permute-done.8.refs_0_.refs_9_.refs_10_), custom_call_target="tpu_custom_call" | custom-call | flops 2147483648 | bytes 5242880 | tf_op jit(solution)/shard_map/scores/pallas_call | solution.py:85
  72.6 1.1 %first.1 = (f32[16,8,640]{2,1,0:T(8,128)S(1)}, f32[2,4096]{1,0:T(2,128)S(1)}) custom-call(s32[5]{0:T(128)S(1)} %stack.32.spot_ref, f32[1,128]{1,0:T(1,128)S(1)} %reshape_tile.3.ids_ref, f32[4,1536]{1,0:T(4,128)S(1)} %get-tuple-element.45.refs_0_, f32[4,512]{1,0:T(4,128)S(1)} %get-tuple-element.55.refs_1_, f32[4,512]{1,0:T(4,128)S(1)} %get-tuple-element.47.refs_2_, ...), custom_call_target="tpu_custom_call" | custom-call | tf_op jit(solution)/shard_map/first/pallas_call | solution.py:351
  73.7 12.4 %all_to_all.5.all_ref = f32[16,8,640]{2,1,0:T(8,128)S(1)} all-to-all(f32[16,8,640]{2,1,0:T(8,128)S(1)} %get-tuple-element.56), channel_id=1, replica_groups={{0,8,64,72,2,10,66,74,4,12,68,76,6,14,70,78},{16,24,80,88,18,26,82,90,2..., dimensions={0} | all-to-all | bytes 655360 | tf_op jit(solution)/shard_map/all_to_all | solution.py:363
  86.2 1.4 %collective-permute-start.13 = (f32[8,640]{1,0:T(8,128)S(1)}, f32[8,640]{1,0:T(8,128)S(1)}, u32[]{:S(2)}, u32[]{:S(2)}) collective-permute-start(f32[8,640]{1,0:T(8,128)S(1)} %plane.1.refs_0_), channel_id=1, source_target_pairs={{48,0},{7,1},{0,16},{23,17},{16,32},{39,33},{32,48},{55,49},{50,2}... | collective-permute-start | bytes 61448 | tf_op jit(solution)/shard_map/ppermute | solution.py:33
  87.5 1.5 %collective-permute-start.14 = (f32[8,640]{1,0:T(8,128)S(1)}, f32[8,640]{1,0:T(8,128)S(1)}, u32[]{:S(2)}, u32[]{:S(2)}) collective-permute-start(f32[8,640]{1,0:T(8,128)S(1)} %plane.1.refs_0_), channel_id=1, source_target_pairs={{32,0},{5,1},{48,16},{21,17},{0,32},{37,33},{16,48},{53,49},{34,2}... | collective-permute-start | bytes 61448 | tf_op jit(solution)/shard_map/ppermute | solution.py:33
  89.1 2.0 %collective-permute-start.15 = (f32[8,640]{1,0:T(8,128)S(1)}, f32[8,640]{1,0:T(8,128)S(1)}, u32[]{:S(2)}, u32[]{:S(2)}) collective-permute-start(f32[8,640]{1,0:T(8,128)S(1)} %plane.1.refs_0_), channel_id=1, source_target_pairs={{16,0},{3,1},{32,16},{19,17},{48,32},{35,33},{0,48},{51,49},{18,2}... | collective-permute-start | bytes 61448 | tf_op jit(solution)/shard_map/ppermute | solution.py:33
  92.0 1.0 merge.1
  93.0 4.5 %sums.3 = f32[512,1152]{1,0:T(8,128)S(1)} custom-call(f32[1,4096]{1,0:T(1,128)S(1)} %get-tuple-element.57.lse_ref, f32[2,4096]{1,0:T(2,128)S(1)} %get-tuple-element.58.top_ref, f32[2,512,512]{2,1,0:T(8,128)S(1)} %get-tuple-element.59.refs_0_, f32[2,512,512]{2,1,0:T(8,128)S(1)} %get-tuple-element.60.refs_1_, f32[2,512,512]{2,1,0:T(8,128)S(1)} %get-tuple-element.61.refs_2_, ...), custom_call_target="tpu_custom_call" | custom-call | flops 4294967296 | bytes 18874368 | tf_op jit(solution)/shard_map/sums/pallas_call | solution.py:227
  97.5 5.3 %collective-permute-start.16 = (f32[512,1152]{1,0:T(8,128)S(1)}, f32[512,1152]{1,0:T(8,128)S(1)}, u32[]{:S(2)}, u32[]{:S(2)}) collective-permute-start(f32[512,1152]{1,0:T(8,128)S(1)} %sums.3), channel_id=1, source_target_pairs={{0,1},{1,0},{2,3},{3,2},{4,5},{5,4},{6,7},{7,6},{8,9},{9,8},{10,11... | collective-permute-start | bytes 7077896 | tf_op jit(solution)/shard_map/ppermute | solution.py:38
  103.0 4.0 %sums.2.ours_ref = f32[512,1152]{1,0:T(8,128)S(1)} custom-call(f32[1,4096]{1,0:T(1,128)S(1)} %get-tuple-element.57.lse_ref, f32[2,4096]{1,0:T(2,128)S(1)} %get-tuple-element.58.top_ref, f32[2,512,512]{2,1,0:T(8,128)S(1)} %get-tuple-element.59.refs_0_, f32[2,512,512]{2,1,0:T(8,128)S(1)} %get-tuple-element.60.refs_1_, ...), custom_call_target="tpu_custom_call" | custom-call | flops 3758096384 | bytes 18874368 | tf_op jit(solution)/shard_map/sums/pallas_call | solution.py:227
  107.1 3.1 %final.1 = (f32[512,1024]{1,0:T(8,128)}, f32[1,64]{1,0:T(1,128)}) custom-call(s32[2]{0:T(128)S(1)} %pad_add_fusion.at_ref, f32[1,4096]{1,0:T(1,128)S(1)} %get-tuple-element.57.lse_ref, f32[2,4096]{1,0:T(2,128)S(1)} %get-tuple-element.58.top_ref, f32[512,1152]{1,0:T(8,128)S(1)} %sums.2.ours_ref, f32[512,1152]{1,0:T(8,128)S(1)} %collective-permute-done.16.theirs_ref, ...), custom_call_target="tpu_custom_call" | custom-call | tf_op jit(solution)/shard_map/final/pallas_call | solution.py:386
  (29 shorter events, 7.1 us)
Async XLA Ops:
  0.6 6.6 %collective-permute-start = (bf16[64,1024]{1,0:T(8,128)(2,1)}, bf16[64,1024]{1,0:T(8,128)(2,1)S(1)}, u32[]{:S(2)}, u32[]{:S(2)}) collective-permute-start(bf16[64,1024]{1,0:T(8,128)(2,1)} %refs_0_.1), channel_id=1, source_target_pairs={{64,0},{65,1},{80,16},{81,17},{96,32},{97,33},{112,48},{113,49},{6... | collective-permute-start | bytes 393224 | tf_op jit(solution)/shard_map/ppermute | solution.py:33
  4.3 6.2 %collective-permute-start.1 = (bf16[64,1024]{1,0:T(8,128)(2,1)}, bf16[64,1024]{1,0:T(8,128)(2,1)S(1)}, u32[]{:S(2)}, u32[]{:S(2)}) collective-permute-start(bf16[64,1024]{1,0:T(8,128)(2,1)} %refs_0_.1), channel_id=1, source_target_pairs={{8,0},{9,1},{24,16},{25,17},{40,32},{41,33},{56,48},{57,49},{10,2}... | collective-permute-start | bytes 393224 | tf_op jit(solution)/shard_map/ppermute | solution.py:33
  5.1 5.4 %collective-permute-start.2 = (bf16[64,1024]{1,0:T(8,128)(2,1)}, bf16[64,1024]{1,0:T(8,128)(2,1)S(1)}, u32[]{:S(2)}, u32[]{:S(2)}) collective-permute-start(bf16[64,1024]{1,0:T(8,128)(2,1)} %refs_0_.1), channel_id=1, source_target_pairs={{72,0},{73,1},{88,16},{89,17},{104,32},{105,33},{120,48},{121,49},... | collective-permute-start | bytes 393224 | tf_op jit(solution)/shard_map/ppermute | solution.py:33
  10.5 0.9 copy-start.1
  11.5 10.7 %collective-permute-start.3 = (bf16[256,1024]{1,0:T(8,128)(2,1)S(1)}, bf16[256,1024]{1,0:T(8,128)(2,1)S(1)}, u32[]{:S(2)}, u32[]{:S(2)}) collective-permute-start(bf16[256,1024]{1,0:T(8,128)(2,1)S(1)} %join.1.refs_0_), channel_id=1, source_target_pairs={{4,0},{33,1},{20,16},{49,17},{36,32},{1,33},{52,48},{17,49},{6,2},... | collective-permute-start | bytes 1572872 | tf_op jit(solution)/shard_map/ppermute | solution.py:33
  15.2 13.3 %collective-permute-start.4 = (bf16[256,1024]{1,0:T(8,128)(2,1)S(1)}, bf16[256,1024]{1,0:T(8,128)(2,1)S(1)}, u32[]{:S(2)}, u32[]{:S(2)}) collective-permute-start(bf16[256,1024]{1,0:T(8,128)(2,1)S(1)} %join.1.refs_0_), channel_id=1, source_target_pairs={{2,0},{17,1},{18,16},{33,17},{34,32},{49,33},{50,48},{1,49},{4,2},... | collective-permute-start | bytes 1572872 | tf_op jit(solution)/shard_map/ppermute | solution.py:33
  15.7 12.8 %collective-permute-start.5 = (bf16[256,1024]{1,0:T(8,128)(2,1)S(1)}, bf16[256,1024]{1,0:T(8,128)(2,1)S(1)}, u32[]{:S(2)}, u32[]{:S(2)}) collective-permute-start(bf16[256,1024]{1,0:T(8,128)(2,1)S(1)} %join.1.refs_0_), channel_id=1, source_target_pairs={{6,0},{49,1},{22,16},{1,17},{38,32},{17,33},{54,48},{33,49},{0,2},... | collective-permute-start | bytes 1572872 | tf_op jit(solution)/shard_map/ppermute | solution.py:33
  29.2 15.5 %collective-permute-start.7 = (bf16[512,1024]{1,0:T(8,128)(2,1)S(1)}, bf16[512,1024]{1,0:T(8,128)(2,1)S(1)}, u32[]{:S(2)}, u32[]{:S(2)}) collective-permute-start(bf16[512,1024]{1,0:T(8,128)(2,1)S(1)} %get-tuple-element.43.refs_1_.refs_7_.refs_8_), channel_id=1, source_target_pairs={{32,0},{5,1},{48,16},{21,17},{0,32},{37,33},{16,48},{53,49},{34,2}... | collective-permute-start | bytes 3145736 | tf_op jit(solution)/shard_map/ppermute | solution.py:33
  32.2 3.4 %copy-start = (bf16[4096,1024]{1,0:T(8,128)(2,1)S(1)}, bf16[4096,1024]{1,0:T(8,128)(2,1)}, u32[]{:S(2)}) copy-start(bf16[4096,1024]{1,0:T(8,128)(2,1)} %cents_ref.1) | copy-start | bytes 25165828
  37.5 12.8 %collective-permute-start.6 = (bf16[512,1024]{1,0:T(8,128)(2,1)S(1)}, bf16[512,1024]{1,0:T(8,128)(2,1)S(1)}, u32[]{:S(2)}, u32[]{:S(2)}) collective-permute-start(bf16[512,1024]{1,0:T(8,128)(2,1)S(1)} %share.1.mine_ref), channel_id=1, source_target_pairs={{0,1},{1,0},{2,3},{3,2},{4,5},{5,4},{6,7},{7,6},{8,9},{9,8},{10,11... | collective-permute-start | bytes 3145736 | tf_op jit(solution)/shard_map/ppermute | solution.py:38
  40.6 15.7 %collective-permute-start.12 = (bf16[512,1024]{1,0:T(8,128)(2,1)S(1)}, bf16[512,1024]{1,0:T(8,128)(2,1)S(1)}, u32[]{:S(2)}, u32[]{:S(2)}) collective-permute-start(bf16[512,1024]{1,0:T(8,128)(2,1)S(1)} %get-tuple-element.44.refs_2_.refs_8_.refs_9_), channel_id=1, source_target_pairs={{16,0},{3,1},{32,16},{19,17},{48,32},{35,33},{0,48},{51,49},{18,2}... | collective-permute-start | bytes 3145736 | tf_op jit(solution)/shard_map/ppermute | solution.py:33
  42.9 15.2 %collective-permute-start.11 = (bf16[512,1024]{1,0:T(8,128)(2,1)S(1)}, bf16[512,1024]{1,0:T(8,128)(2,1)S(1)}, u32[]{:S(2)}, u32[]{:S(2)}) collective-permute-start(bf16[512,1024]{1,0:T(8,128)(2,1)S(1)} %get-tuple-element.43.refs_1_.refs_7_.refs_8_), channel_id=1, source_target_pairs={{48,0},{7,1},{0,16},{23,17},{16,32},{39,33},{32,48},{55,49},{50,2}... | collective-permute-start | bytes 3145736 | tf_op jit(solution)/shard_map/ppermute | solution.py:33
  44.7 15.7 %collective-permute-start.10 = (bf16[512,1024]{1,0:T(8,128)(2,1)S(1)}, bf16[512,1024]{1,0:T(8,128)(2,1)S(1)}, u32[]{:S(2)}, u32[]{:S(2)}) collective-permute-start(bf16[512,1024]{1,0:T(8,128)(2,1)S(1)} %collective-permute-done.7.refs_0_.refs_11_.refs_12_), channel_id=1, source_target_pairs={{8,0},{73,1},{24,16},{89,17},{40,32},{105,33},{56,48},{121,49},{10... | collective-permute-start | bytes 3145736 | tf_op jit(solution)/shard_map/ppermute | solution.py:49
  47.9 23.1 %collective-permute-start.8 = (bf16[512,1024]{1,0:T(8,128)(2,1)S(1)}, bf16[512,1024]{1,0:T(8,128)(2,1)S(1)}, u32[]{:S(2)}, u32[]{:S(2)}) collective-permute-start(bf16[512,1024]{1,0:T(8,128)(2,1)S(1)} %get-tuple-element.43.refs_1_.refs_7_.refs_8_), channel_id=1, source_target_pairs={{16,0},{3,1},{32,16},{19,17},{48,32},{35,33},{0,48},{51,49},{18,2}... | collective-permute-start | bytes 3145736 | tf_op jit(solution)/shard_map/ppermute | solution.py:33
  50.4 18.9 %collective-permute-start.9 = (bf16[512,1024]{1,0:T(8,128)(2,1)S(1)}, bf16[512,1024]{1,0:T(8,128)(2,1)S(1)}, u32[]{:S(2)}, u32[]{:S(2)}) collective-permute-start(bf16[512,1024]{1,0:T(8,128)(2,1)S(1)} %get-tuple-element.44.refs_2_.refs_8_.refs_9_), channel_id=1, source_target_pairs={{48,0},{7,1},{0,16},{23,17},{16,32},{39,33},{32,48},{55,49},{50,2}... | collective-permute-start | bytes 3145736 | tf_op jit(solution)/shard_map/ppermute | solution.py:33
  86.2 4.9 %collective-permute-start.13 = (f32[8,640]{1,0:T(8,128)S(1)}, f32[8,640]{1,0:T(8,128)S(1)}, u32[]{:S(2)}, u32[]{:S(2)}) collective-permute-start(f32[8,640]{1,0:T(8,128)S(1)} %plane.1.refs_0_), channel_id=1, source_target_pairs={{48,0},{7,1},{0,16},{23,17},{16,32},{39,33},{32,48},{55,49},{50,2}... | collective-permute-start | bytes 61448 | tf_op jit(solution)/shard_map/ppermute | solution.py:33
  87.5 4.1 %collective-permute-start.14 = (f32[8,640]{1,0:T(8,128)S(1)}, f32[8,640]{1,0:T(8,128)S(1)}, u32[]{:S(2)}, u32[]{:S(2)}) collective-permute-start(f32[8,640]{1,0:T(8,128)S(1)} %plane.1.refs_0_), channel_id=1, source_target_pairs={{32,0},{5,1},{48,16},{21,17},{0,32},{37,33},{16,48},{53,49},{34,2}... | collective-permute-start | bytes 61448 | tf_op jit(solution)/shard_map/ppermute | solution.py:33
  89.1 2.9 %collective-permute-start.15 = (f32[8,640]{1,0:T(8,128)S(1)}, f32[8,640]{1,0:T(8,128)S(1)}, u32[]{:S(2)}, u32[]{:S(2)}) collective-permute-start(f32[8,640]{1,0:T(8,128)S(1)} %plane.1.refs_0_), channel_id=1, source_target_pairs={{16,0},{3,1},{32,16},{19,17},{48,32},{35,33},{0,48},{51,49},{18,2}... | collective-permute-start | bytes 61448 | tf_op jit(solution)/shard_map/ppermute | solution.py:33
  97.5 9.6 %collective-permute-start.16 = (f32[512,1152]{1,0:T(8,128)S(1)}, f32[512,1152]{1,0:T(8,128)S(1)}, u32[]{:S(2)}, u32[]{:S(2)}) collective-permute-start(f32[512,1152]{1,0:T(8,128)S(1)} %sums.3), channel_id=1, source_target_pairs={{0,1},{1,0},{2,3},{3,2},{4,5},{5,4},{6,7},{7,6},{8,9},{9,8},{10,11... | collective-permute-start | bytes 7077896 | tf_op jit(solution)/shard_map/ppermute | solution.py:38
  102.9 4.2 %collective-permute-start.17 = (f32[64,128]{1,0:T(8,128)S(1)}, f32[64,128]{1,0:T(8,128)S(1)}, u32[]{:S(2)}, u32[]{:S(2)}) collective-permute-start(f32[64,128]{1,0:T(8,128)S(1)} %get-tuple-element.67.pack_ref), channel_id=1, source_target_pairs={{0,1},{1,0},{2,3},{3,2},{4,5},{5,4},{6,7},{7,6},{8,9},{9,8},{10,11... | collective-permute-start | bytes 98312 | tf_op jit(solution)/shard_map/ppermute | solution.py:38

commit v16 on v15

--- a/solution.py
+++ b/solution.py
@@ -161,10 +161,13 @@
 
 
 def join_kernel(slots, *refs):
-    *parts, out_ref = refs
-    rows = parts[0].shape[0]
-    for slot, part in zip(slots, parts):
+    own_ref, *parts, out_ref, sem = refs
+    rows = own_ref.shape[0]
+    copy = pltpu.make_async_copy(own_ref, out_ref.at[pl.ds(slots[0] * rows, rows)], sem)
+    copy.start()
+    for slot, part in zip(slots[1:], parts):
         out_ref[slot * rows : (slot + 1) * rows, :] = part[...]
+    copy.wait()
 
 
 def halves_kernel(spot_ref, *refs):
@@ -186,8 +189,9 @@
     return pl.pallas_call(
         functools.partial(join_kernel, slots),
         out_shape=jax.ShapeDtypeStruct(shape, parts[0].dtype),
-        in_specs=[vmem] * len(parts),
+        in_specs=[pl.BlockSpec(memory_space=pltpu.HBM)] + [vmem] * (len(parts) - 1),
         out_specs=vmem,
+        scratch_shapes=[pltpu.SemaphoreType.DMA(())],
         compiler_params=pltpu.CompilerParams(vmem_limit_bytes=8 << 20),
         name="join",
     )(*parts)

time: 111 us -> 111 us (level)
  no operation moved by 1% of the time
where the time goes in v16:
time: 111 us
  starting transfers between devices  34.8 us (31%)
  Pallas kernels  29.1 us (26%)
  waiting for transfers between devices  28.2 us (25%)
  blocking collectives  12.4 us (11%)
  local copies, waits for them, and re-layouts  4.46 us (4%)
    ppermute x14, waiting for transfers between devices, fetch(): return lax.ppermute(value, BOTH, pairs)  27.5 us
    ppermute x14, starting transfers between devices, fetch(): return lax.ppermute(value, BOTH, pairs)  23.1 us
    pallas_call x6, Pallas kernels, scores_call(): pl.pallas_call(functools.partial(scores_kernel, factor, count), out_shape...  12.4 us
    all_to_all x1, blocking collectives, shards(): lax.all_to_all(local, BOTH, split_axis=0, concat_axis=0, tiled=True, axis...  12.4 us
    pallas_call x2, Pallas kernels, sums_call(): pl.pallas_call(functools.partial(sums_kernel, half, count), out_shape=jax...  8.5 us
    ppermute x3, starting transfers between devices, swap_cores(): return lax.ppermute(value, BOTH, pairs)  8.48 us
    unnamed x4, local copies, waits for them, and re-layouts  4.29 us
    ppermute x1, starting transfers between devices, swap_sides(): return lax.ppermute(value, BOTH, pairs)  3.17 us
  transfers between devices with their start and end apart: 18, of which 12 were waited for; matrix products, arithmetic and copies ran while one was open for 1% of the time, Pallas kernels for 15%

profile of v16, /device:TPU:1, one launch (start us, length us, event | category | flops | bytes accessed | tf_op | source)
XLA Modules:
  0.0 110.5 jit_solution(6634942087307283231)
XLA Ops:
  0.6 3.7 %collective-permute-start = (bf16[64,1024]{1,0:T(8,128)(2,1)}, bf16[64,1024]{1,0:T(8,128)(2,1)S(1)}, u32[]{:S(2)}, u32[]{:S(2)}) collective-permute-start(bf16[64,1024]{1,0:T(8,128)(2,1)} %refs_0_.1), channel_id=1, source_target_pairs={{64,0},{65,1},{80,16},{81,17},{96,32},{97,33},{112,48},{113,49},{6... | collective-permute-start | bytes 393224 | tf_op jit(solution)/shard_map/ppermute | solution.py:33
  7.2 3.3 %collective-permute-done.1.refs_2_ = bf16[64,1024]{1,0:T(8,128)(2,1)S(1)} collective-permute-done((bf16[64,1024]{1,0:T(8,128)(2,1)}, bf16[64,1024]{1,0:T(8,128)(2,1)S(1)}, u32[]{:S(2)}, u32[]{:S(2)}) %collective-permute-start.1) | collective-permute-done | bytes 131104 | tf_op jit(solution)/shard_map/ppermute | solution.py:33
  11.6 3.8 %collective-permute-start.3 = (bf16[256,1024]{1,0:T(8,128)(2,1)S(1)}, bf16[256,1024]{1,0:T(8,128)(2,1)S(1)}, u32[]{:S(2)}, u32[]{:S(2)}) collective-permute-start(bf16[256,1024]{1,0:T(8,128)(2,1)S(1)} %join.1.refs_0_), channel_id=1, source_target_pairs={{4,0},{33,1},{20,16},{49,17},{36,32},{1,33},{52,48},{17,49},{6,2},... | collective-permute-start | bytes 1572872 | tf_op jit(solution)/shard_map/ppermute | solution.py:33
  15.8 1.0 collective-permute-start.5
  16.8 5.4 %collective-permute-done.3.refs_1_ = bf16[256,1024]{1,0:T(8,128)(2,1)S(1)} collective-permute-done((bf16[256,1024]{1,0:T(8,128)(2,1)S(1)}, bf16[256,1024]{1,0:T(8,128)(2,1)S(1)}, u32[]{:S(2)}, u32[]{:S(2)}) %collective-permute-start.3) | collective-permute-done | bytes 524320 | tf_op jit(solution)/shard_map/ppermute | solution.py:33
  22.3 6.3 %collective-permute-done.4.refs_2_ = bf16[256,1024]{1,0:T(8,128)(2,1)S(1)} collective-permute-done((bf16[256,1024]{1,0:T(8,128)(2,1)S(1)}, bf16[256,1024]{1,0:T(8,128)(2,1)S(1)}, u32[]{:S(2)}, u32[]{:S(2)}) %collective-permute-start.4) | collective-permute-done | bytes 524320 | tf_op jit(solution)/shard_map/ppermute | solution.py:33
  29.3 3.0 %collective-permute-start.7 = (bf16[512,1024]{1,0:T(8,128)(2,1)S(1)}, bf16[512,1024]{1,0:T(8,128)(2,1)S(1)}, u32[]{:S(2)}, u32[]{:S(2)}) collective-permute-start(bf16[512,1024]{1,0:T(8,128)(2,1)S(1)} %get-tuple-element.43.refs_1_.refs_7_.refs_8_), channel_id=1, source_target_pairs={{32,0},{5,1},{48,16},{21,17},{0,32},{37,33},{16,48},{53,49},{34,2}... | collective-permute-start | bytes 3145736 | tf_op jit(solution)/shard_map/ppermute | solution.py:33
  32.3 3.4 %copy-done = bf16[4096,1024]{1,0:T(8,128)(2,1)S(1)} copy-done((bf16[4096,1024]{1,0:T(8,128)(2,1)S(1)}, bf16[4096,1024]{1,0:T(8,128)(2,1)}, u32[]{:S(2)}) %copy-start) | copy-done | bytes 8388632
  35.7 2.0 %share.1.mine_ref = bf16[512,1024]{1,0:T(8,128)(2,1)S(1)} custom-call(s32[2]{0:T(128)S(1)} %pad_add_fusion.at_ref, bf16[4096,1024]{1,0:T(8,128)(2,1)S(1)} %copy-done), custom_call_target="tpu_custom_call" | custom-call | tf_op jit(solution)/shard_map/share/pallas_call | solution.py:331
  37.7 3.0 %collective-permute-start.6 = (bf16[512,1024]{1,0:T(8,128)(2,1)S(1)}, bf16[512,1024]{1,0:T(8,128)(2,1)S(1)}, u32[]{:S(2)}, u32[]{:S(2)}) collective-permute-start(bf16[512,1024]{1,0:T(8,128)(2,1)S(1)} %share.1.mine_ref), channel_id=1, source_target_pairs={{0,1},{1,0},{2,3},{3,2},{4,5},{5,4},{6,7},{7,6},{8,9},{9,8},{10,11... | collective-permute-start | bytes 3145736 | tf_op jit(solution)/shard_map/ppermute | solution.py:38
  40.7 2.3 %collective-permute-start.12 = (bf16[512,1024]{1,0:T(8,128)(2,1)S(1)}, bf16[512,1024]{1,0:T(8,128)(2,1)S(1)}, u32[]{:S(2)}, u32[]{:S(2)}) collective-permute-start(bf16[512,1024]{1,0:T(8,128)(2,1)S(1)} %get-tuple-element.44.refs_2_.refs_8_.refs_9_), channel_id=1, source_target_pairs={{16,0},{3,1},{32,16},{19,17},{48,32},{35,33},{0,48},{51,49},{18,2}... | collective-permute-start | bytes 3145736 | tf_op jit(solution)/shard_map/ppermute | solution.py:33
  43.1 1.8 %collective-permute-done.7.refs_0_.refs_11_.refs_12_ = bf16[512,1024]{1,0:T(8,128)(2,1)S(1)} collective-permute-done((bf16[512,1024]{1,0:T(8,128)(2,1)S(1)}, bf16[512,1024]{1,0:T(8,128)(2,1)S(1)}, u32[]{:S(2)}, u32[]{:S(2)}) %collective-permute-start.7) | collective-permute-done | bytes 1048608 | tf_op jit(solution)/shard_map/ppermute | solution.py:33
  44.8 3.2 %collective-permute-start.10 = (bf16[512,1024]{1,0:T(8,128)(2,1)S(1)}, bf16[512,1024]{1,0:T(8,128)(2,1)S(1)}, u32[]{:S(2)}, u32[]{:S(2)}) collective-permute-start(bf16[512,1024]{1,0:T(8,128)(2,1)S(1)} %collective-permute-done.7.refs_0_.refs_11_.refs_12_), channel_id=1, source_target_pairs={{8,0},{73,1},{24,16},{89,17},{40,32},{105,33},{56,48},{121,49},{10... | collective-permute-start | bytes 3145736 | tf_op jit(solution)/shard_map/ppermute | solution.py:49
  48.0 2.5 %collective-permute-start.8 = (bf16[512,1024]{1,0:T(8,128)(2,1)S(1)}, bf16[512,1024]{1,0:T(8,128)(2,1)S(1)}, u32[]{:S(2)}, u32[]{:S(2)}) collective-permute-start(bf16[512,1024]{1,0:T(8,128)(2,1)S(1)} %get-tuple-element.43.refs_1_.refs_7_.refs_8_), channel_id=1, source_target_pairs={{16,0},{3,1},{32,16},{19,17},{48,32},{35,33},{0,48},{51,49},{18,2}... | collective-permute-start | bytes 3145736 | tf_op jit(solution)/shard_map/ppermute | solution.py:33
  50.5 4.3 %scores.6 = (f32[2,512,512]{2,1,0:T(8,128)S(1)}, f32[2,512,512]{2,1,0:T(8,128)S(1)}, f32[2,512,512]{2,1,0:T(8,128)S(1)}, f32[4,1536]{1,0:T(4,128)S(1)}) custom-call(bf16[512,1024]{1,0:T(8,128)(2,1)S(1)} %share.1.mine_ref, bf16[512,1024]{1,0:T(8,128)(2,1)S(1)} %collective-permute-done.6.other_ref, ...), custom_call_target="tpu_custom_call" | custom-call | flops 6442450944 | bytes 11534336 | tf_op jit(solution)/shard_map/scores/pallas_call | solution.py:85
  54.8 1.6 %collective-permute-done.12.refs_0_.refs_10_.refs_11_ = bf16[512,1024]{1,0:T(8,128)(2,1)S(1)} collective-permute-done((bf16[512,1024]{1,0:T(8,128)(2,1)S(1)}, bf16[512,1024]{1,0:T(8,128)(2,1)S(1)}, u32[]{:S(2)}, u32[]{:S(2)}) %collective-permute-start.12) | collective-permute-done | bytes 1048608 | tf_op jit(solution)/shard_map/ppermute | solution.py:33
  56.4 1.6 %scores.7 = (f32[2,512,512]{2,1,0:T(8,128)S(1)}, f32[4,512]{1,0:T(4,128)S(1)}) custom-call(bf16[512,1024]{1,0:T(8,128)(2,1)S(1)} %share.1.mine_ref, bf16[512,1024]{1,0:T(8,128)(2,1)S(1)} %collective-permute-done.6.other_ref, bf16[512,1024]{1,0:T(8,128)(2,1)S(1)} %collective-permute-done.12.refs_0_.refs_10_.refs_11_), custom_call_target="tpu_custom_call" | custom-call | flops 2147483648 | bytes 5242880 | tf_op jit(solution)/shard_map/scores/pallas_call | solution.py:85
  58.2 1.6 %scores.8 = (f32[2,512,512]{2,1,0:T(8,128)S(1)}, f32[4,512]{1,0:T(4,128)S(1)}) custom-call(bf16[512,1024]{1,0:T(8,128)(2,1)S(1)} %share.1.mine_ref, bf16[512,1024]{1,0:T(8,128)(2,1)S(1)} %collective-permute-done.6.other_ref, bf16[512,1024]{1,0:T(8,128)(2,1)S(1)} %collective-permute-done.11.refs_0_.refs_13_.refs_14_), custom_call_target="tpu_custom_call" | custom-call | flops 2147483648 | bytes 5242880 | tf_op jit(solution)/shard_map/scores/pallas_call | solution.py:85
  60.5 1.6 %scores.9 = (f32[2,512,512]{2,1,0:T(8,128)S(1)}, f32[4,512]{1,0:T(4,128)S(1)}) custom-call(bf16[512,1024]{1,0:T(8,128)(2,1)S(1)} %share.1.mine_ref, bf16[512,1024]{1,0:T(8,128)(2,1)S(1)} %collective-permute-done.6.other_ref, bf16[512,1024]{1,0:T(8,128)(2,1)S(1)} %collective-permute-done.10.refs_0_.refs_12_.refs_13_), custom_call_target="tpu_custom_call" | custom-call | flops 2147483648 | bytes 5242880 | tf_op jit(solution)/shard_map/scores/pallas_call | solution.py:85
  62.1 7.3 %collective-permute-done.9.refs_0_.refs_15_.refs_1_ = bf16[512,1024]{1,0:T(8,128)(2,1)S(1)} collective-permute-done((bf16[512,1024]{1,0:T(8,128)(2,1)S(1)}, bf16[512,1024]{1,0:T(8,128)(2,1)S(1)}, u32[]{:S(2)}, u32[]{:S(2)}) %collective-permute-start.9) | collective-permute-done | bytes 1048608 | tf_op jit(solution)/shard_map/ppermute | solution.py:33
  69.5 1.6 %scores.10 = (f32[2,512,512]{2,1,0:T(8,128)S(1)}, f32[4,512]{1,0:T(4,128)S(1)}) custom-call(bf16[512,1024]{1,0:T(8,128)(2,1)S(1)} %share.1.mine_ref, bf16[512,1024]{1,0:T(8,128)(2,1)S(1)} %collective-permute-done.6.other_ref, bf16[512,1024]{1,0:T(8,128)(2,1)S(1)} %collective-permute-done.9.refs_0_.refs_15_.refs_1_), custom_call_target="tpu_custom_call" | custom-call | flops 2147483648 | bytes 5242880 | tf_op jit(solution)/shard_map/scores/pallas_call | solution.py:85
  71.1 1.6 %scores.11 = (f32[2,512,512]{2,1,0:T(8,128)S(1)}, f32[4,512]{1,0:T(4,128)S(1)}) custom-call(bf16[512,1024]{1,0:T(8,128)(2,1)S(1)} %share.1.mine_ref, bf16[512,1024]{1,0:T(8,128)(2,1)S(1)} %collective-permute-done.6.other_ref, bf16[512,1024]{1,0:T(8,128)(2,1)S(1)} %collective-permute-done.8.refs_0_.refs_9_.refs_10_), custom_call_target="tpu_custom_call" | custom-call | flops 2147483648 | bytes 5242880 | tf_op jit(solution)/shard_map/scores/pallas_call | solution.py:85
  72.7 1.1 %first.1 = (f32[16,8,640]{2,1,0:T(8,128)S(1)}, f32[2,4096]{1,0:T(2,128)S(1)}) custom-call(s32[5]{0:T(128)S(1)} %stack.32.spot_ref, f32[1,128]{1,0:T(1,128)S(1)} %reshape_tile.3.ids_ref, f32[4,1536]{1,0:T(4,128)S(1)} %get-tuple-element.45.refs_0_, f32[4,512]{1,0:T(4,128)S(1)} %get-tuple-element.55.refs_1_, f32[4,512]{1,0:T(4,128)S(1)} %get-tuple-element.47.refs_2_, ...), custom_call_target="tpu_custom_call" | custom-call | tf_op jit(solution)/shard_map/first/pallas_call | solution.py:355
  73.9 12.4 %all_to_all.5.all_ref = f32[16,8,640]{2,1,0:T(8,128)S(1)} all-to-all(f32[16,8,640]{2,1,0:T(8,128)S(1)} %get-tuple-element.56), channel_id=1, replica_groups={{0,8,64,72,2,10,66,74,4,12,68,76,6,14,70,78},{16,24,80,88,18,26,82,90,2..., dimensions={0} | all-to-all | bytes 655360 | tf_op jit(solution)/shard_map/all_to_all | solution.py:367
  86.3 1.4 %collective-permute-start.13 = (f32[8,640]{1,0:T(8,128)S(1)}, f32[8,640]{1,0:T(8,128)S(1)}, u32[]{:S(2)}, u32[]{:S(2)}) collective-permute-start(f32[8,640]{1,0:T(8,128)S(1)} %plane.1.refs_0_), channel_id=1, source_target_pairs={{48,0},{7,1},{0,16},{23,17},{16,32},{39,33},{32,48},{55,49},{50,2}... | collective-permute-start | bytes 61448 | tf_op jit(solution)/shard_map/ppermute | solution.py:33
  87.7 1.6 %collective-permute-start.14 = (f32[8,640]{1,0:T(8,128)S(1)}, f32[8,640]{1,0:T(8,128)S(1)}, u32[]{:S(2)}, u32[]{:S(2)}) collective-permute-start(f32[8,640]{1,0:T(8,128)S(1)} %plane.1.refs_0_), channel_id=1, source_target_pairs={{32,0},{5,1},{48,16},{21,17},{0,32},{37,33},{16,48},{53,49},{34,2}... | collective-permute-start | bytes 61448 | tf_op jit(solution)/shard_map/ppermute | solution.py:33
  89.2 2.0 %collective-permute-start.15 = (f32[8,640]{1,0:T(8,128)S(1)}, f32[8,640]{1,0:T(8,128)S(1)}, u32[]{:S(2)}, u32[]{:S(2)}) collective-permute-start(f32[8,640]{1,0:T(8,128)S(1)} %plane.1.refs_0_), channel_id=1, source_target_pairs={{16,0},{3,1},{32,16},{19,17},{48,32},{35,33},{0,48},{51,49},{18,2}... | collective-permute-start | bytes 61448 | tf_op jit(solution)/shard_map/ppermute | solution.py:33
  92.1 1.0 merge.1
  93.2 4.5 %sums.3 = f32[512,1152]{1,0:T(8,128)S(1)} custom-call(f32[1,4096]{1,0:T(1,128)S(1)} %get-tuple-element.57.lse_ref, f32[2,4096]{1,0:T(2,128)S(1)} %get-tuple-element.58.top_ref, f32[2,512,512]{2,1,0:T(8,128)S(1)} %get-tuple-element.59.refs_0_, f32[2,512,512]{2,1,0:T(8,128)S(1)} %get-tuple-element.60.refs_1_, f32[2,512,512]{2,1,0:T(8,128)S(1)} %get-tuple-element.61.refs_2_, ...), custom_call_target="tpu_custom_call" | custom-call | flops 4294967296 | bytes 18874368 | tf_op jit(solution)/shard_map/sums/pallas_call | solution.py:231
  97.7 5.3 %collective-permute-start.16 = (f32[512,1152]{1,0:T(8,128)S(1)}, f32[512,1152]{1,0:T(8,128)S(1)}, u32[]{:S(2)}, u32[]{:S(2)}) collective-permute-start(f32[512,1152]{1,0:T(8,128)S(1)} %sums.3), channel_id=1, source_target_pairs={{0,1},{1,0},{2,3},{3,2},{4,5},{5,4},{6,7},{7,6},{8,9},{9,8},{10,11... | collective-permute-start | bytes 7077896 | tf_op jit(solution)/shard_map/ppermute | solution.py:38
  103.1 4.0 %sums.2.ours_ref = f32[512,1152]{1,0:T(8,128)S(1)} custom-call(f32[1,4096]{1,0:T(1,128)S(1)} %get-tuple-element.57.lse_ref, f32[2,4096]{1,0:T(2,128)S(1)} %get-tuple-element.58.top_ref, f32[2,512,512]{2,1,0:T(8,128)S(1)} %get-tuple-element.59.refs_0_, f32[2,512,512]{2,1,0:T(8,128)S(1)} %get-tuple-element.60.refs_1_, ...), custom_call_target="tpu_custom_call" | custom-call | flops 3758096384 | bytes 18874368 | tf_op jit(solution)/shard_map/sums/pallas_call | solution.py:231
  107.2 3.1 %final.1 = (f32[512,1024]{1,0:T(8,128)}, f32[1,64]{1,0:T(1,128)}) custom-call(s32[2]{0:T(128)S(1)} %pad_add_fusion.at_ref, f32[1,4096]{1,0:T(1,128)S(1)} %get-tuple-element.57.lse_ref, f32[2,4096]{1,0:T(2,128)S(1)} %get-tuple-element.58.top_ref, f32[512,1152]{1,0:T(8,128)S(1)} %sums.2.ours_ref, f32[512,1152]{1,0:T(8,128)S(1)} %collective-permute-done.16.theirs_ref, ...), custom_call_target="tpu_custom_call" | custom-call | tf_op jit(solution)/shard_map/final/pallas_call | solution.py:390
  (29 shorter events, 7.2 us)
Async XLA Ops:
  0.6 6.6 %collective-permute-start = (bf16[64,1024]{1,0:T(8,128)(2,1)}, bf16[64,1024]{1,0:T(8,128)(2,1)S(1)}, u32[]{:S(2)}, u32[]{:S(2)}) collective-permute-start(bf16[64,1024]{1,0:T(8,128)(2,1)} %refs_0_.1), channel_id=1, source_target_pairs={{64,0},{65,1},{80,16},{81,17},{96,32},{97,33},{112,48},{113,49},{6... | collective-permute-start | bytes 393224 | tf_op jit(solution)/shard_map/ppermute | solution.py:33
  4.3 6.2 %collective-permute-start.1 = (bf16[64,1024]{1,0:T(8,128)(2,1)}, bf16[64,1024]{1,0:T(8,128)(2,1)S(1)}, u32[]{:S(2)}, u32[]{:S(2)}) collective-permute-start(bf16[64,1024]{1,0:T(8,128)(2,1)} %refs_0_.1), channel_id=1, source_target_pairs={{8,0},{9,1},{24,16},{25,17},{40,32},{41,33},{56,48},{57,49},{10,2}... | collective-permute-start | bytes 393224 | tf_op jit(solution)/shard_map/ppermute | solution.py:33
  5.1 5.4 %collective-permute-start.2 = (bf16[64,1024]{1,0:T(8,128)(2,1)}, bf16[64,1024]{1,0:T(8,128)(2,1)S(1)}, u32[]{:S(2)}, u32[]{:S(2)}) collective-permute-start(bf16[64,1024]{1,0:T(8,128)(2,1)} %refs_0_.1), channel_id=1, source_target_pairs={{72,0},{73,1},{88,16},{89,17},{104,32},{105,33},{120,48},{121,49},... | collective-permute-start | bytes 393224 | tf_op jit(solution)/shard_map/ppermute | solution.py:33
  10.5 0.9 copy-start.1
  11.6 10.7 %collective-permute-start.3 = (bf16[256,1024]{1,0:T(8,128)(2,1)S(1)}, bf16[256,1024]{1,0:T(8,128)(2,1)S(1)}, u32[]{:S(2)}, u32[]{:S(2)}) collective-permute-start(bf16[256,1024]{1,0:T(8,128)(2,1)S(1)} %join.1.refs_0_), channel_id=1, source_target_pairs={{4,0},{33,1},{20,16},{49,17},{36,32},{1,33},{52,48},{17,49},{6,2},... | collective-permute-start | bytes 1572872 | tf_op jit(solution)/shard_map/ppermute | solution.py:33
  15.4 13.3 %collective-permute-start.4 = (bf16[256,1024]{1,0:T(8,128)(2,1)S(1)}, bf16[256,1024]{1,0:T(8,128)(2,1)S(1)}, u32[]{:S(2)}, u32[]{:S(2)}) collective-permute-start(bf16[256,1024]{1,0:T(8,128)(2,1)S(1)} %join.1.refs_0_), channel_id=1, source_target_pairs={{2,0},{17,1},{18,16},{33,17},{34,32},{49,33},{50,48},{1,49},{4,2},... | collective-permute-start | bytes 1572872 | tf_op jit(solution)/shard_map/ppermute | solution.py:33
  15.8 12.8 %collective-permute-start.5 = (bf16[256,1024]{1,0:T(8,128)(2,1)S(1)}, bf16[256,1024]{1,0:T(8,128)(2,1)S(1)}, u32[]{:S(2)}, u32[]{:S(2)}) collective-permute-start(bf16[256,1024]{1,0:T(8,128)(2,1)S(1)} %join.1.refs_0_), channel_id=1, source_target_pairs={{6,0},{49,1},{22,16},{1,17},{38,32},{17,33},{54,48},{33,49},{0,2},... | collective-permute-start | bytes 1572872 | tf_op jit(solution)/shard_map/ppermute | solution.py:33
  29.3 15.5 %collective-permute-start.7 = (bf16[512,1024]{1,0:T(8,128)(2,1)S(1)}, bf16[512,1024]{1,0:T(8,128)(2,1)S(1)}, u32[]{:S(2)}, u32[]{:S(2)}) collective-permute-start(bf16[512,1024]{1,0:T(8,128)(2,1)S(1)} %get-tuple-element.43.refs_1_.refs_7_.refs_8_), channel_id=1, source_target_pairs={{32,0},{5,1},{48,16},{21,17},{0,32},{37,33},{16,48},{53,49},{34,2}... | collective-permute-start | bytes 3145736 | tf_op jit(solution)/shard_map/ppermute | solution.py:33
  32.3 3.4 %copy-start = (bf16[4096,1024]{1,0:T(8,128)(2,1)S(1)}, bf16[4096,1024]{1,0:T(8,128)(2,1)}, u32[]{:S(2)}) copy-start(bf16[4096,1024]{1,0:T(8,128)(2,1)} %cents_ref.1) | copy-start | bytes 25165828
  37.7 12.8 %collective-permute-start.6 = (bf16[512,1024]{1,0:T(8,128)(2,1)S(1)}, bf16[512,1024]{1,0:T(8,128)(2,1)S(1)}, u32[]{:S(2)}, u32[]{:S(2)}) collective-permute-start(bf16[512,1024]{1,0:T(8,128)(2,1)S(1)} %share.1.mine_ref), channel_id=1, source_target_pairs={{0,1},{1,0},{2,3},{3,2},{4,5},{5,4},{6,7},{7,6},{8,9},{9,8},{10,11... | collective-permute-start | bytes 3145736 | tf_op jit(solution)/shard_map/ppermute | solution.py:38
  40.7 15.7 %collective-permute-start.12 = (bf16[512,1024]{1,0:T(8,128)(2,1)S(1)}, bf16[512,1024]{1,0:T(8,128)(2,1)S(1)}, u32[]{:S(2)}, u32[]{:S(2)}) collective-permute-start(bf16[512,1024]{1,0:T(8,128)(2,1)S(1)} %get-tuple-element.44.refs_2_.refs_8_.refs_9_), channel_id=1, source_target_pairs={{16,0},{3,1},{32,16},{19,17},{48,32},{35,33},{0,48},{51,49},{18,2}... | collective-permute-start | bytes 3145736 | tf_op jit(solution)/shard_map/ppermute | solution.py:33
  43.1 15.2 %collective-permute-start.11 = (bf16[512,1024]{1,0:T(8,128)(2,1)S(1)}, bf16[512,1024]{1,0:T(8,128)(2,1)S(1)}, u32[]{:S(2)}, u32[]{:S(2)}) collective-permute-start(bf16[512,1024]{1,0:T(8,128)(2,1)S(1)} %get-tuple-element.43.refs_1_.refs_7_.refs_8_), channel_id=1, source_target_pairs={{48,0},{7,1},{0,16},{23,17},{16,32},{39,33},{32,48},{55,49},{50,2}... | collective-permute-start | bytes 3145736 | tf_op jit(solution)/shard_map/ppermute | solution.py:33
  44.8 15.7 %collective-permute-start.10 = (bf16[512,1024]{1,0:T(8,128)(2,1)S(1)}, bf16[512,1024]{1,0:T(8,128)(2,1)S(1)}, u32[]{:S(2)}, u32[]{:S(2)}) collective-permute-start(bf16[512,1024]{1,0:T(8,128)(2,1)S(1)} %collective-permute-done.7.refs_0_.refs_11_.refs_12_), channel_id=1, source_target_pairs={{8,0},{73,1},{24,16},{89,17},{40,32},{105,33},{56,48},{121,49},{10... | collective-permute-start | bytes 3145736 | tf_op jit(solution)/shard_map/ppermute | solution.py:49
  48.0 23.1 %collective-permute-start.8 = (bf16[512,1024]{1,0:T(8,128)(2,1)S(1)}, bf16[512,1024]{1,0:T(8,128)(2,1)S(1)}, u32[]{:S(2)}, u32[]{:S(2)}) collective-permute-start(bf16[512,1024]{1,0:T(8,128)(2,1)S(1)} %get-tuple-element.43.refs_1_.refs_7_.refs_8_), channel_id=1, source_target_pairs={{16,0},{3,1},{32,16},{19,17},{48,32},{35,33},{0,48},{51,49},{18,2}... | collective-permute-start | bytes 3145736 | tf_op jit(solution)/shard_map/ppermute | solution.py:33
  50.5 18.9 %collective-permute-start.9 = (bf16[512,1024]{1,0:T(8,128)(2,1)S(1)}, bf16[512,1024]{1,0:T(8,128)(2,1)S(1)}, u32[]{:S(2)}, u32[]{:S(2)}) collective-permute-start(bf16[512,1024]{1,0:T(8,128)(2,1)S(1)} %get-tuple-element.44.refs_2_.refs_8_.refs_9_), channel_id=1, source_target_pairs={{48,0},{7,1},{0,16},{23,17},{16,32},{39,33},{32,48},{55,49},{50,2}... | collective-permute-start | bytes 3145736 | tf_op jit(solution)/shard_map/ppermute | solution.py:33
  86.3 4.9 %collective-permute-start.13 = (f32[8,640]{1,0:T(8,128)S(1)}, f32[8,640]{1,0:T(8,128)S(1)}, u32[]{:S(2)}, u32[]{:S(2)}) collective-permute-start(f32[8,640]{1,0:T(8,128)S(1)} %plane.1.refs_0_), channel_id=1, source_target_pairs={{48,0},{7,1},{0,16},{23,17},{16,32},{39,33},{32,48},{55,49},{50,2}... | collective-permute-start | bytes 61448 | tf_op jit(solution)/shard_map/ppermute | solution.py:33
  87.7 4.1 %collective-permute-start.14 = (f32[8,640]{1,0:T(8,128)S(1)}, f32[8,640]{1,0:T(8,128)S(1)}, u32[]{:S(2)}, u32[]{:S(2)}) collective-permute-start(f32[8,640]{1,0:T(8,128)S(1)} %plane.1.refs_0_), channel_id=1, source_target_pairs={{32,0},{5,1},{48,16},{21,17},{0,32},{37,33},{16,48},{53,49},{34,2}... | collective-permute-start | bytes 61448 | tf_op jit(solution)/shard_map/ppermute | solution.py:33
  89.2 2.9 %collective-permute-start.15 = (f32[8,640]{1,0:T(8,128)S(1)}, f32[8,640]{1,0:T(8,128)S(1)}, u32[]{:S(2)}, u32[]{:S(2)}) collective-permute-start(f32[8,640]{1,0:T(8,128)S(1)} %plane.1.refs_0_), channel_id=1, source_target_pairs={{16,0},{3,1},{32,16},{19,17},{48,32},{35,33},{0,48},{51,49},{18,2}... | collective-permute-start | bytes 61448 | tf_op jit(solution)/shard_map/ppermute | solution.py:33
  97.7 9.6 %collective-permute-start.16 = (f32[512,1152]{1,0:T(8,128)S(1)}, f32[512,1152]{1,0:T(8,128)S(1)}, u32[]{:S(2)}, u32[]{:S(2)}) collective-permute-start(f32[512,1152]{1,0:T(8,128)S(1)} %sums.3), channel_id=1, source_target_pairs={{0,1},{1,0},{2,3},{3,2},{4,5},{5,4},{6,7},{7,6},{8,9},{9,8},{10,11... | collective-permute-start | bytes 7077896 | tf_op jit(solution)/shard_map/ppermute | solution.py:38
  103.0 4.2 %collective-permute-start.17 = (f32[64,128]{1,0:T(8,128)S(1)}, f32[64,128]{1,0:T(8,128)S(1)}, u32[]{:S(2)}, u32[]{:S(2)}) collective-permute-start(f32[64,128]{1,0:T(8,128)S(1)} %get-tuple-element.67.pack_ref), channel_id=1, source_target_pairs={{0,1},{1,0},{2,3},{3,2},{4,5},{5,4},{6,7},{7,6},{8,9},{9,8},{10,11... | collective-permute-start | bytes 98312 | tf_op jit(solution)/shard_map/ppermute | solution.py:38
